TPU v7x, 32 devices: a whole 2x2x4 slice. The times are simulated.
32 devices in a mesh: dp: 4 (over y, x), expert: 8 (over z, core).
Axes of the slice: x: 2, y: 2, z: 4, core: 2. Of those that a mesh axis runs over, the one named last changes fastest.
Arguments:
- tokens: bfloat16 [4096, 2048], P(('dp', 'expert')), may hold values from -6 to 6
- tangent: bfloat16 [4096, 2048], P(('dp', 'expert')), may hold values from -16 to 16
- routes: int32 [4096, 4], P(('dp', 'expert')), may hold values from 0 to 7, all different within a row; in each aligned block of 128 rows (0 to 127, 128 to 255, ...) at most 72 rows name the same one
- gates: float32 [4096, 4], P(('dp', 'expert')), may hold values from 0.05 to 0.5
- w_gate: bfloat16 [8, 2048, 768], P('expert'), may hold values from -0.125 to 0.125
- w_up: bfloat16 [8, 2048, 768], P('expert'), may hold values from -0.125 to 0.125
- w_down: bfloat16 [8, 768, 2048], P('expert'), may hold values from -0.21875 to 0.21875
Outputs:
- product: float32 [4096, 2048], P(('dp', 'expert'))
Inputs may be any that keep to these rules, and one draw needn't show every extreme that they name: `routes`: among the 512 pairs of the rows of one device, no expert is named more than 72 times, a bound that some block reaches.
All inputs are finite; a program needn't handle non-finite values.
Results may differ from a plain program's by a relative error of at most 0.005.
Values may be sent and summed in bfloat16 or wider, within the bound.
No kernel may reach another device: no remote copies, remote signals or barrier semaphores. Data moves between devices by JAX's collectives and lax.ppermute only.
A program may use at most 128 MiB of HBM per device.

v0:
```python
import jax
import jax.numpy as jnp
from jax import lax
from jax.sharding import PartitionSpec as P


def owner_states(x_rows, gate_w, up_w):
    pre_a = jnp.dot(x_rows, gate_w, preferred_element_type=jnp.float32)
    pre_b = jnp.dot(x_rows, up_w, preferred_element_type=jnp.float32)
    sigma = jax.nn.sigmoid(pre_a)
    act = pre_a * sigma
    slope = sigma * (1.0 + pre_a * (1.0 - sigma))
    return (pre_b, act, slope)


def shards(tokens, tangent, routes, gates, w_gate, w_up, w_down):
    model_width = tokens.shape[1]
    token_count = tokens.shape[0]
    top_k = routes.shape[1]
    owners = lax.axis_size("expert")
    expert_total = owners * w_gate.shape[0]
    capacity = max(2, token_count * top_k * 9 // (8 * expert_total))
    slot_total = expert_total * capacity
    pair_count = token_count * top_k
    gate_w = w_gate[0]
    up_w = w_up[0]
    down_w = w_down[0]
    flat_routes = routes.reshape(pair_count)
    onehot = (flat_routes[:, None] == jnp.arange(expert_total, dtype=jnp.int32)[None, :]).astype(
        jnp.int32
    )
    before = jnp.cumsum(onehot, axis=0) - onehot
    slot_of = jnp.sum(before * onehot, axis=1)
    slot_index = flat_routes * capacity + slot_of
    slot_match = slot_index[None, :] == jnp.arange(slot_total, dtype=jnp.int32)[:, None]
    filled = jnp.any(slot_match, axis=1)
    pair_token = jnp.arange(pair_count, dtype=jnp.int32) // top_k
    source_token = jnp.sum(jnp.where(slot_match, pair_token[None, :], 0), axis=1)
    source_gate = jnp.sum(
        jnp.where(slot_match, gates.reshape(pair_count)[None, :], jnp.float32(0.0)), axis=1
    )
    keep_mask = filled.astype(jnp.bfloat16)[:, None]
    send_x = (jnp.take(tokens, source_token, axis=0) * keep_mask).reshape(
        owners, capacity, model_width
    )
    send_v = (jnp.take(tangent, source_token, axis=0) * keep_mask).reshape(
        owners, capacity, model_width
    )
    arrived = (
        lax.all_to_all(send_x, "expert", split_axis=0, concat_axis=0, tiled=True),
        lax.all_to_all(send_v, "expert", split_axis=0, concat_axis=0, tiled=True),
    )
    x_rows = arrived[0].reshape(slot_total, model_width)
    v_rows = arrived[1].reshape(slot_total, model_width)
    pre_b, act, slope = owner_states(x_rows, gate_w, up_w)
    tan_a = jnp.dot(v_rows, gate_w, preferred_element_type=jnp.float32)
    tan_b = jnp.dot(v_rows, up_w, preferred_element_type=jnp.float32)
    hidden_tangent = (slope * tan_a * pre_b + act * tan_b).astype(jnp.bfloat16)
    pair_tangent = jnp.dot(hidden_tangent, down_w, preferred_element_type=jnp.float32).astype(
        jnp.bfloat16
    )
    returned = lax.all_to_all(
        pair_tangent.reshape(owners, capacity, model_width),
        "expert",
        split_axis=0,
        concat_axis=0,
        tiled=True,
    )
    picked_rows = jnp.take(returned.reshape(slot_total, model_width), slot_index, axis=0)
    picked_rows = picked_rows.reshape(token_count, top_k, model_width)
    jv_vals = tangent.astype(jnp.float32) + jnp.sum(
        gates[:, :, None] * picked_rows.astype(jnp.float32), axis=1
    )
    cotangent = (jnp.take(jv_vals, source_token, axis=0) * source_gate[:, None]).astype(
        jnp.bfloat16
    )
    cotangent = cotangent.reshape(owners, capacity, model_width)
    cot_rows = lax.all_to_all(cotangent, "expert", split_axis=0, concat_axis=0, tiled=True).reshape(
        slot_total, model_width
    )
    contract_last = (((1,), (1,)), ((), ()))
    back_vals = lax.dot_general(cot_rows, down_w, contract_last, preferred_element_type=jnp.float32)
    grad_gate = (back_vals * pre_b * slope).astype(jnp.bfloat16)
    grad_up = (back_vals * act).astype(jnp.bfloat16)
    pair_grad = (
        lax.dot_general(grad_gate, gate_w, contract_last, preferred_element_type=jnp.float32)
        + lax.dot_general(grad_up, up_w, contract_last, preferred_element_type=jnp.float32)
    ).astype(jnp.bfloat16)
    grads_home = lax.all_to_all(
        pair_grad.reshape(owners, capacity, model_width),
        "expert",
        split_axis=0,
        concat_axis=0,
        tiled=True,
    )
    grad_rows = jnp.take(grads_home.reshape(slot_total, model_width), slot_index, axis=0)
    grad_rows = grad_rows.reshape(token_count, top_k, model_width)
    summed = jv_vals + jnp.sum(grad_rows.astype(jnp.float32), axis=1)
    local_sum = jnp.sum(jv_vals * jv_vals)
    global_sum = lax.psum(local_sum, ("dp", "expert"))
    element_count = token_count * lax.axis_size("dp") * owners * model_width
    return summed * lax.rsqrt(global_sum / element_count + 1e-06)


def solution(mesh):
    placed = (
        P(("dp", "expert"), None),
        P(("dp", "expert"), None),
        P(("dp", "expert"), None),
        P(("dp", "expert"), None),
        P("expert", None, None),
        P("expert", None, None),
        P("expert", None, None),
    )
    return jax.shard_map(
        shards, mesh=mesh, in_specs=placed, out_specs=P(("dp", "expert"), None), check_vma=False
    )
```

profile of v0, /device:TPU:0, one launch (start us, length us, event | category | flops | bytes accessed | tf_op | source)
XLA Modules:
  0.0 422.6 jit_solution(18199335404955691745)
XLA Ops:
  0.0 0.9 copy.14
  0.9 0.1 reshape.120
  1.1 0.1 eq.39
  1.2 1.1 reduce-window.6
  2.3 0.2 slice_reduce_fusion
  2.6 0.1 fusion.30
  2.7 0.2 fusion.24
  2.9 0.2 select_reduce_fusion.1
  3.2 8.0 %gather_fusion.2 = bf16[576,2048]{1,0:T(8,128)(2,1)} fusion(bf16[128,2048]{1,0:T(8,128)(2,1)} %param.12, s32[1024]{0:T(1024)S(1)} %pad_clamp_fusion.2), kind=kCustom, calls=%fused_computation.2.clone | custom fusion | bytes 4720896 | tf_op jit(solution)/shard_map/jit(_take)/gather | solution.py:46
  11.1 7.9 %gather_fusion.1 = bf16[576,2048]{1,0:T(8,128)(2,1)} fusion(bf16[128,2048]{1,0:T(8,128)(2,1)} %param.11, s32[1024]{0:T(1024)S(1)} %pad_clamp_fusion.2), kind=kCustom, calls=%fused_computation.clone | custom fusion | bytes 4720896 | tf_op jit(solution)/shard_map/jit(_take)/gather | solution.py:43
  19.1 3.8 select_multiply_fusion.1
  22.9 60.9 %all_to_all.25 = bf16[8,72,2048]{2,1,0:T(8,128)(2,1)} all-to-all(bf16[8,72,2048]{2,1,0:T(8,128)(2,1)S(1)} %bitcast.52), channel_id=1, replica_groups=mesh['dp'=4,'expert'=8] {'expert'}, dimensions={0} | all-to-all | bytes 4718592 | tf_op jit(solution)/shard_map/all_to_all | solution.py:50
  83.8 4.5 %all-to-all-start.1 = ((bf16[8,72,2048]{2,1,0:T(8,128)(2,1)}), bf16[8,72,2048]{2,1,0:T(8,128)(2,1)}, u32[]{:S(2)}, u32[]{:S(2)}) async-start(bf16[8,72,2048]{2,1,0:T(8,128)(2,1)} %bitcast.51), calls=%async_computation.1 | async-start | bytes 4718592 | tf_op jit(solution)/shard_map/all_to_all | solution.py:51
  88.3 0.0 copy-done
  88.3 0.0 copy-start.5
  88.3 5.1 %fusion.14 = f32[576,768]{1,0:T(8,128)} fusion(bf16[576,2048]{1,0:T(8,128)(2,1)} %bitcast.55, bf16[1,2048,768]{2,1,0:T(8,128)(2,1)S(1)} %copy-done), kind=kOutput, calls=%fused_computation.22 | convolution fusion | flops 1811939328 | bytes 7274496 | tf_op jit(solution)/shard_map/dot_general | solution.py:8
  93.4 3.2 fusion.8
  96.6 46.2 %all-to-all-done.1 = bf16[8,72,2048]{2,1,0:T(8,128)(2,1)} async-done(((bf16[8,72,2048]{2,1,0:T(8,128)(2,1)}), bf16[8,72,2048]{2,1,0:T(8,128)(2,1)}, u32[]{:S(2)}, u32[]{:S(2)}) %all-to-all-start.1) | async-done | bytes 2359328 | tf_op jit(solution)/shard_map/all_to_all | solution.py:51
  142.8 5.8 %fusion.6 = f32[576,768]{1,0:T(8,128)} fusion(bf16[576,2048]{1,0:T(8,128)(2,1)} %bitcast.6, bf16[1,2048,768]{2,1,0:T(8,128)(2,1)} %param.16), kind=kOutput, calls=%fused_computation.14 | convolution fusion | flops 1811939328 | bytes 7274496 | tf_op jit(solution)/shard_map/dot_general | solution.py:57
  148.6 10.1 %fusion.16 = bf16[576,2048]{1,0:T(8,128)(2,1)} fusion(bf16[1,768,2048]{2,1,0:T(8,128)(2,1)} %param.17, f32[576,768]{1,0:T(8,128)} %fusion.6, f32[576,768]{1,0:T(8,128)} %fusion.8, bf16[576,2048]{1,0:T(8,128)(2,1)} %bitcast.6, bf16[1,2048,768]{2,1,0:T(8,128)(2,1)S(1)} %copy-done, f32[576,768]{1,0:T(8,128)} %fusion.14), kind=kOutput, calls=%fused_computation.24 | convolution fusion | flops 3630809088 | bytes 16318464 | tf_op jit(solution)/shard_map/dot_general | solution.py:59
  158.7 4.7 %all-to-all-start.2 = ((bf16[8,72,2048]{2,1,0:T(8,128)(2,1)}), bf16[8,72,2048]{2,1,0:T(8,128)(2,1)}, u32[]{:S(2)}, u32[]{:S(2)}) async-start(bf16[8,72,2048]{2,1,0:T(8,128)(2,1)} %bitcast.53), calls=%async_computation.2 | async-start | bytes 4718592 | tf_op jit(solution)/shard_map/all_to_all | solution.py:62
  163.5 0.1 reduce_sum.61
  163.6 0.1 copy.13
  163.7 0.1 broadcast_in_dim.65
  163.8 0.2 select_reduce_fusion
  164.0 0.1 mul.96
  164.1 53.8 %all-to-all-done.2 = bf16[8,72,2048]{2,1,0:T(8,128)(2,1)} async-done(((bf16[8,72,2048]{2,1,0:T(8,128)(2,1)}), bf16[8,72,2048]{2,1,0:T(8,128)(2,1)}, u32[]{:S(2)}, u32[]{:S(2)}) %all-to-all-start.2) | async-done | bytes 2359328 | tf_op jit(solution)/shard_map/all_to_all | solution.py:62
  217.9 7.2 %gather_fusion.3 = bf16[512,2048]{1,0:T(8,128)(2,1)} fusion(bf16[576,2048]{1,0:T(8,128)(2,1)} %bitcast.10, s32[1024]{0:T(1024)S(1)} %pad_clamp_fusion.1), kind=kCustom, calls=%fused_computation.1.clone | custom fusion | bytes 4196352 | tf_op jit(solution)/shard_map/jit(_take)/gather | solution.py:69
  225.2 3.9 select_convert_fusion.1
  229.0 5.2 %reshape.131 = f32[128,4,2048]{2,1,0:T(4,128)} reshape(f32[512,2048]{1,0:T(8,128)} %select_convert_fusion.1) | data formatting | bytes 8388608 | tf_op jit(solution)/shard_map/convert_element_type | solution.py:72
  234.2 5.5 %multiply_reduce_fusion = f32[128,2048]{1,0:T(8,128)S(1)} fusion(f32[128,4,2048]{2,1,0:T(4,128)} %reshape.131, f32[128,4]{1,0:T(8,128)S(1)} %copy.13), kind=kLoop, calls=%fused_computation.7 | loop fusion | flops 1835008 | bytes 5244928 | tf_op jit(solution)/shard_map/reduce_sum | solution.py:71
  239.7 1.8 multiply_reduce_fusion.1
  241.5 7.9 %gather_fusion = f32[576,2048]{1,0:T(8,128)} fusion(f32[128,2048]{1,0:T(8,128)} %get-tuple-element.8, s32[1024]{0:T(1024)S(1)} %pad_clamp_fusion), kind=kCustom, calls=%fused_computation.4 | custom fusion | bytes 9439488 | tf_op jit(solution)/shard_map/jit(_take)/gather | solution.py:74
  249.3 2.8 multiply_convert_fusion
  252.2 0.0 copy-start.4
  252.2 57.4 %all_to_all.26 = bf16[8,72,2048]{2,1,0:T(8,128)(2,1)S(1)} all-to-all(bf16[8,72,2048]{2,1,0:T(8,128)(2,1)S(1)} %multiply_convert_fusion), channel_id=1, replica_groups=mesh['dp'=4,'expert'=8] {'expert'}, dimensions={0} | all-to-all | bytes 4718592 | tf_op jit(solution)/shard_map/all_to_all | solution.py:78
  309.6 2.0 fusion
  311.7 0.4 copy-done.7
  312.0 2.0 fusion.4
  314.1 3.8 add_convert_fusion
  317.9 4.4 %all-to-all-start.4 = ((bf16[8,72,2048]{2,1,0:T(8,128)(2,1)}), bf16[8,72,2048]{2,1,0:T(8,128)(2,1)}, u32[]{:S(2)}, u32[]{:S(2)}) async-start(bf16[8,72,2048]{2,1,0:T(8,128)(2,1)} %bitcast.54), calls=%async_computation.4 | async-start | bytes 4718592 | tf_op jit(solution)/shard_map/all_to_all | solution.py:89
  322.2 74.9 %psum.7 = f32[]{:T(128)} all-reduce(f32[]{:T(128)} %get-tuple-element.6), channel_id=1, replica_groups=mesh['dp'=4,'expert'=8] {'dp','expert'}, use_global_device_ids=true, to_apply=%region_9.12 | all-reduce | flops 1 | bytes 8 | tf_op jit(solution)/shard_map/psum | solution.py:100
  397.8 0.0 all-to-all-done.4
  397.9 7.2 %gather_fusion.4 = bf16[512,2048]{1,0:T(8,128)(2,1)} fusion(bf16[576,2048]{1,0:T(8,128)(2,1)} %bitcast.14, s32[1024]{0:T(1024)S(1)} %pad_clamp_fusion.1), kind=kCustom, calls=%fused_computation.3.clone | custom fusion | bytes 4196352 | tf_op jit(solution)/shard_map/jit(_take)/gather | solution.py:96
  405.1 3.9 select_convert_fusion
  409.0 5.2 %reshape.132 = f32[128,4,2048]{2,1,0:T(4,128)} reshape(f32[512,2048]{1,0:T(8,128)} %select_convert_fusion) | data formatting | bytes 8388608 | tf_op jit(solution)/shard_map/convert_element_type | solution.py:98
  414.1 5.8 %reduce_sum.64 = f32[128,2048]{1,0:T(8,128)} reduce(f32[128,4,2048]{2,1,0:T(4,128)} %reshape.132, f32[]{:T(128)} %constant.65.clone.1), dimensions={1}, to_apply=%region_7.10 | reduce | flops 786432 | bytes 5242884 | tf_op jit(solution)/shard_map/reduce_sum | solution.py:98
  420.0 2.6 add_multiply_fusion.1
  (28 shorter events, 0.2 us)
Async XLA Ops:
  0.0 88.3 %copy-start = (bf16[1,2048,768]{2,1,0:T(8,128)(2,1)S(1)}, bf16[1,2048,768]{2,1,0:T(8,128)(2,1)}, u32[]{:S(2)}) copy-start(bf16[1,2048,768]{2,1,0:T(8,128)(2,1)} %param.15) | copy-start | bytes 9437188
  83.8 59.1 %all-to-all-start.1 = ((bf16[8,72,2048]{2,1,0:T(8,128)(2,1)}), bf16[8,72,2048]{2,1,0:T(8,128)(2,1)}, u32[]{:S(2)}, u32[]{:S(2)}) async-start(bf16[8,72,2048]{2,1,0:T(8,128)(2,1)} %bitcast.51), calls=%async_computation.1 | async-start | bytes 4718592 | tf_op jit(solution)/shard_map/all_to_all | solution.py:51
  88.3 5.1 %copy-start.2 = (bf16[8,72,2048]{2,1,0:T(8,128)(2,1)S(1)}, bf16[8,72,2048]{2,1,0:T(8,128)(2,1)}, u32[]{:S(2)}) copy-start(bf16[8,72,2048]{2,1,0:T(8,128)(2,1)} %all_to_all.25) | copy-start | bytes 7077892
  88.3 5.1 %copy-start.5 = (bf16[1,2048,768]{2,1,0:T(8,128)(2,1)S(1)}, bf16[1,2048,768]{2,1,0:T(8,128)(2,1)}, u32[]{:S(2)}) copy-start(bf16[1,2048,768]{2,1,0:T(8,128)(2,1)} %param.16) | copy-start | bytes 9437188
  158.7 4.8 %copy-start.3 = (f32[128,4]{0,1:T(4,128)S(1)}, f32[128,4]{0,1:T(4,128)}, u32[]{:S(2)}) copy-start(f32[128,4]{0,1:T(4,128)} %param.14) | copy-start | bytes 6148
  158.7 59.2 %all-to-all-start.2 = ((bf16[8,72,2048]{2,1,0:T(8,128)(2,1)}), bf16[8,72,2048]{2,1,0:T(8,128)(2,1)}, u32[]{:S(2)}, u32[]{:S(2)}) async-start(bf16[8,72,2048]{2,1,0:T(8,128)(2,1)} %bitcast.53), calls=%async_computation.2 | async-start | bytes 4718592 | tf_op jit(solution)/shard_map/all_to_all | solution.py:62
  234.2 5.5 %copy-start.1 = (bf16[128,2048]{1,0:T(8,128)(2,1)S(1)}, bf16[128,2048]{1,0:T(8,128)(2,1)}, u32[]{:S(2)}) copy-start(bf16[128,2048]{1,0:T(8,128)(2,1)} %param.12) | copy-start | bytes 1572868
  252.2 57.4 %copy-start.4 = (bf16[1,768,2048]{2,1,0:T(8,128)(2,1)S(1)}, bf16[1,768,2048]{2,1,0:T(8,128)(2,1)}, u32[]{:S(2)}) copy-start(bf16[1,768,2048]{2,1,0:T(8,128)(2,1)} %param.17) | copy-start | bytes 9437188
  309.6 2.1 copy-start.6
  309.6 2.4 copy-start.7
  312.0 2.0 copy-start.8
  317.9 80.0 %all-to-all-start.4 = ((bf16[8,72,2048]{2,1,0:T(8,128)(2,1)}), bf16[8,72,2048]{2,1,0:T(8,128)(2,1)}, u32[]{:S(2)}, u32[]{:S(2)}) async-start(bf16[8,72,2048]{2,1,0:T(8,128)(2,1)} %bitcast.54), calls=%async_computation.4 | async-start | bytes 4718592 | tf_op jit(solution)/shard_map/all_to_all | solution.py:89
where the time goes:
time: 424 us; the launch traced here: 423 us
  blocking collectives  193 us (46%)
  waiting for transfers between devices  100 us (24%)
  local copies, waits for them, and re-layouts  50.7 us (12%)
  matrix products  32.1 us (8%)
  other arithmetic  32 us (8%)
  starting transfers between devices  13.6 us (3%)
    psum x1, blocking collectives, shards(): global_sum = lax.psum(local_sum, ('dp', 'expert'))  74.9 us
    all_to_all x1, blocking collectives, shards(): lax.all_to_all(send_x, 'expert', split_axis=0, concat_axis=0, tiled=True)  60.9 us
    all_to_all x1, blocking collectives, shards(): lax.all_to_all(cotangent, 'expert', split_axis=0, concat_axis=0, tiled=True)  57.4 us
    all_to_all x1, waiting for transfers between devices, shards(): lax.all_to_all(pair_tangent.reshape(owners, capacity, model_width), 'expe...  53.8 us
    all_to_all x1, waiting for transfers between devices, shards(): lax.all_to_all(send_v, 'expert', split_axis=0, concat_axis=0, tiled=True)  46.2 us
    dot_general x1, matrix products, shards(): jnp.dot(hidden_tangent, down_w, preferred_element_type=jnp.float32)  10.1 us
  transfers between devices with their start and end apart: 3, of which 2 were waited for; matrix products, arithmetic and copies ran while one was open for 2% of the time, Pallas kernels for 0%

commit v1 on v0

v1 whole, which is shorter than its diff:
```python
import jax
import jax.numpy as jnp
from jax import lax
from jax.sharding import PartitionSpec as P

CONTRACT_LAST = (((1,), (1,)), ((), ()))


def dot(lhs, rhs):
    return jnp.dot(lhs, rhs, preferred_element_type=jnp.float32)


def dot_last(lhs, rhs):
    return lax.dot_general(lhs, rhs, CONTRACT_LAST, preferred_element_type=jnp.float32)


def both_cores(pairs):
    return [(2 * src + core, 2 * dst + core) for src, dst in pairs for core in range(2)]


def hop(rows, pairs):
    return lax.ppermute(rows, "expert", both_cores(pairs))


def line_gather(block, pos, count):
    going_right, going_left = {}, {}
    right = left = block
    for step in range(1, count):
        right_pairs = [(i, i + 1) for i in range(step - 1, count - 1)]
        left_pairs = [(i, i - 1) for i in range(1, count - step + 1)]
        if step - 1 > count - step:
            right = left = hop(jnp.where(pos >= step - 1, right, left), right_pairs + left_pairs)
        else:
            right, left = hop(right, right_pairs), hop(left, left_pairs)
        going_right[step], going_left[step] = right, left
    return [block] + [
        jnp.where(pos >= s, going_right[s], going_left[count - s]) for s in range(1, count)
    ]


def add_rows(own, came):
    return (own.astype(jnp.float32) + came.astype(jnp.float32)).astype(jnp.bfloat16)


def line_reduce(parts, pos, count):
    came_right = came_left = None
    for dist in range(count - 1, 0, -1):
        right, left = parts[count - dist], parts[dist]
        if came_right is not None:
            right, left = add_rows(right, came_right), add_rows(left, came_left)
        right_pairs = [(i, i + 1) for i in range(0, count - dist)]
        left_pairs = [(i, i - 1) for i in range(dist, count)]
        if count - dist < dist - 1:
            came_right = came_left = hop(
                jnp.where(pos <= count - 1 - dist, right, left), right_pairs + left_pairs
            )
        else:
            came_right, came_left = hop(right, right_pairs), hop(left, left_pairs)
    return (
        parts[0].astype(jnp.float32)
        + came_right.astype(jnp.float32)
        + came_left.astype(jnp.float32)
    )


def sum_everywhere(value, axis):
    size = lax.axis_size(axis)
    if size & (size - 1):
        return lax.psum(value, axis)
    step = 1
    while step < size:
        value = value + lax.ppermute(value, axis, [(i, i ^ step) for i in range(size)])
        step *= 2
    return value


def line_shards(tokens, tangent, routes, gates, w_gate, w_up, w_down):
    token_count, width = tokens.shape
    owners = lax.axis_size("expert")
    count = owners // 2
    me = lax.axis_index("expert")
    pos, core = me // 2, me % 2
    swap = [(i, i ^ 1) for i in range(owners)]

    gate_of = jnp.sum(
        jnp.where(
            routes[:, :, None] == jnp.arange(owners, dtype=jnp.int32)[None, None, :],
            gates[:, :, None],
            jnp.float32(0.0),
        ),
        axis=1,
    ).T
    gate_rows = jnp.stack(line_gather(gate_of, pos, count))
    own_gates = lax.dynamic_index_in_dim(gate_rows, me, 1, keepdims=False)
    sib_gates = lax.dynamic_index_in_dim(gate_rows, me ^ 1, 1, keepdims=False)

    weights = [(w_gate[0], w_up[0], w_down[0])]
    weights.append(tuple(lax.ppermute(w, "expert", swap) for w in weights[0]))

    halves = 2
    half = token_count // halves
    gathered = []
    after = None
    for h in range(halves):
        rows = slice(h * half, (h + 1) * half)
        both = jnp.concatenate([tokens[rows], tangent[rows]])
        if after is not None:
            both, _ = lax.optimization_barrier((both, after))
        slots = line_gather(both, pos, count)
        after = slots[-1]
        gathered.append(jnp.concatenate(slots))

    jv_home, kept = [], []
    for h in range(halves):
        rows = slice(h * half, (h + 1) * half)
        partial = None
        states = []
        for (gate_w, up_w, down_w), pair_gates in zip(weights, (own_gates, sib_gates)):
            g = pair_gates[:, rows].reshape(count * half, 1)
            pre = dot(gathered[h], gate_w).reshape(count, 2, half, -1)
            ups = dot(gathered[h], up_w).reshape(count, 2, half, -1)
            a, da = (pre[:, i].reshape(count * half, -1) for i in range(2))
            b, db = (ups[:, i].reshape(count * half, -1) for i in range(2))
            sigma = jax.nn.sigmoid(a)
            act = a * sigma
            slope = sigma * (1.0 + a * (1.0 - sigma))
            b_slope = b * slope
            hidden = (g * (b_slope * da + act * db)).astype(jnp.bfloat16)
            term = dot(hidden, down_w)
            partial = term if partial is None else partial + term
            states.append((g * b_slope, g * act))
        kept.append(states)
        parts = list(partial.astype(jnp.bfloat16).reshape(count, half, width))
        jv_home.append(tangent[rows].astype(jnp.float32) + line_reduce(parts, pos, count))

    summed = []
    for h in range(halves):
        jv_rows = jnp.concatenate(line_gather(jv_home[h].astype(jnp.bfloat16), pos, count))
        partial = None
        for (gate_w, up_w, down_w), (b_slope, act) in zip(weights, kept[h]):
            back = dot_last(jv_rows, down_w)
            grad_gate = (back * b_slope).astype(jnp.bfloat16)
            grad_up = (back * act).astype(jnp.bfloat16)
            term = dot_last(grad_gate, gate_w) + dot_last(grad_up, up_w)
            partial = term if partial is None else partial + term
        parts = list(partial.astype(jnp.bfloat16).reshape(count, half, width))
        summed.append(jv_home[h] + line_reduce(parts, pos, count))

    squares = sum(jnp.sum(jv * jv) for jv in jv_home)
    squares = jnp.full((8, 128), squares)
    squares = sum_everywhere(sum_everywhere(squares, "dp"), "expert")[0, 0]
    elements = token_count * width * lax.axis_size("dp") * owners
    scale = lax.rsqrt(squares / elements + 1e-06)
    return jnp.concatenate(summed) * scale


def owner_states(x_rows, gate_w, up_w):
    pre_a = dot(x_rows, gate_w)
    pre_b = dot(x_rows, up_w)
    sigma = jax.nn.sigmoid(pre_a)
    act = pre_a * sigma
    slope = sigma * (1.0 + pre_a * (1.0 - sigma))
    return (pre_b, act, slope)


def pair_shards(tokens, tangent, routes, gates, w_gate, w_up, w_down):
    token_count, model_width = tokens.shape
    top_k = routes.shape[1]
    owners = lax.axis_size("expert")
    expert_total = owners * w_gate.shape[0]
    capacity = pair_capacity(token_count, top_k, expert_total)
    slot_total = expert_total * capacity
    pair_count = token_count * top_k
    gate_w = w_gate[0]
    up_w = w_up[0]
    down_w = w_down[0]
    flat_routes = routes.reshape(pair_count)
    onehot = (flat_routes[:, None] == jnp.arange(expert_total, dtype=jnp.int32)[None, :]).astype(
        jnp.int32
    )
    before = jnp.cumsum(onehot, axis=0) - onehot
    slot_of = jnp.sum(before * onehot, axis=1)
    slot_index = flat_routes * capacity + slot_of
    slot_match = slot_index[None, :] == jnp.arange(slot_total, dtype=jnp.int32)[:, None]
    filled = jnp.any(slot_match, axis=1)
    pair_token = jnp.arange(pair_count, dtype=jnp.int32) // top_k
    source_token = jnp.sum(jnp.where(slot_match, pair_token[None, :], 0), axis=1)
    source_gate = jnp.sum(
        jnp.where(slot_match, gates.reshape(pair_count)[None, :], jnp.float32(0.0)), axis=1
    )
    keep_mask = filled.astype(jnp.bfloat16)[:, None]

    def exchange(rows):
        blocks = rows.reshape(owners, capacity, model_width)
        moved = lax.all_to_all(blocks, "expert", split_axis=0, concat_axis=0, tiled=True)
        return moved.reshape(slot_total, model_width)

    x_rows = exchange(jnp.take(tokens, source_token, axis=0) * keep_mask)
    v_rows = exchange(jnp.take(tangent, source_token, axis=0) * keep_mask)
    pre_b, act, slope = owner_states(x_rows, gate_w, up_w)
    tan_a = dot(v_rows, gate_w)
    tan_b = dot(v_rows, up_w)
    hidden_tangent = (slope * tan_a * pre_b + act * tan_b).astype(jnp.bfloat16)
    returned = exchange(dot(hidden_tangent, down_w).astype(jnp.bfloat16))
    picked_rows = jnp.take(returned, slot_index, axis=0)
    picked_rows = picked_rows.reshape(token_count, top_k, model_width)
    jv_vals = tangent.astype(jnp.float32) + jnp.sum(
        gates[:, :, None] * picked_rows.astype(jnp.float32), axis=1
    )
    cot_rows = exchange(
        (jnp.take(jv_vals, source_token, axis=0) * source_gate[:, None]).astype(jnp.bfloat16)
    )
    back_vals = dot_last(cot_rows, down_w)
    grad_gate = (back_vals * pre_b * slope).astype(jnp.bfloat16)
    grad_up = (back_vals * act).astype(jnp.bfloat16)
    pair_grad = dot_last(grad_gate, gate_w) + dot_last(grad_up, up_w)
    grad_rows = jnp.take(exchange(pair_grad.astype(jnp.bfloat16)), slot_index, axis=0)
    grad_rows = grad_rows.reshape(token_count, top_k, model_width)
    summed = jv_vals + jnp.sum(grad_rows.astype(jnp.float32), axis=1)
    global_sum = lax.psum(jnp.sum(jv_vals * jv_vals), ("dp", "expert"))
    element_count = token_count * lax.axis_size("dp") * owners * model_width
    return summed * lax.rsqrt(global_sum / element_count + 1e-06)


def pair_capacity(token_count, top_k, expert_total):
    return max(2, token_count * top_k * 9 // (8 * expert_total))


def shards(tokens, tangent, routes, gates, w_gate, w_up, w_down):
    token_count, top_k = routes.shape
    owners = lax.axis_size("expert")
    capacity = pair_capacity(token_count, top_k, owners * w_gate.shape[0])
    whole_blocks = owners % 2 == 0 and w_gate.shape[0] == 1 and token_count <= 2 * capacity
    form = line_shards if whole_blocks else pair_shards
    return form(tokens, tangent, routes, gates, w_gate, w_up, w_down)


def solution(mesh):
    placed = (
        P(("dp", "expert"), None),
        P(("dp", "expert"), None),
        P(("dp", "expert"), None),
        P(("dp", "expert"), None),
        P("expert", None, None),
        P("expert", None, None),
        P("expert", None, None),
    )
    return jax.shard_map(
        shards, mesh=mesh, in_specs=placed, out_specs=P(("dp", "expert"), None), check_vma=False
    )
```

time: 424 us -> 298 us (0.70)
  blocking collectives: 193 us -> 0 us
  starting transfers between devices: 13.6 us -> 93.6 us
  local copies, waits for them, and re-layouts: 50.7 us -> 8.27 us
  matrix products: 32.1 us -> 58.8 us
  other arithmetic: 32 us -> 23.7 us
  waiting for transfers between devices: 100 us -> 108 us
    all_to_all x2 -> x0, blocking collectives: 118 us -> none  [the longest x1 60.9 us: shards(): lax.all_to_all(send_x, 'expert', split_axis=0, concat_axis=0, tiled=True)]
    ppermute x0 -> x53, waiting for transfers between devices: none -> 108 us  [the longest x45 96 us: hop(): return lax.ppermute(rows, 'expert', both_cores(pairs))]
    all_to_all x3 -> x0, waiting for transfers between devices: 100 us -> none  [the longest x1 53.8 us: shards(): lax.all_to_all(pair_tangent.reshape(owners, capacity, model_width), 'expe...]
    ppermute x0 -> x53, starting transfers between devices: none -> 93.6 us  [the longest x45 88.7 us: hop(): return lax.ppermute(rows, 'expert', both_cores(pairs))]
    psum x1 -> x0, blocking collectives: 74.9 us -> none  [shards(): global_sum = lax.psum(local_sum, ('dp', 'expert'))]
    gather x5 -> x0, local copies, waits for them, and re-layouts: 38.3 us -> none  [the longest x1 7.96 us: shards(): jnp.take(tangent, source_token, axis=0) * keep_mask]
    dot_general x7 -> x24, matrix products: 32.1 us -> 58.8 us  [the longest x12 31.4 us: dot(): return jnp.dot(lhs, rhs, preferred_element_type=jnp.float32)]
    all_to_all x3 -> x0, starting transfers between devices: 13.6 us -> none  [the longest x1 4.72 us: shards(): lax.all_to_all(pair_tangent.reshape(owners, capacity, model_width), 'expe...]
  transfers between devices with their start and end apart: 3 -> 53, of which waited for: 2 -> 28; matrix products, arithmetic and copies ran while one was open for 2% -> 26% of each run, Pallas kernels for 0% -> 0%
where the time goes in v1:
time: 298 us; the launch traced here: 296 us
  waiting for transfers between devices  108 us (36%)
  starting transfers between devices  93.6 us (31%)
  matrix products  58.8 us (20%)
  other arithmetic  23.7 us (8%)
  local copies, waits for them, and re-layouts  8.27 us (3%)
  between operations  3.11 us (1%)
    ppermute x45, waiting for transfers between devices, hop(): return lax.ppermute(rows, 'expert', both_cores(pairs))  96 us
    ppermute x45, starting transfers between devices, hop(): return lax.ppermute(rows, 'expert', both_cores(pairs))  88.7 us
    dot_general x12, matrix products, dot(): return jnp.dot(lhs, rhs, preferred_element_type=jnp.float32)  31.4 us
    dot_general x12, matrix products, dot_last(): lax.dot_general(lhs, rhs, CONTRACT_LAST, preferred_element_type=jnp.float32)  27.4 us
    ppermute x5, waiting for transfers between devices, sum_everywhere(): lax.ppermute(value, axis, [(i, i ^ step) for i in range(size)])  12.2 us
  transfers between devices with their start and end apart: 53, of which 28 were waited for; matrix products, arithmetic and copies ran while one was open for 26% of the time, Pallas kernels for 0%

profile of v1, /device:TPU:0, one launch (start us, length us, event | category | flops | bytes accessed | tf_op | source)
XLA Modules:
  0.0 295.7 jit_solution(6043740518099967111)
XLA Ops:
  4.6 5.8 %collective-permute-start.5 = (bf16[128,2048]{1,0:T(8,128)(2,1)}, bf16[128,2048]{1,0:T(8,128)(2,1)}, u32[]{:S(2)}, u32[]{:S(2)}) collective-permute-start(bf16[128,2048]{1,0:T(8,128)(2,1)} %pad_maximum_fusion.3), channel_id=1, source_target_pairs={{0,2},{1,3},{2,4},{3,5},{4,6},{5,7},{8,10},{9,11},{10,12},{11,13},... | collective-permute-start | bytes 1572872 | tf_op jit(solution)/shard_map/ppermute | solution.py:22
  11.7 4.5 %collective-permute-start = (f32[8,128]{1,0:T(8,128)S(1)}, f32[8,128]{1,0:T(8,128)S(1)}, u32[]{:S(2)}, u32[]{:S(2)}) collective-permute-start(f32[8,128]{1,0:T(8,128)S(1)} %bitcast.251), channel_id=1, source_target_pairs={{0,2},{1,3},{2,4},{3,5},{4,6},{5,7},{8,10},{9,11},{10,12},{11,13},... | collective-permute-start | bytes 12296 | tf_op jit(solution)/shard_map/ppermute | solution.py:22
  17.5 3.5 %collective-permute-done = f32[8,128]{1,0:T(8,128)S(1)} collective-permute-done((f32[8,128]{1,0:T(8,128)S(1)}, f32[8,128]{1,0:T(8,128)S(1)}, u32[]{:S(2)}, u32[]{:S(2)}) %collective-permute-start) | collective-permute-done | bytes 4128 | tf_op jit(solution)/shard_map/ppermute | solution.py:22
  21.7 4.3 %collective-permute-done.2 = f32[8,128]{1,0:T(8,128)S(1)} collective-permute-done((f32[8,128]{1,0:T(8,128)S(1)}, f32[8,128]{1,0:T(8,128)S(1)}, u32[]{:S(2)}, u32[]{:S(2)}) %collective-permute-start.2) | collective-permute-done | bytes 4128 | tf_op jit(solution)/shard_map/ppermute | solution.py:22
  27.8 3.6 %collective-permute-done.3 = f32[8,128]{1,0:T(8,128)S(1)} collective-permute-done((f32[8,128]{1,0:T(8,128)S(1)}, f32[8,128]{1,0:T(8,128)S(1)}, u32[]{:S(2)}, u32[]{:S(2)}) %collective-permute-start.3) | collective-permute-done | bytes 4128 | tf_op jit(solution)/shard_map/ppermute | solution.py:22
  37.4 13.7 %collective-permute-done.8 = bf16[128,2048]{1,0:T(8,128)(2,1)} collective-permute-done((bf16[128,2048]{1,0:T(8,128)(2,1)}, bf16[128,2048]{1,0:T(8,128)(2,1)}, u32[]{:S(2)}, u32[]{:S(2)}) %collective-permute-start.8) | collective-permute-done | bytes 524320 | tf_op jit(solution)/shard_map/ppermute | solution.py:22
  54.6 13.0 %collective-permute-done.9 = bf16[128,2048]{1,0:T(8,128)(2,1)} collective-permute-done((bf16[128,2048]{1,0:T(8,128)(2,1)}, bf16[128,2048]{1,0:T(8,128)(2,1)}, u32[]{:S(2)}, u32[]{:S(2)}) %collective-permute-start.9) | collective-permute-done | bytes 524320 | tf_op jit(solution)/shard_map/ppermute | solution.py:22
  67.6 2.2 select_dynamic-update-slice_fusion
  76.5 3.5 %fusion.2 = f32[4,2,64,768]{3,2,1,0:T(8,128)S(1)} fusion(bf16[4,2,64,2048]{3,2,1,0:T(8,128)(2,1)} %bitcast.246, bf16[1,2048,768]{2,1,0:T(8,128)(2,1)S(1)} %copy-done.2), kind=kOutput, calls=%fused_computation.2 | convolution fusion | flops 1610612736 | bytes 6815744 | tf_op jit(solution)/shard_map/dot_general | solution.py:10
  80.0 4.3 %collective-permute-done.28 = bf16[128,2048]{1,0:T(8,128)(2,1)S(1)} collective-permute-done((bf16[128,2048]{1,0:T(8,128)(2,1)S(1)}, bf16[128,2048]{1,0:T(8,128)(2,1)S(1)}, u32[]{:S(2)}, u32[]{:S(2)}) %collective-permute-start.28) | collective-permute-done | bytes 524320 | tf_op jit(solution)/shard_map/ppermute | solution.py:22
  84.9 3.5 %collective-permute-done.30 = bf16[128,2048]{1,0:T(8,128)(2,1)S(1)} collective-permute-done((bf16[128,2048]{1,0:T(8,128)(2,1)S(1)}, bf16[128,2048]{1,0:T(8,128)(2,1)S(1)}, u32[]{:S(2)}, u32[]{:S(2)}) %collective-permute-start.30) | collective-permute-done | bytes 524320 | tf_op jit(solution)/shard_map/ppermute | solution.py:22
  89.7 3.7 %fusion.6 = f32[4,2,64,768]{3,2,1,0:T(8,128)S(1)} fusion(bf16[4,2,64,2048]{3,2,1,0:T(8,128)(2,1)S(1)} %bitcast.247, bf16[1,2048,768]{2,1,0:T(8,128)(2,1)} %param.12), kind=kOutput, calls=%fused_computation.6 | convolution fusion | flops 1610612736 | bytes 6815744 | tf_op jit(solution)/shard_map/dot_general | solution.py:10
  93.4 7.3 %collective-permute-done.31 = bf16[128,2048]{1,0:T(8,128)(2,1)S(1)} collective-permute-done((bf16[128,2048]{1,0:T(8,128)(2,1)S(1)}, bf16[128,2048]{1,0:T(8,128)(2,1)S(1)}, u32[]{:S(2)}, u32[]{:S(2)}) %collective-permute-start.31) | collective-permute-done | bytes 524320 | tf_op jit(solution)/shard_map/ppermute | solution.py:22
  105.7 6.5 %collective-permute-done.32 = bf16[128,2048]{1,0:T(8,128)(2,1)S(1)} collective-permute-done((bf16[128,2048]{1,0:T(8,128)(2,1)S(1)}, bf16[128,2048]{1,0:T(8,128)(2,1)S(1)}, u32[]{:S(2)}, u32[]{:S(2)}) %collective-permute-start.32) | collective-permute-done | bytes 524320 | tf_op jit(solution)/shard_map/ppermute | solution.py:22
  112.5 3.7 %fusion.104 = f32[512,768]{1,0:T(8,128)S(1)} fusion(bf16[512,2048]{1,0:T(8,128)(2,1)S(1)} %copy-done.25, bf16[2048,768]{1,0:T(8,128)(2,1)} %collective-permute-done.10), kind=kOutput, calls=%fused_computation.185 | convolution fusion | flops 1610612736 | bytes 6815744 | tf_op jit(solution)/shard_map/dot_general | solution.py:10
  121.8 3.7 %fusion.4 = f32[4,2,64,768]{3,2,1,0:T(8,128)S(1)} fusion(bf16[4,2,64,2048]{3,2,1,0:T(8,128)(2,1)S(1)} %bitcast.239, bf16[1,2048,768]{2,1,0:T(8,128)(2,1)} %param.12), kind=kOutput, calls=%fused_computation.4 | convolution fusion | flops 1610612736 | bytes 6815744 | tf_op jit(solution)/shard_map/dot_general | solution.py:10
  125.5 2.9 fusion.12
  134.4 3.7 %fusion.91 = f32[512,768]{1,0:T(8,128)S(1)} fusion(bf16[2048,768]{1,0:T(8,128)(2,1)} %collective-permute-done.10, bf16[128,2048]{1,0:T(8,128)(2,1)S(1)} %get-tuple-element.48, bf16[128,2048]{1,0:T(8,128)(2,1)S(1)} %broadcast_select_fusion.2, bf16[128,2048]{1,0:T(8,128)(2,1)S(1)} %get-tuple-element.47, bf16[128,2048]{1,0:T(8,128)(2,1)S(1)} %copy-done.12), kind=kOutput, calls=%fused_computation.174 | convolution fusion | flops 1619001344 | bytes 6815744 | tf_op jit(solution)/shard_map/dot_general | solution.py:10
  140.0 2.9 fusion.13
  146.5 3.3 %collective-permute-done.33 = bf16[64,2048]{1,0:T(8,128)(2,1)S(1)} collective-permute-done((bf16[64,2048]{1,0:T(8,128)(2,1)S(1)}, bf16[64,2048]{1,0:T(8,128)(2,1)S(1)}, u32[]{:S(2)}, u32[]{:S(2)}) %collective-permute-start.33) | collective-permute-done | bytes 262176 | tf_op jit(solution)/shard_map/ppermute | solution.py:22
  149.9 4.4 %collective-permute-start.34 = (bf16[64,2048]{1,0:T(8,128)(2,1)S(1)}, bf16[64,2048]{1,0:T(8,128)(2,1)S(1)}, u32[]{:S(2)}, u32[]{:S(2)}) collective-permute-start(bf16[64,2048]{1,0:T(8,128)(2,1)S(1)} %add_convert_fusion.5), channel_id=1, source_target_pairs={{0,2},{1,3},{2,4},{3,5},{8,10},{9,11},{10,12},{11,13},{16,18},{17,... | collective-permute-start | bytes 786440 | tf_op jit(solution)/shard_map/ppermute | solution.py:22
  155.6 4.4 %collective-permute-start.15 = (bf16[64,2048]{1,0:T(8,128)(2,1)S(1)}, bf16[64,2048]{1,0:T(8,128)(2,1)S(1)}, u32[]{:S(2)}, u32[]{:S(2)}) collective-permute-start(bf16[64,2048]{1,0:T(8,128)(2,1)S(1)} %get-tuple-element.37), channel_id=1, source_target_pairs={{0,2},{1,3},{2,4},{3,5},{4,6},{5,7},{8,10},{9,11},{10,12},{11,13},... | collective-permute-start | bytes 786440 | tf_op jit(solution)/shard_map/ppermute | solution.py:22
  161.5 4.6 %collective-permute-start.35 = (bf16[64,2048]{1,0:T(8,128)(2,1)S(1)}, bf16[64,2048]{1,0:T(8,128)(2,1)S(1)}, u32[]{:S(2)}, u32[]{:S(2)}) collective-permute-start(bf16[64,2048]{1,0:T(8,128)(2,1)S(1)} %get-tuple-element.41), channel_id=1, source_target_pairs={{0,2},{1,3},{2,4},{3,5},{4,6},{5,7},{8,10},{9,11},{10,12},{11,13},... | collective-permute-start | bytes 786440 | tf_op jit(solution)/shard_map/ppermute | solution.py:22
  168.3 2.5 collective-permute-done.35
  170.8 4.0 %collective-permute-done.37 = bf16[64,2048]{1,0:T(8,128)(2,1)S(1)} collective-permute-done((bf16[64,2048]{1,0:T(8,128)(2,1)S(1)}, bf16[64,2048]{1,0:T(8,128)(2,1)S(1)}, u32[]{:S(2)}, u32[]{:S(2)}) %collective-permute-start.37) | collective-permute-done | bytes 262176 | tf_op jit(solution)/shard_map/ppermute | solution.py:22
  175.9 3.6 %collective-permute-start.38 = (bf16[64,2048]{1,0:T(8,128)(2,1)S(1)}, bf16[64,2048]{1,0:T(8,128)(2,1)}, u32[]{:S(2)}, u32[]{:S(2)}) collective-permute-start(bf16[64,2048]{1,0:T(8,128)(2,1)S(1)} %get-tuple-element.46), channel_id=1, source_target_pairs={{0,2},{1,3},{2,4},{3,5},{4,6},{5,7},{8,10},{9,11},{10,12},{11,13},... | collective-permute-start | bytes 786440 | tf_op jit(solution)/shard_map/ppermute | solution.py:22
  180.8 5.3 %collective-permute-start.18 = (bf16[64,2048]{1,0:T(8,128)(2,1)}, bf16[64,2048]{1,0:T(8,128)(2,1)}, u32[]{:S(2)}, u32[]{:S(2)}) collective-permute-start(bf16[64,2048]{1,0:T(8,128)(2,1)} %get-tuple-element.45), channel_id=1, source_target_pairs={{0,2},{1,3},{2,4},{3,5},{4,6},{5,7},{8,10},{9,11},{10,12},{11,13},... | collective-permute-start | bytes 786440 | tf_op jit(solution)/shard_map/ppermute | solution.py:22
  191.9 5.6 %collective-permute-done.20 = bf16[64,2048]{1,0:T(8,128)(2,1)} collective-permute-done((bf16[64,2048]{1,0:T(8,128)(2,1)}, bf16[64,2048]{1,0:T(8,128)(2,1)}, u32[]{:S(2)}, u32[]{:S(2)}) %collective-permute-start.20) | collective-permute-done | bytes 262176 | tf_op jit(solution)/shard_map/ppermute | solution.py:22
  198.8 4.3 %collective-permute-done.41 = bf16[64,2048]{1,0:T(8,128)(2,1)} collective-permute-done((bf16[64,2048]{1,0:T(8,128)(2,1)}, bf16[64,2048]{1,0:T(8,128)(2,1)}, u32[]{:S(2)}, u32[]{:S(2)}) %collective-permute-start.41) | collective-permute-done | bytes 262176 | tf_op jit(solution)/shard_map/ppermute | solution.py:22
  208.7 3.6 %collective-permute-done.42 = bf16[64,2048]{1,0:T(8,128)(2,1)S(1)} collective-permute-done((bf16[64,2048]{1,0:T(8,128)(2,1)S(1)}, bf16[64,2048]{1,0:T(8,128)(2,1)S(1)}, u32[]{:S(2)}, u32[]{:S(2)}) %collective-permute-start.42) | collective-permute-done | bytes 262176 | tf_op jit(solution)/shard_map/ppermute | solution.py:22
  213.4 3.3 %fusion.40 = (bf16[256,768]{1,0:T(8,128)(2,1)S(1)}, bf16[256,768]{1,0:T(8,128)(2,1)S(1)}) fusion(f32[4,1,64,768]{3,2,1,0:T(8,128)S(1)} %copy-done.22, f32[256]{0:T(256)S(1)} %mul.278, f32[4,1,64,768]{3,2,1,0:T(8,128)S(1)} %copy-done.21, bf16[1,768,2048]{2,1,0:T(8,128)(2,1)} %param.13, bf16[64,2048]{1,0:T(8,128)(2,1)S(1)} %get-tuple-element.58, ...), kind=kOutput, calls=%fused_computation.62 | convolution fusion | flops 812449792 | bytes 6554624 | tf_op jit(solution)/shard_map/dot_general | solution.py:14
  217.7 2.9 convolution_add_fusion.1
  220.6 3.0 %fusion.68 = f32[256,768]{1,0:T(8,128)S(1)} fusion(bf16[768,2048]{1,0:T(8,128)(2,1)} %collective-permute-done.12, bf16[64,2048]{1,0:T(8,128)(2,1)S(1)} %get-tuple-element.58, bf16[64,2048]{1,0:T(8,128)(2,1)S(1)} %broadcast_select_fusion.7, bf16[64,2048]{1,0:T(8,128)(2,1)S(1)} %get-tuple-element.57, bf16[64,2048]{1,0:T(8,128)(2,1)S(1)} %copy-done.24), kind=kOutput, calls=%fused_computation.138 | convolution fusion | flops 809500672 | bytes 4980736 | tf_op jit(solution)/shard_map/dot_general | solution.py:14
  223.6 3.0 %fusion.63 = f32[256,2048]{1,0:T(8,128)S(1)} fusion(bf16[2048,768]{1,0:T(8,128)(2,1)} %collective-permute-done.10, f32[256,768]{1,0:T(8,128)S(1)} %fusion.68, f32[256,768]{1,0:T(8,128)S(1)} %copy-done.11, f32[256]{0:T(256)S(1)} %mul.269), kind=kOutput, calls=%fused_computation.123 | convolution fusion | flops 805896192 | bytes 6816768 | tf_op jit(solution)/shard_map/dot_general | solution.py:14
  230.5 2.2 fusion.52
  233.7 2.9 convolution_add_fusion.4
  236.6 3.1 %fusion.70 = f32[256,768]{1,0:T(8,128)S(1)} fusion(bf16[768,2048]{1,0:T(8,128)(2,1)} %collective-permute-done.12, bf16[64,2048]{1,0:T(8,128)(2,1)S(1)} %get-tuple-element.56, bf16[64,2048]{1,0:T(8,128)(2,1)S(1)} %broadcast_select_fusion.8, bf16[64,2048]{1,0:T(8,128)(2,1)S(1)} %get-tuple-element.55, bf16[64,2048]{1,0:T(8,128)(2,1)} %get-tuple-element.45), kind=kOutput, calls=%fused_computation.140 | convolution fusion | flops 809500672 | bytes 4980736 | tf_op jit(solution)/shard_map/dot_general | solution.py:14
  239.7 3.0 %fusion.62 = f32[256,2048]{1,0:T(8,128)S(1)} fusion(bf16[2048,768]{1,0:T(8,128)(2,1)} %collective-permute-done.10, f32[256,768]{1,0:T(8,128)S(1)} %fusion.70, f32[256,768]{1,0:T(8,128)S(1)} %copy-done.10, f32[256]{0:T(256)S(1)} %mul.238), kind=kOutput, calls=%fused_computation.122 | convolution fusion | flops 805896192 | bytes 6816768 | tf_op jit(solution)/shard_map/dot_general | solution.py:14
  247.4 2.0 collective-permute-done.23
  249.5 4.4 %collective-permute-start.24 = (bf16[64,2048]{1,0:T(8,128)(2,1)S(1)}, bf16[64,2048]{1,0:T(8,128)(2,1)S(1)}, u32[]{:S(2)}, u32[]{:S(2)}) collective-permute-start(bf16[64,2048]{1,0:T(8,128)(2,1)S(1)} %add_convert_fusion.8), channel_id=1, source_target_pairs={{0,2},{1,3},{2,4},{3,5},{8,10},{9,11},{10,12},{11,13},{16,18},{17,... | collective-permute-start | bytes 786440 | tf_op jit(solution)/shard_map/ppermute | solution.py:22
  254.8 4.3 %collective-permute-start.45 = (bf16[64,2048]{1,0:T(8,128)(2,1)S(1)}, bf16[64,2048]{1,0:T(8,128)(2,1)S(1)}, u32[]{:S(2)}, u32[]{:S(2)}) collective-permute-start(bf16[64,2048]{1,0:T(8,128)(2,1)S(1)} %get-tuple-element.39), channel_id=1, source_target_pairs={{0,2},{1,3},{2,4},{3,5},{4,6},{5,7},{8,10},{9,11},{10,12},{11,13},... | collective-permute-start | bytes 786440 | tf_op jit(solution)/shard_map/ppermute | solution.py:22
  260.5 4.6 %collective-permute-start.25 = (bf16[64,2048]{1,0:T(8,128)(2,1)S(1)}, bf16[64,2048]{1,0:T(8,128)(2,1)S(1)}, u32[]{:S(2)}, u32[]{:S(2)}) collective-permute-start(bf16[64,2048]{1,0:T(8,128)(2,1)S(1)} %get-tuple-element.35), channel_id=1, source_target_pairs={{0,2},{1,3},{2,4},{3,5},{4,6},{5,7},{8,10},{9,11},{10,12},{11,13},... | collective-permute-start | bytes 786440 | tf_op jit(solution)/shard_map/ppermute | solution.py:22
  269.0 4.4 %collective-permute-done.27 = bf16[64,2048]{1,0:T(8,128)(2,1)S(1)} collective-permute-done((bf16[64,2048]{1,0:T(8,128)(2,1)S(1)}, bf16[64,2048]{1,0:T(8,128)(2,1)S(1)}, u32[]{:S(2)}, u32[]{:S(2)}) %collective-permute-start.27) | collective-permute-done | bytes 262176 | tf_op jit(solution)/shard_map/ppermute | solution.py:22
  273.4 2.2 multiply_reduce_fusion
  278.5 2.1 collective-permute-done.48
  282.1 2.0 collective-permute-done.49
  286.2 2.8 collective-permute-done.51
  289.3 4.2 %collective-permute-done.52 = f32[8,128]{1,0:T(8,128)S(1)} collective-permute-done((f32[8,128]{1,0:T(8,128)S(1)}, f32[8,128]{1,0:T(8,128)S(1)}, u32[]{:S(2)}, u32[]{:S(2)}) %collective-permute-start.52) | collective-permute-done | bytes 4128 | tf_op jit(solution)/shard_map/ppermute | solution.py:72
  (192 shorter events, 94.6 us)
Async XLA Ops:
  4.6 28.2 %collective-permute-start.5 = (bf16[128,2048]{1,0:T(8,128)(2,1)}, bf16[128,2048]{1,0:T(8,128)(2,1)}, u32[]{:S(2)}, u32[]{:S(2)}) collective-permute-start(bf16[128,2048]{1,0:T(8,128)(2,1)} %pad_maximum_fusion.3), channel_id=1, source_target_pairs={{0,2},{1,3},{2,4},{3,5},{4,6},{5,7},{8,10},{9,11},{10,12},{11,13},... | collective-permute-start | bytes 1572872 | tf_op jit(solution)/shard_map/ppermute | solution.py:22
  10.3 23.9 %collective-permute-start.7 = (bf16[128,2048]{1,0:T(8,128)(2,1)}, bf16[128,2048]{1,0:T(8,128)(2,1)}, u32[]{:S(2)}, u32[]{:S(2)}) collective-permute-start(bf16[128,2048]{1,0:T(8,128)(2,1)} %pad_maximum_fusion.3), channel_id=1, source_target_pairs={{2,0},{3,1},{4,2},{5,3},{6,4},{7,5},{10,8},{11,9},{12,10},{13,11},... | collective-permute-start | bytes 1572872 | tf_op jit(solution)/shard_map/ppermute | solution.py:22
  11.7 9.4 %collective-permute-start = (f32[8,128]{1,0:T(8,128)S(1)}, f32[8,128]{1,0:T(8,128)S(1)}, u32[]{:S(2)}, u32[]{:S(2)}) collective-permute-start(f32[8,128]{1,0:T(8,128)S(1)} %bitcast.251), channel_id=1, source_target_pairs={{0,2},{1,3},{2,4},{3,5},{4,6},{5,7},{8,10},{9,11},{10,12},{11,13},... | collective-permute-start | bytes 12296 | tf_op jit(solution)/shard_map/ppermute | solution.py:22
  16.2 9.7 %collective-permute-start.2 = (f32[8,128]{1,0:T(8,128)S(1)}, f32[8,128]{1,0:T(8,128)S(1)}, u32[]{:S(2)}, u32[]{:S(2)}) collective-permute-start(f32[8,128]{1,0:T(8,128)S(1)} %bitcast.252), channel_id=1, source_target_pairs={{2,0},{3,1},{4,2},{5,3},{6,4},{7,5},{10,8},{11,9},{12,10},{13,11},... | collective-permute-start | bytes 12296 | tf_op jit(solution)/shard_map/ppermute | solution.py:22
  21.0 6.3 %collective-permute-start.1 = (f32[8,128]{1,0:T(8,128)S(1)}, f32[8,128]{1,0:T(8,128)S(1)}, u32[]{:S(2)}, u32[]{:S(2)}) collective-permute-start(f32[8,128]{1,0:T(8,128)S(1)} %collective-permute-done), channel_id=1, source_target_pairs={{2,4},{3,5},{4,6},{5,7},{10,12},{11,13},{12,14},{13,15},{18,20},{1... | collective-permute-start | bytes 12296 | tf_op jit(solution)/shard_map/ppermute | solution.py:22
  26.0 5.5 %collective-permute-start.3 = (f32[8,128]{1,0:T(8,128)S(1)}, f32[8,128]{1,0:T(8,128)S(1)}, u32[]{:S(2)}, u32[]{:S(2)}) collective-permute-start(f32[8,128]{1,0:T(8,128)S(1)} %collective-permute-done.2), channel_id=1, source_target_pairs={{2,0},{3,1},{4,2},{5,3},{10,8},{11,9},{12,10},{13,11},{18,16},{19,... | collective-permute-start | bytes 12296 | tf_op jit(solution)/shard_map/ppermute | solution.py:22
  27.3 85.3 %collective-permute-start.10 = (bf16[2048,768]{1,0:T(8,128)(2,1)}, bf16[2048,768]{1,0:T(8,128)(2,1)}, u32[]{:S(2)}, u32[]{:S(2)}) collective-permute-start(bf16[2048,768]{1,0:T(8,128)(2,1)} %bitcast.7), channel_id=1, source_target_pairs={{0,1},{1,0},{2,3},{3,2},{4,5},{5,4},{6,7},{7,6},{8,9},{9,8},{10,11... | collective-permute-start | bytes 9437192 | tf_op jit(solution)/shard_map/ppermute | solution.py:98
  27.4 88.9 %collective-permute-start.11 = (bf16[2048,768]{1,0:T(8,128)(2,1)}, bf16[2048,768]{1,0:T(8,128)(2,1)S(1)}, u32[]{:S(2)}, u32[]{:S(2)}) collective-permute-start(bf16[2048,768]{1,0:T(8,128)(2,1)} %bitcast.237), channel_id=1, source_target_pairs={{0,1},{1,0},{2,3},{3,2},{4,5},{5,4},{6,7},{7,6},{8,9},{9,8},{10,11... | collective-permute-start | bytes 9437192 | tf_op jit(solution)/shard_map/ppermute | solution.py:98
  31.5 5.9 %collective-permute-start.4 = (f32[8,128]{1,0:T(8,128)S(1)}, f32[8,128]{1,0:T(8,128)S(1)}, u32[]{:S(2)}, u32[]{:S(2)}) collective-permute-start(f32[8,128]{1,0:T(8,128)S(1)} %broadcast_select_fusion.15), channel_id=1, source_target_pairs={{4,6},{5,7},{2,0},{3,1},{12,14},{13,15},{10,8},{11,9},{20,22},{21,... | collective-permute-start | bytes 12296 | tf_op jit(solution)/shard_map/ppermute | solution.py:22
  32.8 4.6 %collective-permute-start.6 = (bf16[128,2048]{1,0:T(8,128)(2,1)}, bf16[128,2048]{1,0:T(8,128)(2,1)}, u32[]{:S(2)}, u32[]{:S(2)}) collective-permute-start(bf16[128,2048]{1,0:T(8,128)(2,1)} %collective-permute-done.5), channel_id=1, source_target_pairs={{2,4},{3,5},{4,6},{5,7},{10,12},{11,13},{12,14},{13,15},{18,20},{1... | collective-permute-start | bytes 1572872 | tf_op jit(solution)/shard_map/ppermute | solution.py:22
  34.2 16.8 %collective-permute-start.8 = (bf16[128,2048]{1,0:T(8,128)(2,1)}, bf16[128,2048]{1,0:T(8,128)(2,1)}, u32[]{:S(2)}, u32[]{:S(2)}) collective-permute-start(bf16[128,2048]{1,0:T(8,128)(2,1)} %collective-permute-done.7), channel_id=1, source_target_pairs={{2,0},{3,1},{4,2},{5,3},{10,8},{11,9},{12,10},{13,11},{18,16},{19,... | collective-permute-start | bytes 1572872 | tf_op jit(solution)/shard_map/ppermute | solution.py:22
  37.3 88.1 %collective-permute-start.12 = (bf16[768,2048]{1,0:T(8,128)(2,1)}, bf16[768,2048]{1,0:T(8,128)(2,1)}, u32[]{:S(2)}, u32[]{:S(2)}) collective-permute-start(bf16[768,2048]{1,0:T(8,128)(2,1)} %bitcast.236), channel_id=1, source_target_pairs={{0,1},{1,0},{2,3},{3,2},{4,5},{5,4},{6,7},{7,6},{8,9},{9,8},{10,11... | collective-permute-start | bytes 9437192 | tf_op jit(solution)/shard_map/ppermute | solution.py:98
  52.9 14.6 %collective-permute-start.9 = (bf16[128,2048]{1,0:T(8,128)(2,1)}, bf16[128,2048]{1,0:T(8,128)(2,1)}, u32[]{:S(2)}, u32[]{:S(2)}) collective-permute-start(bf16[128,2048]{1,0:T(8,128)(2,1)} %broadcast_select_fusion.3), channel_id=1, source_target_pairs={{4,6},{5,7},{2,0},{3,1},{12,14},{13,15},{10,8},{11,9},{20,22},{21,... | collective-permute-start | bytes 1572872 | tf_op jit(solution)/shard_map/ppermute | solution.py:22
  73.7 10.6 %collective-permute-start.28 = (bf16[128,2048]{1,0:T(8,128)(2,1)S(1)}, bf16[128,2048]{1,0:T(8,128)(2,1)S(1)}, u32[]{:S(2)}, u32[]{:S(2)}) collective-permute-start(bf16[128,2048]{1,0:T(8,128)(2,1)S(1)} %copy-done.12), channel_id=1, source_target_pairs={{0,2},{1,3},{2,4},{3,5},{4,6},{5,7},{8,10},{9,11},{10,12},{11,13},... | collective-permute-start | bytes 1572872 | tf_op jit(solution)/shard_map/ppermute | solution.py:22
  75.2 13.2 %collective-permute-start.30 = (bf16[128,2048]{1,0:T(8,128)(2,1)S(1)}, bf16[128,2048]{1,0:T(8,128)(2,1)S(1)}, u32[]{:S(2)}, u32[]{:S(2)}) collective-permute-start(bf16[128,2048]{1,0:T(8,128)(2,1)S(1)} %copy-done.12), channel_id=1, source_target_pairs={{2,0},{3,1},{4,2},{5,3},{6,4},{7,5},{10,8},{11,9},{12,10},{13,11},... | collective-permute-start | bytes 1572872 | tf_op jit(solution)/shard_map/ppermute | solution.py:22
  84.3 9.1 %collective-permute-start.29 = (bf16[128,2048]{1,0:T(8,128)(2,1)S(1)}, bf16[128,2048]{1,0:T(8,128)(2,1)S(1)}, u32[]{:S(2)}, u32[]{:S(2)}) collective-permute-start(bf16[128,2048]{1,0:T(8,128)(2,1)S(1)} %collective-permute-done.28), channel_id=1, source_target_pairs={{2,4},{3,5},{4,6},{5,7},{10,12},{11,13},{12,14},{13,15},{18,20},{1... | collective-permute-start | bytes 1572872 | tf_op jit(solution)/shard_map/ppermute | solution.py:22
  88.4 12.3 %collective-permute-start.31 = (bf16[128,2048]{1,0:T(8,128)(2,1)S(1)}, bf16[128,2048]{1,0:T(8,128)(2,1)S(1)}, u32[]{:S(2)}, u32[]{:S(2)}) collective-permute-start(bf16[128,2048]{1,0:T(8,128)(2,1)S(1)} %collective-permute-done.30), channel_id=1, source_target_pairs={{2,0},{3,1},{4,2},{5,3},{10,8},{11,9},{12,10},{13,11},{18,16},{19,... | collective-permute-start | bytes 1572872 | tf_op jit(solution)/shard_map/ppermute | solution.py:22
  100.8 11.4 %collective-permute-start.32 = (bf16[128,2048]{1,0:T(8,128)(2,1)S(1)}, bf16[128,2048]{1,0:T(8,128)(2,1)S(1)}, u32[]{:S(2)}, u32[]{:S(2)}) collective-permute-start(bf16[128,2048]{1,0:T(8,128)(2,1)S(1)} %broadcast_select_fusion.2), channel_id=1, source_target_pairs={{4,6},{5,7},{2,0},{3,1},{12,14},{13,15},{10,8},{11,9},{20,22},{21,... | collective-permute-start | bytes 1572872 | tf_op jit(solution)/shard_map/ppermute | solution.py:22
  128.4 15.9 %collective-permute-start.13 = (bf16[64,2048]{1,0:T(8,128)(2,1)S(1)}, bf16[64,2048]{1,0:T(8,128)(2,1)S(1)}, u32[]{:S(2)}, u32[]{:S(2)}) collective-permute-start(bf16[64,2048]{1,0:T(8,128)(2,1)S(1)} %broadcast_select_fusion.14), channel_id=1, source_target_pairs={{0,2},{1,3},{6,4},{7,5},{8,10},{9,11},{14,12},{15,13},{16,18},{17,... | collective-permute-start | bytes 786440 | tf_op jit(solution)/shard_map/ppermute | solution.py:22
  143.0 6.9 %collective-permute-start.33 = (bf16[64,2048]{1,0:T(8,128)(2,1)S(1)}, bf16[64,2048]{1,0:T(8,128)(2,1)S(1)}, u32[]{:S(2)}, u32[]{:S(2)}) collective-permute-start(bf16[64,2048]{1,0:T(8,128)(2,1)S(1)} %broadcast_select_fusion.12), channel_id=1, source_target_pairs={{0,2},{1,3},{6,4},{7,5},{8,10},{9,11},{14,12},{15,13},{16,18},{17,... | collective-permute-start | bytes 786440 | tf_op jit(solution)/shard_map/ppermute | solution.py:22
  144.4 11.1 %collective-permute-start.14 = (bf16[64,2048]{1,0:T(8,128)(2,1)S(1)}, bf16[64,2048]{1,0:T(8,128)(2,1)S(1)}, u32[]{:S(2)}, u32[]{:S(2)}) collective-permute-start(bf16[64,2048]{1,0:T(8,128)(2,1)S(1)} %add_convert_fusion.11), channel_id=1, source_target_pairs={{0,2},{1,3},{2,4},{3,5},{8,10},{9,11},{10,12},{11,13},{16,18},{17,... | collective-permute-start | bytes 786440 | tf_op jit(solution)/shard_map/ppermute | solution.py:22
  145.8 9.6 %collective-permute-start.16 = (bf16[64,2048]{1,0:T(8,128)(2,1)S(1)}, bf16[64,2048]{1,0:T(8,128)(2,1)S(1)}, u32[]{:S(2)}, u32[]{:S(2)}) collective-permute-start(bf16[64,2048]{1,0:T(8,128)(2,1)S(1)} %add_convert_fusion.11), channel_id=1, source_target_pairs={{4,2},{5,3},{6,4},{7,5},{12,10},{13,11},{14,12},{15,13},{20,18},{2... | collective-permute-start | bytes 786440 | tf_op jit(solution)/shard_map/ppermute | solution.py:22
  149.9 11.4 %collective-permute-start.34 = (bf16[64,2048]{1,0:T(8,128)(2,1)S(1)}, bf16[64,2048]{1,0:T(8,128)(2,1)S(1)}, u32[]{:S(2)}, u32[]{:S(2)}) collective-permute-start(bf16[64,2048]{1,0:T(8,128)(2,1)S(1)} %add_convert_fusion.5), channel_id=1, source_target_pairs={{0,2},{1,3},{2,4},{3,5},{8,10},{9,11},{10,12},{11,13},{16,18},{17,... | collective-permute-start | bytes 786440 | tf_op jit(solution)/shard_map/ppermute | solution.py:22
  154.3 7.0 %collective-permute-start.36 = (bf16[64,2048]{1,0:T(8,128)(2,1)S(1)}, bf16[64,2048]{1,0:T(8,128)(2,1)S(1)}, u32[]{:S(2)}, u32[]{:S(2)}) collective-permute-start(bf16[64,2048]{1,0:T(8,128)(2,1)S(1)} %add_convert_fusion.5), channel_id=1, source_target_pairs={{4,2},{5,3},{6,4},{7,5},{12,10},{13,11},{14,12},{15,13},{20,18},{2... | collective-permute-start | bytes 786440 | tf_op jit(solution)/shard_map/ppermute | solution.py:22
  155.6 11.7 %collective-permute-start.15 = (bf16[64,2048]{1,0:T(8,128)(2,1)S(1)}, bf16[64,2048]{1,0:T(8,128)(2,1)S(1)}, u32[]{:S(2)}, u32[]{:S(2)}) collective-permute-start(bf16[64,2048]{1,0:T(8,128)(2,1)S(1)} %get-tuple-element.37), channel_id=1, source_target_pairs={{0,2},{1,3},{2,4},{3,5},{4,6},{5,7},{8,10},{9,11},{10,12},{11,13},... | collective-permute-start | bytes 786440 | tf_op jit(solution)/shard_map/ppermute | solution.py:22
  160.0 8.3 %collective-permute-start.17 = (bf16[64,2048]{1,0:T(8,128)(2,1)S(1)}, bf16[64,2048]{1,0:T(8,128)(2,1)S(1)}, u32[]{:S(2)}, u32[]{:S(2)}) collective-permute-start(bf16[64,2048]{1,0:T(8,128)(2,1)S(1)} %get-tuple-element.38), channel_id=1, source_target_pairs={{2,0},{3,1},{4,2},{5,3},{6,4},{7,5},{10,8},{11,9},{12,10},{13,11},... | collective-permute-start | bytes 786440 | tf_op jit(solution)/shard_map/ppermute | solution.py:22
  161.5 9.3 %collective-permute-start.35 = (bf16[64,2048]{1,0:T(8,128)(2,1)S(1)}, bf16[64,2048]{1,0:T(8,128)(2,1)S(1)}, u32[]{:S(2)}, u32[]{:S(2)}) collective-permute-start(bf16[64,2048]{1,0:T(8,128)(2,1)S(1)} %get-tuple-element.41), channel_id=1, source_target_pairs={{0,2},{1,3},{2,4},{3,5},{4,6},{5,7},{8,10},{9,11},{10,12},{11,13},... | collective-permute-start | bytes 786440 | tf_op jit(solution)/shard_map/ppermute | solution.py:22
  166.0 8.7 %collective-permute-start.37 = (bf16[64,2048]{1,0:T(8,128)(2,1)S(1)}, bf16[64,2048]{1,0:T(8,128)(2,1)S(1)}, u32[]{:S(2)}, u32[]{:S(2)}) collective-permute-start(bf16[64,2048]{1,0:T(8,128)(2,1)S(1)} %get-tuple-element.42), channel_id=1, source_target_pairs={{2,0},{3,1},{4,2},{5,3},{6,4},{7,5},{10,8},{11,9},{12,10},{13,11},... | collective-permute-start | bytes 786440 | tf_op jit(solution)/shard_map/ppermute | solution.py:22
  175.9 11.5 %collective-permute-start.38 = (bf16[64,2048]{1,0:T(8,128)(2,1)S(1)}, bf16[64,2048]{1,0:T(8,128)(2,1)}, u32[]{:S(2)}, u32[]{:S(2)}) collective-permute-start(bf16[64,2048]{1,0:T(8,128)(2,1)S(1)} %get-tuple-element.46), channel_id=1, source_target_pairs={{0,2},{1,3},{2,4},{3,5},{4,6},{5,7},{8,10},{9,11},{10,12},{11,13},... | collective-permute-start | bytes 786440 | tf_op jit(solution)/shard_map/ppermute | solution.py:22
  179.5 10.2 %collective-permute-start.40 = (bf16[64,2048]{1,0:T(8,128)(2,1)S(1)}, bf16[64,2048]{1,0:T(8,128)(2,1)}, u32[]{:S(2)}, u32[]{:S(2)}) collective-permute-start(bf16[64,2048]{1,0:T(8,128)(2,1)S(1)} %get-tuple-element.46), channel_id=1, source_target_pairs={{2,0},{3,1},{4,2},{5,3},{6,4},{7,5},{10,8},{11,9},{12,10},{13,11},... | collective-permute-start | bytes 786440 | tf_op jit(solution)/shard_map/ppermute | solution.py:22
  180.8 10.3 %collective-permute-start.18 = (bf16[64,2048]{1,0:T(8,128)(2,1)}, bf16[64,2048]{1,0:T(8,128)(2,1)}, u32[]{:S(2)}, u32[]{:S(2)}) collective-permute-start(bf16[64,2048]{1,0:T(8,128)(2,1)} %get-tuple-element.45), channel_id=1, source_target_pairs={{0,2},{1,3},{2,4},{3,5},{4,6},{5,7},{8,10},{9,11},{10,12},{11,13},... | collective-permute-start | bytes 786440 | tf_op jit(solution)/shard_map/ppermute | solution.py:22
  186.0 11.4 %collective-permute-start.20 = (bf16[64,2048]{1,0:T(8,128)(2,1)}, bf16[64,2048]{1,0:T(8,128)(2,1)}, u32[]{:S(2)}, u32[]{:S(2)}) collective-permute-start(bf16[64,2048]{1,0:T(8,128)(2,1)} %get-tuple-element.45), channel_id=1, source_target_pairs={{2,0},{3,1},{4,2},{5,3},{6,4},{7,5},{10,8},{11,9},{12,10},{13,11},... | collective-permute-start | bytes 786440 | tf_op jit(solution)/shard_map/ppermute | solution.py:22
  187.3 11.4 %collective-permute-start.39 = (bf16[64,2048]{1,0:T(8,128)(2,1)}, bf16[64,2048]{1,0:T(8,128)(2,1)}, u32[]{:S(2)}, u32[]{:S(2)}) collective-permute-start(bf16[64,2048]{1,0:T(8,128)(2,1)} %collective-permute-done.38), channel_id=1, source_target_pairs={{2,4},{3,5},{4,6},{5,7},{10,12},{11,13},{12,14},{13,15},{18,20},{1... | collective-permute-start | bytes 786440 | tf_op jit(solution)/shard_map/ppermute | solution.py:22
  189.6 13.5 %collective-permute-start.41 = (bf16[64,2048]{1,0:T(8,128)(2,1)}, bf16[64,2048]{1,0:T(8,128)(2,1)}, u32[]{:S(2)}, u32[]{:S(2)}) collective-permute-start(bf16[64,2048]{1,0:T(8,128)(2,1)} %collective-permute-done.40), channel_id=1, source_target_pairs={{2,0},{3,1},{4,2},{5,3},{10,8},{11,9},{12,10},{13,11},{18,16},{19,... | collective-permute-start | bytes 786440 | tf_op jit(solution)/shard_map/ppermute | solution.py:22
  191.1 14.3 %collective-permute-start.19 = (bf16[64,2048]{1,0:T(8,128)(2,1)}, bf16[64,2048]{1,0:T(8,128)(2,1)S(1)}, u32[]{:S(2)}, u32[]{:S(2)}) collective-permute-start(bf16[64,2048]{1,0:T(8,128)(2,1)} %collective-permute-done.18), channel_id=1, source_target_pairs={{2,4},{3,5},{4,6},{5,7},{10,12},{11,13},{12,14},{13,15},{18,20},{1... | collective-permute-start | bytes 786440 | tf_op jit(solution)/shard_map/ppermute | solution.py:22
  197.5 9.6 %collective-permute-start.21 = (bf16[64,2048]{1,0:T(8,128)(2,1)}, bf16[64,2048]{1,0:T(8,128)(2,1)S(1)}, u32[]{:S(2)}, u32[]{:S(2)}) collective-permute-start(bf16[64,2048]{1,0:T(8,128)(2,1)} %collective-permute-done.20), channel_id=1, source_target_pairs={{2,0},{3,1},{4,2},{5,3},{10,8},{11,9},{12,10},{13,11},{18,16},{19,... | collective-permute-start | bytes 786440 | tf_op jit(solution)/shard_map/ppermute | solution.py:22
  204.1 8.3 %collective-permute-start.42 = (bf16[64,2048]{1,0:T(8,128)(2,1)S(1)}, bf16[64,2048]{1,0:T(8,128)(2,1)S(1)}, u32[]{:S(2)}, u32[]{:S(2)}) collective-permute-start(bf16[64,2048]{1,0:T(8,128)(2,1)S(1)} %broadcast_select_fusion.7), channel_id=1, source_target_pairs={{4,6},{5,7},{2,0},{3,1},{12,14},{13,15},{10,8},{11,9},{20,22},{21,... | collective-permute-start | bytes 786440 | tf_op jit(solution)/shard_map/ppermute | solution.py:22
  207.1 22.3 %collective-permute-start.22 = (bf16[64,2048]{1,0:T(8,128)(2,1)S(1)}, bf16[64,2048]{1,0:T(8,128)(2,1)S(1)}, u32[]{:S(2)}, u32[]{:S(2)}) collective-permute-start(bf16[64,2048]{1,0:T(8,128)(2,1)S(1)} %broadcast_select_fusion.8), channel_id=1, source_target_pairs={{4,6},{5,7},{2,0},{3,1},{12,14},{13,15},{10,8},{11,9},{20,22},{21,... | collective-permute-start | bytes 786440 | tf_op jit(solution)/shard_map/ppermute | solution.py:22
  227.7 17.4 %collective-permute-start.43 = (bf16[64,2048]{1,0:T(8,128)(2,1)S(1)}, bf16[64,2048]{1,0:T(8,128)(2,1)S(1)}, u32[]{:S(2)}, u32[]{:S(2)}) collective-permute-start(bf16[64,2048]{1,0:T(8,128)(2,1)S(1)} %broadcast_select_fusion.11), channel_id=1, source_target_pairs={{0,2},{1,3},{6,4},{7,5},{8,10},{9,11},{14,12},{15,13},{16,18},{17,... | collective-permute-start | bytes 786440 | tf_op jit(solution)/shard_map/ppermute | solution.py:22
  243.8 5.7 %collective-permute-start.23 = (bf16[64,2048]{1,0:T(8,128)(2,1)S(1)}, bf16[64,2048]{1,0:T(8,128)(2,1)S(1)}, u32[]{:S(2)}, u32[]{:S(2)}) collective-permute-start(bf16[64,2048]{1,0:T(8,128)(2,1)S(1)} %broadcast_select_fusion.13), channel_id=1, source_target_pairs={{0,2},{1,3},{6,4},{7,5},{8,10},{9,11},{14,12},{15,13},{16,18},{17,... | collective-permute-start | bytes 786440 | tf_op jit(solution)/shard_map/ppermute | solution.py:22
  245.3 9.3 %collective-permute-start.44 = (bf16[64,2048]{1,0:T(8,128)(2,1)S(1)}, bf16[64,2048]{1,0:T(8,128)(2,1)S(1)}, u32[]{:S(2)}, u32[]{:S(2)}) collective-permute-start(bf16[64,2048]{1,0:T(8,128)(2,1)S(1)} %add_convert_fusion.2), channel_id=1, source_target_pairs={{0,2},{1,3},{2,4},{3,5},{8,10},{9,11},{10,12},{11,13},{16,18},{17,... | collective-permute-start | bytes 786440 | tf_op jit(solution)/shard_map/ppermute | solution.py:22
  246.7 7.9 %collective-permute-start.46 = (bf16[64,2048]{1,0:T(8,128)(2,1)S(1)}, bf16[64,2048]{1,0:T(8,128)(2,1)S(1)}, u32[]{:S(2)}, u32[]{:S(2)}) collective-permute-start(bf16[64,2048]{1,0:T(8,128)(2,1)S(1)} %add_convert_fusion.2), channel_id=1, source_target_pairs={{4,2},{5,3},{6,4},{7,5},{12,10},{13,11},{14,12},{15,13},{20,18},{2... | collective-permute-start | bytes 786440 | tf_op jit(solution)/shard_map/ppermute | solution.py:22
  249.5 10.9 %collective-permute-start.24 = (bf16[64,2048]{1,0:T(8,128)(2,1)S(1)}, bf16[64,2048]{1,0:T(8,128)(2,1)S(1)}, u32[]{:S(2)}, u32[]{:S(2)}) collective-permute-start(bf16[64,2048]{1,0:T(8,128)(2,1)S(1)} %add_convert_fusion.8), channel_id=1, source_target_pairs={{0,2},{1,3},{2,4},{3,5},{8,10},{9,11},{10,12},{11,13},{16,18},{17,... | collective-permute-start | bytes 786440 | tf_op jit(solution)/shard_map/ppermute | solution.py:22
  253.9 6.5 %collective-permute-start.26 = (bf16[64,2048]{1,0:T(8,128)(2,1)S(1)}, bf16[64,2048]{1,0:T(8,128)(2,1)S(1)}, u32[]{:S(2)}, u32[]{:S(2)}) collective-permute-start(bf16[64,2048]{1,0:T(8,128)(2,1)S(1)} %add_convert_fusion.8), channel_id=1, source_target_pairs={{4,2},{5,3},{6,4},{7,5},{12,10},{13,11},{14,12},{15,13},{20,18},{2... | collective-permute-start | bytes 786440 | tf_op jit(solution)/shard_map/ppermute | solution.py:22
  254.8 11.6 %collective-permute-start.45 = (bf16[64,2048]{1,0:T(8,128)(2,1)S(1)}, bf16[64,2048]{1,0:T(8,128)(2,1)S(1)}, u32[]{:S(2)}, u32[]{:S(2)}) collective-permute-start(bf16[64,2048]{1,0:T(8,128)(2,1)S(1)} %get-tuple-element.39), channel_id=1, source_target_pairs={{0,2},{1,3},{2,4},{3,5},{4,6},{5,7},{8,10},{9,11},{10,12},{11,13},... | collective-permute-start | bytes 786440 | tf_op jit(solution)/shard_map/ppermute | solution.py:22
  259.1 8.3 %collective-permute-start.47 = (bf16[64,2048]{1,0:T(8,128)(2,1)S(1)}, bf16[64,2048]{1,0:T(8,128)(2,1)S(1)}, u32[]{:S(2)}, u32[]{:S(2)}) collective-permute-start(bf16[64,2048]{1,0:T(8,128)(2,1)S(1)} %get-tuple-element.40), channel_id=1, source_target_pairs={{2,0},{3,1},{4,2},{5,3},{6,4},{7,5},{10,8},{11,9},{12,10},{13,11},... | collective-permute-start | bytes 786440 | tf_op jit(solution)/shard_map/ppermute | solution.py:22
  260.5 8.4 %collective-permute-start.25 = (bf16[64,2048]{1,0:T(8,128)(2,1)S(1)}, bf16[64,2048]{1,0:T(8,128)(2,1)S(1)}, u32[]{:S(2)}, u32[]{:S(2)}) collective-permute-start(bf16[64,2048]{1,0:T(8,128)(2,1)S(1)} %get-tuple-element.35), channel_id=1, source_target_pairs={{0,2},{1,3},{2,4},{3,5},{4,6},{5,7},{8,10},{9,11},{10,12},{11,13},... | collective-permute-start | bytes 786440 | tf_op jit(solution)/shard_map/ppermute | solution.py:22
  265.1 8.3 %collective-permute-start.27 = (bf16[64,2048]{1,0:T(8,128)(2,1)S(1)}, bf16[64,2048]{1,0:T(8,128)(2,1)S(1)}, u32[]{:S(2)}, u32[]{:S(2)}) collective-permute-start(bf16[64,2048]{1,0:T(8,128)(2,1)S(1)} %get-tuple-element.36), channel_id=1, source_target_pairs={{2,0},{3,1},{4,2},{5,3},{6,4},{7,5},{10,8},{11,9},{12,10},{13,11},... | collective-permute-start | bytes 786440 | tf_op jit(solution)/shard_map/ppermute | solution.py:22
  (33 other events, 405.4 us)

commit v2 on v1

v2 whole, which is shorter than its diff:
```python
import functools

import jax
import jax.numpy as jnp
from jax import lax
from jax.experimental import pallas as pl
from jax.experimental.pallas import tpu as pltpu
from jax.sharding import PartitionSpec as P

CONTRACT_LAST = (((1,), (1,)), ((), ()))


def dot(lhs, rhs):
    return jnp.dot(lhs, rhs, preferred_element_type=jnp.float32)


def dot_last(lhs, rhs):
    return lax.dot_general(lhs, rhs, CONTRACT_LAST, preferred_element_type=jnp.float32)


CORES, SIDES, ENDS = 2, 2, 2
LINE = SIDES * ENDS
SIDE_PAIRS = ((0, 1), (1, 0), (2, 3), (3, 2))
INNER_PAIRS = ((1, 2), (2, 1))


def hop(rows, pairs):
    both_cores = [(CORES * a + core, CORES * b + core) for a, b in pairs for core in range(CORES)]
    return lax.ppermute(rows, "expert", both_cores)


def side_hop(rows):
    return hop(rows, SIDE_PAIRS)


def inner_hop(rows):
    return hop(rows, INNER_PAIRS)


def after(value, *earlier):
    return lax.optimization_barrier((value, earlier))[0]


def add_rows(own, came):
    return (own.astype(jnp.float32) + came.astype(jnp.float32)).astype(jnp.bfloat16)


def chunk_of(hidden):
    return 256 if hidden % 256 == 0 else hidden


def assemble(inner, parts, rows, out, first):
    own, side, near, near_end, far, far_end = parts
    out[pl.ds(first, rows), :] = own[...]
    out[pl.ds(first + rows, rows), :] = side[...]
    out[pl.ds(first + 2 * rows, rows), :] = jnp.where(inner, near[...], near_end[...])
    out[pl.ds(first + 3 * rows, rows), :] = jnp.where(inner, far[...], far_end[...])


def store_parts(total, rows, outs):
    for i, out in enumerate(outs):
        out[...] = total[pl.ds(i * rows, rows), :].astype(out.dtype)


def forward_kernel(chunks, inner_ref, *refs):
    x_parts, v_parts, refs = refs[:6], refs[6:12], refs[12:]
    g_ref, own_w, sib_w, refs = refs[0], refs[1:4], refs[4:7], refs[7:]
    outs, (b_out, a_out, xv, total) = refs[:LINE], refs[LINE:]
    rows = x_parts[0].shape[0]
    step = pl.program_id(0)

    @pl.when(step == 0)
    def _():
        inner = inner_ref[0] == 1
        assemble(inner, x_parts, rows, xv, 0)
        assemble(inner, v_parts, rows, xv, LINE * rows)
        total[...] = jnp.zeros_like(total)

    def work(weights):
        gate_w, up_w, down_w = weights
        pre = dot(xv[...], gate_w[0])
        ups = dot(xv[...], up_w[0])
        a, da = pre[: LINE * rows], pre[LINE * rows :]
        b, db = ups[: LINE * rows], ups[LINE * rows :]
        g = g_ref[0, :, :1]
        sigma = 1.0 / (1.0 + jnp.exp(-a))
        act = g * (a * sigma)
        b_slope = g * (sigma * (1.0 + a * (1.0 - sigma))) * b
        a_out[...] = act
        b_out[...] = b_slope
        hidden = (b_slope * da + act * db).astype(jnp.bfloat16)
        total[...] += dot(hidden, down_w[0])

    @pl.when(step < chunks)
    def _():
        work(own_w)

    @pl.when(step >= chunks)
    def _():
        work(sib_w)

    @pl.when(step == 2 * chunks - 1)
    def _():
        store_parts(total, rows, outs)


def backward_kernel(chunks, inner_ref, *refs):
    parts, (b_ref, a_ref), refs = refs[:6], refs[6:8], refs[8:]
    own_w, sib_w, refs = refs[:3], refs[3:6], refs[6:]
    outs, (jv, total) = refs[:LINE], refs[LINE:]
    rows = parts[0].shape[0]
    step = pl.program_id(0)

    @pl.when(step == 0)
    def _():
        assemble(inner_ref[0] == 1, parts, rows, jv, 0)
        total[...] = jnp.zeros_like(total)

    def work(weights):
        gate_w, up_w, down_w = weights
        back = dot_last(jv[...], down_w[0])
        grad_gate = (back * b_ref[...]).astype(jnp.bfloat16)
        grad_up = (back * a_ref[...]).astype(jnp.bfloat16)
        total[...] += dot_last(grad_gate, gate_w[0]) + dot_last(grad_up, up_w[0])

    @pl.when(step < chunks)
    def _():
        work(own_w)

    @pl.when(step >= chunks)
    def _():
        work(sib_w)

    @pl.when(step == 2 * chunks - 1)
    def _():
        store_parts(total, rows, outs)


def weight_specs(width, chunk, chunks):
    def own(step):
        return jnp.minimum(step, chunks - 1)

    def sib(step):
        return jnp.maximum(step - chunks, 0)

    specs = []
    for of in (own, sib):
        tall = pl.BlockSpec((1, width, chunk), lambda s, of=of: (0, 0, of(s)))
        wide = pl.BlockSpec((1, chunk, width), lambda s, of=of: (0, of(s), 0))
        specs += [tall, tall, wide]
    return specs


def kernel_call(kernel, name, inner, parts, states, weights, state_out):
    rows, width = parts[0].shape
    hidden = weights[0].shape[2]
    chunk = chunk_of(hidden)
    chunks = hidden // chunk
    line_rows = LINE * rows
    part_spec = pl.BlockSpec((rows, width), lambda s: (0, 0))
    state_spec = pl.BlockSpec((line_rows, chunk), lambda s: (0, s))
    part_outs = [jax.ShapeDtypeStruct((rows, width), jnp.float32)]
    part_outs += [jax.ShapeDtypeStruct((rows, width), jnp.bfloat16)] * (LINE - 1)
    state_outs = [jax.ShapeDtypeStruct((line_rows, 2 * hidden), jnp.float32)] * 2
    if state_out:
        state_specs = [pl.BlockSpec((1, line_rows, states[0].shape[2]), lambda s: (s // chunks, 0, 0))]
        out_specs, outs, dots, lines = [part_spec] * LINE + [state_spec] * 2, part_outs + state_outs, 5, 2
    else:
        state_specs = [state_spec] * 2
        out_specs, outs, dots, lines = [part_spec] * LINE, part_outs, 3, 1
    return pl.pallas_call(
        functools.partial(kernel, chunks),
        grid=(2 * chunks,),
        in_specs=[pl.BlockSpec(memory_space=pltpu.SMEM)]
        + [part_spec] * len(parts)
        + state_specs
        + weight_specs(width, chunk, chunks),
        out_specs=out_specs,
        out_shape=outs,
        scratch_shapes=[
            pltpu.VMEM((lines * line_rows, width), jnp.bfloat16),
            pltpu.VMEM((line_rows, width), jnp.float32),
        ],
        compiler_params=pltpu.CompilerParams(vmem_limit_bytes=40 * 2**20),
        cost_estimate=pl.CostEstimate(
            flops=2 * dots * line_rows * width * 2 * hidden,
            bytes_accessed=12 * hidden * width,
            transcendentals=0,
        ),
        name=name,
    )(inner, *parts, *states, *weights)


def sum_everywhere(value, axis):
    size = lax.axis_size(axis)
    if size & (size - 1):
        return lax.psum(value, axis)
    step = 1
    while step < size:
        value = value + lax.ppermute(value, axis, [(i, i ^ step) for i in range(size)])
        step *= 2
    return value


def line_shards(tokens, tangent, routes, gates, w_gate, w_up, w_down):
    token_count, width = tokens.shape
    owners = lax.axis_size("expert")
    me = lax.axis_index("expert")
    pos = me // CORES
    inner = (pos == 1) | (pos == 2)
    inner_flag = inner.astype(jnp.int32).reshape(1)
    half = token_count // 2

    own_weights = (w_gate, w_up, w_down)
    swap = [(i, i ^ 1) for i in range(owners)]
    weights = own_weights + tuple(lax.ppermute(w, "expert", swap) for w in own_weights)

    gate_of = jnp.sum(
        jnp.where(
            routes.T[:, None, :] == jnp.arange(owners, dtype=jnp.int32)[None, :, None],
            gates.T[:, None, :],
            jnp.float32(0.0),
        ),
        axis=0,
    )

    def pick(ends, inners):
        return jnp.where(inner, inners, ends)

    def gather(own):
        side, near = side_hop(own), inner_hop(own)
        near_end, far = side_hop(near), inner_hop(side)
        return (own, side, near, near_end, far, side_hop(far))

    xa, va = tokens[:half], tangent[:half]
    xa_parts, va_parts = gather(xa), gather(va)
    gate_parts = gather(gate_of)
    gate_rows = jnp.stack(
        [
            gate_parts[0],
            gate_parts[1],
            pick(gate_parts[3], gate_parts[2]),
            pick(gate_parts[5], gate_parts[4]),
        ]
    )
    pair_gates = [
        lax.dynamic_index_in_dim(gate_rows, expert, 1, keepdims=False) for expert in (me, me ^ 1)
    ]

    def gates_of(rows):
        columns = jnp.stack([g[:, rows].reshape(LINE * half, 1) for g in pair_gates])
        return jnp.broadcast_to(columns, (2, LINE * half, 128))

    def forward(x_parts, v_parts, rows):
        *parts, b_slope, act = kernel_call(
            forward_kernel, "forward", inner_flag, x_parts + v_parts, (gates_of(rows),), weights, True
        )
        return parts, (b_slope, act)

    def backward(jv_parts, states):
        return kernel_call(backward_kernel, "backward", inner_flag, jv_parts, states, weights, False)

    def home(parts, side, inner_last):
        return parts[0] + side.astype(jnp.float32) + pick(0.0, inner_last.astype(jnp.float32))

    xb, vb = after((tokens[half:], tangent[half:]), xa_parts[5], va_parts[5])
    xb_side, vb_side, xb_near, vb_near = side_hop(xb), side_hop(vb), inner_hop(xb), inner_hop(vb)
    pa, states_a = forward(xa_parts, va_parts, slice(0, half))
    came = side_hop(pick(pa[3], xb_near))
    xb_near_end, vb_near_end = came, side_hop(vb_near)
    xb_far, vb_far = inner_hop(xb_side), inner_hop(vb_side)
    sa_far = add_rows(pa[3], came)
    came = side_hop(pick(pa[2], xb_far))
    xb_far_end, vb_far_end = came, side_hop(vb_far)
    sa_side = inner_hop(sa_far)
    sa_near = add_rows(pa[2], came)
    came = side_hop(pick(pa[1], add_rows(pa[1], sa_side)))
    last = inner_hop(sa_near)
    pb, states_b = forward(
        (xb, xb_side, xb_near, xb_near_end, xb_far, xb_far_end),
        (vb, vb_side, vb_near, vb_near_end, vb_far, vb_far_end),
        slice(half, token_count),
    )
    jv_a = tangent[:half].astype(jnp.float32) + home(pa, came, last)

    def gather_and_reduce(own, parts):
        side, near = side_hop(own), inner_hop(own)
        came = side_hop(pick(parts[3], near))
        near_end, far = came, inner_hop(side)
        s_far = add_rows(parts[3], came)
        came = side_hop(pick(parts[2], far))
        far_end, s_side = came, inner_hop(s_far)
        s_near = add_rows(parts[2], came)
        came = side_hop(pick(parts[1], add_rows(parts[1], s_side)))
        last = inner_hop(s_near)
        return (own, side, near, near_end, far, far_end), home(parts, came, last)

    ja = jv_a.astype(jnp.bfloat16)
    ja_parts, sum_b = gather_and_reduce(ja, pb)
    ga = backward(ja_parts, states_a)
    jv_b = tangent[half:].astype(jnp.float32) + sum_b
    jb = jv_b.astype(jnp.bfloat16)
    jb_parts, grad_a = gather_and_reduce(jb, ga)

    squares = jnp.full((8, 128), jnp.sum(jv_a * jv_a) + jnp.sum(jv_b * jv_b))
    squares = sum_everywhere(sum_everywhere(squares, "dp"), "expert")

    gb = backward(jb_parts, states_b)
    came = side_hop(gb[3])
    s_far = add_rows(gb[3], came)
    came = side_hop(gb[2])
    s_side = inner_hop(s_far)
    s_near = add_rows(gb[2], came)
    q, _ = lax.optimization_barrier((pick(gb[1], add_rows(gb[1], s_side)), squares))
    came = side_hop(q)
    grad_b = home(gb, came, inner_hop(s_near))

    elements = token_count * width * lax.axis_size("dp") * owners
    scale = lax.rsqrt(squares[0, 0] / elements + 1e-06)
    return jnp.concatenate([(jv_a + grad_a) * scale, (jv_b + grad_b) * scale])


def owner_states(x_rows, gate_w, up_w):
    pre_a = dot(x_rows, gate_w)
    pre_b = dot(x_rows, up_w)
    sigma = jax.nn.sigmoid(pre_a)
    act = pre_a * sigma
    slope = sigma * (1.0 + pre_a * (1.0 - sigma))
    return (pre_b, act, slope)


def pair_shards(tokens, tangent, routes, gates, w_gate, w_up, w_down):
    token_count, model_width = tokens.shape
    top_k = routes.shape[1]
    owners = lax.axis_size("expert")
    expert_total = owners * w_gate.shape[0]
    capacity = pair_capacity(token_count, top_k, expert_total)
    slot_total = expert_total * capacity
    pair_count = token_count * top_k
    gate_w = w_gate[0]
    up_w = w_up[0]
    down_w = w_down[0]
    flat_routes = routes.reshape(pair_count)
    onehot = (flat_routes[:, None] == jnp.arange(expert_total, dtype=jnp.int32)[None, :]).astype(
        jnp.int32
    )
    before = jnp.cumsum(onehot, axis=0) - onehot
    slot_of = jnp.sum(before * onehot, axis=1)
    slot_index = flat_routes * capacity + slot_of
    slot_match = slot_index[None, :] == jnp.arange(slot_total, dtype=jnp.int32)[:, None]
    filled = jnp.any(slot_match, axis=1)
    pair_token = jnp.arange(pair_count, dtype=jnp.int32) // top_k
    source_token = jnp.sum(jnp.where(slot_match, pair_token[None, :], 0), axis=1)
    source_gate = jnp.sum(
        jnp.where(slot_match, gates.reshape(pair_count)[None, :], jnp.float32(0.0)), axis=1
    )
    keep_mask = filled.astype(jnp.bfloat16)[:, None]

    def exchange(rows):
        blocks = rows.reshape(owners, capacity, model_width)
        moved = lax.all_to_all(blocks, "expert", split_axis=0, concat_axis=0, tiled=True)
        return moved.reshape(slot_total, model_width)

    x_rows = exchange(jnp.take(tokens, source_token, axis=0) * keep_mask)
    v_rows = exchange(jnp.take(tangent, source_token, axis=0) * keep_mask)
    pre_b, act, slope = owner_states(x_rows, gate_w, up_w)
    tan_a = dot(v_rows, gate_w)
    tan_b = dot(v_rows, up_w)
    hidden_tangent = (slope * tan_a * pre_b + act * tan_b).astype(jnp.bfloat16)
    returned = exchange(dot(hidden_tangent, down_w).astype(jnp.bfloat16))
    picked_rows = jnp.take(returned, slot_index, axis=0)
    picked_rows = picked_rows.reshape(token_count, top_k, model_width)
    jv_vals = tangent.astype(jnp.float32) + jnp.sum(
        gates[:, :, None] * picked_rows.astype(jnp.float32), axis=1
    )
    cot_rows = exchange(
        (jnp.take(jv_vals, source_token, axis=0) * source_gate[:, None]).astype(jnp.bfloat16)
    )
    back_vals = dot_last(cot_rows, down_w)
    grad_gate = (back_vals * pre_b * slope).astype(jnp.bfloat16)
    grad_up = (back_vals * act).astype(jnp.bfloat16)
    pair_grad = dot_last(grad_gate, gate_w) + dot_last(grad_up, up_w)
    grad_rows = jnp.take(exchange(pair_grad.astype(jnp.bfloat16)), slot_index, axis=0)
    grad_rows = grad_rows.reshape(token_count, top_k, model_width)
    summed = jv_vals + jnp.sum(grad_rows.astype(jnp.float32), axis=1)
    global_sum = lax.psum(jnp.sum(jv_vals * jv_vals), ("dp", "expert"))
    element_count = token_count * lax.axis_size("dp") * owners * model_width
    return summed * lax.rsqrt(global_sum / element_count + 1e-06)


def pair_capacity(token_count, top_k, expert_total):
    return max(2, token_count * top_k * 9 // (8 * expert_total))


def shards(tokens, tangent, routes, gates, w_gate, w_up, w_down):
    token_count, top_k = routes.shape
    owners = lax.axis_size("expert")
    capacity = pair_capacity(token_count, top_k, owners * w_gate.shape[0])
    whole_blocks = (
        owners == CORES * LINE and w_gate.shape[0] == 1 and token_count <= CORES * capacity
    )
    form = line_shards if whole_blocks else pair_shards
    return form(tokens, tangent, routes, gates, w_gate, w_up, w_down)


def solution(mesh):
    placed = (
        P(("dp", "expert"), None),
        P(("dp", "expert"), None),
        P(("dp", "expert"), None),
        P(("dp", "expert"), None),
        P("expert", None, None),
        P("expert", None, None),
        P("expert", None, None),
    )
    return jax.shard_map(
        shards, mesh=mesh, in_specs=placed, out_specs=P(("dp", "expert"), None), check_vma=False
    )
```

time: 298 us -> 294 us (0.987)
  matrix products: 58.8 us -> 0 us
  Pallas kernels: 0 us -> 54.6 us
  starting transfers between devices: 93.6 us -> 129 us
  waiting for transfers between devices: 108 us -> 73.6 us
  local copies, waits for them, and re-layouts: 8.27 us -> 21.6 us
  other arithmetic: 23.7 us -> 11.4 us
    dot_general x24 -> x0, matrix products: 58.8 us -> none  [the longest x12 31.4 us: dot(): return jnp.dot(lhs, rhs, preferred_element_type=jnp.float32)]
    pallas_call x0 -> x4, Pallas kernels: none -> 54.6 us  [kernel_call(): pl.pallas_call(functools.partial(kernel, chunks), grid=(2 * chunks,), in_...]
    ppermute x48 -> x52, starting transfers between devices: 89.3 us -> 123 us  [the longest x49 122 us: hop(): return lax.ppermute(rows, 'expert', both_cores)]
    ppermute x48 -> x52, waiting for transfers between devices: 96 us -> 63.8 us  [the longest x49 63.8 us: hop(): return lax.ppermute(rows, 'expert', both_cores)]
    unnamed x57 -> x66, local copies, waits for them, and re-layouts: 3.04 us -> 17.6 us
    convert_element_type x3 -> x2, other arithmetic: 4.39 us -> 0.06 us  [the longest x1 0.03 us: line_shards(): ja = jv_a.astype(jnp.bfloat16)]
    concatenate x4 -> x1, other arithmetic: 4.83 us -> 1.07 us  [line_shards(): return jnp.concatenate([(jv_a + grad_a) * scale, (jv_b + grad_b) * scale])]
    slice x2 -> x0, other arithmetic: 3 us -> none  [line_shards(): b, db = (ups[:, i].reshape(count * half, -1) for i in range(2))]
  transfers between devices with their start and end apart: 53 -> 57, of which waited for: 28 -> 25; matrix products, arithmetic and copies ran while one was open for 26% -> 5% of each run, Pallas kernels for 0% -> 19%
where the time goes in v2:
time: 294 us; the launch traced here: 292 us
  starting transfers between devices  129 us (44%)
  waiting for transfers between devices  73.6 us (25%)
  Pallas kernels  54.6 us (19%)
  local copies, waits for them, and re-layouts  21.6 us (7%)
  other arithmetic  11.4 us (4%)
    ppermute x49, starting transfers between devices, hop(): return lax.ppermute(rows, 'expert', both_cores)  122 us
    ppermute x49, waiting for transfers between devices, hop(): return lax.ppermute(rows, 'expert', both_cores)  63.8 us
    pallas_call x4, Pallas kernels, kernel_call(): pl.pallas_call(functools.partial(kernel, chunks), grid=(2 * chunks,), in_...  54.6 us
    unnamed x66, local copies, waits for them, and re-layouts  17.6 us
    ppermute x5, waiting for transfers between devices, sum_everywhere(): lax.ppermute(value, axis, [(i, i ^ step) for i in range(size)])  9.75 us
  transfers between devices with their start and end apart: 57, of which 25 were waited for; matrix products, arithmetic and copies ran while one was open for 5% of the time, Pallas kernels for 19%

profile of v2, /device:TPU:0, one launch (start us, length us, event | category | flops | bytes accessed | tf_op | source)
XLA Modules:
  0.0 292.4 jit_solution(9814829617148321817)
XLA Ops:
  1.7 2.6 collective-permute-start.10
  7.6 4.9 %collective-permute-start.12 = (f32[8,128]{1,0:T(8,128)S(1)}, f32[8,128]{1,0:T(8,128)S(1)}, u32[]{:S(2)}, u32[]{:S(2)}) collective-permute-start(f32[8,128]{1,0:T(8,128)S(1)} %collective-permute-done.11), channel_id=1, source_target_pairs={{0,2},{1,3},{2,0},{3,1},{4,6},{5,7},{6,4},{7,5},{8,10},{9,11},{10,... | collective-permute-start | bytes 12296 | tf_op jit(solution)/shard_map/ppermute | solution.py:29
  12.5 2.3 collective-permute-start.14
  16.6 2.0 collective-permute-start.5
  18.6 7.2 %collective-permute-done.refs_1_ = bf16[64,2048]{1,0:T(8,128)(2,1)S(1)} collective-permute-done((bf16[64,2048]{1,0:T(8,128)(2,1)S(1)}, bf16[64,2048]{1,0:T(8,128)(2,1)S(1)}, u32[]{:S(2)}, u32[]{:S(2)}) %collective-permute-start) | collective-permute-done | bytes 262176 | tf_op jit(solution)/shard_map/ppermute | solution.py:29
  26.5 2.4 collective-permute-done.5.refs_7_
  31.0 16.3 %collective-permute-start.4 = (bf16[64,2048]{1,0:T(8,128)(2,1)S(1)}, bf16[64,2048]{1,0:T(8,128)(2,1)S(1)}, u32[]{:S(2)}, u32[]{:S(2)}) collective-permute-start(bf16[64,2048]{1,0:T(8,128)(2,1)S(1)} %collective-permute-done.3.refs_4_), channel_id=1, source_target_pairs={{0,2},{1,3},{2,0},{3,1},{4,6},{5,7},{6,4},{7,5},{8,10},{9,11},{10,... | collective-permute-start | bytes 786440 | tf_op jit(solution)/shard_map/ppermute | solution.py:29
  47.4 3.6 %collective-permute-start.9 = (bf16[64,2048]{1,0:T(8,128)(2,1)S(1)}, bf16[64,2048]{1,0:T(8,128)(2,1)S(1)}, u32[]{:S(2)}, u32[]{:S(2)}) collective-permute-start(bf16[64,2048]{1,0:T(8,128)(2,1)S(1)} %collective-permute-done.8.refs_10_), channel_id=1, source_target_pairs={{0,2},{1,3},{2,0},{3,1},{4,6},{5,7},{6,4},{7,5},{8,10},{9,11},{10,... | collective-permute-start | bytes 786440 | tf_op jit(solution)/shard_map/ppermute | solution.py:29
  50.9 2.6 collective-permute-done.4.refs_5_
  53.6 2.3 collective-permute-start.2
  55.9 3.3 %collective-permute-done.9.refs_11_ = bf16[64,2048]{1,0:T(8,128)(2,1)S(1)} collective-permute-done((bf16[64,2048]{1,0:T(8,128)(2,1)S(1)}, bf16[64,2048]{1,0:T(8,128)(2,1)S(1)}, u32[]{:S(2)}, u32[]{:S(2)}) %collective-permute-start.9) | collective-permute-done | bytes 262176 | tf_op jit(solution)/shard_map/ppermute | solution.py:29
  59.2 2.3 collective-permute-start.7
  61.7 3.1 %collective-permute-done.2.refs_3_ = bf16[64,2048]{1,0:T(8,128)(2,1)S(1)} collective-permute-done((bf16[64,2048]{1,0:T(8,128)(2,1)S(1)}, bf16[64,2048]{1,0:T(8,128)(2,1)S(1)}, u32[]{:S(2)}, u32[]{:S(2)}) %collective-permute-start.2) | collective-permute-done | bytes 262176 | tf_op jit(solution)/shard_map/ppermute | solution.py:29
  64.8 2.3 collective-permute-start.22
  67.1 3.3 %collective-permute-done.7.refs_9_ = bf16[64,2048]{1,0:T(8,128)(2,1)S(1)} collective-permute-done((bf16[64,2048]{1,0:T(8,128)(2,1)S(1)}, bf16[64,2048]{1,0:T(8,128)(2,1)S(1)}, u32[]{:S(2)}, u32[]{:S(2)}) %collective-permute-start.7) | collective-permute-done | bytes 262176 | tf_op jit(solution)/shard_map/ppermute | solution.py:29
  70.4 2.3 collective-permute-start.28
  72.9 3.2 %collective-permute-done.22.refs_1_ = bf16[64,2048]{1,0:T(8,128)(2,1)} collective-permute-done((bf16[64,2048]{1,0:T(8,128)(2,1)S(1)}, bf16[64,2048]{1,0:T(8,128)(2,1)}, u32[]{:S(2)}, u32[]{:S(2)}) %collective-permute-start.22) | collective-permute-done | bytes 262176 | tf_op jit(solution)/shard_map/ppermute | solution.py:29
  76.8 3.1 %collective-permute-done.28.refs_7_ = bf16[64,2048]{1,0:T(8,128)(2,1)} collective-permute-done((bf16[64,2048]{1,0:T(8,128)(2,1)}, bf16[64,2048]{1,0:T(8,128)(2,1)}, u32[]{:S(2)}, u32[]{:S(2)}) %collective-permute-start.28) | collective-permute-done | bytes 262176 | tf_op jit(solution)/shard_map/ppermute | solution.py:29
  85.4 1.9 copy-done.2
  87.3 13.6 %forward.2 = (f32[64,2048]{1,0:T(8,128)S(1)}, bf16[64,2048]{1,0:T(8,128)(2,1)S(1)}, bf16[64,2048]{1,0:T(8,128)(2,1)S(1)}, bf16[64,2048]{1,0:T(8,128)(2,1)S(1)}, ...) custom-call(s32[1]{0:T(128)} %bitcast.inner_ref, bf16[64,2048]{1,0:T(8,128)(2,1)S(1)} %get-tuple-element.57.refs_0_, ...), custom_call_target="tpu_custom_call" | custom-call | flops 8053063680 | bytes 18874368 | tf_op jit(solution)/shard_map/forward/pallas_call | solution.py:171
  103.3 8.0 %collective-permute-start.19 = (bf16[64,2048]{1,0:T(8,128)(2,1)S(1)}, bf16[64,2048]{1,0:T(8,128)(2,1)S(1)}, u32[]{:S(2)}, u32[]{:S(2)}) collective-permute-start(bf16[64,2048]{1,0:T(8,128)(2,1)S(1)} %broadcast_select_fusion.5), channel_id=1, source_target_pairs={{0,2},{1,3},{2,0},{3,1},{4,6},{5,7},{6,4},{7,5},{8,10},{9,11},{10,... | collective-permute-start | bytes 786440 | tf_op jit(solution)/shard_map/ppermute | solution.py:29
  111.4 6.5 %collective-permute-done.19.refs_3_ = bf16[64,2048]{1,0:T(8,128)(2,1)S(1)} collective-permute-done((bf16[64,2048]{1,0:T(8,128)(2,1)S(1)}, bf16[64,2048]{1,0:T(8,128)(2,1)S(1)}, u32[]{:S(2)}, u32[]{:S(2)}) %collective-permute-start.19) | collective-permute-done | bytes 262176 | tf_op jit(solution)/shard_map/ppermute | solution.py:29
  118.7 2.1 collective-permute-done.24.refs_5_
  123.7 7.1 %collective-permute-start.21 = (bf16[64,2048]{1,0:T(8,128)(2,1)}, bf16[64,2048]{1,0:T(8,128)(2,1)}, u32[]{:S(2)}, u32[]{:S(2)}) collective-permute-start(bf16[64,2048]{1,0:T(8,128)(2,1)} %fusion), channel_id=1, source_target_pairs={{0,2},{1,3},{2,0},{3,1},{4,6},{5,7},{6,4},{7,5},{8,10},{9,11},{10,... | collective-permute-start | bytes 786440 | tf_op jit(solution)/shard_map/ppermute | solution.py:29
  131.1 2.0 collective-permute-start.32
  133.2 2.4 collective-permute-done.21
  135.5 2.1 multiply_reduce_fusion.1
  138.4 2.7 collective-permute-done.32.refs_11_
  146.9 14.0 %forward.3 = (f32[64,2048]{1,0:T(8,128)S(1)}, bf16[64,2048]{1,0:T(8,128)(2,1)S(1)}, bf16[64,2048]{1,0:T(8,128)(2,1)S(1)}, bf16[64,2048]{1,0:T(8,128)(2,1)S(1)}, ...) custom-call(s32[1]{0:T(128)} %bitcast.inner_ref, bf16[64,2048]{1,0:T(8,128)(2,1)S(1)} %copy-done.22, ...), custom_call_target="tpu_custom_call" | custom-call | flops 8053063680 | bytes 18874368 | tf_op jit(solution)/shard_map/forward/pallas_call | solution.py:171
  161.0 2.1 collective-permute-start.26
  163.2 4.2 %collective-permute-done.26.refs_1_ = bf16[64,2048]{1,0:T(8,128)(2,1)S(1)} collective-permute-done((bf16[64,2048]{1,0:T(8,128)(2,1)S(1)}, bf16[64,2048]{1,0:T(8,128)(2,1)S(1)}, u32[]{:S(2)}, u32[]{:S(2)}) %collective-permute-start.26) | collective-permute-done | bytes 262176 | tf_op jit(solution)/shard_map/ppermute | solution.py:29
  168.1 4.3 %collective-permute-done.33.refs_3_ = bf16[64,2048]{1,0:T(8,128)(2,1)S(1)} collective-permute-done((bf16[64,2048]{1,0:T(8,128)(2,1)S(1)}, bf16[64,2048]{1,0:T(8,128)(2,1)S(1)}, u32[]{:S(2)}, u32[]{:S(2)}) %collective-permute-start.33) | collective-permute-done | bytes 262176 | tf_op jit(solution)/shard_map/ppermute | solution.py:29
  173.2 4.6 %collective-permute-start.35 = (bf16[64,2048]{1,0:T(8,128)(2,1)S(1)}, bf16[64,2048]{1,0:T(8,128)(2,1)S(1)}, u32[]{:S(2)}, u32[]{:S(2)}) collective-permute-start(bf16[64,2048]{1,0:T(8,128)(2,1)S(1)} %broadcast_select_fusion.2), channel_id=1, source_target_pairs={{0,2},{1,3},{2,0},{3,1},{4,6},{5,7},{6,4},{7,5},{8,10},{9,11},{10,... | collective-permute-start | bytes 786440 | tf_op jit(solution)/shard_map/ppermute | solution.py:29
  177.9 7.6 %collective-permute-start.37 = (bf16[64,2048]{1,0:T(8,128)(2,1)S(1)}, bf16[64,2048]{1,0:T(8,128)(2,1)S(1)}, u32[]{:S(2)}, u32[]{:S(2)}) collective-permute-start(bf16[64,2048]{1,0:T(8,128)(2,1)S(1)} %fusion.1), channel_id=1, source_target_pairs={{0,2},{1,3},{2,0},{3,1},{4,6},{5,7},{6,4},{7,5},{8,10},{9,11},{10,... | collective-permute-start | bytes 786440 | tf_op jit(solution)/shard_map/ppermute | solution.py:29
  186.2 3.6 %collective-permute-done.37 = bf16[64,2048]{1,0:T(8,128)(2,1)S(1)} collective-permute-done((bf16[64,2048]{1,0:T(8,128)(2,1)S(1)}, bf16[64,2048]{1,0:T(8,128)(2,1)S(1)}, u32[]{:S(2)}, u32[]{:S(2)}) %collective-permute-start.37) | collective-permute-done | bytes 262176 | tf_op jit(solution)/shard_map/ppermute | solution.py:29
  192.0 13.4 %backward.2 = (f32[64,2048]{1,0:T(8,128)S(1)}, bf16[64,2048]{1,0:T(8,128)(2,1)S(1)}, bf16[64,2048]{1,0:T(8,128)(2,1)S(1)}, bf16[64,2048]{1,0:T(8,128)(2,1)S(1)}) custom-call(s32[1]{0:T(128)} %bitcast.inner_ref, bf16[64,2048]{1,0:T(8,128)(2,1)S(1)} %convert_element_type.157.refs_0_, bf16[64,2048]{1,0:T(8,128)(2,1)S(1)} %collective-permute-done.26.refs_1_, ...), custom_call_target="tpu_custom_call" | custom-call | flops 4831838208 | bytes 18874368 | tf_op jit(solution)/shard_map/backward/pallas_call | solution.py:171
  208.4 7.5 %collective-permute-start.43 = (bf16[64,2048]{1,0:T(8,128)(2,1)S(1)}, bf16[64,2048]{1,0:T(8,128)(2,1)}, u32[]{:S(2)}, u32[]{:S(2)}) collective-permute-start(bf16[64,2048]{1,0:T(8,128)(2,1)S(1)} %convert_element_type.172.refs_0_), channel_id=1, source_target_pairs={{0,2},{1,3},{2,0},{3,1},{4,6},{5,7},{6,4},{7,5},{8,10},{9,11},{10,... | collective-permute-start | bytes 786440 | tf_op jit(solution)/shard_map/ppermute | solution.py:29
  222.3 2.1 collective-permute-done.48
  226.5 2.7 collective-permute-done.50
  231.0 2.7 collective-permute-done.51
  238.2 8.2 %collective-permute-start.45 = (bf16[64,2048]{1,0:T(8,128)(2,1)S(1)}, bf16[64,2048]{1,0:T(8,128)(2,1)S(1)}, u32[]{:S(2)}, u32[]{:S(2)}) collective-permute-start(bf16[64,2048]{1,0:T(8,128)(2,1)S(1)} %broadcast_select_fusion), channel_id=1, source_target_pairs={{0,2},{1,3},{2,0},{3,1},{4,6},{5,7},{6,4},{7,5},{8,10},{9,11},{10,... | collective-permute-start | bytes 786440 | tf_op jit(solution)/shard_map/ppermute | solution.py:29
  247.5 3.5 %collective-permute-start.42 = (bf16[64,2048]{1,0:T(8,128)(2,1)S(1)}, bf16[64,2048]{1,0:T(8,128)(2,1)S(1)}, u32[]{:S(2)}, u32[]{:S(2)}) collective-permute-start(bf16[64,2048]{1,0:T(8,128)(2,1)S(1)} %fusion.2), channel_id=1, source_target_pairs={{0,2},{1,3},{2,0},{3,1},{4,6},{5,7},{6,4},{7,5},{8,10},{9,11},{10,... | collective-permute-start | bytes 786440 | tf_op jit(solution)/shard_map/ppermute | solution.py:29
  254.3 13.5 %backward.3 = (f32[64,2048]{1,0:T(8,128)S(1)}, bf16[64,2048]{1,0:T(8,128)(2,1)S(1)}, bf16[64,2048]{1,0:T(8,128)(2,1)S(1)}, bf16[64,2048]{1,0:T(8,128)(2,1)S(1)}) custom-call(s32[1]{0:T(128)} %bitcast.inner_ref, bf16[64,2048]{1,0:T(8,128)(2,1)S(1)} %convert_element_type.172.refs_0_, bf16[64,2048]{1,0:T(8,128)(2,1)} %collective-permute-done.43.refs_1_, ...), custom_call_target="tpu_custom_call" | custom-call | flops 4831838208 | bytes 18874368 | tf_op jit(solution)/shard_map/backward/pallas_call | solution.py:171
  267.9 2.4 collective-permute-start.52
  271.0 5.2 %collective-permute-start.55 = (bf16[64,2048]{1,0:T(8,128)(2,1)S(1)}, bf16[64,2048]{1,0:T(8,128)(2,1)S(1)}, u32[]{:S(2)}, u32[]{:S(2)}) collective-permute-start(bf16[64,2048]{1,0:T(8,128)(2,1)S(1)} %get-tuple-element.50), channel_id=1, source_target_pairs={{0,2},{1,3},{2,0},{3,1},{4,6},{5,7},{6,4},{7,5},{8,10},{9,11},{10,... | collective-permute-start | bytes 786440 | tf_op jit(solution)/shard_map/ppermute | solution.py:29
  277.1 4.1 %collective-permute-done.55 = bf16[64,2048]{1,0:T(8,128)(2,1)S(1)} collective-permute-done((bf16[64,2048]{1,0:T(8,128)(2,1)S(1)}, bf16[64,2048]{1,0:T(8,128)(2,1)S(1)}, u32[]{:S(2)}, u32[]{:S(2)}) %collective-permute-start.55) | collective-permute-done | bytes 262176 | tf_op jit(solution)/shard_map/ppermute | solution.py:29
  282.1 4.8 %collective-permute-start.54 = (bf16[64,2048]{1,0:T(8,128)(2,1)S(1)}, bf16[64,2048]{1,0:T(8,128)(2,1)S(1)}, u32[]{:S(2)}, u32[]{:S(2)}) collective-permute-start(bf16[64,2048]{1,0:T(8,128)(2,1)S(1)} %fusion.3), channel_id=1, source_target_pairs={{0,2},{1,3},{2,0},{3,1},{4,6},{5,7},{6,4},{7,5},{8,10},{9,11},{10,... | collective-permute-start | bytes 786440 | tf_op jit(solution)/shard_map/ppermute | solution.py:29
  287.0 4.2 %collective-permute-done.54 = bf16[64,2048]{1,0:T(8,128)(2,1)S(1)} collective-permute-done((bf16[64,2048]{1,0:T(8,128)(2,1)S(1)}, bf16[64,2048]{1,0:T(8,128)(2,1)S(1)}, u32[]{:S(2)}, u32[]{:S(2)}) %collective-permute-start.54) | collective-permute-done | bytes 262176 | tf_op jit(solution)/shard_map/ppermute | solution.py:29
  (185 shorter events, 57.5 us)
Async XLA Ops:
  0.0 81.3 %collective-permute-start.15 = (bf16[1,2048,768]{2,1,0:T(8,128)(2,1)}, bf16[1,2048,768]{2,1,0:T(8,128)(2,1)}, u32[]{:S(2)}, u32[]{:S(2)}) collective-permute-start(bf16[1,2048,768]{2,1,0:T(8,128)(2,1)} %refs_8_.3), channel_id=1, source_target_pairs={{0,1},{1,0},{2,3},{3,2},{4,5},{5,4},{6,7},{7,6},{8,9},{9,8},{10,11... | collective-permute-start | bytes 9437192 | tf_op jit(solution)/shard_map/ppermute | solution.py:216
  0.5 81.5 %collective-permute-start.16 = (bf16[1,2048,768]{2,1,0:T(8,128)(2,1)}, bf16[1,2048,768]{2,1,0:T(8,128)(2,1)}, u32[]{:S(2)}, u32[]{:S(2)}) collective-permute-start(bf16[1,2048,768]{2,1,0:T(8,128)(2,1)} %refs_9_.3), channel_id=1, source_target_pairs={{0,1},{1,0},{2,3},{3,2},{4,5},{5,4},{6,7},{7,6},{8,9},{9,8},{10,11... | collective-permute-start | bytes 9437192 | tf_op jit(solution)/shard_map/ppermute | solution.py:216
  0.5 82.8 %collective-permute-start.17 = (bf16[1,768,2048]{2,1,0:T(8,128)(2,1)}, bf16[1,768,2048]{2,1,0:T(8,128)(2,1)}, u32[]{:S(2)}, u32[]{:S(2)}) collective-permute-start(bf16[1,768,2048]{2,1,0:T(8,128)(2,1)} %refs_10_.3), channel_id=1, source_target_pairs={{0,1},{1,0},{2,3},{3,2},{4,5},{5,4},{6,7},{7,6},{8,9},{9,8},{10,11... | collective-permute-start | bytes 9437192 | tf_op jit(solution)/shard_map/ppermute | solution.py:216
  1.7 4.2 %collective-permute-start.10 = (f32[8,128]{1,0:T(8,128)S(1)}, f32[8,128]{1,0:T(8,128)S(1)}, u32[]{:S(2)}, u32[]{:S(2)}) collective-permute-start(f32[8,128]{1,0:T(8,128)S(1)} %select_reduce_fusion), channel_id=1, source_target_pairs={{0,2},{1,3},{2,0},{3,1},{4,6},{5,7},{6,4},{7,5},{8,10},{9,11},{10,... | collective-permute-start | bytes 12296 | tf_op jit(solution)/shard_map/ppermute | solution.py:29
  5.8 6.7 %collective-permute-start.13 = (f32[8,128]{1,0:T(8,128)S(1)}, f32[8,128]{1,0:T(8,128)S(1)}, u32[]{:S(2)}, u32[]{:S(2)}) collective-permute-start(f32[8,128]{1,0:T(8,128)S(1)} %collective-permute-done.10), channel_id=1, source_target_pairs={{2,4},{3,5},{4,2},{5,3},{10,12},{11,13},{12,10},{13,11},{18,20},{1... | collective-permute-start | bytes 12296 | tf_op jit(solution)/shard_map/ppermute | solution.py:29
  7.6 9.0 %collective-permute-start.12 = (f32[8,128]{1,0:T(8,128)S(1)}, f32[8,128]{1,0:T(8,128)S(1)}, u32[]{:S(2)}, u32[]{:S(2)}) collective-permute-start(f32[8,128]{1,0:T(8,128)S(1)} %collective-permute-done.11), channel_id=1, source_target_pairs={{0,2},{1,3},{2,0},{3,1},{4,6},{5,7},{6,4},{7,5},{8,10},{9,11},{10,... | collective-permute-start | bytes 12296 | tf_op jit(solution)/shard_map/ppermute | solution.py:29
  12.5 4.1 %collective-permute-start.14 = (f32[8,128]{1,0:T(8,128)S(1)}, f32[8,128]{1,0:T(8,128)S(1)}, u32[]{:S(2)}, u32[]{:S(2)}) collective-permute-start(f32[8,128]{1,0:T(8,128)S(1)} %collective-permute-done.13), channel_id=1, source_target_pairs={{0,2},{1,3},{2,0},{3,1},{4,6},{5,7},{6,4},{7,5},{8,10},{9,11},{10,... | collective-permute-start | bytes 12296 | tf_op jit(solution)/shard_map/ppermute | solution.py:29
  16.6 9.2 %collective-permute-start = (bf16[64,2048]{1,0:T(8,128)(2,1)S(1)}, bf16[64,2048]{1,0:T(8,128)(2,1)S(1)}, u32[]{:S(2)}, u32[]{:S(2)}) collective-permute-start(bf16[64,2048]{1,0:T(8,128)(2,1)S(1)} %get-tuple-element.57.refs_0_), channel_id=1, source_target_pairs={{0,2},{1,3},{2,0},{3,1},{4,6},{5,7},{6,4},{7,5},{8,10},{9,11},{10,... | collective-permute-start | bytes 786440 | tf_op jit(solution)/shard_map/ppermute | solution.py:29
  16.6 12.3 %collective-permute-start.5 = (bf16[64,2048]{1,0:T(8,128)(2,1)S(1)}, bf16[64,2048]{1,0:T(8,128)(2,1)S(1)}, u32[]{:S(2)}, u32[]{:S(2)}) collective-permute-start(bf16[64,2048]{1,0:T(8,128)(2,1)S(1)} %get-tuple-element.55.refs_6_), channel_id=1, source_target_pairs={{0,2},{1,3},{2,0},{3,1},{4,6},{5,7},{6,4},{7,5},{8,10},{9,11},{10,... | collective-permute-start | bytes 786440 | tf_op jit(solution)/shard_map/ppermute | solution.py:29
  30.3 17.1 %collective-permute-start.8 = (bf16[64,2048]{1,0:T(8,128)(2,1)S(1)}, bf16[64,2048]{1,0:T(8,128)(2,1)S(1)}, u32[]{:S(2)}, u32[]{:S(2)}) collective-permute-start(bf16[64,2048]{1,0:T(8,128)(2,1)S(1)} %collective-permute-done.5.refs_7_), channel_id=1, source_target_pairs={{2,4},{3,5},{4,2},{5,3},{10,12},{11,13},{12,10},{13,11},{18,20},{1... | collective-permute-start | bytes 786440 | tf_op jit(solution)/shard_map/ppermute | solution.py:29
  31.0 22.5 %collective-permute-start.4 = (bf16[64,2048]{1,0:T(8,128)(2,1)S(1)}, bf16[64,2048]{1,0:T(8,128)(2,1)S(1)}, u32[]{:S(2)}, u32[]{:S(2)}) collective-permute-start(bf16[64,2048]{1,0:T(8,128)(2,1)S(1)} %collective-permute-done.3.refs_4_), channel_id=1, source_target_pairs={{0,2},{1,3},{2,0},{3,1},{4,6},{5,7},{6,4},{7,5},{8,10},{9,11},{10,... | collective-permute-start | bytes 786440 | tf_op jit(solution)/shard_map/ppermute | solution.py:29
  47.4 11.8 %collective-permute-start.9 = (bf16[64,2048]{1,0:T(8,128)(2,1)S(1)}, bf16[64,2048]{1,0:T(8,128)(2,1)S(1)}, u32[]{:S(2)}, u32[]{:S(2)}) collective-permute-start(bf16[64,2048]{1,0:T(8,128)(2,1)S(1)} %collective-permute-done.8.refs_10_), channel_id=1, source_target_pairs={{0,2},{1,3},{2,0},{3,1},{4,6},{5,7},{6,4},{7,5},{8,10},{9,11},{10,... | collective-permute-start | bytes 786440 | tf_op jit(solution)/shard_map/ppermute | solution.py:29
  53.6 11.2 %collective-permute-start.2 = (bf16[64,2048]{1,0:T(8,128)(2,1)S(1)}, bf16[64,2048]{1,0:T(8,128)(2,1)S(1)}, u32[]{:S(2)}, u32[]{:S(2)}) collective-permute-start(bf16[64,2048]{1,0:T(8,128)(2,1)S(1)} %collective-permute-done.1.refs_2_), channel_id=1, source_target_pairs={{0,2},{1,3},{2,0},{3,1},{4,6},{5,7},{6,4},{7,5},{8,10},{9,11},{10,... | collective-permute-start | bytes 786440 | tf_op jit(solution)/shard_map/ppermute | solution.py:29
  59.2 11.2 %collective-permute-start.7 = (bf16[64,2048]{1,0:T(8,128)(2,1)S(1)}, bf16[64,2048]{1,0:T(8,128)(2,1)S(1)}, u32[]{:S(2)}, u32[]{:S(2)}) collective-permute-start(bf16[64,2048]{1,0:T(8,128)(2,1)S(1)} %collective-permute-done.6.refs_8_), channel_id=1, source_target_pairs={{0,2},{1,3},{2,0},{3,1},{4,6},{5,7},{6,4},{7,5},{8,10},{9,11},{10,... | collective-permute-start | bytes 786440 | tf_op jit(solution)/shard_map/ppermute | solution.py:29
  64.8 11.3 %collective-permute-start.22 = (bf16[64,2048]{1,0:T(8,128)(2,1)S(1)}, bf16[64,2048]{1,0:T(8,128)(2,1)}, u32[]{:S(2)}, u32[]{:S(2)}) collective-permute-start(bf16[64,2048]{1,0:T(8,128)(2,1)S(1)} %get-tuple-element.31.refs_0_), channel_id=1, source_target_pairs={{0,2},{1,3},{2,0},{3,1},{4,6},{5,7},{6,4},{7,5},{8,10},{9,11},{10,... | collective-permute-start | bytes 786440 | tf_op jit(solution)/shard_map/ppermute | solution.py:29
  70.4 9.5 %collective-permute-start.28 = (bf16[64,2048]{1,0:T(8,128)(2,1)}, bf16[64,2048]{1,0:T(8,128)(2,1)}, u32[]{:S(2)}, u32[]{:S(2)}) collective-permute-start(bf16[64,2048]{1,0:T(8,128)(2,1)} %get-tuple-element.33.refs_6_), channel_id=1, source_target_pairs={{0,2},{1,3},{2,0},{3,1},{4,6},{5,7},{6,4},{7,5},{8,10},{9,11},{10,... | collective-permute-start | bytes 786440 | tf_op jit(solution)/shard_map/ppermute | solution.py:29
  76.1 27.1 %collective-permute-start.18 = (bf16[64,2048]{1,0:T(8,128)(2,1)S(1)}, bf16[64,2048]{1,0:T(8,128)(2,1)S(1)}, u32[]{:S(2)}, u32[]{:S(2)}) collective-permute-start(bf16[64,2048]{1,0:T(8,128)(2,1)S(1)} %get-tuple-element.31.refs_0_), channel_id=1, source_target_pairs={{2,4},{3,5},{4,2},{5,3},{10,12},{11,13},{12,10},{13,11},{18,20},{1... | collective-permute-start | bytes 786440 | tf_op jit(solution)/shard_map/ppermute | solution.py:29
  79.9 51.2 %collective-permute-start.29 = (bf16[64,2048]{1,0:T(8,128)(2,1)}, bf16[64,2048]{1,0:T(8,128)(2,1)}, u32[]{:S(2)}, u32[]{:S(2)}) collective-permute-start(bf16[64,2048]{1,0:T(8,128)(2,1)} %get-tuple-element.33.refs_6_), channel_id=1, source_target_pairs={{2,4},{3,5},{4,2},{5,3},{10,12},{11,13},{12,10},{13,11},{18,20},{1... | collective-permute-start | bytes 786440 | tf_op jit(solution)/shard_map/ppermute | solution.py:29
  81.3 30.0 %collective-permute-start.23 = (bf16[64,2048]{1,0:T(8,128)(2,1)}, bf16[64,2048]{1,0:T(8,128)(2,1)S(1)}, u32[]{:S(2)}, u32[]{:S(2)}) collective-permute-start(bf16[64,2048]{1,0:T(8,128)(2,1)} %collective-permute-done.22.refs_1_), channel_id=1, source_target_pairs={{2,4},{3,5},{4,2},{5,3},{10,12},{11,13},{12,10},{13,11},{18,20},{1... | collective-permute-start | bytes 786440 | tf_op jit(solution)/shard_map/ppermute | solution.py:29
  82.0 49.2 %collective-permute-start.31 = (bf16[64,2048]{1,0:T(8,128)(2,1)}, bf16[64,2048]{1,0:T(8,128)(2,1)}, u32[]{:S(2)}, u32[]{:S(2)}) collective-permute-start(bf16[64,2048]{1,0:T(8,128)(2,1)} %collective-permute-done.28.refs_7_), channel_id=1, source_target_pairs={{2,4},{3,5},{4,2},{5,3},{10,12},{11,13},{12,10},{13,11},{18,20},{1... | collective-permute-start | bytes 786440 | tf_op jit(solution)/shard_map/ppermute | solution.py:29
  103.3 14.6 %collective-permute-start.19 = (bf16[64,2048]{1,0:T(8,128)(2,1)S(1)}, bf16[64,2048]{1,0:T(8,128)(2,1)S(1)}, u32[]{:S(2)}, u32[]{:S(2)}) collective-permute-start(bf16[64,2048]{1,0:T(8,128)(2,1)S(1)} %broadcast_select_fusion.5), channel_id=1, source_target_pairs={{0,2},{1,3},{2,0},{3,1},{4,6},{5,7},{6,4},{7,5},{8,10},{9,11},{10,... | collective-permute-start | bytes 786440 | tf_op jit(solution)/shard_map/ppermute | solution.py:29
  111.3 9.4 %collective-permute-start.24 = (bf16[64,2048]{1,0:T(8,128)(2,1)S(1)}, bf16[64,2048]{1,0:T(8,128)(2,1)S(1)}, u32[]{:S(2)}, u32[]{:S(2)}) collective-permute-start(bf16[64,2048]{1,0:T(8,128)(2,1)S(1)} %broadcast_select_fusion.4), channel_id=1, source_target_pairs={{0,2},{1,3},{2,0},{3,1},{4,6},{5,7},{6,4},{7,5},{8,10},{9,11},{10,... | collective-permute-start | bytes 786440 | tf_op jit(solution)/shard_map/ppermute | solution.py:29
  118.0 5.0 %collective-permute-start.20 = (bf16[64,2048]{1,0:T(8,128)(2,1)S(1)}, bf16[64,2048]{1,0:T(8,128)(2,1)S(1)}, u32[]{:S(2)}, u32[]{:S(2)}) collective-permute-start(bf16[64,2048]{1,0:T(8,128)(2,1)S(1)} %add_convert_fusion.11), channel_id=1, source_target_pairs={{2,4},{3,5},{4,2},{5,3},{10,12},{11,13},{12,10},{13,11},{18,20},{1... | collective-permute-start | bytes 786440 | tf_op jit(solution)/shard_map/ppermute | solution.py:29
  121.6 11.6 %collective-permute-start.25 = (bf16[64,2048]{1,0:T(8,128)(2,1)}, bf16[64,2048]{1,0:T(8,128)(2,1)}, u32[]{:S(2)}, u32[]{:S(2)}) collective-permute-start(bf16[64,2048]{1,0:T(8,128)(2,1)} %add_convert_fusion.9), channel_id=1, source_target_pairs={{2,4},{3,5},{4,2},{5,3},{10,12},{11,13},{12,10},{13,11},{18,20},{1... | collective-permute-start | bytes 786440 | tf_op jit(solution)/shard_map/ppermute | solution.py:29
  123.7 11.8 %collective-permute-start.21 = (bf16[64,2048]{1,0:T(8,128)(2,1)}, bf16[64,2048]{1,0:T(8,128)(2,1)}, u32[]{:S(2)}, u32[]{:S(2)}) collective-permute-start(bf16[64,2048]{1,0:T(8,128)(2,1)} %fusion), channel_id=1, source_target_pairs={{0,2},{1,3},{2,0},{3,1},{4,6},{5,7},{6,4},{7,5},{8,10},{9,11},{10,... | collective-permute-start | bytes 786440 | tf_op jit(solution)/shard_map/ppermute | solution.py:29
  131.1 7.3 %collective-permute-start.30 = (bf16[64,2048]{1,0:T(8,128)(2,1)}, bf16[64,2048]{1,0:T(8,128)(2,1)S(1)}, u32[]{:S(2)}, u32[]{:S(2)}) collective-permute-start(bf16[64,2048]{1,0:T(8,128)(2,1)} %collective-permute-done.29.refs_8_), channel_id=1, source_target_pairs={{0,2},{1,3},{2,0},{3,1},{4,6},{5,7},{6,4},{7,5},{8,10},{9,11},{10,... | collective-permute-start | bytes 786440 | tf_op jit(solution)/shard_map/ppermute | solution.py:29
  131.1 9.9 %collective-permute-start.32 = (bf16[64,2048]{1,0:T(8,128)(2,1)}, bf16[64,2048]{1,0:T(8,128)(2,1)S(1)}, u32[]{:S(2)}, u32[]{:S(2)}) collective-permute-start(bf16[64,2048]{1,0:T(8,128)(2,1)} %collective-permute-done.31.refs_10_), channel_id=1, source_target_pairs={{0,2},{1,3},{2,0},{3,1},{4,6},{5,7},{6,4},{7,5},{8,10},{9,11},{10,... | collective-permute-start | bytes 786440 | tf_op jit(solution)/shard_map/ppermute | solution.py:29
  137.7 25.4 %collective-permute-start.27 = (bf16[64,2048]{1,0:T(8,128)(2,1)S(1)}, bf16[64,2048]{1,0:T(8,128)(2,1)S(1)}, u32[]{:S(2)}, u32[]{:S(2)}) collective-permute-start(bf16[64,2048]{1,0:T(8,128)(2,1)S(1)} %convert_element_type.157.refs_0_), channel_id=1, source_target_pairs={{2,4},{3,5},{4,2},{5,3},{10,12},{11,13},{12,10},{13,11},{18,20},{1... | collective-permute-start | bytes 786440 | tf_op jit(solution)/shard_map/ppermute | solution.py:29
  161.0 6.4 %collective-permute-start.26 = (bf16[64,2048]{1,0:T(8,128)(2,1)S(1)}, bf16[64,2048]{1,0:T(8,128)(2,1)S(1)}, u32[]{:S(2)}, u32[]{:S(2)}) collective-permute-start(bf16[64,2048]{1,0:T(8,128)(2,1)S(1)} %convert_element_type.157.refs_0_), channel_id=1, source_target_pairs={{0,2},{1,3},{2,0},{3,1},{4,6},{5,7},{6,4},{7,5},{8,10},{9,11},{10,... | collective-permute-start | bytes 786440 | tf_op jit(solution)/shard_map/ppermute | solution.py:29
  163.1 9.3 %collective-permute-start.33 = (bf16[64,2048]{1,0:T(8,128)(2,1)S(1)}, bf16[64,2048]{1,0:T(8,128)(2,1)S(1)}, u32[]{:S(2)}, u32[]{:S(2)}) collective-permute-start(bf16[64,2048]{1,0:T(8,128)(2,1)S(1)} %broadcast_select_fusion.3), channel_id=1, source_target_pairs={{0,2},{1,3},{2,0},{3,1},{4,6},{5,7},{6,4},{7,5},{8,10},{9,11},{10,... | collective-permute-start | bytes 786440 | tf_op jit(solution)/shard_map/ppermute | solution.py:29
  167.4 5.7 %collective-permute-start.34 = (bf16[64,2048]{1,0:T(8,128)(2,1)S(1)}, bf16[64,2048]{1,0:T(8,128)(2,1)S(1)}, u32[]{:S(2)}, u32[]{:S(2)}) collective-permute-start(bf16[64,2048]{1,0:T(8,128)(2,1)S(1)} %collective-permute-done.26.refs_1_), channel_id=1, source_target_pairs={{2,4},{3,5},{4,2},{5,3},{10,12},{11,13},{12,10},{13,11},{18,20},{1... | collective-permute-start | bytes 786440 | tf_op jit(solution)/shard_map/ppermute | solution.py:29
  172.4 5.4 %collective-permute-start.36 = (bf16[64,2048]{1,0:T(8,128)(2,1)S(1)}, bf16[64,2048]{1,0:T(8,128)(2,1)S(1)}, u32[]{:S(2)}, u32[]{:S(2)}) collective-permute-start(bf16[64,2048]{1,0:T(8,128)(2,1)S(1)} %add_convert_fusion.8), channel_id=1, source_target_pairs={{2,4},{3,5},{4,2},{5,3},{10,12},{11,13},{12,10},{13,11},{18,20},{1... | collective-permute-start | bytes 786440 | tf_op jit(solution)/shard_map/ppermute | solution.py:29
  173.2 12.3 %collective-permute-start.35 = (bf16[64,2048]{1,0:T(8,128)(2,1)S(1)}, bf16[64,2048]{1,0:T(8,128)(2,1)S(1)}, u32[]{:S(2)}, u32[]{:S(2)}) collective-permute-start(bf16[64,2048]{1,0:T(8,128)(2,1)S(1)} %broadcast_select_fusion.2), channel_id=1, source_target_pairs={{0,2},{1,3},{2,0},{3,1},{4,6},{5,7},{6,4},{7,5},{8,10},{9,11},{10,... | collective-permute-start | bytes 786440 | tf_op jit(solution)/shard_map/ppermute | solution.py:29
  177.9 12.0 %collective-permute-start.37 = (bf16[64,2048]{1,0:T(8,128)(2,1)S(1)}, bf16[64,2048]{1,0:T(8,128)(2,1)S(1)}, u32[]{:S(2)}, u32[]{:S(2)}) collective-permute-start(bf16[64,2048]{1,0:T(8,128)(2,1)S(1)} %fusion.1), channel_id=1, source_target_pairs={{0,2},{1,3},{2,0},{3,1},{4,6},{5,7},{6,4},{7,5},{8,10},{9,11},{10,... | collective-permute-start | bytes 786440 | tf_op jit(solution)/shard_map/ppermute | solution.py:29
  185.6 4.3 %collective-permute-start.38 = (bf16[64,2048]{1,0:T(8,128)(2,1)S(1)}, bf16[64,2048]{1,0:T(8,128)(2,1)S(1)}, u32[]{:S(2)}, u32[]{:S(2)}) collective-permute-start(bf16[64,2048]{1,0:T(8,128)(2,1)S(1)} %add_convert_fusion.6), channel_id=1, source_target_pairs={{2,4},{3,5},{4,2},{5,3},{10,12},{11,13},{12,10},{13,11},{18,20},{1... | collective-permute-start | bytes 786440 | tf_op jit(solution)/shard_map/ppermute | solution.py:29
  190.6 28.0 %collective-permute-start.39 = (bf16[64,2048]{1,0:T(8,128)(2,1)S(1)}, bf16[64,2048]{1,0:T(8,128)(2,1)}, u32[]{:S(2)}, u32[]{:S(2)}) collective-permute-start(bf16[64,2048]{1,0:T(8,128)(2,1)S(1)} %convert_element_type.172.refs_0_), channel_id=1, source_target_pairs={{2,4},{3,5},{4,2},{5,3},{10,12},{11,13},{12,10},{13,11},{18,20},{1... | collective-permute-start | bytes 786440 | tf_op jit(solution)/shard_map/ppermute | solution.py:29
  208.4 26.5 %collective-permute-start.43 = (bf16[64,2048]{1,0:T(8,128)(2,1)S(1)}, bf16[64,2048]{1,0:T(8,128)(2,1)}, u32[]{:S(2)}, u32[]{:S(2)}) collective-permute-start(bf16[64,2048]{1,0:T(8,128)(2,1)S(1)} %convert_element_type.172.refs_0_), channel_id=1, source_target_pairs={{0,2},{1,3},{2,0},{3,1},{4,6},{5,7},{6,4},{7,5},{8,10},{9,11},{10,... | collective-permute-start | bytes 786440 | tf_op jit(solution)/shard_map/ppermute | solution.py:29
  219.7 15.9 %collective-permute-start.40 = (bf16[64,2048]{1,0:T(8,128)(2,1)S(1)}, bf16[64,2048]{1,0:T(8,128)(2,1)S(1)}, u32[]{:S(2)}, u32[]{:S(2)}) collective-permute-start(bf16[64,2048]{1,0:T(8,128)(2,1)S(1)} %broadcast_select_fusion.1), channel_id=1, source_target_pairs={{0,2},{1,3},{2,0},{3,1},{4,6},{5,7},{6,4},{7,5},{8,10},{9,11},{10,... | collective-permute-start | bytes 786440 | tf_op jit(solution)/shard_map/ppermute | solution.py:29
  229.2 4.5 %collective-permute-start.51 = (f32[8,128]{1,0:T(8,128)S(1)}, f32[8,128]{1,0:T(8,128)S(1)}, u32[]{:S(2)}, u32[]{:S(2)}) collective-permute-start(f32[8,128]{1,0:T(8,128)S(1)} %add.126), channel_id=1, source_target_pairs={{0,4},{1,5},{2,6},{3,7},{4,0},{5,1},{6,2},{7,3},{8,12},{9,13},{10,... | collective-permute-start | bytes 12296 | tf_op jit(solution)/shard_map/ppermute | solution.py:200
  236.6 9.9 %collective-permute-start.41 = (bf16[64,2048]{1,0:T(8,128)(2,1)S(1)}, bf16[64,2048]{1,0:T(8,128)(2,1)S(1)}, u32[]{:S(2)}, u32[]{:S(2)}) collective-permute-start(bf16[64,2048]{1,0:T(8,128)(2,1)S(1)} %add_convert_fusion.5), channel_id=1, source_target_pairs={{2,4},{3,5},{4,2},{5,3},{10,12},{11,13},{12,10},{13,11},{18,20},{1... | collective-permute-start | bytes 786440 | tf_op jit(solution)/shard_map/ppermute | solution.py:29
  238.2 13.2 %collective-permute-start.45 = (bf16[64,2048]{1,0:T(8,128)(2,1)S(1)}, bf16[64,2048]{1,0:T(8,128)(2,1)S(1)}, u32[]{:S(2)}, u32[]{:S(2)}) collective-permute-start(bf16[64,2048]{1,0:T(8,128)(2,1)S(1)} %broadcast_select_fusion), channel_id=1, source_target_pairs={{0,2},{1,3},{2,0},{3,1},{4,6},{5,7},{6,4},{7,5},{8,10},{9,11},{10,... | collective-permute-start | bytes 786440 | tf_op jit(solution)/shard_map/ppermute | solution.py:29
  247.5 39.3 %collective-permute-start.42 = (bf16[64,2048]{1,0:T(8,128)(2,1)S(1)}, bf16[64,2048]{1,0:T(8,128)(2,1)S(1)}, u32[]{:S(2)}, u32[]{:S(2)}) collective-permute-start(bf16[64,2048]{1,0:T(8,128)(2,1)S(1)} %fusion.2), channel_id=1, source_target_pairs={{0,2},{1,3},{2,0},{3,1},{4,6},{5,7},{6,4},{7,5},{8,10},{9,11},{10,... | collective-permute-start | bytes 786440 | tf_op jit(solution)/shard_map/ppermute | solution.py:29
  267.9 8.4 %collective-permute-start.52 = (bf16[64,2048]{1,0:T(8,128)(2,1)S(1)}, bf16[64,2048]{1,0:T(8,128)(2,1)S(1)}, u32[]{:S(2)}, u32[]{:S(2)}) collective-permute-start(bf16[64,2048]{1,0:T(8,128)(2,1)S(1)} %get-tuple-element.48), channel_id=1, source_target_pairs={{0,2},{1,3},{2,0},{3,1},{4,6},{5,7},{6,4},{7,5},{8,10},{9,11},{10,... | collective-permute-start | bytes 786440 | tf_op jit(solution)/shard_map/ppermute | solution.py:29
  270.3 16.5 %collective-permute-start.46 = (bf16[64,2048]{1,0:T(8,128)(2,1)S(1)}, bf16[64,2048]{1,0:T(8,128)(2,1)S(1)}, u32[]{:S(2)}, u32[]{:S(2)}) collective-permute-start(bf16[64,2048]{1,0:T(8,128)(2,1)S(1)} %add_convert_fusion.3), channel_id=1, source_target_pairs={{2,4},{3,5},{4,2},{5,3},{10,12},{11,13},{12,10},{13,11},{18,20},{1... | collective-permute-start | bytes 786440 | tf_op jit(solution)/shard_map/ppermute | solution.py:29
  271.0 10.2 %collective-permute-start.55 = (bf16[64,2048]{1,0:T(8,128)(2,1)S(1)}, bf16[64,2048]{1,0:T(8,128)(2,1)S(1)}, u32[]{:S(2)}, u32[]{:S(2)}) collective-permute-start(bf16[64,2048]{1,0:T(8,128)(2,1)S(1)} %get-tuple-element.50), channel_id=1, source_target_pairs={{0,2},{1,3},{2,0},{3,1},{4,6},{5,7},{6,4},{7,5},{8,10},{9,11},{10,... | collective-permute-start | bytes 786440 | tf_op jit(solution)/shard_map/ppermute | solution.py:29
  276.4 5.6 %collective-permute-start.53 = (bf16[64,2048]{1,0:T(8,128)(2,1)S(1)}, bf16[64,2048]{1,0:T(8,128)(2,1)S(1)}, u32[]{:S(2)}, u32[]{:S(2)}) collective-permute-start(bf16[64,2048]{1,0:T(8,128)(2,1)S(1)} %add_convert_fusion.2), channel_id=1, source_target_pairs={{2,4},{3,5},{4,2},{5,3},{10,12},{11,13},{12,10},{13,11},{18,20},{1... | collective-permute-start | bytes 786440 | tf_op jit(solution)/shard_map/ppermute | solution.py:29
  281.3 5.7 %collective-permute-start.56 = (bf16[64,2048]{1,0:T(8,128)(2,1)S(1)}, bf16[64,2048]{1,0:T(8,128)(2,1)S(1)}, u32[]{:S(2)}, u32[]{:S(2)}) collective-permute-start(bf16[64,2048]{1,0:T(8,128)(2,1)S(1)} %add_convert_fusion), channel_id=1, source_target_pairs={{2,4},{3,5},{4,2},{5,3},{10,12},{11,13},{12,10},{13,11},{18,20},{1... | collective-permute-start | bytes 786440 | tf_op jit(solution)/shard_map/ppermute | solution.py:29
  282.1 9.1 %collective-permute-start.54 = (bf16[64,2048]{1,0:T(8,128)(2,1)S(1)}, bf16[64,2048]{1,0:T(8,128)(2,1)S(1)}, u32[]{:S(2)}, u32[]{:S(2)}) collective-permute-start(bf16[64,2048]{1,0:T(8,128)(2,1)S(1)} %fusion.3), channel_id=1, source_target_pairs={{0,2},{1,3},{2,0},{3,1},{4,6},{5,7},{6,4},{7,5},{8,10},{9,11},{10,... | collective-permute-start | bytes 786440 | tf_op jit(solution)/shard_map/ppermute | solution.py:29
  (42 other events, 501.2 us)

commit v3 on v0

v3 whole, which is shorter than its diff:
```python
import functools

import jax
import jax.numpy as jnp
from jax import lax
from jax.experimental import pallas as pl
from jax.experimental.pallas import tpu as pltpu
from jax.sharding import PartitionSpec as P

CONTRACT_LAST = (((1,), (1,)), ((), ()))


def dot(lhs, rhs):
    return jnp.dot(lhs, rhs, preferred_element_type=jnp.float32)


def dot_last(lhs, rhs):
    return lax.dot_general(lhs, rhs, CONTRACT_LAST, preferred_element_type=jnp.float32)


CORES, SIDES, ENDS = 2, 2, 2
LINE = SIDES * ENDS
SIDE_PAIRS = ((0, 1), (1, 0), (2, 3), (3, 2))
INNER_PAIRS = ((1, 2), (2, 1))


def hop(rows, pairs):
    both_cores = [(CORES * a + core, CORES * b + core) for a, b in pairs for core in range(CORES)]
    return lax.ppermute(rows, "expert", both_cores)


def side_hop(rows):
    return hop(rows, SIDE_PAIRS)


def inner_hop(rows):
    return hop(rows, INNER_PAIRS)


def add_rows(own, came):
    return (own.astype(jnp.float32) + came.astype(jnp.float32)).astype(jnp.bfloat16)


def in_vmem(value):
    return pltpu.with_memory_space_constraint(value, pltpu.VMEM)


LANES = 128
GATE_PIECES = 3


def assemble(inner, parts, columns, out):
    own, side, near, near_end, far, far_end = parts
    rows = own.shape[0]
    out[pl.ds(0, rows), :] = own[:, columns]
    out[pl.ds(rows, rows), :] = side[:, columns]

    @pl.when(inner)
    def _():
        out[pl.ds(2 * rows, rows), :] = near[:, columns]
        out[pl.ds(3 * rows, rows), :] = far[:, columns]

    @pl.when(jnp.logical_not(inner))
    def _():
        out[pl.ds(2 * rows, rows), :] = near_end[:, columns]
        out[pl.ds(3 * rows, rows), :] = far_end[:, columns]


def store_parts(total, outs):
    for i, out in enumerate(outs):
        rows = out.shape[0]
        out[...] = total[pl.ds(i * rows, rows), :].astype(out.dtype)


def forward_kernel(owners, where_ref, *refs):
    parts, weights, outs, (b_out, a_out) = refs[:6], refs[6:12], refs[12:16], refs[16:18]
    x, v, gates, total = refs[18:]
    width, hidden = total.shape[1], weights[0].shape[2]
    inner = where_ref[0] == 1
    assemble(inner, parts, pl.ds(0, width), x)
    assemble(inner, parts, pl.ds(width, width), v)
    assemble(inner, parts, pl.ds(2 * width, LANES), gates)
    lane = lax.broadcasted_iota(jnp.int32, (1, LANES), 1)
    for i in range(CORES):
        gate_w, up_w, down_w = weights[3 * i : 3 * i + 3]
        expert = where_ref[1 + i]
        named = lane == expert
        for piece in range(1, GATE_PIECES):
            named = named | (lane == expert + piece * owners)
        g = jnp.sum(jnp.where(named, gates[...].astype(jnp.float32), 0.0), axis=1, keepdims=True)
        a, b = dot(x[...], gate_w[0]), dot(x[...], up_w[0])
        da, db = dot(v[...], gate_w[0]), dot(v[...], up_w[0])
        sigma = 1.0 / (1.0 + jnp.exp(-a))
        act = g * (a * sigma)
        b_slope = g * (sigma * (1.0 + a * (1.0 - sigma))) * b
        columns = pl.ds(i * hidden, hidden)
        a_out[:, columns] = act
        b_out[:, columns] = b_slope
        term = dot((b_slope * da + act * db).astype(jnp.bfloat16), down_w[0])
        if i == 0:
            total[...] = term
        else:
            total[...] += term
    store_parts(total, outs)


def backward_kernel(where_ref, *refs):
    parts, (b_ref, a_ref), weights, outs = refs[:6], refs[6:8], refs[8:14], refs[14:18]
    squares, jv, total = refs[18:]
    hidden = weights[0].shape[2]
    assemble(where_ref[0] == 1, parts, slice(None), jv)
    sums = jnp.zeros((1, LANES), jnp.float32)
    for start in range(0, jv.shape[1], LANES):
        piece = jv[:, pl.ds(start, LANES)].astype(jnp.float32)
        sums = sums + jnp.sum(piece * piece, axis=0, keepdims=True)
    squares[...] = jnp.broadcast_to(sums, squares.shape)
    for i in range(CORES):
        gate_w, up_w, down_w = weights[3 * i : 3 * i + 3]
        columns = pl.ds(i * hidden, hidden)
        back = dot_last(jv[...], down_w[0])
        grad_gate = (back * b_ref[:, columns]).astype(jnp.bfloat16)
        grad_up = (back * a_ref[:, columns]).astype(jnp.bfloat16)
        term = dot_last(grad_gate, gate_w[0]) + dot_last(grad_up, up_w[0])
        if i == 0:
            total[...] = term
        else:
            total[...] += term
    store_parts(total, outs)


def kernel_call(kernel, name, where, operands, rows, width, extra_outs, scratch, flops):
    vmem = pl.BlockSpec(memory_space=pltpu.VMEM)
    outs = [pltpu.VMEM((rows, width), jnp.float32)]
    outs += [pltpu.VMEM((rows, width), jnp.bfloat16)] * (LINE - 1) + extra_outs
    return pl.pallas_call(
        kernel,
        in_specs=[pl.BlockSpec(memory_space=pltpu.SMEM)] + [vmem] * len(operands),
        out_specs=[vmem] * len(outs),
        out_shape=outs,
        scratch_shapes=scratch + [pltpu.VMEM((LINE * rows, width), jnp.float32)],
        compiler_params=pltpu.CompilerParams(vmem_limit_bytes=24 * 2**20),
        cost_estimate=pl.CostEstimate(flops=flops, bytes_accessed=0, transcendentals=0),
        name=name,
    )(where, *[in_vmem(value) for value in operands])


def exchange_sum(value, axis, step):
    pairs = [(i, i ^ step) for i in range(lax.axis_size(axis))]
    return value + lax.ppermute(value, axis, pairs)


def gate_pieces(routes, gates, owners):
    rest = jnp.sum(
        jnp.where(
            routes[:, :, None] == jnp.arange(owners, dtype=jnp.int32)[None, None, :],
            gates[:, :, None],
            jnp.float32(0.0),
        ),
        axis=1,
    )
    pieces = []
    for _ in range(GATE_PIECES):
        piece = lax.reduce_precision(rest, 8, 7)
        pieces.append(piece.astype(jnp.bfloat16))
        rest = rest - piece
    return jnp.pad(jnp.concatenate(pieces, axis=1), ((0, 0), (0, LANES - GATE_PIECES * owners)))


def line_shards(tokens, tangent, routes, gates, w_gate, w_up, w_down):
    token_count, width = tokens.shape
    hidden = w_gate.shape[2]
    owners = lax.axis_size("expert")
    me = lax.axis_index("expert")
    pos = me // CORES
    inner = (pos == 1) | (pos == 2)
    where = jnp.stack([inner.astype(jnp.int32), me, me ^ 1])
    half = token_count // 2
    line_rows = LINE * half
    swap = [(i, i ^ 1) for i in range(owners)]

    def pick(ends, inners):
        return jnp.where(inner, inners, ends)

    def home(parts, side, inner_last):
        return parts[0] + side.astype(jnp.float32) + pick(0.0, inner_last.astype(jnp.float32))

    def forward(parts):
        state = pltpu.VMEM((line_rows, CORES * hidden), jnp.float32)
        rows = pltpu.VMEM((line_rows, width), jnp.bfloat16)
        *outs, b_slope, act = kernel_call(
            functools.partial(forward_kernel, owners),
            "forward",
            where,
            (*parts, *weights),
            half,
            width,
            [state, state],
            [rows, rows, pltpu.VMEM((line_rows, LANES), jnp.bfloat16)],
            2 * 5 * line_rows * width * CORES * hidden,
        )
        return outs, (b_slope, act)

    def backward(parts, states):
        *outs, squares = kernel_call(
            backward_kernel,
            "backward",
            where,
            (*parts, *states, *weights),
            half,
            width,
            [pltpu.VMEM((8, LANES), jnp.float32)],
            [pltpu.VMEM((line_rows, width), jnp.bfloat16)],
            2 * 3 * line_rows * width * CORES * hidden,
        )
        return outs, squares

    pieces = gate_pieces(routes, gates, owners)
    halves = [slice(0, half), slice(half, token_count)]
    load_a, load_b = (
        jnp.concatenate([tokens[rows], tangent[rows], pieces[rows]], axis=1) for rows in halves
    )

    def slot(*results):
        return lax.optimization_barrier(results)

    def both_ways(part, payload):
        first = pick(part, payload[:, :width])
        if payload.shape[1] > width:
            first = jnp.concatenate([first, payload[:, width:]], axis=1)
        return side_hop(first)

    a_side, a_near, sib_gate, w_up, w_down, load_b = slot(
        side_hop(load_a), inner_hop(load_a), lax.ppermute(w_gate, "expert", swap), w_up, w_down, load_b
    )
    a_near_end, a_far, sib_up, w_down, load_b = slot(
        side_hop(a_near), inner_hop(a_side), lax.ppermute(w_up, "expert", swap), w_down, load_b
    )
    a_far_end, sib_down, load_b = slot(side_hop(a_far), lax.ppermute(w_down, "expert", swap), load_b)
    weights = (w_gate, w_up, w_down, sib_gate, sib_up, sib_down)

    b_side, b_near, (pa, states_a) = slot(
        side_hop(load_b),
        inner_hop(load_b),
        forward((load_a, a_side, a_near, a_near_end, a_far, a_far_end)),
    )
    b_near_end, b_far = slot(both_ways(pa[3], b_near), inner_hop(b_side))
    sa_far = add_rows(pa[3], b_near_end[:, :width])
    b_far_end, sa_side = slot(both_ways(pa[2], b_far), inner_hop(sa_far))
    sa_near = add_rows(pa[2], b_far_end[:, :width])
    came, last, (pb, states_b) = slot(
        both_ways(pa[1], add_rows(pa[1], sa_side)),
        inner_hop(sa_near),
        forward((load_b, b_side, b_near, b_near_end, b_far, b_far_end)),
    )
    jv_a = tangent[:half].astype(jnp.float32) + home(pa, came, last)

    def gather_and_reduce(own, parts, work):
        side, near = slot(side_hop(own), inner_hop(own))
        near_end, far = slot(both_ways(parts[3], near), inner_hop(side))
        s_far = add_rows(parts[3], near_end)
        far_end, s_side = slot(both_ways(parts[2], far), inner_hop(s_far))
        s_near = add_rows(parts[2], far_end)
        came, last, worked = slot(
            both_ways(parts[1], add_rows(parts[1], s_side)),
            inner_hop(s_near),
            work((own, side, near, near_end, far, far_end)),
        )
        return worked, home(parts, came, last)

    (ga, squares_a), sum_b = gather_and_reduce(
        jv_a.astype(jnp.bfloat16), pb, lambda parts: backward(parts, states_a)
    )
    jv_b = tangent[half:].astype(jnp.float32) + sum_b
    (gb, squares_b), grad_a = gather_and_reduce(
        jv_b.astype(jnp.bfloat16), ga, lambda parts: backward(parts, states_b)
    )

    sum_a = jv_a + grad_a
    lines = lax.axis_size("dp")
    first, second = side_hop(gb[3]), side_hop(gb[2])
    first, squares = slot(first, exchange_sum(squares_a + squares_b, "expert", 1))
    step = 1
    while step < lines // 2:
        squares = exchange_sum(squares, "dp", step)
        step *= 2
    s_near = add_rows(gb[2], second)
    s_side, second, squares = slot(inner_hop(add_rows(gb[3], first)), second, squares)
    came, last = side_hop(pick(gb[1], add_rows(gb[1], s_side))), inner_hop(s_near)
    while step < lines:
        squares = exchange_sum(squares, "dp", step)
        step *= 2
    grad_b = home(gb, came, last)

    elements = token_count * width * lax.axis_size("dp") * owners
    scale = lax.rsqrt(jnp.sum(squares[0]) / elements + 1e-06)
    return jnp.concatenate([sum_a * scale, (jv_b + grad_b) * scale])


def owner_states(x_rows, gate_w, up_w):
    pre_a = dot(x_rows, gate_w)
    pre_b = dot(x_rows, up_w)
    sigma = jax.nn.sigmoid(pre_a)
    act = pre_a * sigma
    slope = sigma * (1.0 + pre_a * (1.0 - sigma))
    return (pre_b, act, slope)


def pair_shards(tokens, tangent, routes, gates, w_gate, w_up, w_down):
    token_count, model_width = tokens.shape
    top_k = routes.shape[1]
    owners = lax.axis_size("expert")
    expert_total = owners * w_gate.shape[0]
    capacity = pair_capacity(token_count, top_k, expert_total)
    slot_total = expert_total * capacity
    pair_count = token_count * top_k
    gate_w = w_gate[0]
    up_w = w_up[0]
    down_w = w_down[0]
    flat_routes = routes.reshape(pair_count)
    onehot = (flat_routes[:, None] == jnp.arange(expert_total, dtype=jnp.int32)[None, :]).astype(
        jnp.int32
    )
    before = jnp.cumsum(onehot, axis=0) - onehot
    slot_of = jnp.sum(before * onehot, axis=1)
    slot_index = flat_routes * capacity + slot_of
    slot_match = slot_index[None, :] == jnp.arange(slot_total, dtype=jnp.int32)[:, None]
    filled = jnp.any(slot_match, axis=1)
    pair_token = jnp.arange(pair_count, dtype=jnp.int32) // top_k
    source_token = jnp.sum(jnp.where(slot_match, pair_token[None, :], 0), axis=1)
    source_gate = jnp.sum(
        jnp.where(slot_match, gates.reshape(pair_count)[None, :], jnp.float32(0.0)), axis=1
    )
    keep_mask = filled.astype(jnp.bfloat16)[:, None]

    def exchange(rows):
        blocks = rows.reshape(owners, capacity, model_width)
        moved = lax.all_to_all(blocks, "expert", split_axis=0, concat_axis=0, tiled=True)
        return moved.reshape(slot_total, model_width)

    x_rows = exchange(jnp.take(tokens, source_token, axis=0) * keep_mask)
    v_rows = exchange(jnp.take(tangent, source_token, axis=0) * keep_mask)
    pre_b, act, slope = owner_states(x_rows, gate_w, up_w)
    tan_a = dot(v_rows, gate_w)
    tan_b = dot(v_rows, up_w)
    hidden_tangent = (slope * tan_a * pre_b + act * tan_b).astype(jnp.bfloat16)
    returned = exchange(dot(hidden_tangent, down_w).astype(jnp.bfloat16))
    picked_rows = jnp.take(returned, slot_index, axis=0)
    picked_rows = picked_rows.reshape(token_count, top_k, model_width)
    jv_vals = tangent.astype(jnp.float32) + jnp.sum(
        gates[:, :, None] * picked_rows.astype(jnp.float32), axis=1
    )
    cot_rows = exchange(
        (jnp.take(jv_vals, source_token, axis=0) * source_gate[:, None]).astype(jnp.bfloat16)
    )
    back_vals = dot_last(cot_rows, down_w)
    grad_gate = (back_vals * pre_b * slope).astype(jnp.bfloat16)
    grad_up = (back_vals * act).astype(jnp.bfloat16)
    pair_grad = dot_last(grad_gate, gate_w) + dot_last(grad_up, up_w)
    grad_rows = jnp.take(exchange(pair_grad.astype(jnp.bfloat16)), slot_index, axis=0)
    grad_rows = grad_rows.reshape(token_count, top_k, model_width)
    summed = jv_vals + jnp.sum(grad_rows.astype(jnp.float32), axis=1)
    global_sum = lax.psum(jnp.sum(jv_vals * jv_vals), ("dp", "expert"))
    element_count = token_count * lax.axis_size("dp") * owners * model_width
    return summed * lax.rsqrt(global_sum / element_count + 1e-06)


def pair_capacity(token_count, top_k, expert_total):
    return max(2, token_count * top_k * 9 // (8 * expert_total))


def shards(tokens, tangent, routes, gates, w_gate, w_up, w_down):
    token_count, top_k = routes.shape
    owners = lax.axis_size("expert")
    capacity = pair_capacity(token_count, top_k, owners * w_gate.shape[0])
    dp = lax.axis_size("dp")
    whole_blocks = (
        owners == CORES * LINE
        and dp & (dp - 1) == 0
        and w_gate.shape[0] == 1
        and token_count <= CORES * capacity
    )
    form = line_shards if whole_blocks else pair_shards
    return form(tokens, tangent, routes, gates, w_gate, w_up, w_down)


def solution(mesh):
    placed = (
        P(("dp", "expert"), None),
        P(("dp", "expert"), None),
        P(("dp", "expert"), None),
        P(("dp", "expert"), None),
        P("expert", None, None),
        P("expert", None, None),
        P("expert", None, None),
    )
    return jax.shard_map(
        shards, mesh=mesh, in_specs=placed, out_specs=P(("dp", "expert"), None), check_vma=False
    )
```

time: 424 us -> 243 us (0.57)
  blocking collectives: 193 us -> 0 us
  starting transfers between devices: 13.6 us -> 76.5 us
  Pallas kernels: 0 us -> 42.6 us
  local copies, waits for them, and re-layouts: 50.7 us -> 16.4 us
  matrix products: 32.1 us -> 0 us
  other arithmetic: 32 us -> 6.89 us
    all_to_all x2 -> x0, blocking collectives: 118 us -> none  [the longest x1 60.9 us: shards(): lax.all_to_all(send_x, 'expert', split_axis=0, concat_axis=0, tiled=True)]
    all_to_all x3 -> x0, waiting for transfers between devices: 100 us -> none  [the longest x1 53.8 us: shards(): lax.all_to_all(pair_tangent.reshape(owners, capacity, model_width), 'expe...]
    ppermute x0 -> x40, waiting for transfers between devices: none -> 98.5 us  [the longest x34 96.3 us: hop(): return lax.ppermute(rows, 'expert', both_cores)]
    ppermute x0 -> x40, starting transfers between devices: none -> 76.5 us  [the longest x34 73 us: hop(): return lax.ppermute(rows, 'expert', both_cores)]
    psum x1 -> x0, blocking collectives: 74.9 us -> none  [shards(): global_sum = lax.psum(local_sum, ('dp', 'expert'))]
    pallas_call x0 -> x4, Pallas kernels: none -> 42.6 us  [kernel_call(): pl.pallas_call(kernel, in_specs=[pl.BlockSpec(memory_space=pltpu.SMEM)] +...]
    gather x5 -> x0, local copies, waits for them, and re-layouts: 38.3 us -> none  [the longest x1 7.96 us: shards(): jnp.take(tangent, source_token, axis=0) * keep_mask]
    dot_general x7 -> x0, matrix products: 32.1 us -> none  [the longest x1 10.1 us: shards(): jnp.dot(hidden_tangent, down_w, preferred_element_type=jnp.float32)]
  transfers between devices with their start and end apart: 3 -> 40, of which waited for: 2 -> 14; matrix products, arithmetic and copies ran while one was open for 2% -> 2% of each run, Pallas kernels for 0% -> 18%
where the time goes in v3:
time: 243 us; the launch traced here: 242 us
  waiting for transfers between devices  98.5 us (41%)
  starting transfers between devices  76.5 us (31%)
  Pallas kernels  42.6 us (18%)
  local copies, waits for them, and re-layouts  16.4 us (7%)
  other arithmetic  6.89 us (3%)
    ppermute x34, waiting for transfers between devices, hop(): return lax.ppermute(rows, 'expert', both_cores)  96.3 us
    ppermute x34, starting transfers between devices, hop(): return lax.ppermute(rows, 'expert', both_cores)  73 us
    pallas_call x4, Pallas kernels, kernel_call(): pl.pallas_call(kernel, in_specs=[pl.BlockSpec(memory_space=pltpu.SMEM)] +...  42.6 us
    unnamed x64, local copies, waits for them, and re-layouts  14.8 us
  transfers between devices with their start and end apart: 40, of which 14 were waited for; matrix products, arithmetic and copies ran while one was open for 2% of the time, Pallas kernels for 18%

profile of v3, /device:TPU:0, one launch (start us, length us, event | category | flops | bytes accessed | tf_op | source)
XLA Modules:
  0.0 242.2 jit_solution(4073971307382508957)
XLA Ops:
  1.3 1.4 fusion.8
  3.5 5.4 %collective-permute-start = (bf16[64,4224]{1,0:T(8,128)(2,1)S(1)}, bf16[64,4224]{1,0:T(8,128)(2,1)S(1)}, u32[]{:S(2)}, u32[]{:S(2)}) collective-permute-start(bf16[64,4224]{1,0:T(8,128)(2,1)S(1)} %pad_maximum_fusion.1.refs_0_), channel_id=1, source_target_pairs={{0,2},{1,3},{2,0},{3,1},{4,6},{5,7},{6,4},{7,5},{8,10},{9,11},{10,... | collective-permute-start | bytes 1622024 | tf_op jit(solution)/shard_map/ppermute | solution.py:29
  8.9 0.8 pad_maximum_fusion.2.refs_0_
  9.8 11.8 %collective-permute-done.refs_1_ = bf16[64,4224]{1,0:T(8,128)(2,1)S(1)} collective-permute-done((bf16[64,4224]{1,0:T(8,128)(2,1)S(1)}, bf16[64,4224]{1,0:T(8,128)(2,1)S(1)}, u32[]{:S(2)}, u32[]{:S(2)}) %collective-permute-start) | collective-permute-done | bytes 540704 | tf_op jit(solution)/shard_map/ppermute | solution.py:29
  21.6 1.7 collective-permute-start.3
  24.2 1.5 collective-permute-start.4
  26.4 9.9 %collective-permute-done.3.refs_3_ = bf16[64,4224]{1,0:T(8,128)(2,1)S(1)} collective-permute-done((bf16[64,4224]{1,0:T(8,128)(2,1)S(1)}, bf16[64,4224]{1,0:T(8,128)(2,1)S(1)}, u32[]{:S(2)}, u32[]{:S(2)}) %collective-permute-start.3) | collective-permute-done | bytes 540704 | tf_op jit(solution)/shard_map/ppermute | solution.py:29
  37.2 1.7 copy-done.5
  38.9 3.7 %collective-permute-start.6 = (bf16[64,4224]{1,0:T(8,128)(2,1)}, bf16[64,4224]{1,0:T(8,128)(2,1)}, u32[]{:S(2)}, u32[]{:S(2)}) collective-permute-start(bf16[64,4224]{1,0:T(8,128)(2,1)} %collective-permute-done.4.refs_4_), channel_id=1, source_target_pairs={{0,2},{1,3},{2,0},{3,1},{4,6},{5,7},{6,4},{7,5},{8,10},{9,11},{10,... | collective-permute-start | bytes 1622024 | tf_op jit(solution)/shard_map/ppermute | solution.py:29
  42.6 13.2 %collective-permute-done.6.refs_5_ = bf16[64,4224]{1,0:T(8,128)(2,1)} collective-permute-done((bf16[64,4224]{1,0:T(8,128)(2,1)}, bf16[64,4224]{1,0:T(8,128)(2,1)}, u32[]{:S(2)}, u32[]{:S(2)}) %collective-permute-start.6) | collective-permute-done | bytes 540704 | tf_op jit(solution)/shard_map/ppermute | solution.py:29
  56.5 3.5 %collective-permute-start.8 = (bf16[64,4224]{1,0:T(8,128)(2,1)}, bf16[64,4224]{1,0:T(8,128)(2,1)S(1)}, u32[]{:S(2)}, u32[]{:S(2)}) collective-permute-start(bf16[64,4224]{1,0:T(8,128)(2,1)} %pad_maximum_fusion.2.refs_0_), channel_id=1, source_target_pairs={{0,2},{1,3},{2,0},{3,1},{4,6},{5,7},{6,4},{7,5},{8,10},{9,11},{10,... | collective-permute-start | bytes 1622024 | tf_op jit(solution)/shard_map/ppermute | solution.py:29
  60.0 1.9 copy-done.1
  61.9 1.9 copy-done.3
  63.8 1.9 copy-done.6
  65.7 1.0 copy-done.14
  66.7 1.0 copy-done.19
  67.8 1.0 copy-done.21
  68.8 1.0 copy-done.23
  69.9 12.1 %forward.2 = (f32[64,2048]{1,0:T(8,128)S(1)}, bf16[64,2048]{1,0:T(8,128)(2,1)S(1)}, bf16[64,2048]{1,0:T(8,128)(2,1)S(1)}, bf16[64,2048]{1,0:T(8,128)(2,1)S(1)}, ...) custom-call(s32[3]{0:T(128)S(1)} %pad_add_fusion.where_ref, bf16[64,4224]{1,0:T(8,128)(2,1)S(1)} %copy-done.14, ...), custom_call_target="tpu_custom_call" | custom-call | flops 8053063680 | tf_op jit(solution)/shard_map/forward/pallas_call | solution.py:135
  83.1 12.5 %collective-permute-done.10.refs_3_ = bf16[64,4224]{1,0:T(8,128)(2,1)S(1)} collective-permute-done((bf16[64,4224]{1,0:T(8,128)(2,1)S(1)}, bf16[64,4224]{1,0:T(8,128)(2,1)S(1)}, u32[]{:S(2)}, u32[]{:S(2)}) %collective-permute-start.10) | collective-permute-done | bytes 540704 | tf_op jit(solution)/shard_map/ppermute | solution.py:29
  95.7 3.7 %collective-permute-start.12 = (bf16[64,4224]{1,0:T(8,128)(2,1)S(1)}, bf16[64,4224]{1,0:T(8,128)(2,1)S(1)}, u32[]{:S(2)}, u32[]{:S(2)}) collective-permute-start(bf16[64,4224]{1,0:T(8,128)(2,1)S(1)} %pad_maximum_fusion.4), channel_id=1, source_target_pairs={{0,2},{1,3},{2,0},{3,1},{4,6},{5,7},{6,4},{7,5},{8,10},{9,11},{10,... | collective-permute-start | bytes 1622024 | tf_op jit(solution)/shard_map/ppermute | solution.py:29
  100.1 9.6 %collective-permute-done.12.refs_5_ = bf16[64,4224]{1,0:T(8,128)(2,1)S(1)} collective-permute-done((bf16[64,4224]{1,0:T(8,128)(2,1)S(1)}, bf16[64,4224]{1,0:T(8,128)(2,1)S(1)}, u32[]{:S(2)}, u32[]{:S(2)}) %collective-permute-start.12) | collective-permute-done | bytes 540704 | tf_op jit(solution)/shard_map/ppermute | solution.py:29
  110.6 4.6 %collective-permute-start.14 = (bf16[64,2048]{1,0:T(8,128)(2,1)S(1)}, bf16[64,2048]{1,0:T(8,128)(2,1)S(1)}, u32[]{:S(2)}, u32[]{:S(2)}) collective-permute-start(bf16[64,2048]{1,0:T(8,128)(2,1)S(1)} %fusion), channel_id=1, source_target_pairs={{0,2},{1,3},{2,0},{3,1},{4,6},{5,7},{6,4},{7,5},{8,10},{9,11},{10,... | collective-permute-start | bytes 786440 | tf_op jit(solution)/shard_map/ppermute | solution.py:29
  115.2 11.8 %forward.3 = (f32[64,2048]{1,0:T(8,128)S(1)}, bf16[64,2048]{1,0:T(8,128)(2,1)S(1)}, bf16[64,2048]{1,0:T(8,128)(2,1)S(1)}, bf16[64,2048]{1,0:T(8,128)(2,1)S(1)}, ...) custom-call(s32[3]{0:T(128)S(1)} %pad_add_fusion.where_ref, bf16[64,4224]{1,0:T(8,128)(2,1)S(1)} %copy-done.12, ...), custom_call_target="tpu_custom_call" | custom-call | flops 8053063680 | tf_op jit(solution)/shard_map/forward/pallas_call | solution.py:135
  128.0 1.8 collective-permute-start.16
  129.8 6.6 %collective-permute-done.16.refs_1_ = bf16[64,2048]{1,0:T(8,128)(2,1)S(1)} collective-permute-done((bf16[64,2048]{1,0:T(8,128)(2,1)S(1)}, bf16[64,2048]{1,0:T(8,128)(2,1)S(1)}, u32[]{:S(2)}, u32[]{:S(2)}) %collective-permute-start.16) | collective-permute-done | bytes 262176 | tf_op jit(solution)/shard_map/ppermute | solution.py:29
  136.4 1.8 collective-permute-start.18
  139.0 6.5 %collective-permute-done.18.refs_3_ = bf16[64,2048]{1,0:T(8,128)(2,1)S(1)} collective-permute-done((bf16[64,2048]{1,0:T(8,128)(2,1)S(1)}, bf16[64,2048]{1,0:T(8,128)(2,1)S(1)}, u32[]{:S(2)}, u32[]{:S(2)}) %collective-permute-start.18) | collective-permute-done | bytes 262176 | tf_op jit(solution)/shard_map/ppermute | solution.py:29
  145.6 3.7 %collective-permute-start.20 = (bf16[64,2048]{1,0:T(8,128)(2,1)S(1)}, bf16[64,2048]{1,0:T(8,128)(2,1)S(1)}, u32[]{:S(2)}, u32[]{:S(2)}) collective-permute-start(bf16[64,2048]{1,0:T(8,128)(2,1)S(1)} %broadcast_select_fusion.2), channel_id=1, source_target_pairs={{0,2},{1,3},{2,0},{3,1},{4,6},{5,7},{6,4},{7,5},{8,10},{9,11},{10,... | collective-permute-start | bytes 786440 | tf_op jit(solution)/shard_map/ppermute | solution.py:29
  150.0 4.0 %collective-permute-done.20.refs_5_ = bf16[64,2048]{1,0:T(8,128)(2,1)S(1)} collective-permute-done((bf16[64,2048]{1,0:T(8,128)(2,1)S(1)}, bf16[64,2048]{1,0:T(8,128)(2,1)S(1)}, u32[]{:S(2)}, u32[]{:S(2)}) %collective-permute-start.20) | collective-permute-done | bytes 262176 | tf_op jit(solution)/shard_map/ppermute | solution.py:29
  154.8 8.0 %collective-permute-start.22 = (bf16[64,2048]{1,0:T(8,128)(2,1)S(1)}, bf16[64,2048]{1,0:T(8,128)(2,1)S(1)}, u32[]{:S(2)}, u32[]{:S(2)}) collective-permute-start(bf16[64,2048]{1,0:T(8,128)(2,1)S(1)} %fusion.1), channel_id=1, source_target_pairs={{0,2},{1,3},{2,0},{3,1},{4,6},{5,7},{6,4},{7,5},{8,10},{9,11},{10,... | collective-permute-start | bytes 786440 | tf_op jit(solution)/shard_map/ppermute | solution.py:29
  162.8 9.4 %backward.2 = (f32[64,2048]{1,0:T(8,128)S(1)}, bf16[64,2048]{1,0:T(8,128)(2,1)S(1)}, bf16[64,2048]{1,0:T(8,128)(2,1)S(1)}, bf16[64,2048]{1,0:T(8,128)(2,1)S(1)}, f32[8,128]{1,0:T(8,128)S(1)}) custom-call(s32[3]{0:T(128)S(1)} %pad_add_fusion.where_ref, bf16[64,2048]{1,0:T(8,128)(2,1)S(1)} %fusion.4.refs_0_, ...), custom_call_target="tpu_custom_call" | custom-call | flops 4831838208 | tf_op jit(solution)/shard_map/backward/pallas_call | solution.py:135
  173.2 1.6 collective-permute-start.24
  174.8 4.8 %collective-permute-done.24.refs_1_ = bf16[64,2048]{1,0:T(8,128)(2,1)S(1)} collective-permute-done((bf16[64,2048]{1,0:T(8,128)(2,1)S(1)}, bf16[64,2048]{1,0:T(8,128)(2,1)S(1)}, u32[]{:S(2)}, u32[]{:S(2)}) %collective-permute-start.24) | collective-permute-done | bytes 262176 | tf_op jit(solution)/shard_map/ppermute | solution.py:29
  179.7 2.6 %collective-permute-start.26 = (bf16[64,2048]{1,0:T(8,128)(2,1)S(1)}, bf16[64,2048]{1,0:T(8,128)(2,1)S(1)}, u32[]{:S(2)}, u32[]{:S(2)}) collective-permute-start(bf16[64,2048]{1,0:T(8,128)(2,1)S(1)} %broadcast_select_fusion.1), channel_id=1, source_target_pairs={{0,2},{1,3},{2,0},{3,1},{4,6},{5,7},{6,4},{7,5},{8,10},{9,11},{10,... | collective-permute-start | bytes 786440 | tf_op jit(solution)/shard_map/ppermute | solution.py:29
  182.9 4.4 %collective-permute-done.26.refs_3_ = bf16[64,2048]{1,0:T(8,128)(2,1)S(1)} collective-permute-done((bf16[64,2048]{1,0:T(8,128)(2,1)S(1)}, bf16[64,2048]{1,0:T(8,128)(2,1)S(1)}, u32[]{:S(2)}, u32[]{:S(2)}) %collective-permute-start.26) | collective-permute-done | bytes 262176 | tf_op jit(solution)/shard_map/ppermute | solution.py:29
  187.4 3.7 %collective-permute-start.28 = (bf16[64,2048]{1,0:T(8,128)(2,1)S(1)}, bf16[64,2048]{1,0:T(8,128)(2,1)S(1)}, u32[]{:S(2)}, u32[]{:S(2)}) collective-permute-start(bf16[64,2048]{1,0:T(8,128)(2,1)S(1)} %broadcast_select_fusion), channel_id=1, source_target_pairs={{0,2},{1,3},{2,0},{3,1},{4,6},{5,7},{6,4},{7,5},{8,10},{9,11},{10,... | collective-permute-start | bytes 786440 | tf_op jit(solution)/shard_map/ppermute | solution.py:29
  191.8 5.5 %collective-permute-done.28.refs_5_ = bf16[64,2048]{1,0:T(8,128)(2,1)S(1)} collective-permute-done((bf16[64,2048]{1,0:T(8,128)(2,1)S(1)}, bf16[64,2048]{1,0:T(8,128)(2,1)S(1)}, u32[]{:S(2)}, u32[]{:S(2)}) %collective-permute-start.28) | collective-permute-done | bytes 262176 | tf_op jit(solution)/shard_map/ppermute | solution.py:29
  198.1 4.6 %collective-permute-start.30 = (bf16[64,2048]{1,0:T(8,128)(2,1)S(1)}, bf16[64,2048]{1,0:T(8,128)(2,1)S(1)}, u32[]{:S(2)}, u32[]{:S(2)}) collective-permute-start(bf16[64,2048]{1,0:T(8,128)(2,1)S(1)} %fusion.2), channel_id=1, source_target_pairs={{0,2},{1,3},{2,0},{3,1},{4,6},{5,7},{6,4},{7,5},{8,10},{9,11},{10,... | collective-permute-start | bytes 786440 | tf_op jit(solution)/shard_map/ppermute | solution.py:29
  202.7 9.2 %backward.3 = (f32[64,2048]{1,0:T(8,128)S(1)}, bf16[64,2048]{1,0:T(8,128)(2,1)S(1)}, bf16[64,2048]{1,0:T(8,128)(2,1)S(1)}, bf16[64,2048]{1,0:T(8,128)(2,1)S(1)}, f32[8,128]{1,0:T(8,128)S(1)}) custom-call(s32[3]{0:T(128)S(1)} %pad_add_fusion.where_ref, bf16[64,2048]{1,0:T(8,128)(2,1)S(1)} %fusion.5.refs_0_, ...), custom_call_target="tpu_custom_call" | custom-call | flops 4831838208 | tf_op jit(solution)/shard_map/backward/pallas_call | solution.py:135
  212.2 1.9 collective-permute-start.35
  214.2 6.9 %collective-permute-done.32 = bf16[64,2048]{1,0:T(8,128)(2,1)S(1)} collective-permute-done((bf16[64,2048]{1,0:T(8,128)(2,1)S(1)}, bf16[64,2048]{1,0:T(8,128)(2,1)S(1)}, u32[]{:S(2)}, u32[]{:S(2)}) %collective-permute-start.32) | collective-permute-done | bytes 262176 | tf_op jit(solution)/shard_map/ppermute | solution.py:29
  221.1 1.5 collective-permute-start.36
  224.8 8.5 %collective-permute-start.38 = (bf16[64,2048]{1,0:T(8,128)(2,1)S(1)}, bf16[64,2048]{1,0:T(8,128)(2,1)}, u32[]{:S(2)}, u32[]{:S(2)}) collective-permute-start(bf16[64,2048]{1,0:T(8,128)(2,1)S(1)} %fusion.3), channel_id=1, source_target_pairs={{0,2},{1,3},{2,0},{3,1},{4,6},{5,7},{6,4},{7,5},{8,10},{9,11},{10,... | collective-permute-start | bytes 786440 | tf_op jit(solution)/shard_map/ppermute | solution.py:29
  233.4 1.5 collective-permute-start.37
  234.9 2.1 collective-permute-done.37
  239.0 2.1 add_multiply_fusion.1
  241.1 1.1 pad_maximum_fusion
  (140 shorter events, 18.0 us)
Async XLA Ops:
  0.0 21.6 %collective-permute-start.2 = (bf16[1,2048,768]{2,1,0:T(8,128)(2,1)}, bf16[1,2048,768]{2,1,0:T(8,128)(2,1)}, u32[]{:S(2)}, u32[]{:S(2)}) collective-permute-start(bf16[1,2048,768]{2,1,0:T(8,128)(2,1)} %refs_8_.5), channel_id=1, source_target_pairs={{0,1},{1,0},{2,3},{3,2},{4,5},{5,4},{6,7},{7,6},{8,9},{9,8},{10,11... | collective-permute-start | bytes 9437192 | tf_op jit(solution)/shard_map/ppermute | solution.py:233
  1.3 58.7 %copy-start = (bf16[1,2048,768]{2,1,0:T(8,128)(2,1)S(1)}, bf16[1,2048,768]{2,1,0:T(8,128)(2,1)}, u32[]{:S(2)}) copy-start(bf16[1,2048,768]{2,1,0:T(8,128)(2,1)} %refs_8_.5) | copy-start | bytes 9437188
  2.8 34.3 %copy-start.13 = (bf16[64,4224]{1,0:T(8,128)(2,1)}, bf16[64,4224]{1,0:T(8,128)(2,1)S(1)}, u32[]{:S(2)}) copy-start(bf16[64,4224]{1,0:T(8,128)(2,1)S(1)} %pad_maximum_fusion.1.refs_0_) | copy-start | bytes 1622020
  2.8 7.0 %collective-permute-start.1 = (bf16[64,4224]{1,0:T(8,128)(2,1)S(1)}, bf16[64,4224]{1,0:T(8,128)(2,1)S(1)}, u32[]{:S(2)}, u32[]{:S(2)}) collective-permute-start(bf16[64,4224]{1,0:T(8,128)(2,1)S(1)} %pad_maximum_fusion.1.refs_0_), channel_id=1, source_target_pairs={{2,4},{3,5},{4,2},{5,3},{10,12},{11,13},{12,10},{13,11},{18,20},{1... | collective-permute-start | bytes 1622024 | tf_op jit(solution)/shard_map/ppermute | solution.py:29
  3.5 18.1 %collective-permute-start = (bf16[64,4224]{1,0:T(8,128)(2,1)S(1)}, bf16[64,4224]{1,0:T(8,128)(2,1)S(1)}, u32[]{:S(2)}, u32[]{:S(2)}) collective-permute-start(bf16[64,4224]{1,0:T(8,128)(2,1)S(1)} %pad_maximum_fusion.1.refs_0_), channel_id=1, source_target_pairs={{0,2},{1,3},{2,0},{3,1},{4,6},{5,7},{6,4},{7,5},{8,10},{9,11},{10,... | collective-permute-start | bytes 1622024 | tf_op jit(solution)/shard_map/ppermute | solution.py:29
  21.6 15.5 %collective-permute-start.5 = (bf16[1,2048,768]{2,1,0:T(8,128)(2,1)}, bf16[1,2048,768]{2,1,0:T(8,128)(2,1)S(1)}, u32[]{:S(2)}, u32[]{:S(2)}) collective-permute-start(bf16[1,2048,768]{2,1,0:T(8,128)(2,1)} %refs_9_.1), channel_id=1, source_target_pairs={{0,1},{1,0},{2,3},{3,2},{4,5},{5,4},{6,7},{7,6},{8,9},{9,8},{10,11... | collective-permute-start | bytes 9437192 | tf_op jit(solution)/shard_map/ppermute | solution.py:236
  21.6 14.7 %collective-permute-start.3 = (bf16[64,4224]{1,0:T(8,128)(2,1)S(1)}, bf16[64,4224]{1,0:T(8,128)(2,1)S(1)}, u32[]{:S(2)}, u32[]{:S(2)}) collective-permute-start(bf16[64,4224]{1,0:T(8,128)(2,1)S(1)} %collective-permute-done.1.refs_2_), channel_id=1, source_target_pairs={{0,2},{1,3},{2,0},{3,1},{4,6},{5,7},{6,4},{7,5},{8,10},{9,11},{10,... | collective-permute-start | bytes 1622024 | tf_op jit(solution)/shard_map/ppermute | solution.py:29
  24.2 13.0 %collective-permute-start.4 = (bf16[64,4224]{1,0:T(8,128)(2,1)S(1)}, bf16[64,4224]{1,0:T(8,128)(2,1)}, u32[]{:S(2)}, u32[]{:S(2)}) collective-permute-start(bf16[64,4224]{1,0:T(8,128)(2,1)S(1)} %collective-permute-done.refs_1_), channel_id=1, source_target_pairs={{2,4},{3,5},{4,2},{5,3},{10,12},{11,13},{12,10},{13,11},{18,20},{1... | collective-permute-start | bytes 1622024 | tf_op jit(solution)/shard_map/ppermute | solution.py:29
  38.8 17.0 %collective-permute-start.7 = (bf16[1,768,2048]{2,1,0:T(8,128)(2,1)}, bf16[1,768,2048]{2,1,0:T(8,128)(2,1)}, u32[]{:S(2)}, u32[]{:S(2)}) collective-permute-start(bf16[1,768,2048]{2,1,0:T(8,128)(2,1)} %refs_10_.1), channel_id=1, source_target_pairs={{0,1},{1,0},{2,3},{3,2},{4,5},{5,4},{6,7},{7,6},{8,9},{9,8},{10,11... | collective-permute-start | bytes 9437192 | tf_op jit(solution)/shard_map/ppermute | solution.py:238
  38.9 17.0 %collective-permute-start.6 = (bf16[64,4224]{1,0:T(8,128)(2,1)}, bf16[64,4224]{1,0:T(8,128)(2,1)}, u32[]{:S(2)}, u32[]{:S(2)}) collective-permute-start(bf16[64,4224]{1,0:T(8,128)(2,1)} %collective-permute-done.4.refs_4_), channel_id=1, source_target_pairs={{0,2},{1,3},{2,0},{3,1},{4,6},{5,7},{6,4},{7,5},{8,10},{9,11},{10,... | collective-permute-start | bytes 1622024 | tf_op jit(solution)/shard_map/ppermute | solution.py:29
  55.8 26.2 %collective-permute-start.9 = (bf16[64,4224]{1,0:T(8,128)(2,1)}, bf16[64,4224]{1,0:T(8,128)(2,1)S(1)}, u32[]{:S(2)}, u32[]{:S(2)}) collective-permute-start(bf16[64,4224]{1,0:T(8,128)(2,1)} %pad_maximum_fusion.2.refs_0_), channel_id=1, source_target_pairs={{2,4},{3,5},{4,2},{5,3},{10,12},{11,13},{12,10},{13,11},{18,20},{1... | collective-permute-start | bytes 1622024 | tf_op jit(solution)/shard_map/ppermute | solution.py:29
  56.5 25.5 %collective-permute-start.8 = (bf16[64,4224]{1,0:T(8,128)(2,1)}, bf16[64,4224]{1,0:T(8,128)(2,1)S(1)}, u32[]{:S(2)}, u32[]{:S(2)}) collective-permute-start(bf16[64,4224]{1,0:T(8,128)(2,1)} %pad_maximum_fusion.2.refs_0_), channel_id=1, source_target_pairs={{0,2},{1,3},{2,0},{3,1},{4,6},{5,7},{6,4},{7,5},{8,10},{9,11},{10,... | collective-permute-start | bytes 1622024 | tf_op jit(solution)/shard_map/ppermute | solution.py:29
  69.9 45.4 %copy-start.7 = (bf16[1,2048,768]{2,1,0:T(8,128)(2,1)S(1)}, bf16[1,2048,768]{2,1,0:T(8,128)(2,1)}, u32[]{:S(2)}) copy-start(bf16[1,2048,768]{2,1,0:T(8,128)(2,1)} %copy-done.5) | copy-start | bytes 9437188
  82.0 45.2 %copy-start.8 = (f32[64,2048]{1,0:T(8,128)}, f32[64,2048]{1,0:T(8,128)S(1)}, u32[]{:S(2)}) copy-start(f32[64,2048]{1,0:T(8,128)S(1)} %get-tuple-element.111) | copy-start | bytes 1572868
  82.0 33.2 %copy-start.12 = (bf16[64,4224]{1,0:T(8,128)(2,1)S(1)}, bf16[64,4224]{1,0:T(8,128)(2,1)}, u32[]{:S(2)}) copy-start(bf16[64,4224]{1,0:T(8,128)(2,1)} %pad_maximum_fusion.2.refs_0_) | copy-start | bytes 1622020
  82.0 33.2 %copy-start.4 = (bf16[1,768,2048]{2,1,0:T(8,128)(2,1)S(1)}, bf16[1,768,2048]{2,1,0:T(8,128)(2,1)}, u32[]{:S(2)}) copy-start(bf16[1,768,2048]{2,1,0:T(8,128)(2,1)} %refs_10_.1) | copy-start | bytes 9437188
  82.1 13.4 %collective-permute-start.10 = (bf16[64,4224]{1,0:T(8,128)(2,1)S(1)}, bf16[64,4224]{1,0:T(8,128)(2,1)S(1)}, u32[]{:S(2)}, u32[]{:S(2)}) collective-permute-start(bf16[64,4224]{1,0:T(8,128)(2,1)S(1)} %pad_maximum_fusion.3), channel_id=1, source_target_pairs={{0,2},{1,3},{2,0},{3,1},{4,6},{5,7},{6,4},{7,5},{8,10},{9,11},{10,... | collective-permute-start | bytes 1622024 | tf_op jit(solution)/shard_map/ppermute | solution.py:29
  82.2 13.3 %collective-permute-start.11 = (bf16[64,4224]{1,0:T(8,128)(2,1)S(1)}, bf16[64,4224]{1,0:T(8,128)(2,1)S(1)}, u32[]{:S(2)}, u32[]{:S(2)}) collective-permute-start(bf16[64,4224]{1,0:T(8,128)(2,1)S(1)} %collective-permute-done.8.refs_1_), channel_id=1, source_target_pairs={{2,4},{3,5},{4,2},{5,3},{10,12},{11,13},{12,10},{13,11},{18,20},{1... | collective-permute-start | bytes 1622024 | tf_op jit(solution)/shard_map/ppermute | solution.py:29
  95.7 14.1 %collective-permute-start.12 = (bf16[64,4224]{1,0:T(8,128)(2,1)S(1)}, bf16[64,4224]{1,0:T(8,128)(2,1)S(1)}, u32[]{:S(2)}, u32[]{:S(2)}) collective-permute-start(bf16[64,4224]{1,0:T(8,128)(2,1)S(1)} %pad_maximum_fusion.4), channel_id=1, source_target_pairs={{0,2},{1,3},{2,0},{3,1},{4,6},{5,7},{6,4},{7,5},{8,10},{9,11},{10,... | collective-permute-start | bytes 1622024 | tf_op jit(solution)/shard_map/ppermute | solution.py:29
  99.4 0.7 collective-permute-start.13
  109.8 17.3 %collective-permute-start.15 = (bf16[64,2048]{1,0:T(8,128)(2,1)S(1)}, bf16[64,2048]{1,0:T(8,128)(2,1)S(1)}, u32[]{:S(2)}, u32[]{:S(2)}) collective-permute-start(bf16[64,2048]{1,0:T(8,128)(2,1)S(1)} %add_convert_fusion.9), channel_id=1, source_target_pairs={{2,4},{3,5},{4,2},{5,3},{10,12},{11,13},{12,10},{13,11},{18,20},{1... | collective-permute-start | bytes 786440 | tf_op jit(solution)/shard_map/ppermute | solution.py:29
  110.6 16.5 %collective-permute-start.14 = (bf16[64,2048]{1,0:T(8,128)(2,1)S(1)}, bf16[64,2048]{1,0:T(8,128)(2,1)S(1)}, u32[]{:S(2)}, u32[]{:S(2)}) collective-permute-start(bf16[64,2048]{1,0:T(8,128)(2,1)S(1)} %fusion), channel_id=1, source_target_pairs={{0,2},{1,3},{2,0},{3,1},{4,6},{5,7},{6,4},{7,5},{8,10},{9,11},{10,... | collective-permute-start | bytes 786440 | tf_op jit(solution)/shard_map/ppermute | solution.py:29
  127.1 45.2 %copy-start.10 = (f32[64,2048]{1,0:T(8,128)}, f32[64,2048]{1,0:T(8,128)S(1)}, u32[]{:S(2)}) copy-start(f32[64,2048]{1,0:T(8,128)S(1)} %get-tuple-element.147) | copy-start | bytes 1572868
  127.3 2.5 %collective-permute-start.17 = (bf16[64,2048]{1,0:T(8,128)(2,1)S(1)}, bf16[64,2048]{1,0:T(8,128)(2,1)S(1)}, u32[]{:S(2)}, u32[]{:S(2)}) collective-permute-start(bf16[64,2048]{1,0:T(8,128)(2,1)S(1)} %fusion.4.refs_0_), channel_id=1, source_target_pairs={{2,4},{3,5},{4,2},{5,3},{10,12},{11,13},{12,10},{13,11},{18,20},{1... | collective-permute-start | bytes 786440 | tf_op jit(solution)/shard_map/ppermute | solution.py:29
  128.0 8.4 %collective-permute-start.16 = (bf16[64,2048]{1,0:T(8,128)(2,1)S(1)}, bf16[64,2048]{1,0:T(8,128)(2,1)S(1)}, u32[]{:S(2)}, u32[]{:S(2)}) collective-permute-start(bf16[64,2048]{1,0:T(8,128)(2,1)S(1)} %fusion.4.refs_0_), channel_id=1, source_target_pairs={{0,2},{1,3},{2,0},{3,1},{4,6},{5,7},{6,4},{7,5},{8,10},{9,11},{10,... | collective-permute-start | bytes 786440 | tf_op jit(solution)/shard_map/ppermute | solution.py:29
  136.4 9.0 %collective-permute-start.18 = (bf16[64,2048]{1,0:T(8,128)(2,1)S(1)}, bf16[64,2048]{1,0:T(8,128)(2,1)S(1)}, u32[]{:S(2)}, u32[]{:S(2)}) collective-permute-start(bf16[64,2048]{1,0:T(8,128)(2,1)S(1)} %broadcast_select_fusion.3), channel_id=1, source_target_pairs={{0,2},{1,3},{2,0},{3,1},{4,6},{5,7},{6,4},{7,5},{8,10},{9,11},{10,... | collective-permute-start | bytes 786440 | tf_op jit(solution)/shard_map/ppermute | solution.py:29
  138.3 7.2 %collective-permute-start.19 = (bf16[64,2048]{1,0:T(8,128)(2,1)S(1)}, bf16[64,2048]{1,0:T(8,128)(2,1)S(1)}, u32[]{:S(2)}, u32[]{:S(2)}) collective-permute-start(bf16[64,2048]{1,0:T(8,128)(2,1)S(1)} %collective-permute-done.16.refs_1_), channel_id=1, source_target_pairs={{2,4},{3,5},{4,2},{5,3},{10,12},{11,13},{12,10},{13,11},{18,20},{1... | collective-permute-start | bytes 786440 | tf_op jit(solution)/shard_map/ppermute | solution.py:29
  145.6 8.4 %collective-permute-start.20 = (bf16[64,2048]{1,0:T(8,128)(2,1)S(1)}, bf16[64,2048]{1,0:T(8,128)(2,1)S(1)}, u32[]{:S(2)}, u32[]{:S(2)}) collective-permute-start(bf16[64,2048]{1,0:T(8,128)(2,1)S(1)} %broadcast_select_fusion.2), channel_id=1, source_target_pairs={{0,2},{1,3},{2,0},{3,1},{4,6},{5,7},{6,4},{7,5},{8,10},{9,11},{10,... | collective-permute-start | bytes 786440 | tf_op jit(solution)/shard_map/ppermute | solution.py:29
  149.3 4.7 %collective-permute-start.21 = (bf16[64,2048]{1,0:T(8,128)(2,1)S(1)}, bf16[64,2048]{1,0:T(8,128)(2,1)S(1)}, u32[]{:S(2)}, u32[]{:S(2)}) collective-permute-start(bf16[64,2048]{1,0:T(8,128)(2,1)S(1)} %add_convert_fusion.8), channel_id=1, source_target_pairs={{2,4},{3,5},{4,2},{5,3},{10,12},{11,13},{12,10},{13,11},{18,20},{1... | collective-permute-start | bytes 786440 | tf_op jit(solution)/shard_map/ppermute | solution.py:29
  154.0 18.3 %collective-permute-start.23 = (bf16[64,2048]{1,0:T(8,128)(2,1)S(1)}, bf16[64,2048]{1,0:T(8,128)(2,1)S(1)}, u32[]{:S(2)}, u32[]{:S(2)}) collective-permute-start(bf16[64,2048]{1,0:T(8,128)(2,1)S(1)} %add_convert_fusion.6), channel_id=1, source_target_pairs={{2,4},{3,5},{4,2},{5,3},{10,12},{11,13},{12,10},{13,11},{18,20},{1... | collective-permute-start | bytes 786440 | tf_op jit(solution)/shard_map/ppermute | solution.py:29
  154.8 17.5 %collective-permute-start.22 = (bf16[64,2048]{1,0:T(8,128)(2,1)S(1)}, bf16[64,2048]{1,0:T(8,128)(2,1)S(1)}, u32[]{:S(2)}, u32[]{:S(2)}) collective-permute-start(bf16[64,2048]{1,0:T(8,128)(2,1)S(1)} %fusion.1), channel_id=1, source_target_pairs={{0,2},{1,3},{2,0},{3,1},{4,6},{5,7},{6,4},{7,5},{8,10},{9,11},{10,... | collective-permute-start | bytes 786440 | tf_op jit(solution)/shard_map/ppermute | solution.py:29
  172.5 2.3 collective-permute-start.25
  173.2 6.4 %collective-permute-start.24 = (bf16[64,2048]{1,0:T(8,128)(2,1)S(1)}, bf16[64,2048]{1,0:T(8,128)(2,1)S(1)}, u32[]{:S(2)}, u32[]{:S(2)}) collective-permute-start(bf16[64,2048]{1,0:T(8,128)(2,1)S(1)} %fusion.5.refs_0_), channel_id=1, source_target_pairs={{0,2},{1,3},{2,0},{3,1},{4,6},{5,7},{6,4},{7,5},{8,10},{9,11},{10,... | collective-permute-start | bytes 786440 | tf_op jit(solution)/shard_map/ppermute | solution.py:29
  179.7 7.6 %collective-permute-start.26 = (bf16[64,2048]{1,0:T(8,128)(2,1)S(1)}, bf16[64,2048]{1,0:T(8,128)(2,1)S(1)}, u32[]{:S(2)}, u32[]{:S(2)}) collective-permute-start(bf16[64,2048]{1,0:T(8,128)(2,1)S(1)} %broadcast_select_fusion.1), channel_id=1, source_target_pairs={{0,2},{1,3},{2,0},{3,1},{4,6},{5,7},{6,4},{7,5},{8,10},{9,11},{10,... | collective-permute-start | bytes 786440 | tf_op jit(solution)/shard_map/ppermute | solution.py:29
  182.2 5.1 %collective-permute-start.27 = (bf16[64,2048]{1,0:T(8,128)(2,1)S(1)}, bf16[64,2048]{1,0:T(8,128)(2,1)S(1)}, u32[]{:S(2)}, u32[]{:S(2)}) collective-permute-start(bf16[64,2048]{1,0:T(8,128)(2,1)S(1)} %collective-permute-done.24.refs_1_), channel_id=1, source_target_pairs={{2,4},{3,5},{4,2},{5,3},{10,12},{11,13},{12,10},{13,11},{18,20},{1... | collective-permute-start | bytes 786440 | tf_op jit(solution)/shard_map/ppermute | solution.py:29
  187.4 9.8 %collective-permute-start.28 = (bf16[64,2048]{1,0:T(8,128)(2,1)S(1)}, bf16[64,2048]{1,0:T(8,128)(2,1)S(1)}, u32[]{:S(2)}, u32[]{:S(2)}) collective-permute-start(bf16[64,2048]{1,0:T(8,128)(2,1)S(1)} %broadcast_select_fusion), channel_id=1, source_target_pairs={{0,2},{1,3},{2,0},{3,1},{4,6},{5,7},{6,4},{7,5},{8,10},{9,11},{10,... | collective-permute-start | bytes 786440 | tf_op jit(solution)/shard_map/ppermute | solution.py:29
  191.1 6.1 %collective-permute-start.29 = (bf16[64,2048]{1,0:T(8,128)(2,1)S(1)}, bf16[64,2048]{1,0:T(8,128)(2,1)S(1)}, u32[]{:S(2)}, u32[]{:S(2)}) collective-permute-start(bf16[64,2048]{1,0:T(8,128)(2,1)S(1)} %add_convert_fusion.5), channel_id=1, source_target_pairs={{2,4},{3,5},{4,2},{5,3},{10,12},{11,13},{12,10},{13,11},{18,20},{1... | collective-permute-start | bytes 786440 | tf_op jit(solution)/shard_map/ppermute | solution.py:29
  197.3 14.7 %collective-permute-start.31 = (bf16[64,2048]{1,0:T(8,128)(2,1)S(1)}, bf16[64,2048]{1,0:T(8,128)(2,1)S(1)}, u32[]{:S(2)}, u32[]{:S(2)}) collective-permute-start(bf16[64,2048]{1,0:T(8,128)(2,1)S(1)} %add_convert_fusion.3), channel_id=1, source_target_pairs={{2,4},{3,5},{4,2},{5,3},{10,12},{11,13},{12,10},{13,11},{18,20},{1... | collective-permute-start | bytes 786440 | tf_op jit(solution)/shard_map/ppermute | solution.py:29
  198.1 13.9 %collective-permute-start.30 = (bf16[64,2048]{1,0:T(8,128)(2,1)S(1)}, bf16[64,2048]{1,0:T(8,128)(2,1)S(1)}, u32[]{:S(2)}, u32[]{:S(2)}) collective-permute-start(bf16[64,2048]{1,0:T(8,128)(2,1)S(1)} %fusion.2), channel_id=1, source_target_pairs={{0,2},{1,3},{2,0},{3,1},{4,6},{5,7},{6,4},{7,5},{8,10},{9,11},{10,... | collective-permute-start | bytes 786440 | tf_op jit(solution)/shard_map/ppermute | solution.py:29
  212.0 9.1 %collective-permute-start.32 = (bf16[64,2048]{1,0:T(8,128)(2,1)S(1)}, bf16[64,2048]{1,0:T(8,128)(2,1)S(1)}, u32[]{:S(2)}, u32[]{:S(2)}) collective-permute-start(bf16[64,2048]{1,0:T(8,128)(2,1)S(1)} %get-tuple-element.167), channel_id=1, source_target_pairs={{0,2},{1,3},{2,0},{3,1},{4,6},{5,7},{6,4},{7,5},{8,10},{9,11},{10,... | collective-permute-start | bytes 786440 | tf_op jit(solution)/shard_map/ppermute | solution.py:29
  212.1 2.0 collective-permute-start.33
  212.2 11.7 %collective-permute-start.35 = (bf16[64,2048]{1,0:T(8,128)(2,1)S(1)}, bf16[64,2048]{1,0:T(8,128)(2,1)S(1)}, u32[]{:S(2)}, u32[]{:S(2)}) collective-permute-start(bf16[64,2048]{1,0:T(8,128)(2,1)S(1)} %get-tuple-element.171), channel_id=1, source_target_pairs={{0,2},{1,3},{2,0},{3,1},{4,6},{5,7},{6,4},{7,5},{8,10},{9,11},{10,... | collective-permute-start | bytes 786440 | tf_op jit(solution)/shard_map/ppermute | solution.py:29
  214.1 24.9 %copy-start.9 = (f32[64,2048]{1,0:T(8,128)S(1)}, f32[64,2048]{1,0:T(8,128)}, u32[]{:S(2)}) copy-start(f32[64,2048]{1,0:T(8,128)} %copy-done.8) | copy-start | bytes 1572868
  221.1 3.6 %collective-permute-start.36 = (f32[8,128]{1,0:T(8,128)S(1)}, f32[8,128]{1,0:T(8,128)S(1)}, u32[]{:S(2)}, u32[]{:S(2)}) collective-permute-start(f32[8,128]{1,0:T(8,128)S(1)} %add.109), channel_id=1, source_target_pairs={{0,8},{8,0},{16,24},{24,16},{1,9},{9,1},{17,25},{25,17},{2,10},{10... | collective-permute-start | bytes 12296 | tf_op jit(solution)/shard_map/ppermute | solution.py:149
  222.6 2.1 collective-permute-start.34
  224.0 14.3 %collective-permute-start.39 = (bf16[64,2048]{1,0:T(8,128)(2,1)S(1)}, bf16[64,2048]{1,0:T(8,128)(2,1)S(1)}, u32[]{:S(2)}, u32[]{:S(2)}) collective-permute-start(bf16[64,2048]{1,0:T(8,128)(2,1)S(1)} %add_convert_fusion), channel_id=1, source_target_pairs={{2,4},{3,5},{4,2},{5,3},{10,12},{11,13},{12,10},{13,11},{18,20},{1... | collective-permute-start | bytes 786440 | tf_op jit(solution)/shard_map/ppermute | solution.py:29
  224.8 14.2 %collective-permute-start.38 = (bf16[64,2048]{1,0:T(8,128)(2,1)S(1)}, bf16[64,2048]{1,0:T(8,128)(2,1)}, u32[]{:S(2)}, u32[]{:S(2)}) collective-permute-start(bf16[64,2048]{1,0:T(8,128)(2,1)S(1)} %fusion.3), channel_id=1, source_target_pairs={{0,2},{1,3},{2,0},{3,1},{4,6},{5,7},{6,4},{7,5},{8,10},{9,11},{10,... | collective-permute-start | bytes 786440 | tf_op jit(solution)/shard_map/ppermute | solution.py:29
  233.4 3.6 %collective-permute-start.37 = (f32[8,128]{1,0:T(8,128)S(1)}, f32[8,128]{1,0:T(8,128)S(1)}, u32[]{:S(2)}, u32[]{:S(2)}) collective-permute-start(f32[8,128]{1,0:T(8,128)S(1)} %add.111), channel_id=1, source_target_pairs={{0,16},{8,24},{16,0},{24,8},{1,17},{9,25},{17,1},{25,9},{2,18},{10... | collective-permute-start | bytes 12296 | tf_op jit(solution)/shard_map/ppermute | solution.py:149
  (24 other events, 195.2 us)

commit v4 on v3

--- a/solution.py
+++ b/solution.py
@@ -24,17 +24,20 @@
 INNER_PAIRS = ((1, 2), (2, 1))
 
 
-def hop(rows, pairs):
-    both_cores = [(CORES * a + core, CORES * b + core) for a, b in pairs for core in range(CORES)]
-    return lax.ppermute(rows, "expert", both_cores)
+END_CHIPS = (0, 3)
+
+
+def both_cores(pairs):
+    return [(CORES * a + core, CORES * b + core) for a, b in pairs for core in range(CORES)]
 
 
 def side_hop(rows):
-    return hop(rows, SIDE_PAIRS)
+    return lax.ppermute(rows, "expert", both_cores(SIDE_PAIRS))
 
 
 def inner_hop(rows):
-    return hop(rows, INNER_PAIRS)
+    idle = [(CORES * a + core, CORES * a + 1 - core) for a in END_CHIPS for core in range(CORES)]
+    return lax.ppermute(rows, "expert", both_cores(INNER_PAIRS) + idle)
 
 
 def add_rows(own, came):
@@ -49,21 +52,28 @@
 GATE_PIECES = 3
 
 
-def assemble(inner, parts, columns, out):
+def fetch(inner, parts, out, sems):
     own, side, near, near_end, far, far_end = parts
     rows = own.shape[0]
-    out[pl.ds(0, rows), :] = own[:, columns]
-    out[pl.ds(rows, rows), :] = side[:, columns]
-
-    @pl.when(inner)
-    def _():
-        out[pl.ds(2 * rows, rows), :] = near[:, columns]
-        out[pl.ds(3 * rows, rows), :] = far[:, columns]
-
-    @pl.when(jnp.logical_not(inner))
-    def _():
-        out[pl.ds(2 * rows, rows), :] = near_end[:, columns]
-        out[pl.ds(3 * rows, rows), :] = far_end[:, columns]
+
+    def copies(blocks, first):
+        return [
+            pltpu.make_async_copy(block, out.at[pl.ds(i * rows, rows), :], sems.at[i])
+            for i, block in enumerate(blocks, first)
+        ]
+
+    def begin(blocks, first):
+        for copy in copies(blocks, first):
+            copy.start()
+
+    def finish(blocks, first):
+        for copy in copies(blocks, first):
+            copy.wait()
+
+    for act in (begin, finish):
+        act((own, side), 0)
+        pl.when(inner)(functools.partial(act, (near, far), 2))
+        pl.when(jnp.logical_not(inner))(functools.partial(act, (near_end, far_end), 2))
 
 
 def store_parts(total, outs):
@@ -74,12 +84,11 @@
 
 def forward_kernel(owners, where_ref, *refs):
     parts, weights, outs, (b_out, a_out) = refs[:6], refs[6:12], refs[12:16], refs[16:18]
-    x, v, gates, total = refs[18:]
+    sems, load, total = refs[18:]
     width, hidden = total.shape[1], weights[0].shape[2]
-    inner = where_ref[0] == 1
-    assemble(inner, parts, pl.ds(0, width), x)
-    assemble(inner, parts, pl.ds(width, width), v)
-    assemble(inner, parts, pl.ds(2 * width, LANES), gates)
+    fetch(where_ref[0] == 1, parts, load, sems)
+    x, v = load.at[:, pl.ds(0, width)], load.at[:, pl.ds(width, width)]
+    gates = load.at[:, pl.ds(2 * width, LANES)]
     lane = lax.broadcasted_iota(jnp.int32, (1, LANES), 1)
     for i in range(CORES):
         gate_w, up_w, down_w = weights[3 * i : 3 * i + 3]
@@ -106,9 +115,9 @@
 
 def backward_kernel(where_ref, *refs):
     parts, (b_ref, a_ref), weights, outs = refs[:6], refs[6:8], refs[8:14], refs[14:18]
-    squares, jv, total = refs[18:]
+    squares, sems, jv, total = refs[18:]
     hidden = weights[0].shape[2]
-    assemble(where_ref[0] == 1, parts, slice(None), jv)
+    fetch(where_ref[0] == 1, parts, jv, sems)
     sums = jnp.zeros((1, LANES), jnp.float32)
     for start in range(0, jv.shape[1], LANES):
         piece = jv[:, pl.ds(start, LANES)].astype(jnp.float32)
@@ -128,20 +137,26 @@
     store_parts(total, outs)
 
 
-def kernel_call(kernel, name, where, operands, rows, width, extra_outs, scratch, flops):
+def kernel_call(kernel, name, where, parts, operands, rows, width, extra_outs, flops):
     vmem = pl.BlockSpec(memory_space=pltpu.VMEM)
     outs = [pltpu.VMEM((rows, width), jnp.float32)]
     outs += [pltpu.VMEM((rows, width), jnp.bfloat16)] * (LINE - 1) + extra_outs
     return pl.pallas_call(
         kernel,
-        in_specs=[pl.BlockSpec(memory_space=pltpu.SMEM)] + [vmem] * len(operands),
+        in_specs=[pl.BlockSpec(memory_space=pltpu.SMEM)]
+        + [pl.BlockSpec(memory_space=pl.ANY)] * len(parts)
+        + [vmem] * len(operands),
         out_specs=[vmem] * len(outs),
         out_shape=outs,
-        scratch_shapes=scratch + [pltpu.VMEM((LINE * rows, width), jnp.float32)],
-        compiler_params=pltpu.CompilerParams(vmem_limit_bytes=24 * 2**20),
+        scratch_shapes=[
+            pltpu.SemaphoreType.DMA((LINE,)),
+            pltpu.VMEM((LINE * rows, parts[0].shape[1]), jnp.bfloat16),
+            pltpu.VMEM((LINE * rows, width), jnp.float32),
+        ],
+        compiler_params=pltpu.CompilerParams(vmem_limit_bytes=16 * 2**20),
         cost_estimate=pl.CostEstimate(flops=flops, bytes_accessed=0, transcendentals=0),
         name=name,
-    )(where, *[in_vmem(value) for value in operands])
+    )(where, *parts, *[in_vmem(value) for value in operands])
 
 
 def exchange_sum(value, axis, step):
@@ -186,16 +201,15 @@
 
     def forward(parts):
         state = pltpu.VMEM((line_rows, CORES * hidden), jnp.float32)
-        rows = pltpu.VMEM((line_rows, width), jnp.bfloat16)
         *outs, b_slope, act = kernel_call(
             functools.partial(forward_kernel, owners),
             "forward",
             where,
-            (*parts, *weights),
+            parts,
+            weights,
             half,
             width,
             [state, state],
-            [rows, rows, pltpu.VMEM((line_rows, LANES), jnp.bfloat16)],
             2 * 5 * line_rows * width * CORES * hidden,
         )
         return outs, (b_slope, act)
@@ -205,11 +219,11 @@
             backward_kernel,
             "backward",
             where,
-            (*parts, *states, *weights),
+            parts,
+            (*states, *weights),
             half,
             width,
             [pltpu.VMEM((8, LANES), jnp.float32)],
-            [pltpu.VMEM((line_rows, width), jnp.bfloat16)],
             2 * 3 * line_rows * width * CORES * hidden,
         )
         return outs, squares

time: 243 us -> 222 us (0.914)
  starting transfers between devices: 76.5 us -> 41.1 us
  waiting for transfers between devices: 98.5 us -> 112 us
    ppermute x34, starting transfers between devices: 73 us -> 37.5 us  [the longest x18 36.5 us: side_hop(): return lax.ppermute(rows, 'expert', both_cores(SIDE_PAIRS))]
    ppermute x34, waiting for transfers between devices: 96.3 us -> 109 us  [the longest x18 107 us: side_hop(): return lax.ppermute(rows, 'expert', both_cores(SIDE_PAIRS))]
  transfers between devices with their start and end apart: 40 -> 40, of which waited for: 14 -> 18; matrix products, arithmetic and copies ran while one was open for 2% -> 2% of each run, Pallas kernels for 18% -> 20%
where the time goes in v4:
time: 222 us; the launch traced here: 221 us
  waiting for transfers between devices  112 us (50%)
  Pallas kernels  43.9 us (20%)
  starting transfers between devices  41.1 us (19%)
  local copies, waits for them, and re-layouts  16.4 us (7%)
  other arithmetic  6.89 us (3%)
    ppermute x18, waiting for transfers between devices, side_hop(): return lax.ppermute(rows, 'expert', both_cores(SIDE_PAIRS))  107 us
    pallas_call x4, Pallas kernels, kernel_call(): pl.pallas_call(kernel, in_specs=[pl.BlockSpec(memory_space=pltpu.SMEM)] +...  43.9 us
    ppermute x18, starting transfers between devices, side_hop(): return lax.ppermute(rows, 'expert', both_cores(SIDE_PAIRS))  36.5 us
    unnamed x64, local copies, waits for them, and re-layouts  14.8 us
  transfers between devices with their start and end apart: 40, of which 18 were waited for; matrix products, arithmetic and copies ran while one was open for 2% of the time, Pallas kernels for 20%

profile of v4, /device:TPU:0, one launch (start us, length us, event | category | flops | bytes accessed | tf_op | source)
XLA Modules:
  0.0 221.3 jit_solution(13319503979281137299)
XLA Ops:
  1.3 1.4 fusion.8
  2.9 4.1 %collective-permute-start = (bf16[64,4224]{1,0:T(8,128)(2,1)S(1)}, bf16[64,4224]{1,0:T(8,128)(2,1)S(1)}, u32[]{:S(2)}, u32[]{:S(2)}) collective-permute-start(bf16[64,4224]{1,0:T(8,128)(2,1)S(1)} %pad_maximum_fusion.1.refs_0_), channel_id=1, source_target_pairs={{0,2},{1,3},{2,0},{3,1},{4,6},{5,7},{6,4},{7,5},{8,10},{9,11},{10,... | collective-permute-start | bytes 1622024 | tf_op jit(solution)/shard_map/ppermute | solution.py:35
  7.0 0.8 pad_maximum_fusion.2.refs_0_
  7.9 11.8 %collective-permute-done.refs_1_ = bf16[64,4224]{1,0:T(8,128)(2,1)S(1)} collective-permute-done((bf16[64,4224]{1,0:T(8,128)(2,1)S(1)}, bf16[64,4224]{1,0:T(8,128)(2,1)S(1)}, u32[]{:S(2)}, u32[]{:S(2)}) %collective-permute-start) | collective-permute-done | bytes 540704 | tf_op jit(solution)/shard_map/ppermute | solution.py:35
  19.7 1.7 collective-permute-start.3
  23.3 11.1 %collective-permute-done.3.refs_3_ = bf16[64,4224]{1,0:T(8,128)(2,1)S(1)} collective-permute-done((bf16[64,4224]{1,0:T(8,128)(2,1)S(1)}, bf16[64,4224]{1,0:T(8,128)(2,1)S(1)}, u32[]{:S(2)}, u32[]{:S(2)}) %collective-permute-start.3) | collective-permute-done | bytes 540704 | tf_op jit(solution)/shard_map/ppermute | solution.py:35
  34.4 0.8 copy-done.22
  35.2 1.7 copy-done.5
  36.9 1.8 collective-permute-start.6
  38.8 13.2 %collective-permute-done.6.refs_5_ = bf16[64,4224]{1,0:T(8,128)(2,1)} collective-permute-done((bf16[64,4224]{1,0:T(8,128)(2,1)}, bf16[64,4224]{1,0:T(8,128)(2,1)}, u32[]{:S(2)}, u32[]{:S(2)}) %collective-permute-start.6) | collective-permute-done | bytes 540704 | tf_op jit(solution)/shard_map/ppermute | solution.py:35
  52.0 3.4 %collective-permute-start.8 = (bf16[64,4224]{1,0:T(8,128)(2,1)}, bf16[64,4224]{1,0:T(8,128)(2,1)S(1)}, u32[]{:S(2)}, u32[]{:S(2)}) collective-permute-start(bf16[64,4224]{1,0:T(8,128)(2,1)} %pad_maximum_fusion.2.refs_0_), channel_id=1, source_target_pairs={{0,2},{1,3},{2,0},{3,1},{4,6},{5,7},{6,4},{7,5},{8,10},{9,11},{10,... | collective-permute-start | bytes 1622024 | tf_op jit(solution)/shard_map/ppermute | solution.py:35
  55.4 1.9 copy-done.1
  57.3 1.9 copy-done.3
  59.2 1.9 copy-done.6
  61.1 1.0 copy-done.14
  62.1 1.0 copy-done.19
  63.2 1.0 copy-done.21
  64.2 1.0 copy-done.23
  65.3 12.9 %forward.2 = (f32[64,2048]{1,0:T(8,128)S(1)}, bf16[64,2048]{1,0:T(8,128)(2,1)S(1)}, bf16[64,2048]{1,0:T(8,128)(2,1)S(1)}, bf16[64,2048]{1,0:T(8,128)(2,1)S(1)}, ...) custom-call(s32[3]{0:T(128)S(1)} %pad_add_fusion.where_ref, bf16[64,4224]{1,0:T(8,128)(2,1)S(1)} %copy-done.14, ...), custom_call_target="tpu_custom_call" | custom-call | flops 8053063680 | tf_op jit(solution)/shard_map/forward/pallas_call | solution.py:144
  78.5 13.3 %collective-permute-done.10.refs_3_ = bf16[64,4224]{1,0:T(8,128)(2,1)S(1)} collective-permute-done((bf16[64,4224]{1,0:T(8,128)(2,1)S(1)}, bf16[64,4224]{1,0:T(8,128)(2,1)S(1)}, u32[]{:S(2)}, u32[]{:S(2)}) %collective-permute-start.10) | collective-permute-done | bytes 540704 | tf_op jit(solution)/shard_map/ppermute | solution.py:35
  91.9 1.8 collective-permute-start.12
  93.8 1.5 collective-permute-done.13
  95.4 9.0 %collective-permute-done.12.refs_5_ = bf16[64,4224]{1,0:T(8,128)(2,1)S(1)} collective-permute-done((bf16[64,4224]{1,0:T(8,128)(2,1)S(1)}, bf16[64,4224]{1,0:T(8,128)(2,1)S(1)}, u32[]{:S(2)}, u32[]{:S(2)}) %collective-permute-start.12) | collective-permute-done | bytes 540704 | tf_op jit(solution)/shard_map/ppermute | solution.py:35
  104.6 2.4 %collective-permute-start.14 = (bf16[64,2048]{1,0:T(8,128)(2,1)S(1)}, bf16[64,2048]{1,0:T(8,128)(2,1)S(1)}, u32[]{:S(2)}, u32[]{:S(2)}) collective-permute-start(bf16[64,2048]{1,0:T(8,128)(2,1)S(1)} %fusion), channel_id=1, source_target_pairs={{0,2},{1,3},{2,0},{3,1},{4,6},{5,7},{6,4},{7,5},{8,10},{9,11},{10,... | collective-permute-start | bytes 786440 | tf_op jit(solution)/shard_map/ppermute | solution.py:35
  107.1 12.0 %forward.3 = (f32[64,2048]{1,0:T(8,128)S(1)}, bf16[64,2048]{1,0:T(8,128)(2,1)S(1)}, bf16[64,2048]{1,0:T(8,128)(2,1)S(1)}, bf16[64,2048]{1,0:T(8,128)(2,1)S(1)}, ...) custom-call(s32[3]{0:T(128)S(1)} %pad_add_fusion.where_ref, bf16[64,4224]{1,0:T(8,128)(2,1)S(1)} %copy-done.12, ...), custom_call_target="tpu_custom_call" | custom-call | flops 8053063680 | tf_op jit(solution)/shard_map/forward/pallas_call | solution.py:144
  119.3 1.1 collective-permute-start.16
  120.9 7.2 %collective-permute-done.16.refs_1_ = bf16[64,2048]{1,0:T(8,128)(2,1)S(1)} collective-permute-done((bf16[64,2048]{1,0:T(8,128)(2,1)S(1)}, bf16[64,2048]{1,0:T(8,128)(2,1)S(1)}, u32[]{:S(2)}, u32[]{:S(2)}) %collective-permute-start.16) | collective-permute-done | bytes 262176 | tf_op jit(solution)/shard_map/ppermute | solution.py:35
  128.4 7.6 %collective-permute-done.18.refs_3_ = bf16[64,2048]{1,0:T(8,128)(2,1)S(1)} collective-permute-done((bf16[64,2048]{1,0:T(8,128)(2,1)S(1)}, bf16[64,2048]{1,0:T(8,128)(2,1)S(1)}, u32[]{:S(2)}, u32[]{:S(2)}) %collective-permute-start.18) | collective-permute-done | bytes 262176 | tf_op jit(solution)/shard_map/ppermute | solution.py:35
  136.1 1.8 collective-permute-start.20
  138.0 5.2 %collective-permute-done.20.refs_5_ = bf16[64,2048]{1,0:T(8,128)(2,1)S(1)} collective-permute-done((bf16[64,2048]{1,0:T(8,128)(2,1)S(1)}, bf16[64,2048]{1,0:T(8,128)(2,1)S(1)}, u32[]{:S(2)}, u32[]{:S(2)}) %collective-permute-start.20) | collective-permute-done | bytes 262176 | tf_op jit(solution)/shard_map/ppermute | solution.py:35
  143.4 2.9 %collective-permute-start.22 = (bf16[64,2048]{1,0:T(8,128)(2,1)S(1)}, bf16[64,2048]{1,0:T(8,128)(2,1)S(1)}, u32[]{:S(2)}, u32[]{:S(2)}) collective-permute-start(bf16[64,2048]{1,0:T(8,128)(2,1)S(1)} %fusion.1), channel_id=1, source_target_pairs={{0,2},{1,3},{2,0},{3,1},{4,6},{5,7},{6,4},{7,5},{8,10},{9,11},{10,... | collective-permute-start | bytes 786440 | tf_op jit(solution)/shard_map/ppermute | solution.py:35
  146.3 9.5 %backward.2 = (f32[64,2048]{1,0:T(8,128)S(1)}, bf16[64,2048]{1,0:T(8,128)(2,1)S(1)}, bf16[64,2048]{1,0:T(8,128)(2,1)S(1)}, bf16[64,2048]{1,0:T(8,128)(2,1)S(1)}, f32[8,128]{1,0:T(8,128)S(1)}) custom-call(s32[3]{0:T(128)S(1)} %pad_add_fusion.where_ref, bf16[64,2048]{1,0:T(8,128)(2,1)S(1)} %fusion.4.refs_0_, ...), custom_call_target="tpu_custom_call" | custom-call | flops 4831838208 | tf_op jit(solution)/shard_map/backward/pallas_call | solution.py:144
  156.1 0.9 collective-permute-start.24
  157.6 7.2 %collective-permute-done.24.refs_1_ = bf16[64,2048]{1,0:T(8,128)(2,1)S(1)} collective-permute-done((bf16[64,2048]{1,0:T(8,128)(2,1)S(1)}, bf16[64,2048]{1,0:T(8,128)(2,1)S(1)}, u32[]{:S(2)}, u32[]{:S(2)}) %collective-permute-start.24) | collective-permute-done | bytes 262176 | tf_op jit(solution)/shard_map/ppermute | solution.py:35
  165.2 7.6 %collective-permute-done.26.refs_3_ = bf16[64,2048]{1,0:T(8,128)(2,1)S(1)} collective-permute-done((bf16[64,2048]{1,0:T(8,128)(2,1)S(1)}, bf16[64,2048]{1,0:T(8,128)(2,1)S(1)}, u32[]{:S(2)}, u32[]{:S(2)}) %collective-permute-start.26) | collective-permute-done | bytes 262176 | tf_op jit(solution)/shard_map/ppermute | solution.py:35
  172.9 1.8 collective-permute-start.28
  174.7 5.2 %collective-permute-done.28.refs_5_ = bf16[64,2048]{1,0:T(8,128)(2,1)S(1)} collective-permute-done((bf16[64,2048]{1,0:T(8,128)(2,1)S(1)}, bf16[64,2048]{1,0:T(8,128)(2,1)S(1)}, u32[]{:S(2)}, u32[]{:S(2)}) %collective-permute-start.28) | collective-permute-done | bytes 262176 | tf_op jit(solution)/shard_map/ppermute | solution.py:35
  180.2 2.7 %collective-permute-start.30 = (bf16[64,2048]{1,0:T(8,128)(2,1)S(1)}, bf16[64,2048]{1,0:T(8,128)(2,1)S(1)}, u32[]{:S(2)}, u32[]{:S(2)}) collective-permute-start(bf16[64,2048]{1,0:T(8,128)(2,1)S(1)} %fusion.2), channel_id=1, source_target_pairs={{0,2},{1,3},{2,0},{3,1},{4,6},{5,7},{6,4},{7,5},{8,10},{9,11},{10,... | collective-permute-start | bytes 786440 | tf_op jit(solution)/shard_map/ppermute | solution.py:35
  182.9 9.5 %backward.3 = (f32[64,2048]{1,0:T(8,128)S(1)}, bf16[64,2048]{1,0:T(8,128)(2,1)S(1)}, bf16[64,2048]{1,0:T(8,128)(2,1)S(1)}, bf16[64,2048]{1,0:T(8,128)(2,1)S(1)}, f32[8,128]{1,0:T(8,128)S(1)}) custom-call(s32[3]{0:T(128)S(1)} %pad_add_fusion.where_ref, bf16[64,2048]{1,0:T(8,128)(2,1)S(1)} %fusion.5.refs_0_, ...), custom_call_target="tpu_custom_call" | custom-call | flops 4831838208 | tf_op jit(solution)/shard_map/backward/pallas_call | solution.py:144
  192.7 1.9 collective-permute-start.35
  194.7 6.9 %collective-permute-done.32 = bf16[64,2048]{1,0:T(8,128)(2,1)S(1)} collective-permute-done((bf16[64,2048]{1,0:T(8,128)(2,1)S(1)}, bf16[64,2048]{1,0:T(8,128)(2,1)S(1)}, u32[]{:S(2)}, u32[]{:S(2)}) %collective-permute-start.32) | collective-permute-done | bytes 262176 | tf_op jit(solution)/shard_map/ppermute | solution.py:35
  201.6 1.5 collective-permute-start.36
  203.3 1.2 collective-permute-done.35
  205.3 7.2 %collective-permute-start.38 = (bf16[64,2048]{1,0:T(8,128)(2,1)S(1)}, bf16[64,2048]{1,0:T(8,128)(2,1)}, u32[]{:S(2)}, u32[]{:S(2)}) collective-permute-start(bf16[64,2048]{1,0:T(8,128)(2,1)S(1)} %fusion.3), channel_id=1, source_target_pairs={{0,2},{1,3},{2,0},{3,1},{4,6},{5,7},{6,4},{7,5},{8,10},{9,11},{10,... | collective-permute-start | bytes 786440 | tf_op jit(solution)/shard_map/ppermute | solution.py:35
  212.5 1.6 collective-permute-start.37
  214.1 2.0 collective-permute-done.37
  218.1 2.1 add_multiply_fusion.1
  220.3 1.1 pad_maximum_fusion
  (140 shorter events, 9.5 us)
Async XLA Ops:
  0.0 19.7 %collective-permute-start.2 = (bf16[1,2048,768]{2,1,0:T(8,128)(2,1)}, bf16[1,2048,768]{2,1,0:T(8,128)(2,1)}, u32[]{:S(2)}, u32[]{:S(2)}) collective-permute-start(bf16[1,2048,768]{2,1,0:T(8,128)(2,1)} %refs_8_.5), channel_id=1, source_target_pairs={{0,1},{1,0},{2,3},{3,2},{4,5},{5,4},{6,7},{7,6},{8,9},{9,8},{10,11... | collective-permute-start | bytes 9437192 | tf_op jit(solution)/shard_map/ppermute | solution.py:247
  1.3 54.1 %copy-start = (bf16[1,2048,768]{2,1,0:T(8,128)(2,1)S(1)}, bf16[1,2048,768]{2,1,0:T(8,128)(2,1)}, u32[]{:S(2)}) copy-start(bf16[1,2048,768]{2,1,0:T(8,128)(2,1)} %refs_8_.5) | copy-start | bytes 9437188
  2.8 32.4 %copy-start.13 = (bf16[64,4224]{1,0:T(8,128)(2,1)}, bf16[64,4224]{1,0:T(8,128)(2,1)S(1)}, u32[]{:S(2)}) copy-start(bf16[64,4224]{1,0:T(8,128)(2,1)S(1)} %pad_maximum_fusion.1.refs_0_) | copy-start | bytes 1622020
  2.8 5.1 %collective-permute-start.1 = (bf16[64,4224]{1,0:T(8,128)(2,1)S(1)}, bf16[64,4224]{1,0:T(8,128)(2,1)S(1)}, u32[]{:S(2)}, u32[]{:S(2)}) collective-permute-start(bf16[64,4224]{1,0:T(8,128)(2,1)S(1)} %pad_maximum_fusion.1.refs_0_), channel_id=1, source_target_pairs={{2,4},{3,5},{4,2},{5,3},{0,1},{1,0},{6,7},{7,6},{10,12},{11,13},{1... | collective-permute-start | bytes 1622024 | tf_op jit(solution)/shard_map/ppermute | solution.py:40
  2.9 16.8 %collective-permute-start = (bf16[64,4224]{1,0:T(8,128)(2,1)S(1)}, bf16[64,4224]{1,0:T(8,128)(2,1)S(1)}, u32[]{:S(2)}, u32[]{:S(2)}) collective-permute-start(bf16[64,4224]{1,0:T(8,128)(2,1)S(1)} %pad_maximum_fusion.1.refs_0_), channel_id=1, source_target_pairs={{0,2},{1,3},{2,0},{3,1},{4,6},{5,7},{6,4},{7,5},{8,10},{9,11},{10,... | collective-permute-start | bytes 1622024 | tf_op jit(solution)/shard_map/ppermute | solution.py:35
  19.7 15.5 %collective-permute-start.5 = (bf16[1,2048,768]{2,1,0:T(8,128)(2,1)}, bf16[1,2048,768]{2,1,0:T(8,128)(2,1)S(1)}, u32[]{:S(2)}, u32[]{:S(2)}) collective-permute-start(bf16[1,2048,768]{2,1,0:T(8,128)(2,1)} %refs_9_.1), channel_id=1, source_target_pairs={{0,1},{1,0},{2,3},{3,2},{4,5},{5,4},{6,7},{7,6},{8,9},{9,8},{10,11... | collective-permute-start | bytes 9437192 | tf_op jit(solution)/shard_map/ppermute | solution.py:250
  19.7 14.7 %collective-permute-start.3 = (bf16[64,4224]{1,0:T(8,128)(2,1)S(1)}, bf16[64,4224]{1,0:T(8,128)(2,1)S(1)}, u32[]{:S(2)}, u32[]{:S(2)}) collective-permute-start(bf16[64,4224]{1,0:T(8,128)(2,1)S(1)} %collective-permute-done.1.refs_2_), channel_id=1, source_target_pairs={{0,2},{1,3},{2,0},{3,1},{4,6},{5,7},{6,4},{7,5},{8,10},{9,11},{10,... | collective-permute-start | bytes 1622024 | tf_op jit(solution)/shard_map/ppermute | solution.py:35
  22.2 13.0 %collective-permute-start.4 = (bf16[64,4224]{1,0:T(8,128)(2,1)S(1)}, bf16[64,4224]{1,0:T(8,128)(2,1)}, u32[]{:S(2)}, u32[]{:S(2)}) collective-permute-start(bf16[64,4224]{1,0:T(8,128)(2,1)S(1)} %collective-permute-done.refs_1_), channel_id=1, source_target_pairs={{2,4},{3,5},{4,2},{5,3},{0,1},{1,0},{6,7},{7,6},{10,12},{11,13},{1... | collective-permute-start | bytes 1622024 | tf_op jit(solution)/shard_map/ppermute | solution.py:40
  36.9 15.1 %collective-permute-start.7 = (bf16[1,768,2048]{2,1,0:T(8,128)(2,1)}, bf16[1,768,2048]{2,1,0:T(8,128)(2,1)}, u32[]{:S(2)}, u32[]{:S(2)}) collective-permute-start(bf16[1,768,2048]{2,1,0:T(8,128)(2,1)} %refs_10_.1), channel_id=1, source_target_pairs={{0,1},{1,0},{2,3},{3,2},{4,5},{5,4},{6,7},{7,6},{8,9},{9,8},{10,11... | collective-permute-start | bytes 9437192 | tf_op jit(solution)/shard_map/ppermute | solution.py:252
  36.9 15.1 %collective-permute-start.6 = (bf16[64,4224]{1,0:T(8,128)(2,1)}, bf16[64,4224]{1,0:T(8,128)(2,1)}, u32[]{:S(2)}, u32[]{:S(2)}) collective-permute-start(bf16[64,4224]{1,0:T(8,128)(2,1)} %collective-permute-done.4.refs_4_), channel_id=1, source_target_pairs={{0,2},{1,3},{2,0},{3,1},{4,6},{5,7},{6,4},{7,5},{8,10},{9,11},{10,... | collective-permute-start | bytes 1622024 | tf_op jit(solution)/shard_map/ppermute | solution.py:35
  52.0 26.2 %collective-permute-start.9 = (bf16[64,4224]{1,0:T(8,128)(2,1)}, bf16[64,4224]{1,0:T(8,128)(2,1)S(1)}, u32[]{:S(2)}, u32[]{:S(2)}) collective-permute-start(bf16[64,4224]{1,0:T(8,128)(2,1)} %pad_maximum_fusion.2.refs_0_), channel_id=1, source_target_pairs={{2,4},{3,5},{4,2},{5,3},{0,1},{1,0},{6,7},{7,6},{10,12},{11,13},{1... | collective-permute-start | bytes 1622024 | tf_op jit(solution)/shard_map/ppermute | solution.py:40
  52.0 26.2 %collective-permute-start.8 = (bf16[64,4224]{1,0:T(8,128)(2,1)}, bf16[64,4224]{1,0:T(8,128)(2,1)S(1)}, u32[]{:S(2)}, u32[]{:S(2)}) collective-permute-start(bf16[64,4224]{1,0:T(8,128)(2,1)} %pad_maximum_fusion.2.refs_0_), channel_id=1, source_target_pairs={{0,2},{1,3},{2,0},{3,1},{4,6},{5,7},{6,4},{7,5},{8,10},{9,11},{10,... | collective-permute-start | bytes 1622024 | tf_op jit(solution)/shard_map/ppermute | solution.py:35
  65.3 41.8 %copy-start.7 = (bf16[1,2048,768]{2,1,0:T(8,128)(2,1)S(1)}, bf16[1,2048,768]{2,1,0:T(8,128)(2,1)}, u32[]{:S(2)}) copy-start(bf16[1,2048,768]{2,1,0:T(8,128)(2,1)} %copy-done.5) | copy-start | bytes 9437188
  78.2 40.9 %copy-start.8 = (f32[64,2048]{1,0:T(8,128)}, f32[64,2048]{1,0:T(8,128)S(1)}, u32[]{:S(2)}) copy-start(f32[64,2048]{1,0:T(8,128)S(1)} %get-tuple-element.111) | copy-start | bytes 1572868
  78.2 28.9 %copy-start.12 = (bf16[64,4224]{1,0:T(8,128)(2,1)S(1)}, bf16[64,4224]{1,0:T(8,128)(2,1)}, u32[]{:S(2)}) copy-start(bf16[64,4224]{1,0:T(8,128)(2,1)} %pad_maximum_fusion.2.refs_0_) | copy-start | bytes 1622020
  78.3 28.8 %copy-start.4 = (bf16[1,768,2048]{2,1,0:T(8,128)(2,1)S(1)}, bf16[1,768,2048]{2,1,0:T(8,128)(2,1)}, u32[]{:S(2)}) copy-start(bf16[1,768,2048]{2,1,0:T(8,128)(2,1)} %refs_10_.1) | copy-start | bytes 9437188
  78.4 13.4 %collective-permute-start.10 = (bf16[64,4224]{1,0:T(8,128)(2,1)S(1)}, bf16[64,4224]{1,0:T(8,128)(2,1)S(1)}, u32[]{:S(2)}, u32[]{:S(2)}) collective-permute-start(bf16[64,4224]{1,0:T(8,128)(2,1)S(1)} %pad_maximum_fusion.3), channel_id=1, source_target_pairs={{0,2},{1,3},{2,0},{3,1},{4,6},{5,7},{6,4},{7,5},{8,10},{9,11},{10,... | collective-permute-start | bytes 1622024 | tf_op jit(solution)/shard_map/ppermute | solution.py:35
  78.4 13.3 %collective-permute-start.11 = (bf16[64,4224]{1,0:T(8,128)(2,1)S(1)}, bf16[64,4224]{1,0:T(8,128)(2,1)S(1)}, u32[]{:S(2)}, u32[]{:S(2)}) collective-permute-start(bf16[64,4224]{1,0:T(8,128)(2,1)S(1)} %collective-permute-done.8.refs_1_), channel_id=1, source_target_pairs={{2,4},{3,5},{4,2},{5,3},{0,1},{1,0},{6,7},{7,6},{10,12},{11,13},{1... | collective-permute-start | bytes 1622024 | tf_op jit(solution)/shard_map/ppermute | solution.py:40
  91.9 12.5 %collective-permute-start.12 = (bf16[64,4224]{1,0:T(8,128)(2,1)S(1)}, bf16[64,4224]{1,0:T(8,128)(2,1)S(1)}, u32[]{:S(2)}, u32[]{:S(2)}) collective-permute-start(bf16[64,4224]{1,0:T(8,128)(2,1)S(1)} %pad_maximum_fusion.4), channel_id=1, source_target_pairs={{0,2},{1,3},{2,0},{3,1},{4,6},{5,7},{6,4},{7,5},{8,10},{9,11},{10,... | collective-permute-start | bytes 1622024 | tf_op jit(solution)/shard_map/ppermute | solution.py:35
  93.8 1.6 collective-permute-start.13
  104.4 14.6 %collective-permute-start.15 = (bf16[64,2048]{1,0:T(8,128)(2,1)S(1)}, bf16[64,2048]{1,0:T(8,128)(2,1)S(1)}, u32[]{:S(2)}, u32[]{:S(2)}) collective-permute-start(bf16[64,2048]{1,0:T(8,128)(2,1)S(1)} %add_convert_fusion.9), channel_id=1, source_target_pairs={{2,4},{3,5},{4,2},{5,3},{0,1},{1,0},{6,7},{7,6},{10,12},{11,13},{1... | collective-permute-start | bytes 786440 | tf_op jit(solution)/shard_map/ppermute | solution.py:40
  104.6 14.4 %collective-permute-start.14 = (bf16[64,2048]{1,0:T(8,128)(2,1)S(1)}, bf16[64,2048]{1,0:T(8,128)(2,1)S(1)}, u32[]{:S(2)}, u32[]{:S(2)}) collective-permute-start(bf16[64,2048]{1,0:T(8,128)(2,1)S(1)} %fusion), channel_id=1, source_target_pairs={{0,2},{1,3},{2,0},{3,1},{4,6},{5,7},{6,4},{7,5},{8,10},{9,11},{10,... | collective-permute-start | bytes 786440 | tf_op jit(solution)/shard_map/ppermute | solution.py:35
  119.0 36.8 %copy-start.10 = (f32[64,2048]{1,0:T(8,128)}, f32[64,2048]{1,0:T(8,128)S(1)}, u32[]{:S(2)}) copy-start(f32[64,2048]{1,0:T(8,128)S(1)} %get-tuple-element.147) | copy-start | bytes 1572868
  119.3 1.6 collective-permute-start.17
  119.3 8.7 %collective-permute-start.16 = (bf16[64,2048]{1,0:T(8,128)(2,1)S(1)}, bf16[64,2048]{1,0:T(8,128)(2,1)S(1)}, u32[]{:S(2)}, u32[]{:S(2)}) collective-permute-start(bf16[64,2048]{1,0:T(8,128)(2,1)S(1)} %fusion.4.refs_0_), channel_id=1, source_target_pairs={{0,2},{1,3},{2,0},{3,1},{4,6},{5,7},{6,4},{7,5},{8,10},{9,11},{10,... | collective-permute-start | bytes 786440 | tf_op jit(solution)/shard_map/ppermute | solution.py:35
  128.1 7.9 %collective-permute-start.18 = (bf16[64,2048]{1,0:T(8,128)(2,1)S(1)}, bf16[64,2048]{1,0:T(8,128)(2,1)S(1)}, u32[]{:S(2)}, u32[]{:S(2)}) collective-permute-start(bf16[64,2048]{1,0:T(8,128)(2,1)S(1)} %broadcast_select_fusion.3), channel_id=1, source_target_pairs={{0,2},{1,3},{2,0},{3,1},{4,6},{5,7},{6,4},{7,5},{8,10},{9,11},{10,... | collective-permute-start | bytes 786440 | tf_op jit(solution)/shard_map/ppermute | solution.py:35
  128.4 7.6 %collective-permute-start.19 = (bf16[64,2048]{1,0:T(8,128)(2,1)S(1)}, bf16[64,2048]{1,0:T(8,128)(2,1)S(1)}, u32[]{:S(2)}, u32[]{:S(2)}) collective-permute-start(bf16[64,2048]{1,0:T(8,128)(2,1)S(1)} %collective-permute-done.16.refs_1_), channel_id=1, source_target_pairs={{2,4},{3,5},{4,2},{5,3},{0,1},{1,0},{6,7},{7,6},{10,12},{11,13},{1... | collective-permute-start | bytes 786440 | tf_op jit(solution)/shard_map/ppermute | solution.py:40
  136.1 7.0 %collective-permute-start.20 = (bf16[64,2048]{1,0:T(8,128)(2,1)S(1)}, bf16[64,2048]{1,0:T(8,128)(2,1)S(1)}, u32[]{:S(2)}, u32[]{:S(2)}) collective-permute-start(bf16[64,2048]{1,0:T(8,128)(2,1)S(1)} %broadcast_select_fusion.2), channel_id=1, source_target_pairs={{0,2},{1,3},{2,0},{3,1},{4,6},{5,7},{6,4},{7,5},{8,10},{9,11},{10,... | collective-permute-start | bytes 786440 | tf_op jit(solution)/shard_map/ppermute | solution.py:35
  138.0 5.2 %collective-permute-start.21 = (bf16[64,2048]{1,0:T(8,128)(2,1)S(1)}, bf16[64,2048]{1,0:T(8,128)(2,1)S(1)}, u32[]{:S(2)}, u32[]{:S(2)}) collective-permute-start(bf16[64,2048]{1,0:T(8,128)(2,1)S(1)} %add_convert_fusion.8), channel_id=1, source_target_pairs={{2,4},{3,5},{4,2},{5,3},{0,1},{1,0},{6,7},{7,6},{10,12},{11,13},{1... | collective-permute-start | bytes 786440 | tf_op jit(solution)/shard_map/ppermute | solution.py:40
  143.3 12.6 %collective-permute-start.23 = (bf16[64,2048]{1,0:T(8,128)(2,1)S(1)}, bf16[64,2048]{1,0:T(8,128)(2,1)S(1)}, u32[]{:S(2)}, u32[]{:S(2)}) collective-permute-start(bf16[64,2048]{1,0:T(8,128)(2,1)S(1)} %add_convert_fusion.6), channel_id=1, source_target_pairs={{2,4},{3,5},{4,2},{5,3},{0,1},{1,0},{6,7},{7,6},{10,12},{11,13},{1... | collective-permute-start | bytes 786440 | tf_op jit(solution)/shard_map/ppermute | solution.py:40
  143.4 12.4 %collective-permute-start.22 = (bf16[64,2048]{1,0:T(8,128)(2,1)S(1)}, bf16[64,2048]{1,0:T(8,128)(2,1)S(1)}, u32[]{:S(2)}, u32[]{:S(2)}) collective-permute-start(bf16[64,2048]{1,0:T(8,128)(2,1)S(1)} %fusion.1), channel_id=1, source_target_pairs={{0,2},{1,3},{2,0},{3,1},{4,6},{5,7},{6,4},{7,5},{8,10},{9,11},{10,... | collective-permute-start | bytes 786440 | tf_op jit(solution)/shard_map/ppermute | solution.py:35
  156.0 1.6 collective-permute-start.25
  156.1 8.7 %collective-permute-start.24 = (bf16[64,2048]{1,0:T(8,128)(2,1)S(1)}, bf16[64,2048]{1,0:T(8,128)(2,1)S(1)}, u32[]{:S(2)}, u32[]{:S(2)}) collective-permute-start(bf16[64,2048]{1,0:T(8,128)(2,1)S(1)} %fusion.5.refs_0_), channel_id=1, source_target_pairs={{0,2},{1,3},{2,0},{3,1},{4,6},{5,7},{6,4},{7,5},{8,10},{9,11},{10,... | collective-permute-start | bytes 786440 | tf_op jit(solution)/shard_map/ppermute | solution.py:35
  164.9 7.9 %collective-permute-start.26 = (bf16[64,2048]{1,0:T(8,128)(2,1)S(1)}, bf16[64,2048]{1,0:T(8,128)(2,1)S(1)}, u32[]{:S(2)}, u32[]{:S(2)}) collective-permute-start(bf16[64,2048]{1,0:T(8,128)(2,1)S(1)} %broadcast_select_fusion.1), channel_id=1, source_target_pairs={{0,2},{1,3},{2,0},{3,1},{4,6},{5,7},{6,4},{7,5},{8,10},{9,11},{10,... | collective-permute-start | bytes 786440 | tf_op jit(solution)/shard_map/ppermute | solution.py:35
  165.2 7.6 %collective-permute-start.27 = (bf16[64,2048]{1,0:T(8,128)(2,1)S(1)}, bf16[64,2048]{1,0:T(8,128)(2,1)S(1)}, u32[]{:S(2)}, u32[]{:S(2)}) collective-permute-start(bf16[64,2048]{1,0:T(8,128)(2,1)S(1)} %collective-permute-done.24.refs_1_), channel_id=1, source_target_pairs={{2,4},{3,5},{4,2},{5,3},{0,1},{1,0},{6,7},{7,6},{10,12},{11,13},{1... | collective-permute-start | bytes 786440 | tf_op jit(solution)/shard_map/ppermute | solution.py:40
  172.9 7.0 %collective-permute-start.28 = (bf16[64,2048]{1,0:T(8,128)(2,1)S(1)}, bf16[64,2048]{1,0:T(8,128)(2,1)S(1)}, u32[]{:S(2)}, u32[]{:S(2)}) collective-permute-start(bf16[64,2048]{1,0:T(8,128)(2,1)S(1)} %broadcast_select_fusion), channel_id=1, source_target_pairs={{0,2},{1,3},{2,0},{3,1},{4,6},{5,7},{6,4},{7,5},{8,10},{9,11},{10,... | collective-permute-start | bytes 786440 | tf_op jit(solution)/shard_map/ppermute | solution.py:35
  174.7 5.2 %collective-permute-start.29 = (bf16[64,2048]{1,0:T(8,128)(2,1)S(1)}, bf16[64,2048]{1,0:T(8,128)(2,1)S(1)}, u32[]{:S(2)}, u32[]{:S(2)}) collective-permute-start(bf16[64,2048]{1,0:T(8,128)(2,1)S(1)} %add_convert_fusion.5), channel_id=1, source_target_pairs={{2,4},{3,5},{4,2},{5,3},{0,1},{1,0},{6,7},{7,6},{10,12},{11,13},{1... | collective-permute-start | bytes 786440 | tf_op jit(solution)/shard_map/ppermute | solution.py:40
  180.1 12.4 %collective-permute-start.31 = (bf16[64,2048]{1,0:T(8,128)(2,1)S(1)}, bf16[64,2048]{1,0:T(8,128)(2,1)S(1)}, u32[]{:S(2)}, u32[]{:S(2)}) collective-permute-start(bf16[64,2048]{1,0:T(8,128)(2,1)S(1)} %add_convert_fusion.3), channel_id=1, source_target_pairs={{2,4},{3,5},{4,2},{5,3},{0,1},{1,0},{6,7},{7,6},{10,12},{11,13},{1... | collective-permute-start | bytes 786440 | tf_op jit(solution)/shard_map/ppermute | solution.py:40
  180.2 12.3 %collective-permute-start.30 = (bf16[64,2048]{1,0:T(8,128)(2,1)S(1)}, bf16[64,2048]{1,0:T(8,128)(2,1)S(1)}, u32[]{:S(2)}, u32[]{:S(2)}) collective-permute-start(bf16[64,2048]{1,0:T(8,128)(2,1)S(1)} %fusion.2), channel_id=1, source_target_pairs={{0,2},{1,3},{2,0},{3,1},{4,6},{5,7},{6,4},{7,5},{8,10},{9,11},{10,... | collective-permute-start | bytes 786440 | tf_op jit(solution)/shard_map/ppermute | solution.py:35
  192.5 9.1 %collective-permute-start.32 = (bf16[64,2048]{1,0:T(8,128)(2,1)S(1)}, bf16[64,2048]{1,0:T(8,128)(2,1)S(1)}, u32[]{:S(2)}, u32[]{:S(2)}) collective-permute-start(bf16[64,2048]{1,0:T(8,128)(2,1)S(1)} %get-tuple-element.167), channel_id=1, source_target_pairs={{0,2},{1,3},{2,0},{3,1},{4,6},{5,7},{6,4},{7,5},{8,10},{9,11},{10,... | collective-permute-start | bytes 786440 | tf_op jit(solution)/shard_map/ppermute | solution.py:35
  192.6 2.0 collective-permute-start.33
  192.7 11.7 %collective-permute-start.35 = (bf16[64,2048]{1,0:T(8,128)(2,1)S(1)}, bf16[64,2048]{1,0:T(8,128)(2,1)S(1)}, u32[]{:S(2)}, u32[]{:S(2)}) collective-permute-start(bf16[64,2048]{1,0:T(8,128)(2,1)S(1)} %get-tuple-element.171), channel_id=1, source_target_pairs={{0,2},{1,3},{2,0},{3,1},{4,6},{5,7},{6,4},{7,5},{8,10},{9,11},{10,... | collective-permute-start | bytes 786440 | tf_op jit(solution)/shard_map/ppermute | solution.py:35
  194.6 23.5 %copy-start.9 = (f32[64,2048]{1,0:T(8,128)S(1)}, f32[64,2048]{1,0:T(8,128)}, u32[]{:S(2)}) copy-start(f32[64,2048]{1,0:T(8,128)} %copy-done.8) | copy-start | bytes 1572868
  201.6 3.6 %collective-permute-start.36 = (f32[8,128]{1,0:T(8,128)S(1)}, f32[8,128]{1,0:T(8,128)S(1)}, u32[]{:S(2)}, u32[]{:S(2)}) collective-permute-start(f32[8,128]{1,0:T(8,128)S(1)} %add.109), channel_id=1, source_target_pairs={{0,8},{8,0},{16,24},{24,16},{1,9},{9,1},{17,25},{25,17},{2,10},{10... | collective-permute-start | bytes 12296 | tf_op jit(solution)/shard_map/ppermute | solution.py:164
  203.2 2.1 collective-permute-start.34
  204.5 12.9 %collective-permute-start.39 = (bf16[64,2048]{1,0:T(8,128)(2,1)S(1)}, bf16[64,2048]{1,0:T(8,128)(2,1)S(1)}, u32[]{:S(2)}, u32[]{:S(2)}) collective-permute-start(bf16[64,2048]{1,0:T(8,128)(2,1)S(1)} %add_convert_fusion), channel_id=1, source_target_pairs={{2,4},{3,5},{4,2},{5,3},{0,1},{1,0},{6,7},{7,6},{10,12},{11,13},{1... | collective-permute-start | bytes 786440 | tf_op jit(solution)/shard_map/ppermute | solution.py:40
  205.3 12.8 %collective-permute-start.38 = (bf16[64,2048]{1,0:T(8,128)(2,1)S(1)}, bf16[64,2048]{1,0:T(8,128)(2,1)}, u32[]{:S(2)}, u32[]{:S(2)}) collective-permute-start(bf16[64,2048]{1,0:T(8,128)(2,1)S(1)} %fusion.3), channel_id=1, source_target_pairs={{0,2},{1,3},{2,0},{3,1},{4,6},{5,7},{6,4},{7,5},{8,10},{9,11},{10,... | collective-permute-start | bytes 786440 | tf_op jit(solution)/shard_map/ppermute | solution.py:35
  212.5 3.6 %collective-permute-start.37 = (f32[8,128]{1,0:T(8,128)S(1)}, f32[8,128]{1,0:T(8,128)S(1)}, u32[]{:S(2)}, u32[]{:S(2)}) collective-permute-start(f32[8,128]{1,0:T(8,128)S(1)} %add.111), channel_id=1, source_target_pairs={{0,16},{8,24},{16,0},{24,8},{1,17},{9,25},{17,1},{25,9},{2,18},{10... | collective-permute-start | bytes 12296 | tf_op jit(solution)/shard_map/ppermute | solution.py:164
  (24 other events, 189.4 us)

commit v5 on v4

--- a/solution.py
+++ b/solution.py
@@ -52,28 +52,32 @@
 GATE_PIECES = 3
 
 
-def fetch(inner, parts, out, sems):
+def fetch(inner, parts, blocks, out, sems):
     own, side, near, near_end, far, far_end = parts
     rows = own.shape[0]
-
-    def copies(blocks, first):
+    chosen = ((own, side, near, far), (own, side, near_end, far_end))
+
+    def copies(mine):
         return [
-            pltpu.make_async_copy(block, out.at[pl.ds(i * rows, rows), :], sems.at[i])
-            for i, block in enumerate(blocks, first)
+            pltpu.make_async_copy(mine[block], out.at[pl.ds(i * rows, rows), :], sems.at[i])
+            for i, block in enumerate(blocks)
         ]
 
-    def begin(blocks, first):
-        for copy in copies(blocks, first):
+    def begin(mine):
+        for copy in copies(mine):
             copy.start()
 
-    def finish(blocks, first):
-        for copy in copies(blocks, first):
+    def finish(mine):
+        for copy in copies(mine):
             copy.wait()
 
     for act in (begin, finish):
-        act((own, side), 0)
-        pl.when(inner)(functools.partial(act, (near, far), 2))
-        pl.when(jnp.logical_not(inner))(functools.partial(act, (near_end, far_end), 2))
+        pl.when(inner)(functools.partial(act, chosen[0]))
+        pl.when(jnp.logical_not(inner))(functools.partial(act, chosen[1]))
+
+
+def add_term(total, earlier, term):
+    total[...] = term if earlier is None else earlier[...] + term
 
 
 def store_parts(total, outs):
@@ -82,17 +86,24 @@
         out[...] = total[pl.ds(i * rows, rows), :].astype(out.dtype)
 
 
-def forward_kernel(owners, where_ref, *refs):
-    parts, weights, outs, (b_out, a_out) = refs[:6], refs[6:12], refs[12:16], refs[16:18]
-    sems, load, total = refs[18:]
-    width, hidden = total.shape[1], weights[0].shape[2]
-    fetch(where_ref[0] == 1, parts, load, sems)
+def forward_kernel(owners, experts, start, finish, unused, where_ref, *refs):
+    refs = list(refs[unused:])
+    parts, refs = refs[:6], refs[6:]
+    earlier = None if start else refs.pop(0)
+    weights, refs = refs[: 3 * len(experts)], refs[3 * len(experts) :]
+    sems, load, total = refs[-3:]
+    states = refs[-3 - 2 * len(experts) : -3]
+    outs = refs[: -3 - 2 * len(experts)]
+    if not finish:
+        total = outs[0]
+    width = total.shape[1]
+    fetch(where_ref[0] == 1, parts, range(LINE), load, sems)
     x, v = load.at[:, pl.ds(0, width)], load.at[:, pl.ds(width, width)]
     gates = load.at[:, pl.ds(2 * width, LANES)]
     lane = lax.broadcasted_iota(jnp.int32, (1, LANES), 1)
-    for i in range(CORES):
+    for i, which in enumerate(experts):
         gate_w, up_w, down_w = weights[3 * i : 3 * i + 3]
-        expert = where_ref[1 + i]
+        expert = where_ref[1 + which]
         named = lane == expert
         for piece in range(1, GATE_PIECES):
             named = named | (lane == expert + piece * owners)
@@ -102,61 +113,83 @@
         sigma = 1.0 / (1.0 + jnp.exp(-a))
         act = g * (a * sigma)
         b_slope = g * (sigma * (1.0 + a * (1.0 - sigma))) * b
-        columns = pl.ds(i * hidden, hidden)
-        a_out[:, columns] = act
-        b_out[:, columns] = b_slope
+        states[2 * i][...] = b_slope
+        states[2 * i + 1][...] = act
         term = dot((b_slope * da + act * db).astype(jnp.bfloat16), down_w[0])
-        if i == 0:
-            total[...] = term
-        else:
-            total[...] += term
-    store_parts(total, outs)
-
-
-def backward_kernel(where_ref, *refs):
-    parts, (b_ref, a_ref), weights, outs = refs[:6], refs[6:8], refs[8:14], refs[14:18]
-    squares, sems, jv, total = refs[18:]
-    hidden = weights[0].shape[2]
-    fetch(where_ref[0] == 1, parts, jv, sems)
-    sums = jnp.zeros((1, LANES), jnp.float32)
-    for start in range(0, jv.shape[1], LANES):
-        piece = jv[:, pl.ds(start, LANES)].astype(jnp.float32)
-        sums = sums + jnp.sum(piece * piece, axis=0, keepdims=True)
-    squares[...] = jnp.broadcast_to(sums, squares.shape)
-    for i in range(CORES):
+        add_term(total, earlier, term)
+        earlier = total
+    if finish:
+        store_parts(total, outs)
+
+
+def backward_kernel(experts, blocks, start, finish, unused, where_ref, *refs):
+    refs = list(refs[unused:])
+    parts, refs = refs[:6], refs[6:]
+    earlier = None if start else refs.pop(0)
+    states, refs = refs[: 2 * len(experts)], refs[2 * len(experts) :]
+    weights, refs = refs[: 3 * len(experts)], refs[3 * len(experts) :]
+    sems, jv, total = refs[-3:]
+    outs = refs[:-3]
+    squares = outs.pop() if start else None
+    if not finish:
+        total = outs[0]
+    rows = parts[0].shape[0]
+    here = pl.ds(blocks[0] * rows, len(blocks) * rows)
+    fetch(where_ref[0] == 1, parts, blocks, jv, sems)
+    if start:
+        sums = jnp.zeros((1, LANES), jnp.float32)
+        for column in range(0, jv.shape[1], LANES):
+            piece = jv[:, pl.ds(column, LANES)].astype(jnp.float32)
+            sums = sums + jnp.sum(piece * piece, axis=0, keepdims=True)
+        squares[...] = jnp.broadcast_to(sums, squares.shape)
+    for i in range(len(experts)):
         gate_w, up_w, down_w = weights[3 * i : 3 * i + 3]
-        columns = pl.ds(i * hidden, hidden)
         back = dot_last(jv[...], down_w[0])
-        grad_gate = (back * b_ref[:, columns]).astype(jnp.bfloat16)
-        grad_up = (back * a_ref[:, columns]).astype(jnp.bfloat16)
+        grad_gate = (back * states[2 * i][here, :]).astype(jnp.bfloat16)
+        grad_up = (back * states[2 * i + 1][here, :]).astype(jnp.bfloat16)
         term = dot_last(grad_gate, gate_w[0]) + dot_last(grad_up, up_w[0])
-        if i == 0:
-            total[...] = term
-        else:
-            total[...] += term
-    store_parts(total, outs)
-
-
-def kernel_call(kernel, name, where, parts, operands, rows, width, extra_outs, flops):
-    vmem = pl.BlockSpec(memory_space=pltpu.VMEM)
-    outs = [pltpu.VMEM((rows, width), jnp.float32)]
-    outs += [pltpu.VMEM((rows, width), jnp.bfloat16)] * (LINE - 1) + extra_outs
+        add_term(total, earlier, term)
+        earlier = total
+    if finish:
+        store_parts(total, outs)
+
+
+def kernel_call(kernel, name, where, parts, operands, outs, blocks, width, flops, unused=()):
+    anywhere, vmem = pl.BlockSpec(memory_space=pl.ANY), pl.BlockSpec(memory_space=pltpu.VMEM)
+    called = functools.partial(kernel, len(unused))
+    rows = parts[0].shape[0] * blocks
     return pl.pallas_call(
-        kernel,
+        called,
         in_specs=[pl.BlockSpec(memory_space=pltpu.SMEM)]
-        + [pl.BlockSpec(memory_space=pl.ANY)] * len(parts)
+        + [anywhere] * (len(parts) + len(unused))
         + [vmem] * len(operands),
         out_specs=[vmem] * len(outs),
-        out_shape=outs,
+        out_shape=[pltpu.VMEM(shape, kind) for shape, kind in outs],
         scratch_shapes=[
-            pltpu.SemaphoreType.DMA((LINE,)),
-            pltpu.VMEM((LINE * rows, parts[0].shape[1]), jnp.bfloat16),
-            pltpu.VMEM((LINE * rows, width), jnp.float32),
+            pltpu.SemaphoreType.DMA((blocks,)),
+            pltpu.VMEM((rows, parts[0].shape[1]), jnp.bfloat16),
+            pltpu.VMEM((rows, width), jnp.float32),
         ],
         compiler_params=pltpu.CompilerParams(vmem_limit_bytes=16 * 2**20),
         cost_estimate=pl.CostEstimate(flops=flops, bytes_accessed=0, transcendentals=0),
         name=name,
-    )(where, *parts, *[in_vmem(value) for value in operands])
+    )(where, *unused, *parts, *[in_vmem(value) for value in operands])
+
+
+def touch_kernel(*refs):
+    refs[-1][...] = refs[0][0, pl.ds(0, 16), pl.ds(0, LANES)]
+
+
+def touch(weights):
+    vmem = pl.BlockSpec(memory_space=pltpu.VMEM)
+    return pl.pallas_call(
+        touch_kernel,
+        in_specs=[vmem] * len(weights),
+        out_specs=vmem,
+        out_shape=pltpu.VMEM((16, LANES), jnp.bfloat16),
+        compiler_params=pltpu.CompilerParams(vmem_limit_bytes=12 * 2**20),
+        name="touch",
+    )(*[in_vmem(value) for value in weights])
 
 
 def exchange_sum(value, axis, step):
@@ -199,34 +232,46 @@
     def home(parts, side, inner_last):
         return parts[0] + side.astype(jnp.float32) + pick(0.0, inner_last.astype(jnp.float32))
 
-    def forward(parts):
-        state = pltpu.VMEM((line_rows, CORES * hidden), jnp.float32)
-        *outs, b_slope, act = kernel_call(
-            functools.partial(forward_kernel, owners),
+    def part_outs(blocks):
+        return [((half, width), jnp.float32 if block == 0 else jnp.bfloat16) for block in blocks]
+
+    def forward(parts, experts, earlier=None, unused=()):
+        finish = experts[-1] == CORES - 1
+        outs = part_outs(range(LINE)) if finish else [((line_rows, width), jnp.float32)]
+        result = kernel_call(
+            functools.partial(forward_kernel, owners, experts, experts[0] == 0, finish),
             "forward",
             where,
             parts,
-            weights,
-            half,
+            ([] if earlier is None else [earlier]) + [w for e in experts for w in weights[e]],
+            outs + [((line_rows, hidden), jnp.float32)] * (2 * len(experts)),
+            LINE,
             width,
-            [state, state],
-            2 * 5 * line_rows * width * CORES * hidden,
+            2 * 5 * line_rows * width * hidden * len(experts),
+            unused,
         )
-        return outs, (b_slope, act)
-
-    def backward(parts, states):
-        *outs, squares = kernel_call(
-            backward_kernel,
+        states = result[len(outs) :]
+        return (result[: len(outs)] if finish else result[0]), states
+
+    def backward(parts, states, experts, blocks=tuple(range(LINE)), earlier=None):
+        start, finish = experts[0] == 0, experts[-1] == CORES - 1
+        rows = len(blocks) * half
+        outs = part_outs(blocks) if finish else [((rows, width), jnp.float32)]
+        result = kernel_call(
+            functools.partial(backward_kernel, experts, blocks, start, finish),
             "backward",
             where,
             parts,
-            (*states, *weights),
-            half,
+            ([] if earlier is None else [earlier])
+            + [s for e in experts for s in states[2 * e : 2 * e + 2]]
+            + [w for e in experts for w in weights[e]],
+            outs + ([((8, LANES), jnp.float32)] if start else []),
+            len(blocks),
             width,
-            [pltpu.VMEM((8, LANES), jnp.float32)],
-            2 * 3 * line_rows * width * CORES * hidden,
+            2 * 3 * rows * width * hidden * len(experts),
         )
-        return outs, squares
+        squares = result[-1] if start else None
+        return (result[: len(outs)] if finish else result[0]), squares
 
     pieces = gate_pieces(routes, gates, owners)
     halves = [slice(0, half), slice(half, token_count)]
@@ -246,68 +291,88 @@
     a_side, a_near, sib_gate, w_up, w_down, load_b = slot(
         side_hop(load_a), inner_hop(load_a), lax.ppermute(w_gate, "expert", swap), w_up, w_down, load_b
     )
-    a_near_end, a_far, sib_up, w_down, load_b = slot(
-        side_hop(a_near), inner_hop(a_side), lax.ppermute(w_up, "expert", swap), w_down, load_b
-    )
-    a_far_end, sib_down, load_b = slot(side_hop(a_far), lax.ppermute(w_down, "expert", swap), load_b)
-    weights = (w_gate, w_up, w_down, sib_gate, sib_up, sib_down)
-
+    a_near_end, a_far, sib_up, own_piece, w_down, load_b = slot(
+        side_hop(a_near),
+        inner_hop(a_side),
+        lax.ppermute(w_up, "expert", swap),
+        touch((w_gate, w_up, w_down)),
+        w_down,
+        load_b,
+    )
+    a_far_end, sib_down, sib_piece, load_b = slot(
+        side_hop(a_far), lax.ppermute(w_down, "expert", swap), touch((sib_gate, sib_up)), load_b
+    )
+    weights = ((w_gate, w_up, w_down), (sib_gate, sib_up, sib_down))
+
+    everyone = tuple(range(CORES))
     b_side, b_near, (pa, states_a) = slot(
         side_hop(load_b),
         inner_hop(load_b),
-        forward((load_a, a_side, a_near, a_near_end, a_far, a_far_end)),
+        forward(
+            (load_a, a_side, a_near, a_near_end, a_far, a_far_end), everyone, unused=(own_piece, sib_piece)
+        ),
     )
     b_near_end, b_far = slot(both_ways(pa[3], b_near), inner_hop(b_side))
     sa_far = add_rows(pa[3], b_near_end[:, :width])
     b_far_end, sa_side = slot(both_ways(pa[2], b_far), inner_hop(sa_far))
     sa_near = add_rows(pa[2], b_far_end[:, :width])
-    came, last, (pb, states_b) = slot(
-        both_ways(pa[1], add_rows(pa[1], sa_side)),
-        inner_hop(sa_near),
-        forward((load_b, b_side, b_near, b_near_end, b_far, b_far_end)),
+    b_parts = (load_b, b_side, b_near, b_near_end, b_far, b_far_end)
+    came, last, (sum_b, states_b) = slot(
+        both_ways(pa[1], add_rows(pa[1], sa_side)), inner_hop(sa_near), forward(b_parts, everyone[:1])
     )
     jv_a = tangent[:half].astype(jnp.float32) + home(pa, came, last)
 
-    def gather_and_reduce(own, parts, work):
-        side, near = slot(side_hop(own), inner_hop(own))
-        near_end, far = slot(both_ways(parts[3], near), inner_hop(side))
-        s_far = add_rows(parts[3], near_end)
-        far_end, s_side = slot(both_ways(parts[2], far), inner_hop(s_far))
-        s_near = add_rows(parts[2], far_end)
-        came, last, worked = slot(
-            both_ways(parts[1], add_rows(parts[1], s_side)),
-            inner_hop(s_near),
-            work((own, side, near, near_end, far, far_end)),
-        )
-        return worked, home(parts, came, last)
-
-    (ga, squares_a), sum_b = gather_and_reduce(
-        jv_a.astype(jnp.bfloat16), pb, lambda parts: backward(parts, states_a)
-    )
-    jv_b = tangent[half:].astype(jnp.float32) + sum_b
-    (gb, squares_b), grad_a = gather_and_reduce(
-        jv_b.astype(jnp.bfloat16), ga, lambda parts: backward(parts, states_b)
-    )
-
-    sum_a = jv_a + grad_a
+    ja = jv_a.astype(jnp.bfloat16)
+    side, near, (pb, rest_b) = slot(
+        side_hop(ja), inner_hop(ja), forward(b_parts, everyone[1:], sum_b)
+    )
+    states_b = [*states_b, *rest_b]
+    near_end, far = slot(both_ways(pb[3], near), inner_hop(side))
+    s_far = add_rows(pb[3], near_end)
+    far_end, s_side = slot(both_ways(pb[2], far), inner_hop(s_far))
+    s_near = add_rows(pb[2], far_end)
+    ja_parts = (ja, side, near, near_end, far, far_end)
+    came, last, (sum_a, squares_a) = slot(
+        both_ways(pb[1], add_rows(pb[1], s_side)),
+        inner_hop(s_near),
+        backward(ja_parts, states_a, everyone[:1]),
+    )
+    jv_b = tangent[half:].astype(jnp.float32) + home(pb, came, last)
+
+    jb = jv_b.astype(jnp.bfloat16)
+    side, near, (ga, _) = slot(
+        side_hop(jb), inner_hop(jb), backward(ja_parts, states_a, everyone[1:], earlier=sum_a)
+    )
+    near_end, far = slot(both_ways(ga[3], near), inner_hop(side))
+    s_far = add_rows(ga[3], near_end)
+    far_end, s_side = slot(both_ways(ga[2], far), inner_hop(s_far))
+    s_near = add_rows(ga[2], far_end)
+    jb_parts = (jb, side, near, near_end, far, far_end)
+    came, last, (gb, squares_b) = slot(
+        both_ways(ga[1], add_rows(ga[1], s_side)),
+        inner_hop(s_near),
+        backward(jb_parts, states_b, everyone),
+    )
+    whole_a = jv_a + home(ga, came, last)
+
     lines = lax.axis_size("dp")
-    first, second = side_hop(gb[3]), side_hop(gb[2])
-    first, squares = slot(first, exchange_sum(squares_a + squares_b, "expert", 1))
+    squares = exchange_sum(squares_a + squares_b, "expert", 1)
     step = 1
     while step < lines // 2:
         squares = exchange_sum(squares, "dp", step)
         step *= 2
-    s_near = add_rows(gb[2], second)
-    s_side, second, squares = slot(inner_hop(add_rows(gb[3], first)), second, squares)
-    came, last = side_hop(pick(gb[1], add_rows(gb[1], s_side))), inner_hop(s_near)
+    came, squares = slot(side_hop(gb[3]), squares)
+    came, s_side = slot(side_hop(gb[2]), inner_hop(add_rows(gb[3], came)))
+    s_near = add_rows(gb[2], came)
     while step < lines:
         squares = exchange_sum(squares, "dp", step)
         step *= 2
+    came, last = side_hop(pick(gb[1], add_rows(gb[1], s_side))), inner_hop(s_near)
     grad_b = home(gb, came, last)
 
     elements = token_count * width * lax.axis_size("dp") * owners
     scale = lax.rsqrt(jnp.sum(squares[0]) / elements + 1e-06)
-    return jnp.concatenate([sum_a * scale, (jv_b + grad_b) * scale])
+    return jnp.concatenate([whole_a * scale, (jv_b + grad_b) * scale])
 
 
 def owner_states(x_rows, gate_w, up_w):

time: 222 us -> 205 us (0.923)
  waiting for transfers between devices: 112 us -> 90.6 us
  Pallas kernels: 43.9 us -> 54.5 us
  starting transfers between devices: 41.1 us -> 37.6 us
  local copies, waits for them, and re-layouts: 16.4 us -> 14 us
    ppermute x18, waiting for transfers between devices: 107 us -> 85.6 us  [side_hop(): return lax.ppermute(rows, 'expert', both_cores(SIDE_PAIRS))]
    pallas_call x4 -> x8, Pallas kernels: 43.9 us -> 54.5 us  [the longest x6 50.5 us: kernel_call(): pl.pallas_call(called, in_specs=[pl.BlockSpec(memory_space=pltpu.SMEM)] +...]
    ppermute x18, starting transfers between devices: 36.5 us -> 33.1 us  [side_hop(): return lax.ppermute(rows, 'expert', both_cores(SIDE_PAIRS))]
    unnamed x64 -> x60, local copies, waits for them, and re-layouts: 14.8 us -> 12.4 us
  transfers between devices with their start and end apart: 40 -> 40, of which waited for: 18 -> 18; matrix products, arithmetic and copies ran while one was open for 2% -> 2% of each run, Pallas kernels for 20% -> 27%
where the time goes in v5:
time: 205 us
  waiting for transfers between devices  90.6 us (44%)
  Pallas kernels  54.5 us (27%)
  starting transfers between devices  37.6 us (18%)
  local copies, waits for them, and re-layouts  14 us (7%)
  other arithmetic  6.91 us (3%)
    ppermute x18, waiting for transfers between devices, side_hop(): return lax.ppermute(rows, 'expert', both_cores(SIDE_PAIRS))  85.6 us
    pallas_call x6, Pallas kernels, kernel_call(): pl.pallas_call(called, in_specs=[pl.BlockSpec(memory_space=pltpu.SMEM)] +...  50.5 us
    ppermute x18, starting transfers between devices, side_hop(): return lax.ppermute(rows, 'expert', both_cores(SIDE_PAIRS))  33.1 us
    unnamed x60, local copies, waits for them, and re-layouts  12.4 us
  transfers between devices with their start and end apart: 40, of which 18 were waited for; matrix products, arithmetic and copies ran while one was open for 2% of the time, Pallas kernels for 27%

profile of v5, /device:TPU:0, one launch (start us, length us, event | category | flops | bytes accessed | tf_op | source)
XLA Modules:
  0.0 204.8 jit_solution(4821289210000926329)
XLA Ops:
  1.3 1.4 fusion.8
  2.9 4.1 %collective-permute-start = (bf16[64,4224]{1,0:T(8,128)(2,1)S(1)}, bf16[64,4224]{1,0:T(8,128)(2,1)S(1)}, u32[]{:S(2)}, u32[]{:S(2)}) collective-permute-start(bf16[64,4224]{1,0:T(8,128)(2,1)S(1)} %pad_maximum_fusion.1.refs_2_), channel_id=1, source_target_pairs={{0,2},{1,3},{2,0},{3,1},{4,6},{5,7},{6,4},{7,5},{8,10},{9,11},{10,... | collective-permute-start | bytes 1622024 | tf_op jit(solution)/shard_map/ppermute | solution.py:35
  7.9 11.8 %collective-permute-done.refs_3_ = bf16[64,4224]{1,0:T(8,128)(2,1)S(1)} collective-permute-done((bf16[64,4224]{1,0:T(8,128)(2,1)S(1)}, bf16[64,4224]{1,0:T(8,128)(2,1)S(1)}, u32[]{:S(2)}, u32[]{:S(2)}) %collective-permute-start) | collective-permute-done | bytes 540704 | tf_op jit(solution)/shard_map/ppermute | solution.py:35
  19.8 1.8 collective-permute-start.3
  21.8 1.9 copy-done.1
  23.7 1.9 touch.2.refs_0_
  25.6 8.9 %collective-permute-done.3.refs_5_ = bf16[64,4224]{1,0:T(8,128)(2,1)S(1)} collective-permute-done((bf16[64,4224]{1,0:T(8,128)(2,1)S(1)}, bf16[64,4224]{1,0:T(8,128)(2,1)S(1)}, u32[]{:S(2)}, u32[]{:S(2)}) %collective-permute-start.3) | collective-permute-done | bytes 540704 | tf_op jit(solution)/shard_map/ppermute | solution.py:35
  35.3 1.7 copy-done.3
  37.0 1.7 collective-permute-start.6
  38.9 1.9 copy-done.4
  40.7 2.0 touch.3.refs_1_
  42.8 9.2 %collective-permute-done.6.refs_7_ = bf16[64,4224]{1,0:T(8,128)(2,1)} collective-permute-done((bf16[64,4224]{1,0:T(8,128)(2,1)}, bf16[64,4224]{1,0:T(8,128)(2,1)}, u32[]{:S(2)}, u32[]{:S(2)}) %collective-permute-start.6) | collective-permute-done | bytes 540704 | tf_op jit(solution)/shard_map/ppermute | solution.py:35
  52.0 2.7 %collective-permute-start.8 = (bf16[64,4224]{1,0:T(8,128)(2,1)}, bf16[64,4224]{1,0:T(8,128)(2,1)S(1)}, u32[]{:S(2)}, u32[]{:S(2)}) collective-permute-start(bf16[64,4224]{1,0:T(8,128)(2,1)} %pad_maximum_fusion.2.refs_0_), channel_id=1, source_target_pairs={{0,2},{1,3},{2,0},{3,1},{4,6},{5,7},{6,4},{7,5},{8,10},{9,11},{10,... | collective-permute-start | bytes 1622024 | tf_op jit(solution)/shard_map/ppermute | solution.py:35
  54.7 1.0 copy-done.12
  55.8 1.0 copy-done.17
  56.8 1.0 copy-done.19
  57.9 1.0 copy-done.21
  58.9 13.7 %forward.3 = (f32[64,2048]{1,0:T(8,128)S(1)}, bf16[64,2048]{1,0:T(8,128)(2,1)S(1)}, bf16[64,2048]{1,0:T(8,128)(2,1)S(1)}, bf16[64,2048]{1,0:T(8,128)(2,1)S(1)}, ...) custom-call(s32[3]{0:T(128)S(1)} %pad_add_fusion.where_ref, ...), custom_call_target="tpu_custom_call" | custom-call | flops 8053063680 | tf_op jit(solution)/shard_map/forward/pallas_call | solution.py:161
  72.9 13.3 %collective-permute-done.10.refs_3_ = bf16[64,4224]{1,0:T(8,128)(2,1)S(1)} collective-permute-done((bf16[64,4224]{1,0:T(8,128)(2,1)S(1)}, bf16[64,4224]{1,0:T(8,128)(2,1)S(1)}, u32[]{:S(2)}, u32[]{:S(2)}) %collective-permute-start.10) | collective-permute-done | bytes 540704 | tf_op jit(solution)/shard_map/ppermute | solution.py:35
  86.3 1.8 collective-permute-start.12
  88.2 1.5 collective-permute-done.13
  89.7 9.0 %collective-permute-done.12.refs_5_ = bf16[64,4224]{1,0:T(8,128)(2,1)S(1)} collective-permute-done((bf16[64,4224]{1,0:T(8,128)(2,1)S(1)}, bf16[64,4224]{1,0:T(8,128)(2,1)S(1)}, u32[]{:S(2)}, u32[]{:S(2)}) %collective-permute-start.12) | collective-permute-done | bytes 540704 | tf_op jit(solution)/shard_map/ppermute | solution.py:35
  99.0 3.2 %collective-permute-start.14 = (bf16[64,2048]{1,0:T(8,128)(2,1)S(1)}, bf16[64,2048]{1,0:T(8,128)(2,1)S(1)}, u32[]{:S(2)}, u32[]{:S(2)}) collective-permute-start(bf16[64,2048]{1,0:T(8,128)(2,1)S(1)} %fusion), channel_id=1, source_target_pairs={{0,2},{1,3},{2,0},{3,1},{4,6},{5,7},{6,4},{7,5},{8,10},{9,11},{10,... | collective-permute-start | bytes 786440 | tf_op jit(solution)/shard_map/ppermute | solution.py:35
  102.2 6.8 %forward.4 = (f32[256,2048]{1,0:T(8,128)S(1)}, f32[256,768]{1,0:T(8,128)S(1)}, f32[256,768]{1,0:T(8,128)S(1)}) custom-call(s32[3]{0:T(128)S(1)} %pad_add_fusion.where_ref, bf16[64,4224]{1,0:T(8,128)(2,1)S(1)} %copy-done.10, bf16[64,4224]{1,0:T(8,128)(2,1)S(1)} %collective-permute-done.8.refs_1_, bf16[64,4224]{1,0:T(8,128)(2,1)S(1)} %collective-permute-done.9.refs_2_, ...), custom_call_target="tpu_custom_call" | custom-call | flops 4026531840 | tf_op jit(solution)/shard_map/forward/pallas_call | solution.py:161
  109.9 7.6 %forward.5 = (f32[64,2048]{1,0:T(8,128)S(1)}, bf16[64,2048]{1,0:T(8,128)(2,1)S(1)}, bf16[64,2048]{1,0:T(8,128)(2,1)S(1)}, bf16[64,2048]{1,0:T(8,128)(2,1)S(1)}, ...) custom-call(s32[3]{0:T(128)S(1)} %pad_add_fusion.where_ref, bf16[64,4224]{1,0:T(8,128)(2,1)S(1)} %copy-done.10, ...), custom_call_target="tpu_custom_call" | custom-call | flops 4026531840 | tf_op jit(solution)/shard_map/forward/pallas_call | solution.py:161
  118.0 1.5 collective-permute-start.18
  119.6 6.2 %collective-permute-done.18.refs_3_ = bf16[64,2048]{1,0:T(8,128)(2,1)S(1)} collective-permute-done((bf16[64,2048]{1,0:T(8,128)(2,1)S(1)}, bf16[64,2048]{1,0:T(8,128)(2,1)S(1)}, u32[]{:S(2)}, u32[]{:S(2)}) %collective-permute-start.18) | collective-permute-done | bytes 262176 | tf_op jit(solution)/shard_map/ppermute | solution.py:35
  125.9 1.9 collective-permute-start.20
  127.8 5.2 %collective-permute-done.20.refs_5_ = bf16[64,2048]{1,0:T(8,128)(2,1)S(1)} collective-permute-done((bf16[64,2048]{1,0:T(8,128)(2,1)S(1)}, bf16[64,2048]{1,0:T(8,128)(2,1)S(1)}, u32[]{:S(2)}, u32[]{:S(2)}) %collective-permute-start.20) | collective-permute-done | bytes 262176 | tf_op jit(solution)/shard_map/ppermute | solution.py:35
  133.2 2.2 %collective-permute-start.22 = (bf16[64,2048]{1,0:T(8,128)(2,1)S(1)}, bf16[64,2048]{1,0:T(8,128)(2,1)S(1)}, u32[]{:S(2)}, u32[]{:S(2)}) collective-permute-start(bf16[64,2048]{1,0:T(8,128)(2,1)S(1)} %fusion.1), channel_id=1, source_target_pairs={{0,2},{1,3},{2,0},{3,1},{4,6},{5,7},{6,4},{7,5},{8,10},{9,11},{10,... | collective-permute-start | bytes 786440 | tf_op jit(solution)/shard_map/ppermute | solution.py:35
  135.5 5.6 %backward.3 = (f32[256,2048]{1,0:T(8,128)S(1)}, f32[8,128]{1,0:T(8,128)S(1)}) custom-call(s32[3]{0:T(128)S(1)} %pad_add_fusion.where_ref, bf16[64,2048]{1,0:T(8,128)(2,1)S(1)} %fusion.4.refs_0_, bf16[64,2048]{1,0:T(8,128)(2,1)S(1)} %collective-permute-done.16.refs_1_, bf16[64,2048]{1,0:T(8,128)(2,1)S(1)} %collective-permute-done.17.refs_2_, ...), custom_call_target="tpu_custom_call" | custom-call | flops 2415919104 | tf_op jit(solution)/shard_map/backward/pallas_call | solution.py:161
  142.7 1.5 collective-permute-start.24
  144.2 6.6 %backward.4 = (f32[64,2048]{1,0:T(8,128)S(1)}, bf16[64,2048]{1,0:T(8,128)(2,1)S(1)}, bf16[64,2048]{1,0:T(8,128)(2,1)S(1)}, bf16[64,2048]{1,0:T(8,128)(2,1)S(1)}) custom-call(s32[3]{0:T(128)S(1)} %pad_add_fusion.where_ref, bf16[64,2048]{1,0:T(8,128)(2,1)S(1)} %fusion.4.refs_0_, bf16[64,2048]{1,0:T(8,128)(2,1)S(1)} %collective-permute-done.16.refs_1_, ...), custom_call_target="tpu_custom_call" | custom-call | flops 2415919104 | tf_op jit(solution)/shard_map/backward/pallas_call | solution.py:161
  151.8 7.7 %collective-permute-done.26.refs_3_ = bf16[64,2048]{1,0:T(8,128)(2,1)S(1)} collective-permute-done((bf16[64,2048]{1,0:T(8,128)(2,1)S(1)}, bf16[64,2048]{1,0:T(8,128)(2,1)S(1)}, u32[]{:S(2)}, u32[]{:S(2)}) %collective-permute-start.26) | collective-permute-done | bytes 262176 | tf_op jit(solution)/shard_map/ppermute | solution.py:35
  159.6 1.8 collective-permute-start.28
  161.4 5.3 %collective-permute-done.28.refs_5_ = bf16[64,2048]{1,0:T(8,128)(2,1)S(1)} collective-permute-done((bf16[64,2048]{1,0:T(8,128)(2,1)S(1)}, bf16[64,2048]{1,0:T(8,128)(2,1)S(1)}, u32[]{:S(2)}, u32[]{:S(2)}) %collective-permute-start.28) | collective-permute-done | bytes 262176 | tf_op jit(solution)/shard_map/ppermute | solution.py:35
  167.0 2.6 %collective-permute-start.30 = (bf16[64,2048]{1,0:T(8,128)(2,1)S(1)}, bf16[64,2048]{1,0:T(8,128)(2,1)S(1)}, u32[]{:S(2)}, u32[]{:S(2)}) collective-permute-start(bf16[64,2048]{1,0:T(8,128)(2,1)S(1)} %fusion.2), channel_id=1, source_target_pairs={{0,2},{1,3},{2,0},{3,1},{4,6},{5,7},{6,4},{7,5},{8,10},{9,11},{10,... | collective-permute-start | bytes 786440 | tf_op jit(solution)/shard_map/ppermute | solution.py:35
  169.6 10.2 %backward.5 = (f32[64,2048]{1,0:T(8,128)S(1)}, bf16[64,2048]{1,0:T(8,128)(2,1)S(1)}, bf16[64,2048]{1,0:T(8,128)(2,1)S(1)}, bf16[64,2048]{1,0:T(8,128)(2,1)S(1)}, f32[8,128]{1,0:T(8,128)S(1)}) custom-call(s32[3]{0:T(128)S(1)} %pad_add_fusion.where_ref, bf16[64,2048]{1,0:T(8,128)(2,1)S(1)} %fusion.5.refs_0_, ...), custom_call_target="tpu_custom_call" | custom-call | flops 4831838208 | tf_op jit(solution)/shard_map/backward/pallas_call | solution.py:161
  180.0 1.2 collective-permute-done.33
  181.2 1.5 collective-permute-start.34
  182.7 1.9 collective-permute-start.36
  184.8 2.3 %collective-permute-done.32 = bf16[64,2048]{1,0:T(8,128)(2,1)S(1)} collective-permute-done((bf16[64,2048]{1,0:T(8,128)(2,1)S(1)}, bf16[64,2048]{1,0:T(8,128)(2,1)S(1)}, u32[]{:S(2)}, u32[]{:S(2)}) %collective-permute-start.32) | collective-permute-done | bytes 262176 | tf_op jit(solution)/shard_map/ppermute | solution.py:35
  187.3 4.6 %collective-permute-done.36 = bf16[64,2048]{1,0:T(8,128)(2,1)S(1)} collective-permute-done((bf16[64,2048]{1,0:T(8,128)(2,1)S(1)}, bf16[64,2048]{1,0:T(8,128)(2,1)S(1)}, u32[]{:S(2)}, u32[]{:S(2)}) %collective-permute-start.36) | collective-permute-done | bytes 262176 | tf_op jit(solution)/shard_map/ppermute | solution.py:35
  192.2 3.8 %collective-permute-start.38 = (bf16[64,2048]{1,0:T(8,128)(2,1)S(1)}, bf16[64,2048]{1,0:T(8,128)(2,1)}, u32[]{:S(2)}, u32[]{:S(2)}) collective-permute-start(bf16[64,2048]{1,0:T(8,128)(2,1)S(1)} %fusion.3), channel_id=1, source_target_pairs={{0,2},{1,3},{2,0},{3,1},{4,6},{5,7},{6,4},{7,5},{8,10},{9,11},{10,... | collective-permute-start | bytes 786440 | tf_op jit(solution)/shard_map/ppermute | solution.py:35
  195.9 1.5 collective-permute-start.35
  197.5 2.1 %collective-permute-done.35 = f32[8,128]{1,0:T(8,128)S(1)} collective-permute-done((f32[8,128]{1,0:T(8,128)S(1)}, f32[8,128]{1,0:T(8,128)S(1)}, u32[]{:S(2)}, u32[]{:S(2)}) %collective-permute-start.35) | collective-permute-done | bytes 4128 | tf_op jit(solution)/shard_map/ppermute | solution.py:197
  201.6 2.1 %add_multiply_fusion.1 = (f32[64,2048]{1,0:T(8,128)S(1)}, f32[64,2048]{1,0:T(8,128)S(1)}) fusion(bf16[64,2048]{1,0:T(8,128)(2,1)} %copy-done.27, f32[64,2048]{1,0:T(8,128)S(1)} %copy-done.14, bf16[64,2048]{1,0:T(8,128)(2,1)} %copy-done.28, f32[]{:T(128)S(6)} %rsqrt.3, pred[]{:T(512)S(6)} %or.3, bf16[64,2048]{1,0:T(8,128)(2,1)S(1)} %collective-permute-done.15, ...), kind=kLoop, calls=%fused_computation.9 | loop fusion | flops 3670016 | bytes 5767173 | tf_op jit(solution)/shard_map/mul | solution.py:375
  203.7 1.1 pad_maximum_fusion
  (140 shorter events, 10.9 us)
Async XLA Ops:
  0.0 19.7 %collective-permute-start.2 = (bf16[1,2048,768]{2,1,0:T(8,128)(2,1)}, bf16[1,2048,768]{2,1,0:T(8,128)(2,1)}, u32[]{:S(2)}, u32[]{:S(2)}) collective-permute-start(bf16[1,2048,768]{2,1,0:T(8,128)(2,1)} %refs_10_.3), channel_id=1, source_target_pairs={{0,1},{1,0},{2,3},{3,2},{4,5},{5,4},{6,7},{7,6},{8,9},{9,8},{10,11... | collective-permute-start | bytes 9437192 | tf_op jit(solution)/shard_map/ppermute | solution.py:292
  1.3 20.4 %copy-start = (bf16[1,2048,768]{2,1,0:T(8,128)(2,1)S(1)}, bf16[1,2048,768]{2,1,0:T(8,128)(2,1)}, u32[]{:S(2)}) copy-start(bf16[1,2048,768]{2,1,0:T(8,128)(2,1)} %refs_10_.3) | copy-start | bytes 9437188
  2.8 16.9 %copy-start.11 = (bf16[64,4224]{1,0:T(8,128)(2,1)}, bf16[64,4224]{1,0:T(8,128)(2,1)S(1)}, u32[]{:S(2)}) copy-start(bf16[64,4224]{1,0:T(8,128)(2,1)S(1)} %pad_maximum_fusion.1.refs_2_) | copy-start | bytes 1622020
  2.8 5.1 %collective-permute-start.1 = (bf16[64,4224]{1,0:T(8,128)(2,1)S(1)}, bf16[64,4224]{1,0:T(8,128)(2,1)S(1)}, u32[]{:S(2)}, u32[]{:S(2)}) collective-permute-start(bf16[64,4224]{1,0:T(8,128)(2,1)S(1)} %pad_maximum_fusion.1.refs_2_), channel_id=1, source_target_pairs={{2,4},{3,5},{4,2},{5,3},{0,1},{1,0},{6,7},{7,6},{10,12},{11,13},{1... | collective-permute-start | bytes 1622024 | tf_op jit(solution)/shard_map/ppermute | solution.py:40
  2.9 16.8 %collective-permute-start = (bf16[64,4224]{1,0:T(8,128)(2,1)S(1)}, bf16[64,4224]{1,0:T(8,128)(2,1)S(1)}, u32[]{:S(2)}, u32[]{:S(2)}) collective-permute-start(bf16[64,4224]{1,0:T(8,128)(2,1)S(1)} %pad_maximum_fusion.1.refs_2_), channel_id=1, source_target_pairs={{0,2},{1,3},{2,0},{3,1},{4,6},{5,7},{6,4},{7,5},{8,10},{9,11},{10,... | collective-permute-start | bytes 1622024 | tf_op jit(solution)/shard_map/ppermute | solution.py:35
  7.9 17.7 %copy-start.16 = (bf16[64,4224]{1,0:T(8,128)(2,1)}, bf16[64,4224]{1,0:T(8,128)(2,1)S(1)}, u32[]{:S(2)}) copy-start(bf16[64,4224]{1,0:T(8,128)(2,1)S(1)} %collective-permute-done.1.refs_4_) | copy-start | bytes 1622020
  19.7 15.6 %collective-permute-start.5 = (bf16[1,2048,768]{2,1,0:T(8,128)(2,1)}, bf16[1,2048,768]{2,1,0:T(8,128)(2,1)S(1)}, u32[]{:S(2)}, u32[]{:S(2)}) collective-permute-start(bf16[1,2048,768]{2,1,0:T(8,128)(2,1)} %refs_11_), channel_id=1, source_target_pairs={{0,1},{1,0},{2,3},{3,2},{4,5},{5,4},{6,7},{7,6},{8,9},{9,8},{10,11... | collective-permute-start | bytes 9437192 | tf_op jit(solution)/shard_map/ppermute | solution.py:297
  19.8 14.7 %collective-permute-start.3 = (bf16[64,4224]{1,0:T(8,128)(2,1)S(1)}, bf16[64,4224]{1,0:T(8,128)(2,1)S(1)}, u32[]{:S(2)}, u32[]{:S(2)}) collective-permute-start(bf16[64,4224]{1,0:T(8,128)(2,1)S(1)} %collective-permute-done.1.refs_4_), channel_id=1, source_target_pairs={{0,2},{1,3},{2,0},{3,1},{4,6},{5,7},{6,4},{7,5},{8,10},{9,11},{10,... | collective-permute-start | bytes 1622024 | tf_op jit(solution)/shard_map/ppermute | solution.py:35
  21.6 13.7 %collective-permute-start.4 = (bf16[64,4224]{1,0:T(8,128)(2,1)S(1)}, bf16[64,4224]{1,0:T(8,128)(2,1)}, u32[]{:S(2)}, u32[]{:S(2)}) collective-permute-start(bf16[64,4224]{1,0:T(8,128)(2,1)S(1)} %collective-permute-done.refs_3_), channel_id=1, source_target_pairs={{2,4},{3,5},{4,2},{5,3},{0,1},{1,0},{6,7},{7,6},{10,12},{11,13},{1... | collective-permute-start | bytes 1622024 | tf_op jit(solution)/shard_map/ppermute | solution.py:40
  37.0 15.0 %collective-permute-start.7 = (bf16[1,768,2048]{2,1,0:T(8,128)(2,1)}, bf16[1,768,2048]{2,1,0:T(8,128)(2,1)}, u32[]{:S(2)}, u32[]{:S(2)}) collective-permute-start(bf16[1,768,2048]{2,1,0:T(8,128)(2,1)} %refs_12_), channel_id=1, source_target_pairs={{0,1},{1,0},{2,3},{3,2},{4,5},{5,4},{6,7},{7,6},{8,9},{9,8},{10,11... | collective-permute-start | bytes 9437192 | tf_op jit(solution)/shard_map/ppermute | solution.py:303
  37.0 15.0 %collective-permute-start.6 = (bf16[64,4224]{1,0:T(8,128)(2,1)}, bf16[64,4224]{1,0:T(8,128)(2,1)}, u32[]{:S(2)}, u32[]{:S(2)}) collective-permute-start(bf16[64,4224]{1,0:T(8,128)(2,1)} %collective-permute-done.4.refs_6_), channel_id=1, source_target_pairs={{0,2},{1,3},{2,0},{3,1},{4,6},{5,7},{6,4},{7,5},{8,10},{9,11},{10,... | collective-permute-start | bytes 1622024 | tf_op jit(solution)/shard_map/ppermute | solution.py:35
  52.0 20.6 %collective-permute-start.9 = (bf16[64,4224]{1,0:T(8,128)(2,1)}, bf16[64,4224]{1,0:T(8,128)(2,1)S(1)}, u32[]{:S(2)}, u32[]{:S(2)}) collective-permute-start(bf16[64,4224]{1,0:T(8,128)(2,1)} %pad_maximum_fusion.2.refs_0_), channel_id=1, source_target_pairs={{2,4},{3,5},{4,2},{5,3},{0,1},{1,0},{6,7},{7,6},{10,12},{11,13},{1... | collective-permute-start | bytes 1622024 | tf_op jit(solution)/shard_map/ppermute | solution.py:40
  52.0 20.6 %collective-permute-start.8 = (bf16[64,4224]{1,0:T(8,128)(2,1)}, bf16[64,4224]{1,0:T(8,128)(2,1)S(1)}, u32[]{:S(2)}, u32[]{:S(2)}) collective-permute-start(bf16[64,4224]{1,0:T(8,128)(2,1)} %pad_maximum_fusion.2.refs_0_), channel_id=1, source_target_pairs={{0,2},{1,3},{2,0},{3,1},{4,6},{5,7},{6,4},{7,5},{8,10},{9,11},{10,... | collective-permute-start | bytes 1622024 | tf_op jit(solution)/shard_map/ppermute | solution.py:35
  72.6 36.4 %copy-start.6 = (f32[64,2048]{1,0:T(8,128)}, f32[64,2048]{1,0:T(8,128)S(1)}, u32[]{:S(2)}) copy-start(f32[64,2048]{1,0:T(8,128)S(1)} %get-tuple-element.129) | copy-start | bytes 1572868
  72.7 13.4 %collective-permute-start.10 = (bf16[64,4224]{1,0:T(8,128)(2,1)S(1)}, bf16[64,4224]{1,0:T(8,128)(2,1)S(1)}, u32[]{:S(2)}, u32[]{:S(2)}) collective-permute-start(bf16[64,4224]{1,0:T(8,128)(2,1)S(1)} %pad_maximum_fusion.3), channel_id=1, source_target_pairs={{0,2},{1,3},{2,0},{3,1},{4,6},{5,7},{6,4},{7,5},{8,10},{9,11},{10,... | collective-permute-start | bytes 1622024 | tf_op jit(solution)/shard_map/ppermute | solution.py:35
  72.8 13.3 %collective-permute-start.11 = (bf16[64,4224]{1,0:T(8,128)(2,1)S(1)}, bf16[64,4224]{1,0:T(8,128)(2,1)S(1)}, u32[]{:S(2)}, u32[]{:S(2)}) collective-permute-start(bf16[64,4224]{1,0:T(8,128)(2,1)S(1)} %collective-permute-done.8.refs_1_), channel_id=1, source_target_pairs={{2,4},{3,5},{4,2},{5,3},{0,1},{1,0},{6,7},{7,6},{10,12},{11,13},{1... | collective-permute-start | bytes 1622024 | tf_op jit(solution)/shard_map/ppermute | solution.py:40
  86.3 12.5 %collective-permute-start.12 = (bf16[64,4224]{1,0:T(8,128)(2,1)S(1)}, bf16[64,4224]{1,0:T(8,128)(2,1)S(1)}, u32[]{:S(2)}, u32[]{:S(2)}) collective-permute-start(bf16[64,4224]{1,0:T(8,128)(2,1)S(1)} %pad_maximum_fusion.4), channel_id=1, source_target_pairs={{0,2},{1,3},{2,0},{3,1},{4,6},{5,7},{6,4},{7,5},{8,10},{9,11},{10,... | collective-permute-start | bytes 1622024 | tf_op jit(solution)/shard_map/ppermute | solution.py:35
  88.1 1.6 collective-permute-start.13
  98.8 10.2 %collective-permute-start.15 = (bf16[64,2048]{1,0:T(8,128)(2,1)S(1)}, bf16[64,2048]{1,0:T(8,128)(2,1)S(1)}, u32[]{:S(2)}, u32[]{:S(2)}) collective-permute-start(bf16[64,2048]{1,0:T(8,128)(2,1)S(1)} %add_convert_fusion.9), channel_id=1, source_target_pairs={{2,4},{3,5},{4,2},{5,3},{0,1},{1,0},{6,7},{7,6},{10,12},{11,13},{1... | collective-permute-start | bytes 786440 | tf_op jit(solution)/shard_map/ppermute | solution.py:40
  99.0 10.0 %collective-permute-start.14 = (bf16[64,2048]{1,0:T(8,128)(2,1)S(1)}, bf16[64,2048]{1,0:T(8,128)(2,1)S(1)}, u32[]{:S(2)}, u32[]{:S(2)}) collective-permute-start(bf16[64,2048]{1,0:T(8,128)(2,1)S(1)} %fusion), channel_id=1, source_target_pairs={{0,2},{1,3},{2,0},{3,1},{4,6},{5,7},{6,4},{7,5},{8,10},{9,11},{10,... | collective-permute-start | bytes 786440 | tf_op jit(solution)/shard_map/ppermute | solution.py:35
  109.2 8.3 %collective-permute-start.17 = (bf16[64,2048]{1,0:T(8,128)(2,1)S(1)}, bf16[64,2048]{1,0:T(8,128)(2,1)S(1)}, u32[]{:S(2)}, u32[]{:S(2)}) collective-permute-start(bf16[64,2048]{1,0:T(8,128)(2,1)S(1)} %fusion.4.refs_0_), channel_id=1, source_target_pairs={{2,4},{3,5},{4,2},{5,3},{0,1},{1,0},{6,7},{7,6},{10,12},{11,13},{1... | collective-permute-start | bytes 786440 | tf_op jit(solution)/shard_map/ppermute | solution.py:40
  109.8 8.2 %collective-permute-start.16 = (bf16[64,2048]{1,0:T(8,128)(2,1)S(1)}, bf16[64,2048]{1,0:T(8,128)(2,1)S(1)}, u32[]{:S(2)}, u32[]{:S(2)}) collective-permute-start(bf16[64,2048]{1,0:T(8,128)(2,1)S(1)} %fusion.4.refs_0_), channel_id=1, source_target_pairs={{0,2},{1,3},{2,0},{3,1},{4,6},{5,7},{6,4},{7,5},{8,10},{9,11},{10,... | collective-permute-start | bytes 786440 | tf_op jit(solution)/shard_map/ppermute | solution.py:35
  117.5 24.5 %copy-start.8 = (f32[64,2048]{1,0:T(8,128)}, f32[64,2048]{1,0:T(8,128)S(1)}, u32[]{:S(2)}) copy-start(f32[64,2048]{1,0:T(8,128)S(1)} %get-tuple-element.151) | copy-start | bytes 1572868
  118.0 7.7 %collective-permute-start.18 = (bf16[64,2048]{1,0:T(8,128)(2,1)S(1)}, bf16[64,2048]{1,0:T(8,128)(2,1)S(1)}, u32[]{:S(2)}, u32[]{:S(2)}) collective-permute-start(bf16[64,2048]{1,0:T(8,128)(2,1)S(1)} %broadcast_select_fusion.3), channel_id=1, source_target_pairs={{0,2},{1,3},{2,0},{3,1},{4,6},{5,7},{6,4},{7,5},{8,10},{9,11},{10,... | collective-permute-start | bytes 786440 | tf_op jit(solution)/shard_map/ppermute | solution.py:35
  119.6 6.2 %collective-permute-start.19 = (bf16[64,2048]{1,0:T(8,128)(2,1)S(1)}, bf16[64,2048]{1,0:T(8,128)(2,1)S(1)}, u32[]{:S(2)}, u32[]{:S(2)}) collective-permute-start(bf16[64,2048]{1,0:T(8,128)(2,1)S(1)} %collective-permute-done.16.refs_1_), channel_id=1, source_target_pairs={{2,4},{3,5},{4,2},{5,3},{0,1},{1,0},{6,7},{7,6},{10,12},{11,13},{1... | collective-permute-start | bytes 786440 | tf_op jit(solution)/shard_map/ppermute | solution.py:40
  125.9 7.1 %collective-permute-start.20 = (bf16[64,2048]{1,0:T(8,128)(2,1)S(1)}, bf16[64,2048]{1,0:T(8,128)(2,1)S(1)}, u32[]{:S(2)}, u32[]{:S(2)}) collective-permute-start(bf16[64,2048]{1,0:T(8,128)(2,1)S(1)} %broadcast_select_fusion.2), channel_id=1, source_target_pairs={{0,2},{1,3},{2,0},{3,1},{4,6},{5,7},{6,4},{7,5},{8,10},{9,11},{10,... | collective-permute-start | bytes 786440 | tf_op jit(solution)/shard_map/ppermute | solution.py:35
  127.8 5.2 %collective-permute-start.21 = (bf16[64,2048]{1,0:T(8,128)(2,1)S(1)}, bf16[64,2048]{1,0:T(8,128)(2,1)S(1)}, u32[]{:S(2)}, u32[]{:S(2)}) collective-permute-start(bf16[64,2048]{1,0:T(8,128)(2,1)S(1)} %add_convert_fusion.8), channel_id=1, source_target_pairs={{2,4},{3,5},{4,2},{5,3},{0,1},{1,0},{6,7},{7,6},{10,12},{11,13},{1... | collective-permute-start | bytes 786440 | tf_op jit(solution)/shard_map/ppermute | solution.py:40
  133.1 8.0 %collective-permute-start.23 = (bf16[64,2048]{1,0:T(8,128)(2,1)S(1)}, bf16[64,2048]{1,0:T(8,128)(2,1)S(1)}, u32[]{:S(2)}, u32[]{:S(2)}) collective-permute-start(bf16[64,2048]{1,0:T(8,128)(2,1)S(1)} %add_convert_fusion.6), channel_id=1, source_target_pairs={{2,4},{3,5},{4,2},{5,3},{0,1},{1,0},{6,7},{7,6},{10,12},{11,13},{1... | collective-permute-start | bytes 786440 | tf_op jit(solution)/shard_map/ppermute | solution.py:40
  133.2 8.8 %collective-permute-start.22 = (bf16[64,2048]{1,0:T(8,128)(2,1)S(1)}, bf16[64,2048]{1,0:T(8,128)(2,1)S(1)}, u32[]{:S(2)}, u32[]{:S(2)}) collective-permute-start(bf16[64,2048]{1,0:T(8,128)(2,1)S(1)} %fusion.1), channel_id=1, source_target_pairs={{0,2},{1,3},{2,0},{3,1},{4,6},{5,7},{6,4},{7,5},{8,10},{9,11},{10,... | collective-permute-start | bytes 786440 | tf_op jit(solution)/shard_map/ppermute | solution.py:35
  142.7 8.1 %collective-permute-start.25 = (bf16[64,2048]{1,0:T(8,128)(2,1)S(1)}, bf16[64,2048]{1,0:T(8,128)(2,1)S(1)}, u32[]{:S(2)}, u32[]{:S(2)}) collective-permute-start(bf16[64,2048]{1,0:T(8,128)(2,1)S(1)} %fusion.5.refs_0_), channel_id=1, source_target_pairs={{2,4},{3,5},{4,2},{5,3},{0,1},{1,0},{6,7},{7,6},{10,12},{11,13},{1... | collective-permute-start | bytes 786440 | tf_op jit(solution)/shard_map/ppermute | solution.py:40
  142.7 8.7 %collective-permute-start.24 = (bf16[64,2048]{1,0:T(8,128)(2,1)S(1)}, bf16[64,2048]{1,0:T(8,128)(2,1)S(1)}, u32[]{:S(2)}, u32[]{:S(2)}) collective-permute-start(bf16[64,2048]{1,0:T(8,128)(2,1)S(1)} %fusion.5.refs_0_), channel_id=1, source_target_pairs={{0,2},{1,3},{2,0},{3,1},{4,6},{5,7},{6,4},{7,5},{8,10},{9,11},{10,... | collective-permute-start | bytes 786440 | tf_op jit(solution)/shard_map/ppermute | solution.py:35
  151.5 8.0 %collective-permute-start.26 = (bf16[64,2048]{1,0:T(8,128)(2,1)S(1)}, bf16[64,2048]{1,0:T(8,128)(2,1)S(1)}, u32[]{:S(2)}, u32[]{:S(2)}) collective-permute-start(bf16[64,2048]{1,0:T(8,128)(2,1)S(1)} %broadcast_select_fusion.1), channel_id=1, source_target_pairs={{0,2},{1,3},{2,0},{3,1},{4,6},{5,7},{6,4},{7,5},{8,10},{9,11},{10,... | collective-permute-start | bytes 786440 | tf_op jit(solution)/shard_map/ppermute | solution.py:35
  151.8 7.7 %collective-permute-start.27 = (bf16[64,2048]{1,0:T(8,128)(2,1)S(1)}, bf16[64,2048]{1,0:T(8,128)(2,1)S(1)}, u32[]{:S(2)}, u32[]{:S(2)}) collective-permute-start(bf16[64,2048]{1,0:T(8,128)(2,1)S(1)} %collective-permute-done.24.refs_1_), channel_id=1, source_target_pairs={{2,4},{3,5},{4,2},{5,3},{0,1},{1,0},{6,7},{7,6},{10,12},{11,13},{1... | collective-permute-start | bytes 786440 | tf_op jit(solution)/shard_map/ppermute | solution.py:40
  159.6 7.1 %collective-permute-start.28 = (bf16[64,2048]{1,0:T(8,128)(2,1)S(1)}, bf16[64,2048]{1,0:T(8,128)(2,1)S(1)}, u32[]{:S(2)}, u32[]{:S(2)}) collective-permute-start(bf16[64,2048]{1,0:T(8,128)(2,1)S(1)} %broadcast_select_fusion), channel_id=1, source_target_pairs={{0,2},{1,3},{2,0},{3,1},{4,6},{5,7},{6,4},{7,5},{8,10},{9,11},{10,... | collective-permute-start | bytes 786440 | tf_op jit(solution)/shard_map/ppermute | solution.py:35
  161.4 5.3 %collective-permute-start.29 = (bf16[64,2048]{1,0:T(8,128)(2,1)S(1)}, bf16[64,2048]{1,0:T(8,128)(2,1)S(1)}, u32[]{:S(2)}, u32[]{:S(2)}) collective-permute-start(bf16[64,2048]{1,0:T(8,128)(2,1)S(1)} %add_convert_fusion.5), channel_id=1, source_target_pairs={{2,4},{3,5},{4,2},{5,3},{0,1},{1,0},{6,7},{7,6},{10,12},{11,13},{1... | collective-permute-start | bytes 786440 | tf_op jit(solution)/shard_map/ppermute | solution.py:40
  166.8 13.0 %collective-permute-start.31 = (bf16[64,2048]{1,0:T(8,128)(2,1)S(1)}, bf16[64,2048]{1,0:T(8,128)(2,1)S(1)}, u32[]{:S(2)}, u32[]{:S(2)}) collective-permute-start(bf16[64,2048]{1,0:T(8,128)(2,1)S(1)} %add_convert_fusion.3), channel_id=1, source_target_pairs={{2,4},{3,5},{4,2},{5,3},{0,1},{1,0},{6,7},{7,6},{10,12},{11,13},{1... | collective-permute-start | bytes 786440 | tf_op jit(solution)/shard_map/ppermute | solution.py:40
  167.0 12.9 %collective-permute-start.30 = (bf16[64,2048]{1,0:T(8,128)(2,1)S(1)}, bf16[64,2048]{1,0:T(8,128)(2,1)S(1)}, u32[]{:S(2)}, u32[]{:S(2)}) collective-permute-start(bf16[64,2048]{1,0:T(8,128)(2,1)S(1)} %fusion.2), channel_id=1, source_target_pairs={{0,2},{1,3},{2,0},{3,1},{4,6},{5,7},{6,4},{7,5},{8,10},{9,11},{10,... | collective-permute-start | bytes 786440 | tf_op jit(solution)/shard_map/ppermute | solution.py:35
  179.8 7.3 %collective-permute-start.32 = (bf16[64,2048]{1,0:T(8,128)(2,1)S(1)}, bf16[64,2048]{1,0:T(8,128)(2,1)S(1)}, u32[]{:S(2)}, u32[]{:S(2)}) collective-permute-start(bf16[64,2048]{1,0:T(8,128)(2,1)S(1)} %get-tuple-element.195), channel_id=1, source_target_pairs={{0,2},{1,3},{2,0},{3,1},{4,6},{5,7},{6,4},{7,5},{8,10},{9,11},{10,... | collective-permute-start | bytes 786440 | tf_op jit(solution)/shard_map/ppermute | solution.py:35
  179.9 1.2 collective-permute-start.33
  181.2 3.6 %collective-permute-start.34 = (f32[8,128]{1,0:T(8,128)S(1)}, f32[8,128]{1,0:T(8,128)S(1)}, u32[]{:S(2)}, u32[]{:S(2)}) collective-permute-start(f32[8,128]{1,0:T(8,128)S(1)} %add.109), channel_id=1, source_target_pairs={{0,8},{8,0},{16,24},{24,16},{1,9},{9,1},{17,25},{25,17},{2,10},{10... | collective-permute-start | bytes 12296 | tf_op jit(solution)/shard_map/ppermute | solution.py:197
  182.7 9.2 %collective-permute-start.36 = (bf16[64,2048]{1,0:T(8,128)(2,1)S(1)}, bf16[64,2048]{1,0:T(8,128)(2,1)S(1)}, u32[]{:S(2)}, u32[]{:S(2)}) collective-permute-start(bf16[64,2048]{1,0:T(8,128)(2,1)S(1)} %get-tuple-element.201), channel_id=1, source_target_pairs={{0,2},{1,3},{2,0},{3,1},{4,6},{5,7},{6,4},{7,5},{8,10},{9,11},{10,... | collective-permute-start | bytes 786440 | tf_op jit(solution)/shard_map/ppermute | solution.py:35
  184.8 16.8 %copy-start.9 = (f32[64,2048]{1,0:T(8,128)S(1)}, f32[64,2048]{1,0:T(8,128)}, u32[]{:S(2)}) copy-start(f32[64,2048]{1,0:T(8,128)} %copy-done.8) | copy-start | bytes 1572868
  184.8 16.8 %copy-start.14 = (f32[64,2048]{1,0:T(8,128)S(1)}, f32[64,2048]{1,0:T(8,128)}, u32[]{:S(2)}) copy-start(f32[64,2048]{1,0:T(8,128)} %copy-done.13) | copy-start | bytes 1572868
  184.8 16.8 %copy-start.23 = (bf16[128,2048]{1,0:T(8,128)(2,1)S(1)}, bf16[128,2048]{1,0:T(8,128)(2,1)}, u32[]{:S(2)}) copy-start(bf16[128,2048]{1,0:T(8,128)(2,1)} %param.8) | copy-start | bytes 1572868
  187.2 4.7 %collective-permute-start.37 = (bf16[64,2048]{1,0:T(8,128)(2,1)S(1)}, bf16[64,2048]{1,0:T(8,128)(2,1)S(1)}, u32[]{:S(2)}, u32[]{:S(2)}) collective-permute-start(bf16[64,2048]{1,0:T(8,128)(2,1)S(1)} %add_convert_fusion.2), channel_id=1, source_target_pairs={{2,4},{3,5},{4,2},{5,3},{0,1},{1,0},{6,7},{7,6},{10,12},{11,13},{1... | collective-permute-start | bytes 786440 | tf_op jit(solution)/shard_map/ppermute | solution.py:40
  192.0 8.9 %collective-permute-start.39 = (bf16[64,2048]{1,0:T(8,128)(2,1)S(1)}, bf16[64,2048]{1,0:T(8,128)(2,1)S(1)}, u32[]{:S(2)}, u32[]{:S(2)}) collective-permute-start(bf16[64,2048]{1,0:T(8,128)(2,1)S(1)} %add_convert_fusion), channel_id=1, source_target_pairs={{2,4},{3,5},{4,2},{5,3},{0,1},{1,0},{6,7},{7,6},{10,12},{11,13},{1... | collective-permute-start | bytes 786440 | tf_op jit(solution)/shard_map/ppermute | solution.py:40
  192.2 9.4 %collective-permute-start.38 = (bf16[64,2048]{1,0:T(8,128)(2,1)S(1)}, bf16[64,2048]{1,0:T(8,128)(2,1)}, u32[]{:S(2)}, u32[]{:S(2)}) collective-permute-start(bf16[64,2048]{1,0:T(8,128)(2,1)S(1)} %fusion.3), channel_id=1, source_target_pairs={{0,2},{1,3},{2,0},{3,1},{4,6},{5,7},{6,4},{7,5},{8,10},{9,11},{10,... | collective-permute-start | bytes 786440 | tf_op jit(solution)/shard_map/ppermute | solution.py:35
  195.9 3.6 %collective-permute-start.35 = (f32[8,128]{1,0:T(8,128)S(1)}, f32[8,128]{1,0:T(8,128)S(1)}, u32[]{:S(2)}, u32[]{:S(2)}) collective-permute-start(f32[8,128]{1,0:T(8,128)S(1)} %add.110), channel_id=1, source_target_pairs={{0,16},{8,24},{16,0},{24,8},{1,17},{9,25},{17,1},{25,9},{2,18},{10... | collective-permute-start | bytes 12296 | tf_op jit(solution)/shard_map/ppermute | solution.py:197
  (22 other events, 136.0 us)

commit v6 on v5

--- a/solution.py
+++ b/solution.py
@@ -176,6 +176,22 @@
     )(where, *unused, *parts, *[in_vmem(value) for value in operands])
 
 
+def output_kernel(elements, where_ref, squares, whole_a, jv_b, own, side, inner_last, out):
+    scale = lax.rsqrt(jnp.sum(squares[pl.ds(0, 1), :], axis=1, keepdims=True) / elements + 1e-06)
+    half = whole_a.shape[0]
+    out[pl.ds(0, half), :] = whole_a[...] * scale
+    total = jv_b[...] + own[...] + side[...].astype(jnp.float32)
+    inner = where_ref[0] == 1
+
+    @pl.when(inner)
+    def _():
+        out[pl.ds(half, half), :] = (total + inner_last[...].astype(jnp.float32)) * scale
+
+    @pl.when(jnp.logical_not(inner))
+    def _():
+        out[pl.ds(half, half), :] = total * scale
+
+
 def touch_kernel(*refs):
     refs[-1][...] = refs[0][0, pl.ds(0, 16), pl.ds(0, LANES)]
 
@@ -300,7 +316,10 @@
         load_b,
     )
     a_far_end, sib_down, sib_piece, load_b = slot(
-        side_hop(a_far), lax.ppermute(w_down, "expert", swap), touch((sib_gate, sib_up)), load_b
+        side_hop(a_far),
+        lax.ppermute(w_down, "expert", swap),
+        touch((sib_gate, sib_up, load_a, a_side, a_near, a_near_end, a_far)),
+        load_b,
     )
     weights = ((w_gate, w_up, w_down), (sib_gate, sib_up, sib_down))
 
@@ -368,11 +387,15 @@
         squares = exchange_sum(squares, "dp", step)
         step *= 2
     came, last = side_hop(pick(gb[1], add_rows(gb[1], s_side))), inner_hop(s_near)
-    grad_b = home(gb, came, last)
-
-    elements = token_count * width * lax.axis_size("dp") * owners
-    scale = lax.rsqrt(jnp.sum(squares[0]) / elements + 1e-06)
-    return jnp.concatenate([whole_a * scale, (jv_b + grad_b) * scale])
+    vmem = pl.BlockSpec(memory_space=pltpu.VMEM)
+    return pl.pallas_call(
+        functools.partial(output_kernel, token_count * width * lines * owners),
+        in_specs=[pl.BlockSpec(memory_space=pltpu.SMEM)] + [vmem] * 6,
+        out_specs=vmem,
+        out_shape=jax.ShapeDtypeStruct((token_count, width), jnp.float32),
+        compiler_params=pltpu.CompilerParams(vmem_limit_bytes=8 * 2**20),
+        name="output",
+    )(where, *[in_vmem(value) for value in (squares, whole_a, jv_b, gb[0], came, last)])
 
 
 def owner_states(x_rows, gate_w, up_w):

time: 205 us -> 199 us (0.971)
  other arithmetic: 6.91 us -> 3.4 us
  waiting for transfers between devices: 90.6 us -> 88.2 us
    mul x1 -> x0, other arithmetic: 2.11 us -> none  [line_shards(): return jnp.concatenate([whole_a * scale, (jv_b + grad_b) * scale])]
    ppermute x3, waiting for transfers between devices: 3.42 us -> 1.34 us  [exchange_sum(): return value + lax.ppermute(value, axis, pairs)]
    unnamed x60 -> x34, local copies, waits for them, and re-layouts: 12.4 us -> 10.5 us
  transfers between devices with their start and end apart: 40 -> 40, of which waited for: 18 -> 18; matrix products, arithmetic and copies ran while one was open for 2% -> 2% of each run, Pallas kernels for 27% -> 28%
where the time goes in v6:
time: 199 us; the launch traced here: 198 us
  waiting for transfers between devices  88.2 us (44%)
  Pallas kernels  56.3 us (28%)
  starting transfers between devices  37.5 us (19%)
  local copies, waits for them, and re-layouts  12.1 us (6%)
  other arithmetic  3.4 us (2%)
    ppermute x18, waiting for transfers between devices, side_hop(): return lax.ppermute(rows, 'expert', both_cores(SIDE_PAIRS))  85.3 us
    pallas_call x6, Pallas kernels, kernel_call(): pl.pallas_call(called, in_specs=[pl.BlockSpec(memory_space=pltpu.SMEM)] +...  50.6 us
    ppermute x18, starting transfers between devices, side_hop(): return lax.ppermute(rows, 'expert', both_cores(SIDE_PAIRS))  33 us
    unnamed x34, local copies, waits for them, and re-layouts  10.5 us
    pallas_call x2, Pallas kernels, touch(): pl.pallas_call(touch_kernel, in_specs=[vmem] * len(weights), out_specs=vm...  4.04 us
  transfers between devices with their start and end apart: 40, of which 18 were waited for; matrix products, arithmetic and copies ran while one was open for 2% of the time, Pallas kernels for 28%

profile of v6, /device:TPU:0, one launch (start us, length us, event | category | flops | bytes accessed | tf_op | source)
XLA Modules:
  0.0 198.0 jit_solution(2521107062481256443)
XLA Ops:
  1.3 1.4 fusion.8
  2.9 4.1 %collective-permute-start = (bf16[64,4224]{1,0:T(8,128)(2,1)S(1)}, bf16[64,4224]{1,0:T(8,128)(2,1)S(1)}, u32[]{:S(2)}, u32[]{:S(2)}) collective-permute-start(bf16[64,4224]{1,0:T(8,128)(2,1)S(1)} %pad_maximum_fusion.refs_2_), channel_id=1, source_target_pairs={{0,2},{1,3},{2,0},{3,1},{4,6},{5,7},{6,4},{7,5},{8,10},{9,11},{10,... | collective-permute-start | bytes 1622024 | tf_op jit(solution)/shard_map/ppermute | solution.py:35
  7.9 11.8 %collective-permute-done.refs_3_ = bf16[64,4224]{1,0:T(8,128)(2,1)S(1)} collective-permute-done((bf16[64,4224]{1,0:T(8,128)(2,1)S(1)}, bf16[64,4224]{1,0:T(8,128)(2,1)S(1)}, u32[]{:S(2)}, u32[]{:S(2)}) %collective-permute-start) | collective-permute-done | bytes 540704 | tf_op jit(solution)/shard_map/ppermute | solution.py:35
  19.7 1.8 collective-permute-start.3
  21.7 1.9 copy-done.1
  23.6 1.9 touch.2.refs_0_
  25.5 8.9 %collective-permute-done.3.refs_5_ = bf16[64,4224]{1,0:T(8,128)(2,1)S(1)} collective-permute-done((bf16[64,4224]{1,0:T(8,128)(2,1)S(1)}, bf16[64,4224]{1,0:T(8,128)(2,1)S(1)}, u32[]{:S(2)}, u32[]{:S(2)}) %collective-permute-start.3) | collective-permute-done | bytes 540704 | tf_op jit(solution)/shard_map/ppermute | solution.py:35
  35.2 1.7 copy-done.3
  36.9 1.7 collective-permute-start.6
  38.7 1.9 copy-done.4
  40.6 1.0 copy-done.7
  41.7 1.0 copy-done.9
  42.7 1.0 copy-done.11
  43.8 1.0 copy-done.13
  44.8 2.1 %touch.3.refs_1_ = bf16[16,128]{1,0:T(8,128)(2,1)S(1)} custom-call(bf16[1,2048,768]{2,1,0:T(8,128)(2,1)} %collective-permute-done.2.refs_0_.refs_11_.refs_7_.refs_9_.refs_13_, bf16[1,2048,768]{2,1,0:T(8,128)(2,1)S(1)} %copy-done.4, bf16[64,4224]{1,0:T(8,128)(2,1)S(1)} %copy-done.7, bf16[64,4224]{1,0:T(8,128)(2,1)S(1)} %copy-done.11, ...), custom_call_target="tpu_custom_call" | custom-call | tf_op jit(solution)/shard_map/touch/pallas_call | solution.py:201
  47.0 4.9 %collective-permute-done.6.refs_7_ = bf16[64,4224]{1,0:T(8,128)(2,1)} collective-permute-done((bf16[64,4224]{1,0:T(8,128)(2,1)}, bf16[64,4224]{1,0:T(8,128)(2,1)}, u32[]{:S(2)}, u32[]{:S(2)}) %collective-permute-start.6) | collective-permute-done | bytes 540704 | tf_op jit(solution)/shard_map/ppermute | solution.py:35
  51.9 2.7 %collective-permute-start.8 = (bf16[64,4224]{1,0:T(8,128)(2,1)S(1)}, bf16[64,4224]{1,0:T(8,128)(2,1)S(1)}, u32[]{:S(2)}, u32[]{:S(2)}) collective-permute-start(bf16[64,4224]{1,0:T(8,128)(2,1)S(1)} %copy-done.15), channel_id=1, source_target_pairs={{0,2},{1,3},{2,0},{3,1},{4,6},{5,7},{6,4},{7,5},{8,10},{9,11},{10,... | collective-permute-start | bytes 1622024 | tf_op jit(solution)/shard_map/ppermute | solution.py:35
  54.6 13.7 %forward.3 = (f32[64,2048]{1,0:T(8,128)S(1)}, bf16[64,2048]{1,0:T(8,128)(2,1)S(1)}, bf16[64,2048]{1,0:T(8,128)(2,1)S(1)}, bf16[64,2048]{1,0:T(8,128)(2,1)S(1)}, ...) custom-call(s32[3]{0:T(128)S(1)} %pad_add_fusion.where_ref, ...), custom_call_target="tpu_custom_call" | custom-call | flops 8053063680 | tf_op jit(solution)/shard_map/forward/pallas_call | solution.py:161
  68.6 13.2 %collective-permute-done.10.refs_3_ = bf16[64,4224]{1,0:T(8,128)(2,1)S(1)} collective-permute-done((bf16[64,4224]{1,0:T(8,128)(2,1)S(1)}, bf16[64,4224]{1,0:T(8,128)(2,1)S(1)}, u32[]{:S(2)}, u32[]{:S(2)}) %collective-permute-start.10) | collective-permute-done | bytes 540704 | tf_op jit(solution)/shard_map/ppermute | solution.py:35
  82.0 1.8 collective-permute-start.12
  84.0 1.5 collective-permute-done.13
  85.5 9.0 %collective-permute-done.12.refs_5_ = bf16[64,4224]{1,0:T(8,128)(2,1)S(1)} collective-permute-done((bf16[64,4224]{1,0:T(8,128)(2,1)S(1)}, bf16[64,4224]{1,0:T(8,128)(2,1)S(1)}, u32[]{:S(2)}, u32[]{:S(2)}) %collective-permute-start.12) | collective-permute-done | bytes 540704 | tf_op jit(solution)/shard_map/ppermute | solution.py:35
  94.7 3.1 %collective-permute-start.14 = (bf16[64,2048]{1,0:T(8,128)(2,1)S(1)}, bf16[64,2048]{1,0:T(8,128)(2,1)S(1)}, u32[]{:S(2)}, u32[]{:S(2)}) collective-permute-start(bf16[64,2048]{1,0:T(8,128)(2,1)S(1)} %fusion), channel_id=1, source_target_pairs={{0,2},{1,3},{2,0},{3,1},{4,6},{5,7},{6,4},{7,5},{8,10},{9,11},{10,... | collective-permute-start | bytes 786440 | tf_op jit(solution)/shard_map/ppermute | solution.py:35
  97.8 6.8 %forward.4 = (f32[256,2048]{1,0:T(8,128)S(1)}, f32[256,768]{1,0:T(8,128)S(1)}, f32[256,768]{1,0:T(8,128)S(1)}) custom-call(s32[3]{0:T(128)S(1)} %pad_add_fusion.where_ref, bf16[64,4224]{1,0:T(8,128)(2,1)S(1)} %copy-done.15, bf16[64,4224]{1,0:T(8,128)(2,1)S(1)} %collective-permute-done.8.refs_1_, bf16[64,4224]{1,0:T(8,128)(2,1)S(1)} %collective-permute-done.9.refs_2_, ...), custom_call_target="tpu_custom_call" | custom-call | flops 4026531840 | tf_op jit(solution)/shard_map/forward/pallas_call | solution.py:161
  105.4 7.6 %forward.5 = (f32[64,2048]{1,0:T(8,128)S(1)}, bf16[64,2048]{1,0:T(8,128)(2,1)S(1)}, bf16[64,2048]{1,0:T(8,128)(2,1)S(1)}, bf16[64,2048]{1,0:T(8,128)(2,1)S(1)}, ...) custom-call(s32[3]{0:T(128)S(1)} %pad_add_fusion.where_ref, bf16[64,4224]{1,0:T(8,128)(2,1)S(1)} %copy-done.15, ...), custom_call_target="tpu_custom_call" | custom-call | flops 4026531840 | tf_op jit(solution)/shard_map/forward/pallas_call | solution.py:161
  113.7 1.1 collective-permute-start.18
  114.8 6.8 %collective-permute-done.18.refs_3_ = bf16[64,2048]{1,0:T(8,128)(2,1)S(1)} collective-permute-done((bf16[64,2048]{1,0:T(8,128)(2,1)S(1)}, bf16[64,2048]{1,0:T(8,128)(2,1)S(1)}, u32[]{:S(2)}, u32[]{:S(2)}) %collective-permute-start.18) | collective-permute-done | bytes 262176 | tf_op jit(solution)/shard_map/ppermute | solution.py:35
  121.8 1.8 collective-permute-start.20
  123.6 5.6 %collective-permute-done.20.refs_5_ = bf16[64,2048]{1,0:T(8,128)(2,1)S(1)} collective-permute-done((bf16[64,2048]{1,0:T(8,128)(2,1)S(1)}, bf16[64,2048]{1,0:T(8,128)(2,1)S(1)}, u32[]{:S(2)}, u32[]{:S(2)}) %collective-permute-start.20) | collective-permute-done | bytes 262176 | tf_op jit(solution)/shard_map/ppermute | solution.py:35
  129.4 2.3 %collective-permute-start.22 = (bf16[64,2048]{1,0:T(8,128)(2,1)S(1)}, bf16[64,2048]{1,0:T(8,128)(2,1)S(1)}, u32[]{:S(2)}, u32[]{:S(2)}) collective-permute-start(bf16[64,2048]{1,0:T(8,128)(2,1)S(1)} %fusion.1), channel_id=1, source_target_pairs={{0,2},{1,3},{2,0},{3,1},{4,6},{5,7},{6,4},{7,5},{8,10},{9,11},{10,... | collective-permute-start | bytes 786440 | tf_op jit(solution)/shard_map/ppermute | solution.py:35
  131.7 5.6 %backward.3 = (f32[256,2048]{1,0:T(8,128)S(1)}, f32[8,128]{1,0:T(8,128)S(1)}) custom-call(s32[3]{0:T(128)S(1)} %pad_add_fusion.where_ref, bf16[64,2048]{1,0:T(8,128)(2,1)S(1)} %fusion.4.refs_0_, bf16[64,2048]{1,0:T(8,128)(2,1)S(1)} %collective-permute-done.16.refs_1_, bf16[64,2048]{1,0:T(8,128)(2,1)S(1)} %collective-permute-done.17.refs_2_, ...), custom_call_target="tpu_custom_call" | custom-call | flops 2415919104 | tf_op jit(solution)/shard_map/backward/pallas_call | solution.py:161
  137.3 0.9 collective-permute-done.22
  138.4 1.5 collective-permute-start.24
  139.9 6.6 %backward.4 = (f32[64,2048]{1,0:T(8,128)S(1)}, bf16[64,2048]{1,0:T(8,128)(2,1)S(1)}, bf16[64,2048]{1,0:T(8,128)(2,1)S(1)}, bf16[64,2048]{1,0:T(8,128)(2,1)S(1)}) custom-call(s32[3]{0:T(128)S(1)} %pad_add_fusion.where_ref, bf16[64,2048]{1,0:T(8,128)(2,1)S(1)} %fusion.4.refs_0_, bf16[64,2048]{1,0:T(8,128)(2,1)S(1)} %collective-permute-done.16.refs_1_, ...), custom_call_target="tpu_custom_call" | custom-call | flops 2415919104 | tf_op jit(solution)/shard_map/backward/pallas_call | solution.py:161
  147.5 7.6 %collective-permute-done.26.refs_3_ = bf16[64,2048]{1,0:T(8,128)(2,1)S(1)} collective-permute-done((bf16[64,2048]{1,0:T(8,128)(2,1)S(1)}, bf16[64,2048]{1,0:T(8,128)(2,1)S(1)}, u32[]{:S(2)}, u32[]{:S(2)}) %collective-permute-start.26) | collective-permute-done | bytes 262176 | tf_op jit(solution)/shard_map/ppermute | solution.py:35
  155.2 1.8 collective-permute-start.28
  157.0 5.2 %collective-permute-done.28.refs_5_ = bf16[64,2048]{1,0:T(8,128)(2,1)S(1)} collective-permute-done((bf16[64,2048]{1,0:T(8,128)(2,1)S(1)}, bf16[64,2048]{1,0:T(8,128)(2,1)S(1)}, u32[]{:S(2)}, u32[]{:S(2)}) %collective-permute-start.28) | collective-permute-done | bytes 262176 | tf_op jit(solution)/shard_map/ppermute | solution.py:35
  162.5 2.5 %collective-permute-start.30 = (bf16[64,2048]{1,0:T(8,128)(2,1)S(1)}, bf16[64,2048]{1,0:T(8,128)(2,1)S(1)}, u32[]{:S(2)}, u32[]{:S(2)}) collective-permute-start(bf16[64,2048]{1,0:T(8,128)(2,1)S(1)} %fusion.2), channel_id=1, source_target_pairs={{0,2},{1,3},{2,0},{3,1},{4,6},{5,7},{6,4},{7,5},{8,10},{9,11},{10,... | collective-permute-start | bytes 786440 | tf_op jit(solution)/shard_map/ppermute | solution.py:35
  165.0 10.2 %backward.5 = (f32[64,2048]{1,0:T(8,128)S(1)}, bf16[64,2048]{1,0:T(8,128)(2,1)S(1)}, bf16[64,2048]{1,0:T(8,128)(2,1)S(1)}, bf16[64,2048]{1,0:T(8,128)(2,1)S(1)}, f32[8,128]{1,0:T(8,128)S(1)}) custom-call(s32[3]{0:T(128)S(1)} %pad_add_fusion.where_ref, bf16[64,2048]{1,0:T(8,128)(2,1)S(1)} %get-tuple-element.205.refs_0_, ...), custom_call_target="tpu_custom_call" | custom-call | flops 4831838208 | tf_op jit(solution)/shard_map/backward/pallas_call | solution.py:161
  175.4 1.2 collective-permute-done.33
  176.6 1.5 collective-permute-start.34
  178.1 1.9 collective-permute-start.36
  180.2 2.4 %collective-permute-done.32 = bf16[64,2048]{1,0:T(8,128)(2,1)S(1)} collective-permute-done((bf16[64,2048]{1,0:T(8,128)(2,1)S(1)}, bf16[64,2048]{1,0:T(8,128)(2,1)S(1)}, u32[]{:S(2)}, u32[]{:S(2)}) %collective-permute-start.32) | collective-permute-done | bytes 262176 | tf_op jit(solution)/shard_map/ppermute | solution.py:35
  182.7 1.6 collective-permute-start.35
  184.3 3.0 %collective-permute-done.36 = bf16[64,2048]{1,0:T(8,128)(2,1)S(1)} collective-permute-done((bf16[64,2048]{1,0:T(8,128)(2,1)S(1)}, bf16[64,2048]{1,0:T(8,128)(2,1)S(1)}, u32[]{:S(2)}, u32[]{:S(2)}) %collective-permute-start.36) | collective-permute-done | bytes 262176 | tf_op jit(solution)/shard_map/ppermute | solution.py:35
  187.6 3.8 %collective-permute-start.38 = (bf16[64,2048]{1,0:T(8,128)(2,1)S(1)}, bf16[64,2048]{1,0:T(8,128)(2,1)S(1)}, u32[]{:S(2)}, u32[]{:S(2)}) collective-permute-start(bf16[64,2048]{1,0:T(8,128)(2,1)S(1)} %fusion.3), channel_id=1, source_target_pairs={{0,2},{1,3},{2,0},{3,1},{4,6},{5,7},{6,4},{7,5},{8,10},{9,11},{10,... | collective-permute-start | bytes 786440 | tf_op jit(solution)/shard_map/ppermute | solution.py:35
  191.7 4.7 %collective-permute-done.38.side = bf16[64,2048]{1,0:T(8,128)(2,1)S(1)} collective-permute-done((bf16[64,2048]{1,0:T(8,128)(2,1)S(1)}, bf16[64,2048]{1,0:T(8,128)(2,1)S(1)}, u32[]{:S(2)}, u32[]{:S(2)}) %collective-permute-start.38) | collective-permute-done | bytes 262176 | tf_op jit(solution)/shard_map/ppermute | solution.py:35
  196.3 1.7 output.1
  (113 shorter events, 8.3 us)
Async XLA Ops:
  0.0 19.7 %collective-permute-start.2 = (bf16[1,2048,768]{2,1,0:T(8,128)(2,1)}, bf16[1,2048,768]{2,1,0:T(8,128)(2,1)}, u32[]{:S(2)}, u32[]{:S(2)}) collective-permute-start(bf16[1,2048,768]{2,1,0:T(8,128)(2,1)} %refs_10_.3), channel_id=1, source_target_pairs={{0,1},{1,0},{2,3},{3,2},{4,5},{5,4},{6,7},{7,6},{8,9},{9,8},{10,11... | collective-permute-start | bytes 9437192 | tf_op jit(solution)/shard_map/ppermute | solution.py:308
  1.3 20.4 %copy-start = (bf16[1,2048,768]{2,1,0:T(8,128)(2,1)S(1)}, bf16[1,2048,768]{2,1,0:T(8,128)(2,1)}, u32[]{:S(2)}) copy-start(bf16[1,2048,768]{2,1,0:T(8,128)(2,1)} %refs_10_.3) | copy-start | bytes 9437188
  2.8 18.7 %copy-start.6 = (bf16[64,4224]{1,0:T(8,128)(2,1)}, bf16[64,4224]{1,0:T(8,128)(2,1)S(1)}, u32[]{:S(2)}) copy-start(bf16[64,4224]{1,0:T(8,128)(2,1)S(1)} %pad_maximum_fusion.refs_2_) | copy-start | bytes 1622020
  2.8 5.1 %collective-permute-start.1 = (bf16[64,4224]{1,0:T(8,128)(2,1)S(1)}, bf16[64,4224]{1,0:T(8,128)(2,1)S(1)}, u32[]{:S(2)}, u32[]{:S(2)}) collective-permute-start(bf16[64,4224]{1,0:T(8,128)(2,1)S(1)} %pad_maximum_fusion.refs_2_), channel_id=1, source_target_pairs={{2,4},{3,5},{4,2},{5,3},{0,1},{1,0},{6,7},{7,6},{10,12},{11,13},{1... | collective-permute-start | bytes 1622024 | tf_op jit(solution)/shard_map/ppermute | solution.py:40
  2.9 16.8 %collective-permute-start = (bf16[64,4224]{1,0:T(8,128)(2,1)S(1)}, bf16[64,4224]{1,0:T(8,128)(2,1)S(1)}, u32[]{:S(2)}, u32[]{:S(2)}) collective-permute-start(bf16[64,4224]{1,0:T(8,128)(2,1)S(1)} %pad_maximum_fusion.refs_2_), channel_id=1, source_target_pairs={{0,2},{1,3},{2,0},{3,1},{4,6},{5,7},{6,4},{7,5},{8,10},{9,11},{10,... | collective-permute-start | bytes 1622024 | tf_op jit(solution)/shard_map/ppermute | solution.py:35
  7.9 17.6 %copy-start.8 = (bf16[64,4224]{1,0:T(8,128)(2,1)}, bf16[64,4224]{1,0:T(8,128)(2,1)S(1)}, u32[]{:S(2)}) copy-start(bf16[64,4224]{1,0:T(8,128)(2,1)S(1)} %collective-permute-done.1.refs_4_) | copy-start | bytes 1622020
  19.7 15.5 %collective-permute-start.5 = (bf16[1,2048,768]{2,1,0:T(8,128)(2,1)}, bf16[1,2048,768]{2,1,0:T(8,128)(2,1)S(1)}, u32[]{:S(2)}, u32[]{:S(2)}) collective-permute-start(bf16[1,2048,768]{2,1,0:T(8,128)(2,1)} %refs_11_), channel_id=1, source_target_pairs={{0,1},{1,0},{2,3},{3,2},{4,5},{5,4},{6,7},{7,6},{8,9},{9,8},{10,11... | collective-permute-start | bytes 9437192 | tf_op jit(solution)/shard_map/ppermute | solution.py:313
  19.7 14.7 %collective-permute-start.3 = (bf16[64,4224]{1,0:T(8,128)(2,1)S(1)}, bf16[64,4224]{1,0:T(8,128)(2,1)S(1)}, u32[]{:S(2)}, u32[]{:S(2)}) collective-permute-start(bf16[64,4224]{1,0:T(8,128)(2,1)S(1)} %collective-permute-done.1.refs_4_), channel_id=1, source_target_pairs={{0,2},{1,3},{2,0},{3,1},{4,6},{5,7},{6,4},{7,5},{8,10},{9,11},{10,... | collective-permute-start | bytes 1622024 | tf_op jit(solution)/shard_map/ppermute | solution.py:35
  21.5 13.7 %collective-permute-start.4 = (bf16[64,4224]{1,0:T(8,128)(2,1)S(1)}, bf16[64,4224]{1,0:T(8,128)(2,1)}, u32[]{:S(2)}, u32[]{:S(2)}) collective-permute-start(bf16[64,4224]{1,0:T(8,128)(2,1)S(1)} %collective-permute-done.refs_3_), channel_id=1, source_target_pairs={{2,4},{3,5},{4,2},{5,3},{0,1},{1,0},{6,7},{7,6},{10,12},{11,13},{1... | collective-permute-start | bytes 1622024 | tf_op jit(solution)/shard_map/ppermute | solution.py:40
  36.9 15.0 %collective-permute-start.7 = (bf16[1,768,2048]{2,1,0:T(8,128)(2,1)}, bf16[1,768,2048]{2,1,0:T(8,128)(2,1)}, u32[]{:S(2)}, u32[]{:S(2)}) collective-permute-start(bf16[1,768,2048]{2,1,0:T(8,128)(2,1)} %refs_12_), channel_id=1, source_target_pairs={{0,1},{1,0},{2,3},{3,2},{4,5},{5,4},{6,7},{7,6},{8,9},{9,8},{10,11... | collective-permute-start | bytes 9437192 | tf_op jit(solution)/shard_map/ppermute | solution.py:320
  36.9 15.0 %collective-permute-start.6 = (bf16[64,4224]{1,0:T(8,128)(2,1)}, bf16[64,4224]{1,0:T(8,128)(2,1)}, u32[]{:S(2)}, u32[]{:S(2)}) collective-permute-start(bf16[64,4224]{1,0:T(8,128)(2,1)} %collective-permute-done.4.refs_6_), channel_id=1, source_target_pairs={{0,2},{1,3},{2,0},{3,1},{4,6},{5,7},{6,4},{7,5},{8,10},{9,11},{10,... | collective-permute-start | bytes 1622024 | tf_op jit(solution)/shard_map/ppermute | solution.py:35
  44.8 7.1 %copy-start.15 = (bf16[64,4224]{1,0:T(8,128)(2,1)S(1)}, bf16[64,4224]{1,0:T(8,128)(2,1)}, u32[]{:S(2)}) copy-start(bf16[64,4224]{1,0:T(8,128)(2,1)} %pad_maximum_fusion.1.refs_0_) | copy-start | bytes 1622020
  44.8 9.8 %copy-start.2 = (bf16[1,2048,768]{2,1,0:T(8,128)(2,1)S(1)}, bf16[1,2048,768]{2,1,0:T(8,128)(2,1)}, u32[]{:S(2)}) copy-start(bf16[1,2048,768]{2,1,0:T(8,128)(2,1)} %refs_11_) | copy-start | bytes 9437188
  44.8 9.8 %copy-start.5 = (bf16[1,2048,768]{2,1,0:T(8,128)(2,1)S(1)}, bf16[1,2048,768]{2,1,0:T(8,128)(2,1)}, u32[]{:S(2)}) copy-start(bf16[1,2048,768]{2,1,0:T(8,128)(2,1)} %copy-done.3) | copy-start | bytes 9437188
  44.8 9.8 %copy-start.14 = (bf16[64,4224]{1,0:T(8,128)(2,1)S(1)}, bf16[64,4224]{1,0:T(8,128)(2,1)}, u32[]{:S(2)}) copy-start(bf16[64,4224]{1,0:T(8,128)(2,1)} %copy-done.12) | copy-start | bytes 1622020
  51.9 16.4 %collective-permute-start.9 = (bf16[64,4224]{1,0:T(8,128)(2,1)S(1)}, bf16[64,4224]{1,0:T(8,128)(2,1)S(1)}, u32[]{:S(2)}, u32[]{:S(2)}) collective-permute-start(bf16[64,4224]{1,0:T(8,128)(2,1)S(1)} %copy-done.15), channel_id=1, source_target_pairs={{2,4},{3,5},{4,2},{5,3},{0,1},{1,0},{6,7},{7,6},{10,12},{11,13},{1... | collective-permute-start | bytes 1622024 | tf_op jit(solution)/shard_map/ppermute | solution.py:40
  51.9 16.4 %collective-permute-start.8 = (bf16[64,4224]{1,0:T(8,128)(2,1)S(1)}, bf16[64,4224]{1,0:T(8,128)(2,1)S(1)}, u32[]{:S(2)}, u32[]{:S(2)}) collective-permute-start(bf16[64,4224]{1,0:T(8,128)(2,1)S(1)} %copy-done.15), channel_id=1, source_target_pairs={{0,2},{1,3},{2,0},{3,1},{4,6},{5,7},{6,4},{7,5},{8,10},{9,11},{10,... | collective-permute-start | bytes 1622024 | tf_op jit(solution)/shard_map/ppermute | solution.py:35
  68.5 13.4 %collective-permute-start.10 = (bf16[64,4224]{1,0:T(8,128)(2,1)S(1)}, bf16[64,4224]{1,0:T(8,128)(2,1)S(1)}, u32[]{:S(2)}, u32[]{:S(2)}) collective-permute-start(bf16[64,4224]{1,0:T(8,128)(2,1)S(1)} %pad_maximum_fusion.2), channel_id=1, source_target_pairs={{0,2},{1,3},{2,0},{3,1},{4,6},{5,7},{6,4},{7,5},{8,10},{9,11},{10,... | collective-permute-start | bytes 1622024 | tf_op jit(solution)/shard_map/ppermute | solution.py:35
  68.5 13.3 %collective-permute-start.11 = (bf16[64,4224]{1,0:T(8,128)(2,1)S(1)}, bf16[64,4224]{1,0:T(8,128)(2,1)S(1)}, u32[]{:S(2)}, u32[]{:S(2)}) collective-permute-start(bf16[64,4224]{1,0:T(8,128)(2,1)S(1)} %collective-permute-done.8.refs_1_), channel_id=1, source_target_pairs={{2,4},{3,5},{4,2},{5,3},{0,1},{1,0},{6,7},{7,6},{10,12},{11,13},{1... | collective-permute-start | bytes 1622024 | tf_op jit(solution)/shard_map/ppermute | solution.py:40
  82.0 12.5 %collective-permute-start.12 = (bf16[64,4224]{1,0:T(8,128)(2,1)S(1)}, bf16[64,4224]{1,0:T(8,128)(2,1)S(1)}, u32[]{:S(2)}, u32[]{:S(2)}) collective-permute-start(bf16[64,4224]{1,0:T(8,128)(2,1)S(1)} %pad_maximum_fusion.3), channel_id=1, source_target_pairs={{0,2},{1,3},{2,0},{3,1},{4,6},{5,7},{6,4},{7,5},{8,10},{9,11},{10,... | collective-permute-start | bytes 1622024 | tf_op jit(solution)/shard_map/ppermute | solution.py:35
  83.9 1.6 collective-permute-start.13
  94.5 10.1 %collective-permute-start.15 = (bf16[64,2048]{1,0:T(8,128)(2,1)S(1)}, bf16[64,2048]{1,0:T(8,128)(2,1)S(1)}, u32[]{:S(2)}, u32[]{:S(2)}) collective-permute-start(bf16[64,2048]{1,0:T(8,128)(2,1)S(1)} %add_convert_fusion.9), channel_id=1, source_target_pairs={{2,4},{3,5},{4,2},{5,3},{0,1},{1,0},{6,7},{7,6},{10,12},{11,13},{1... | collective-permute-start | bytes 786440 | tf_op jit(solution)/shard_map/ppermute | solution.py:40
  94.7 10.0 %copy-start.16 = (bf16[128,2048]{1,0:T(8,128)(2,1)S(1)}, bf16[128,2048]{1,0:T(8,128)(2,1)}, u32[]{:S(2)}) copy-start(bf16[128,2048]{1,0:T(8,128)(2,1)} %param.8) | copy-start | bytes 1572868
  94.7 10.0 %collective-permute-start.14 = (bf16[64,2048]{1,0:T(8,128)(2,1)S(1)}, bf16[64,2048]{1,0:T(8,128)(2,1)S(1)}, u32[]{:S(2)}, u32[]{:S(2)}) collective-permute-start(bf16[64,2048]{1,0:T(8,128)(2,1)S(1)} %fusion), channel_id=1, source_target_pairs={{0,2},{1,3},{2,0},{3,1},{4,6},{5,7},{6,4},{7,5},{8,10},{9,11},{10,... | collective-permute-start | bytes 786440 | tf_op jit(solution)/shard_map/ppermute | solution.py:35
  104.9 8.2 %collective-permute-start.17 = (bf16[64,2048]{1,0:T(8,128)(2,1)S(1)}, bf16[64,2048]{1,0:T(8,128)(2,1)S(1)}, u32[]{:S(2)}, u32[]{:S(2)}) collective-permute-start(bf16[64,2048]{1,0:T(8,128)(2,1)S(1)} %fusion.4.refs_0_), channel_id=1, source_target_pairs={{2,4},{3,5},{4,2},{5,3},{0,1},{1,0},{6,7},{7,6},{10,12},{11,13},{1... | collective-permute-start | bytes 786440 | tf_op jit(solution)/shard_map/ppermute | solution.py:40
  104.9 8.7 %collective-permute-start.16 = (bf16[64,2048]{1,0:T(8,128)(2,1)S(1)}, bf16[64,2048]{1,0:T(8,128)(2,1)S(1)}, u32[]{:S(2)}, u32[]{:S(2)}) collective-permute-start(bf16[64,2048]{1,0:T(8,128)(2,1)S(1)} %fusion.4.refs_0_), channel_id=1, source_target_pairs={{0,2},{1,3},{2,0},{3,1},{4,6},{5,7},{6,4},{7,5},{8,10},{9,11},{10,... | collective-permute-start | bytes 786440 | tf_op jit(solution)/shard_map/ppermute | solution.py:35
  113.7 7.9 %collective-permute-start.18 = (bf16[64,2048]{1,0:T(8,128)(2,1)S(1)}, bf16[64,2048]{1,0:T(8,128)(2,1)S(1)}, u32[]{:S(2)}, u32[]{:S(2)}) collective-permute-start(bf16[64,2048]{1,0:T(8,128)(2,1)S(1)} %broadcast_select_fusion.3), channel_id=1, source_target_pairs={{0,2},{1,3},{2,0},{3,1},{4,6},{5,7},{6,4},{7,5},{8,10},{9,11},{10,... | collective-permute-start | bytes 786440 | tf_op jit(solution)/shard_map/ppermute | solution.py:35
  114.8 6.9 %collective-permute-start.19 = (bf16[64,2048]{1,0:T(8,128)(2,1)S(1)}, bf16[64,2048]{1,0:T(8,128)(2,1)S(1)}, u32[]{:S(2)}, u32[]{:S(2)}) collective-permute-start(bf16[64,2048]{1,0:T(8,128)(2,1)S(1)} %collective-permute-done.16.refs_1_), channel_id=1, source_target_pairs={{2,4},{3,5},{4,2},{5,3},{0,1},{1,0},{6,7},{7,6},{10,12},{11,13},{1... | collective-permute-start | bytes 786440 | tf_op jit(solution)/shard_map/ppermute | solution.py:40
  121.8 7.4 %collective-permute-start.20 = (bf16[64,2048]{1,0:T(8,128)(2,1)S(1)}, bf16[64,2048]{1,0:T(8,128)(2,1)S(1)}, u32[]{:S(2)}, u32[]{:S(2)}) collective-permute-start(bf16[64,2048]{1,0:T(8,128)(2,1)S(1)} %broadcast_select_fusion.2), channel_id=1, source_target_pairs={{0,2},{1,3},{2,0},{3,1},{4,6},{5,7},{6,4},{7,5},{8,10},{9,11},{10,... | collective-permute-start | bytes 786440 | tf_op jit(solution)/shard_map/ppermute | solution.py:35
  123.6 5.6 %collective-permute-start.21 = (bf16[64,2048]{1,0:T(8,128)(2,1)S(1)}, bf16[64,2048]{1,0:T(8,128)(2,1)S(1)}, u32[]{:S(2)}, u32[]{:S(2)}) collective-permute-start(bf16[64,2048]{1,0:T(8,128)(2,1)S(1)} %add_convert_fusion.8), channel_id=1, source_target_pairs={{2,4},{3,5},{4,2},{5,3},{0,1},{1,0},{6,7},{7,6},{10,12},{11,13},{1... | collective-permute-start | bytes 786440 | tf_op jit(solution)/shard_map/ppermute | solution.py:40
  129.2 8.1 %collective-permute-start.23 = (bf16[64,2048]{1,0:T(8,128)(2,1)S(1)}, bf16[64,2048]{1,0:T(8,128)(2,1)S(1)}, u32[]{:S(2)}, u32[]{:S(2)}) collective-permute-start(bf16[64,2048]{1,0:T(8,128)(2,1)S(1)} %add_convert_fusion.6), channel_id=1, source_target_pairs={{2,4},{3,5},{4,2},{5,3},{0,1},{1,0},{6,7},{7,6},{10,12},{11,13},{1... | collective-permute-start | bytes 786440 | tf_op jit(solution)/shard_map/ppermute | solution.py:40
  129.4 8.8 %collective-permute-start.22 = (bf16[64,2048]{1,0:T(8,128)(2,1)S(1)}, bf16[64,2048]{1,0:T(8,128)(2,1)S(1)}, u32[]{:S(2)}, u32[]{:S(2)}) collective-permute-start(bf16[64,2048]{1,0:T(8,128)(2,1)S(1)} %fusion.1), channel_id=1, source_target_pairs={{0,2},{1,3},{2,0},{3,1},{4,6},{5,7},{6,4},{7,5},{8,10},{9,11},{10,... | collective-permute-start | bytes 786440 | tf_op jit(solution)/shard_map/ppermute | solution.py:35
  138.3 8.2 %collective-permute-start.25 = (bf16[64,2048]{1,0:T(8,128)(2,1)S(1)}, bf16[64,2048]{1,0:T(8,128)(2,1)S(1)}, u32[]{:S(2)}, u32[]{:S(2)}) collective-permute-start(bf16[64,2048]{1,0:T(8,128)(2,1)S(1)} %get-tuple-element.205.refs_0_), channel_id=1, source_target_pairs={{2,4},{3,5},{4,2},{5,3},{0,1},{1,0},{6,7},{7,6},{10,12},{11,13},{1... | collective-permute-start | bytes 786440 | tf_op jit(solution)/shard_map/ppermute | solution.py:40
  138.4 8.7 %collective-permute-start.24 = (bf16[64,2048]{1,0:T(8,128)(2,1)S(1)}, bf16[64,2048]{1,0:T(8,128)(2,1)S(1)}, u32[]{:S(2)}, u32[]{:S(2)}) collective-permute-start(bf16[64,2048]{1,0:T(8,128)(2,1)S(1)} %get-tuple-element.205.refs_0_), channel_id=1, source_target_pairs={{0,2},{1,3},{2,0},{3,1},{4,6},{5,7},{6,4},{7,5},{8,10},{9,11},{10,... | collective-permute-start | bytes 786440 | tf_op jit(solution)/shard_map/ppermute | solution.py:35
  147.1 7.9 %collective-permute-start.26 = (bf16[64,2048]{1,0:T(8,128)(2,1)S(1)}, bf16[64,2048]{1,0:T(8,128)(2,1)S(1)}, u32[]{:S(2)}, u32[]{:S(2)}) collective-permute-start(bf16[64,2048]{1,0:T(8,128)(2,1)S(1)} %broadcast_select_fusion.1), channel_id=1, source_target_pairs={{0,2},{1,3},{2,0},{3,1},{4,6},{5,7},{6,4},{7,5},{8,10},{9,11},{10,... | collective-permute-start | bytes 786440 | tf_op jit(solution)/shard_map/ppermute | solution.py:35
  147.5 7.6 %collective-permute-start.27 = (bf16[64,2048]{1,0:T(8,128)(2,1)S(1)}, bf16[64,2048]{1,0:T(8,128)(2,1)S(1)}, u32[]{:S(2)}, u32[]{:S(2)}) collective-permute-start(bf16[64,2048]{1,0:T(8,128)(2,1)S(1)} %collective-permute-done.24.refs_1_), channel_id=1, source_target_pairs={{2,4},{3,5},{4,2},{5,3},{0,1},{1,0},{6,7},{7,6},{10,12},{11,13},{1... | collective-permute-start | bytes 786440 | tf_op jit(solution)/shard_map/ppermute | solution.py:40
  155.2 7.0 %collective-permute-start.28 = (bf16[64,2048]{1,0:T(8,128)(2,1)S(1)}, bf16[64,2048]{1,0:T(8,128)(2,1)S(1)}, u32[]{:S(2)}, u32[]{:S(2)}) collective-permute-start(bf16[64,2048]{1,0:T(8,128)(2,1)S(1)} %broadcast_select_fusion), channel_id=1, source_target_pairs={{0,2},{1,3},{2,0},{3,1},{4,6},{5,7},{6,4},{7,5},{8,10},{9,11},{10,... | collective-permute-start | bytes 786440 | tf_op jit(solution)/shard_map/ppermute | solution.py:35
  157.0 5.2 %collective-permute-start.29 = (bf16[64,2048]{1,0:T(8,128)(2,1)S(1)}, bf16[64,2048]{1,0:T(8,128)(2,1)S(1)}, u32[]{:S(2)}, u32[]{:S(2)}) collective-permute-start(bf16[64,2048]{1,0:T(8,128)(2,1)S(1)} %add_convert_fusion.5), channel_id=1, source_target_pairs={{2,4},{3,5},{4,2},{5,3},{0,1},{1,0},{6,7},{7,6},{10,12},{11,13},{1... | collective-permute-start | bytes 786440 | tf_op jit(solution)/shard_map/ppermute | solution.py:40
  162.3 13.0 %collective-permute-start.31 = (bf16[64,2048]{1,0:T(8,128)(2,1)S(1)}, bf16[64,2048]{1,0:T(8,128)(2,1)S(1)}, u32[]{:S(2)}, u32[]{:S(2)}) collective-permute-start(bf16[64,2048]{1,0:T(8,128)(2,1)S(1)} %add_convert_fusion.3), channel_id=1, source_target_pairs={{2,4},{3,5},{4,2},{5,3},{0,1},{1,0},{6,7},{7,6},{10,12},{11,13},{1... | collective-permute-start | bytes 786440 | tf_op jit(solution)/shard_map/ppermute | solution.py:40
  162.5 12.8 %collective-permute-start.30 = (bf16[64,2048]{1,0:T(8,128)(2,1)S(1)}, bf16[64,2048]{1,0:T(8,128)(2,1)S(1)}, u32[]{:S(2)}, u32[]{:S(2)}) collective-permute-start(bf16[64,2048]{1,0:T(8,128)(2,1)S(1)} %fusion.2), channel_id=1, source_target_pairs={{0,2},{1,3},{2,0},{3,1},{4,6},{5,7},{6,4},{7,5},{8,10},{9,11},{10,... | collective-permute-start | bytes 786440 | tf_op jit(solution)/shard_map/ppermute | solution.py:35
  175.3 7.3 %collective-permute-start.32 = (bf16[64,2048]{1,0:T(8,128)(2,1)S(1)}, bf16[64,2048]{1,0:T(8,128)(2,1)S(1)}, u32[]{:S(2)}, u32[]{:S(2)}) collective-permute-start(bf16[64,2048]{1,0:T(8,128)(2,1)S(1)} %get-tuple-element.192), channel_id=1, source_target_pairs={{0,2},{1,3},{2,0},{3,1},{4,6},{5,7},{6,4},{7,5},{8,10},{9,11},{10,... | collective-permute-start | bytes 786440 | tf_op jit(solution)/shard_map/ppermute | solution.py:35
  175.4 1.2 collective-permute-start.33
  176.6 3.6 %collective-permute-start.34 = (f32[8,128]{1,0:T(8,128)S(1)}, f32[8,128]{1,0:T(8,128)S(1)}, u32[]{:S(2)}, u32[]{:S(2)}) collective-permute-start(f32[8,128]{1,0:T(8,128)S(1)} %add.94), channel_id=1, source_target_pairs={{0,8},{8,0},{16,24},{24,16},{1,9},{9,1},{17,25},{25,17},{2,10},{10... | collective-permute-start | bytes 12296 | tf_op jit(solution)/shard_map/ppermute | solution.py:213
  178.1 9.2 %collective-permute-start.36 = (bf16[64,2048]{1,0:T(8,128)(2,1)S(1)}, bf16[64,2048]{1,0:T(8,128)(2,1)S(1)}, u32[]{:S(2)}, u32[]{:S(2)}) collective-permute-start(bf16[64,2048]{1,0:T(8,128)(2,1)S(1)} %get-tuple-element.201), channel_id=1, source_target_pairs={{0,2},{1,3},{2,0},{3,1},{4,6},{5,7},{6,4},{7,5},{8,10},{9,11},{10,... | collective-permute-start | bytes 786440 | tf_op jit(solution)/shard_map/ppermute | solution.py:35
  182.7 4.7 %collective-permute-start.37 = (bf16[64,2048]{1,0:T(8,128)(2,1)S(1)}, bf16[64,2048]{1,0:T(8,128)(2,1)S(1)}, u32[]{:S(2)}, u32[]{:S(2)}) collective-permute-start(bf16[64,2048]{1,0:T(8,128)(2,1)S(1)} %add_convert_fusion.2), channel_id=1, source_target_pairs={{2,4},{3,5},{4,2},{5,3},{0,1},{1,0},{6,7},{7,6},{10,12},{11,13},{1... | collective-permute-start | bytes 786440 | tf_op jit(solution)/shard_map/ppermute | solution.py:40
  182.7 8.9 %collective-permute-start.35 = (f32[8,128]{1,0:T(8,128)S(1)}, f32[8,128]{1,0:T(8,128)S(1)}, u32[]{:S(2)}, u32[]{:S(2)}) collective-permute-start(f32[8,128]{1,0:T(8,128)S(1)} %add.95), channel_id=1, source_target_pairs={{0,16},{8,24},{16,0},{24,8},{1,17},{9,25},{17,1},{25,9},{2,18},{10... | collective-permute-start | bytes 12296 | tf_op jit(solution)/shard_map/ppermute | solution.py:213
  187.4 4.3 %collective-permute-start.39 = (bf16[64,2048]{1,0:T(8,128)(2,1)S(1)}, bf16[64,2048]{1,0:T(8,128)(2,1)S(1)}, u32[]{:S(2)}, u32[]{:S(2)}) collective-permute-start(bf16[64,2048]{1,0:T(8,128)(2,1)S(1)} %add_convert_fusion), channel_id=1, source_target_pairs={{2,4},{3,5},{4,2},{5,3},{0,1},{1,0},{6,7},{7,6},{10,12},{11,13},{1... | collective-permute-start | bytes 786440 | tf_op jit(solution)/shard_map/ppermute | solution.py:40
  187.6 8.8 %collective-permute-start.38 = (bf16[64,2048]{1,0:T(8,128)(2,1)S(1)}, bf16[64,2048]{1,0:T(8,128)(2,1)S(1)}, u32[]{:S(2)}, u32[]{:S(2)}) collective-permute-start(bf16[64,2048]{1,0:T(8,128)(2,1)S(1)} %fusion.3), channel_id=1, source_target_pairs={{0,2},{1,3},{2,0},{3,1},{4,6},{5,7},{6,4},{7,5},{8,10},{9,11},{10,... | collective-permute-start | bytes 786440 | tf_op jit(solution)/shard_map/ppermute | solution.py:35
  (9 other events, 16.3 us)

commit v7 on v6

--- a/solution.py
+++ b/solution.py
@@ -86,8 +86,8 @@
         out[...] = total[pl.ds(i * rows, rows), :].astype(out.dtype)
 
 
-def forward_kernel(owners, experts, start, finish, unused, where_ref, *refs):
-    refs = list(refs[unused:])
+def forward_kernel(owners, experts, start, finish, where_ref, *refs):
+    refs = list(refs)
     parts, refs = refs[:6], refs[6:]
     earlier = None if start else refs.pop(0)
     weights, refs = refs[: 3 * len(experts)], refs[3 * len(experts) :]
@@ -122,8 +122,8 @@
         store_parts(total, outs)
 
 
-def backward_kernel(experts, blocks, start, finish, unused, where_ref, *refs):
-    refs = list(refs[unused:])
+def backward_kernel(experts, blocks, start, finish, where_ref, *refs):
+    refs = list(refs)
     parts, refs = refs[:6], refs[6:]
     earlier = None if start else refs.pop(0)
     states, refs = refs[: 2 * len(experts)], refs[2 * len(experts) :]
@@ -154,14 +154,13 @@
         store_parts(total, outs)
 
 
-def kernel_call(kernel, name, where, parts, operands, outs, blocks, width, flops, unused=()):
+def kernel_call(kernel, name, where, parts, operands, outs, blocks, width, flops):
     anywhere, vmem = pl.BlockSpec(memory_space=pl.ANY), pl.BlockSpec(memory_space=pltpu.VMEM)
-    called = functools.partial(kernel, len(unused))
     rows = parts[0].shape[0] * blocks
     return pl.pallas_call(
-        called,
+        kernel,
         in_specs=[pl.BlockSpec(memory_space=pltpu.SMEM)]
-        + [anywhere] * (len(parts) + len(unused))
+        + [anywhere] * len(parts)
         + [vmem] * len(operands),
         out_specs=[vmem] * len(outs),
         out_shape=[pltpu.VMEM(shape, kind) for shape, kind in outs],
@@ -170,10 +169,10 @@
             pltpu.VMEM((rows, parts[0].shape[1]), jnp.bfloat16),
             pltpu.VMEM((rows, width), jnp.float32),
         ],
-        compiler_params=pltpu.CompilerParams(vmem_limit_bytes=16 * 2**20),
+        compiler_params=pltpu.CompilerParams(vmem_limit_bytes=10 * 2**20),
         cost_estimate=pl.CostEstimate(flops=flops, bytes_accessed=0, transcendentals=0),
         name=name,
-    )(where, *unused, *parts, *[in_vmem(value) for value in operands])
+    )(where, *parts, *[in_vmem(value) for value in operands])
 
 
 def output_kernel(elements, where_ref, squares, whole_a, jv_b, own, side, inner_last, out):
@@ -192,20 +191,27 @@
         out[pl.ds(half, half), :] = total * scale
 
 
-def touch_kernel(*refs):
-    refs[-1][...] = refs[0][0, pl.ds(0, 16), pl.ds(0, LANES)]
-
-
-def touch(weights):
-    vmem = pl.BlockSpec(memory_space=pltpu.VMEM)
+def load_kernel(count, *refs):
+    arrays, outs, sems = refs[:count], refs[count : 2 * count], refs[2 * count]
+    copies = [
+        pltpu.make_async_copy(array, out, sems.at[i]) for i, (array, out) in enumerate(zip(arrays, outs))
+    ]
+    for copy in copies:
+        copy.start()
+    for copy in copies:
+        copy.wait()
+
+
+def load(arrays):
     return pl.pallas_call(
-        touch_kernel,
-        in_specs=[vmem] * len(weights),
-        out_specs=vmem,
-        out_shape=pltpu.VMEM((16, LANES), jnp.bfloat16),
-        compiler_params=pltpu.CompilerParams(vmem_limit_bytes=12 * 2**20),
-        name="touch",
-    )(*[in_vmem(value) for value in weights])
+        functools.partial(load_kernel, len(arrays)),
+        in_specs=[pl.BlockSpec(memory_space=pl.ANY)] * len(arrays),
+        out_specs=[pl.BlockSpec(memory_space=pltpu.VMEM)] * len(arrays),
+        out_shape=[pltpu.VMEM(array.shape, array.dtype) for array in arrays],
+        scratch_shapes=[pltpu.SemaphoreType.DMA((len(arrays),))],
+        compiler_params=pltpu.CompilerParams(vmem_limit_bytes=2**20),
+        name="load",
+    )(*arrays)
 
 
 def exchange_sum(value, axis, step):
@@ -251,7 +257,7 @@
     def part_outs(blocks):
         return [((half, width), jnp.float32 if block == 0 else jnp.bfloat16) for block in blocks]
 
-    def forward(parts, experts, earlier=None, unused=()):
+    def forward(parts, experts, earlier=None):
         finish = experts[-1] == CORES - 1
         outs = part_outs(range(LINE)) if finish else [((line_rows, width), jnp.float32)]
         result = kernel_call(
@@ -264,7 +270,6 @@
             LINE,
             width,
             2 * 5 * line_rows * width * hidden * len(experts),
-            unused,
         )
         states = result[len(outs) :]
         return (result[: len(outs)] if finish else result[0]), states
@@ -304,32 +309,21 @@
             first = jnp.concatenate([first, payload[:, width:]], axis=1)
         return side_hop(first)
 
-    a_side, a_near, sib_gate, w_up, w_down, load_b = slot(
-        side_hop(load_a), inner_hop(load_a), lax.ppermute(w_gate, "expert", swap), w_up, w_down, load_b
-    )
-    a_near_end, a_far, sib_up, own_piece, w_down, load_b = slot(
-        side_hop(a_near),
-        inner_hop(a_side),
-        lax.ppermute(w_up, "expert", swap),
-        touch((w_gate, w_up, w_down)),
-        w_down,
-        load_b,
-    )
-    a_far_end, sib_down, sib_piece, load_b = slot(
-        side_hop(a_far),
-        lax.ppermute(w_down, "expert", swap),
-        touch((sib_gate, sib_up, load_a, a_side, a_near, a_near_end, a_far)),
-        load_b,
-    )
-    weights = ((w_gate, w_up, w_down), (sib_gate, sib_up, sib_down))
+    sib = [lax.ppermute(w, "expert", swap) for w in (w_gate, w_up, w_down)]
+    a_side, a_near, own_weights, load_b = slot(
+        side_hop(load_a), inner_hop(load_a), load((w_gate, w_up, w_down)), load_b
+    )
+    a_near_end, a_far, sib, load_b = slot(side_hop(a_near), inner_hop(a_side), sib, load_b)
+    a_far_end, sib_weights, a_parts, load_b = slot(
+        side_hop(a_far), load(sib), load((load_a, a_side, a_near, a_near_end, a_far)), load_b
+    )
+    weights = (own_weights, sib_weights)
 
     everyone = tuple(range(CORES))
     b_side, b_near, (pa, states_a) = slot(
         side_hop(load_b),
         inner_hop(load_b),
-        forward(
-            (load_a, a_side, a_near, a_near_end, a_far, a_far_end), everyone, unused=(own_piece, sib_piece)
-        ),
+        forward((*a_parts, a_far_end), everyone),
     )
     b_near_end, b_far = slot(both_ways(pa[3], b_near), inner_hop(b_side))
     sa_far = add_rows(pa[3], b_near_end[:, :width])

time: 199 us -> 190 us (0.955)
  Pallas kernels: 56.3 us -> 44.3 us
  local copies, waits for them, and re-layouts: 12.1 us -> 15.3 us
  waiting for transfers between devices: 88.2 us -> 91.1 us
  starting transfers between devices: 37.5 us -> 34.8 us
    pallas_call x8 -> x9, Pallas kernels: 54.6 us -> 42.6 us  [the longest x6 36.7 us: kernel_call(): pl.pallas_call(kernel, in_specs=[pl.BlockSpec(memory_space=pltpu.SMEM)] +...]
    unnamed x34, local copies, waits for them, and re-layouts: 10.5 us -> 13.7 us
    ppermute x18, starting transfers between devices: 33 us -> 30 us  [side_hop(): return lax.ppermute(rows, 'expert', both_cores(SIDE_PAIRS))]
    ppermute x18, waiting for transfers between devices: 85.3 us -> 88.2 us  [side_hop(): return lax.ppermute(rows, 'expert', both_cores(SIDE_PAIRS))]
  transfers between devices with their start and end apart: 40 -> 40, of which waited for: 18 -> 20; matrix products, arithmetic and copies ran while one was open for 2% -> 2% of each run, Pallas kernels for 28% -> 23%
where the time goes in v7:
time: 190 us; the launch traced here: 189 us
  waiting for transfers between devices  91.1 us (48%)
  Pallas kernels  44.3 us (23%)
  starting transfers between devices  34.8 us (18%)
  local copies, waits for them, and re-layouts  15.3 us (8%)
  other arithmetic  3.3 us (2%)
    ppermute x18, waiting for transfers between devices, side_hop(): return lax.ppermute(rows, 'expert', both_cores(SIDE_PAIRS))  88.2 us
    pallas_call x6, Pallas kernels, kernel_call(): pl.pallas_call(kernel, in_specs=[pl.BlockSpec(memory_space=pltpu.SMEM)] +...  36.7 us
    ppermute x18, starting transfers between devices, side_hop(): return lax.ppermute(rows, 'expert', both_cores(SIDE_PAIRS))  30 us
    unnamed x34, local copies, waits for them, and re-layouts  13.7 us
    pallas_call x3, Pallas kernels, load(): pl.pallas_call(functools.partial(load_kernel, len(arrays)), in_specs=[pl....  5.89 us
  transfers between devices with their start and end apart: 40, of which 20 were waited for; matrix products, arithmetic and copies ran while one was open for 2% of the time, Pallas kernels for 23%

profile of v7, /device:TPU:0, one launch (start us, length us, event | category | flops | bytes accessed | tf_op | source)
XLA Modules:
  0.0 189.3 jit_solution(17761366412776062729)
XLA Ops:
  1.8 1.4 fusion.8
  3.4 4.1 %collective-permute-start = (bf16[64,4224]{1,0:T(8,128)(2,1)S(1)}, bf16[64,4224]{1,0:T(8,128)(2,1)S(1)}, u32[]{:S(2)}, u32[]{:S(2)}) collective-permute-start(bf16[64,4224]{1,0:T(8,128)(2,1)S(1)} %pad_maximum_fusion.refs_0_), channel_id=1, source_target_pairs={{0,2},{1,3},{2,0},{3,1},{4,6},{5,7},{6,4},{7,5},{8,10},{9,11},{10,... | collective-permute-start | bytes 1622024 | tf_op jit(solution)/shard_map/ppermute | solution.py:35
  7.5 1.9 copy-done.5
  9.4 1.9 copy-done.6
  12.0 1.6 copy-done
  13.6 1.7 copy-done.2
  16.1 4.1 %collective-permute-done.refs_1_ = bf16[64,4224]{1,0:T(8,128)(2,1)S(1)} collective-permute-done((bf16[64,4224]{1,0:T(8,128)(2,1)S(1)}, bf16[64,4224]{1,0:T(8,128)(2,1)S(1)}, u32[]{:S(2)}, u32[]{:S(2)}) %collective-permute-start) | collective-permute-done | bytes 540704 | tf_op jit(solution)/shard_map/ppermute | solution.py:35
  20.2 1.7 collective-permute-start.2
  23.6 10.5 %collective-permute-done.2.refs_3_ = bf16[64,4224]{1,0:T(8,128)(2,1)S(1)} collective-permute-done((bf16[64,4224]{1,0:T(8,128)(2,1)S(1)}, bf16[64,4224]{1,0:T(8,128)(2,1)S(1)}, u32[]{:S(2)}, u32[]{:S(2)}) %collective-permute-start.2) | collective-permute-done | bytes 540704 | tf_op jit(solution)/shard_map/ppermute | solution.py:35
  34.9 1.9 %collective-permute-start.7 = (bf16[64,4224]{1,0:T(8,128)(2,1)}, bf16[64,4224]{1,0:T(8,128)(2,1)}, u32[]{:S(2)}, u32[]{:S(2)}) collective-permute-start(bf16[64,4224]{1,0:T(8,128)(2,1)} %collective-permute-done.3.refs_4_), channel_id=1, source_target_pairs={{0,2},{1,3},{2,0},{3,1},{4,6},{5,7},{6,4},{7,5},{8,10},{9,11},{10,... | collective-permute-start | bytes 1622024 | tf_op jit(solution)/shard_map/ppermute | solution.py:35
  41.1 1.3 load.5
  42.5 3.9 %load.4 = (bf16[1,2048,768]{2,1,0:T(8,128)(2,1)S(1)}, bf16[1,2048,768]{2,1,0:T(8,128)(2,1)S(1)}, bf16[1,768,2048]{2,1,0:T(8,128)(2,1)S(1)}) custom-call(bf16[1,2048,768]{2,1,0:T(8,128)(2,1)} %collective-permute-done.4.refs_0_, bf16[1,2048,768]{2,1,0:T(8,128)(2,1)} %collective-permute-done.5.refs_1_, bf16[1,768,2048]{2,1,0:T(8,128)(2,1)} %collective-permute-done.6.refs_2_), custom_call_target="tpu_custom_call" | custom-call | tf_op jit(solution)/shard_map/load/pallas_call | solution.py:206
  46.4 1.9 %collective-permute-done.7.refs_5_ = bf16[64,4224]{1,0:T(8,128)(2,1)} collective-permute-done((bf16[64,4224]{1,0:T(8,128)(2,1)}, bf16[64,4224]{1,0:T(8,128)(2,1)}, u32[]{:S(2)}, u32[]{:S(2)}) %collective-permute-start.7) | collective-permute-done | bytes 540704 | tf_op jit(solution)/shard_map/ppermute | solution.py:35
  48.3 2.2 %collective-permute-start.8 = (bf16[64,4224]{1,0:T(8,128)(2,1)S(1)}, bf16[64,4224]{1,0:T(8,128)(2,1)S(1)}, u32[]{:S(2)}, u32[]{:S(2)}) collective-permute-start(bf16[64,4224]{1,0:T(8,128)(2,1)S(1)} %copy-done.9), channel_id=1, source_target_pairs={{0,2},{1,3},{2,0},{3,1},{4,6},{5,7},{6,4},{7,5},{8,10},{9,11},{10,... | collective-permute-start | bytes 1622024 | tf_op jit(solution)/shard_map/ppermute | solution.py:35
  50.5 10.5 %forward.3 = (f32[64,2048]{1,0:T(8,128)S(1)}, bf16[64,2048]{1,0:T(8,128)(2,1)S(1)}, bf16[64,2048]{1,0:T(8,128)(2,1)S(1)}, bf16[64,2048]{1,0:T(8,128)(2,1)S(1)}, ...) custom-call(s32[3]{0:T(128)S(1)} %pad_add_fusion.where_ref, ...), custom_call_target="tpu_custom_call" | custom-call | flops 8053063680 | tf_op jit(solution)/shard_map/forward/pallas_call | solution.py:160
  61.0 2.0 %collective-permute-done.8.refs_1_ = bf16[64,4224]{1,0:T(8,128)(2,1)S(1)} collective-permute-done((bf16[64,4224]{1,0:T(8,128)(2,1)S(1)}, bf16[64,4224]{1,0:T(8,128)(2,1)S(1)}, u32[]{:S(2)}, u32[]{:S(2)}) %collective-permute-start.8) | collective-permute-done | bytes 540704 | tf_op jit(solution)/shard_map/ppermute | solution.py:35
  63.5 13.4 %collective-permute-done.10.refs_3_ = bf16[64,4224]{1,0:T(8,128)(2,1)S(1)} collective-permute-done((bf16[64,4224]{1,0:T(8,128)(2,1)S(1)}, bf16[64,4224]{1,0:T(8,128)(2,1)S(1)}, u32[]{:S(2)}, u32[]{:S(2)}) %collective-permute-start.10) | collective-permute-done | bytes 540704 | tf_op jit(solution)/shard_map/ppermute | solution.py:35
  77.0 1.8 collective-permute-start.12
  79.0 1.5 collective-permute-done.13
  80.5 9.4 %collective-permute-done.12.refs_5_ = bf16[64,4224]{1,0:T(8,128)(2,1)S(1)} collective-permute-done((bf16[64,4224]{1,0:T(8,128)(2,1)S(1)}, bf16[64,4224]{1,0:T(8,128)(2,1)S(1)}, u32[]{:S(2)}, u32[]{:S(2)}) %collective-permute-start.12) | collective-permute-done | bytes 540704 | tf_op jit(solution)/shard_map/ppermute | solution.py:35
  90.1 1.5 collective-permute-start.14
  91.6 5.5 %forward.4 = (f32[256,2048]{1,0:T(8,128)S(1)}, f32[256,768]{1,0:T(8,128)S(1)}, f32[256,768]{1,0:T(8,128)S(1)}) custom-call(s32[3]{0:T(128)S(1)} %pad_add_fusion.where_ref, bf16[64,4224]{1,0:T(8,128)(2,1)S(1)} %copy-done.9, bf16[64,4224]{1,0:T(8,128)(2,1)S(1)} %collective-permute-done.8.refs_1_, bf16[64,4224]{1,0:T(8,128)(2,1)S(1)} %collective-permute-done.9.refs_2_, ...), custom_call_target="tpu_custom_call" | custom-call | flops 4026531840 | tf_op jit(solution)/shard_map/forward/pallas_call | solution.py:160
  97.1 1.8 collective-permute-done.14
  100.2 5.3 %forward.5 = (f32[64,2048]{1,0:T(8,128)S(1)}, bf16[64,2048]{1,0:T(8,128)(2,1)S(1)}, bf16[64,2048]{1,0:T(8,128)(2,1)S(1)}, bf16[64,2048]{1,0:T(8,128)(2,1)S(1)}, ...) custom-call(s32[3]{0:T(128)S(1)} %pad_add_fusion.where_ref, bf16[64,4224]{1,0:T(8,128)(2,1)S(1)} %copy-done.9, ...), custom_call_target="tpu_custom_call" | custom-call | flops 4026531840 | tf_op jit(solution)/shard_map/forward/pallas_call | solution.py:160
  105.5 2.3 %collective-permute-done.16.refs_1_ = bf16[64,2048]{1,0:T(8,128)(2,1)S(1)} collective-permute-done((bf16[64,2048]{1,0:T(8,128)(2,1)S(1)}, bf16[64,2048]{1,0:T(8,128)(2,1)S(1)}, u32[]{:S(2)}, u32[]{:S(2)}) %collective-permute-start.16) | collective-permute-done | bytes 262176 | tf_op jit(solution)/shard_map/ppermute | solution.py:35
  108.2 7.6 %collective-permute-done.18.refs_3_ = bf16[64,2048]{1,0:T(8,128)(2,1)S(1)} collective-permute-done((bf16[64,2048]{1,0:T(8,128)(2,1)S(1)}, bf16[64,2048]{1,0:T(8,128)(2,1)S(1)}, u32[]{:S(2)}, u32[]{:S(2)}) %collective-permute-start.18) | collective-permute-done | bytes 262176 | tf_op jit(solution)/shard_map/ppermute | solution.py:35
  115.9 1.8 collective-permute-start.20
  117.7 5.2 %collective-permute-done.20.refs_5_ = bf16[64,2048]{1,0:T(8,128)(2,1)S(1)} collective-permute-done((bf16[64,2048]{1,0:T(8,128)(2,1)S(1)}, bf16[64,2048]{1,0:T(8,128)(2,1)S(1)}, u32[]{:S(2)}, u32[]{:S(2)}) %collective-permute-start.20) | collective-permute-done | bytes 262176 | tf_op jit(solution)/shard_map/ppermute | solution.py:35
  123.2 2.1 %collective-permute-start.22 = (bf16[64,2048]{1,0:T(8,128)(2,1)S(1)}, bf16[64,2048]{1,0:T(8,128)(2,1)S(1)}, u32[]{:S(2)}, u32[]{:S(2)}) collective-permute-start(bf16[64,2048]{1,0:T(8,128)(2,1)S(1)} %fusion.1), channel_id=1, source_target_pairs={{0,2},{1,3},{2,0},{3,1},{4,6},{5,7},{6,4},{7,5},{8,10},{9,11},{10,... | collective-permute-start | bytes 786440 | tf_op jit(solution)/shard_map/ppermute | solution.py:35
  125.3 4.2 %backward.3 = (f32[256,2048]{1,0:T(8,128)S(1)}, f32[8,128]{1,0:T(8,128)S(1)}) custom-call(s32[3]{0:T(128)S(1)} %pad_add_fusion.where_ref, bf16[64,2048]{1,0:T(8,128)(2,1)S(1)} %fusion.4.refs_0_, bf16[64,2048]{1,0:T(8,128)(2,1)S(1)} %collective-permute-done.16.refs_1_, bf16[64,2048]{1,0:T(8,128)(2,1)S(1)} %collective-permute-done.17.refs_2_, ...), custom_call_target="tpu_custom_call" | custom-call | flops 2415919104 | tf_op jit(solution)/shard_map/backward/pallas_call | solution.py:160
  129.5 2.4 %collective-permute-done.22 = bf16[64,2048]{1,0:T(8,128)(2,1)S(1)} collective-permute-done((bf16[64,2048]{1,0:T(8,128)(2,1)S(1)}, bf16[64,2048]{1,0:T(8,128)(2,1)S(1)}, u32[]{:S(2)}, u32[]{:S(2)}) %collective-permute-start.22) | collective-permute-done | bytes 262176 | tf_op jit(solution)/shard_map/ppermute | solution.py:35
  132.2 1.4 collective-permute-start.24
  133.6 4.3 %backward.4 = (f32[64,2048]{1,0:T(8,128)S(1)}, bf16[64,2048]{1,0:T(8,128)(2,1)S(1)}, bf16[64,2048]{1,0:T(8,128)(2,1)S(1)}, bf16[64,2048]{1,0:T(8,128)(2,1)S(1)}) custom-call(s32[3]{0:T(128)S(1)} %pad_add_fusion.where_ref, bf16[64,2048]{1,0:T(8,128)(2,1)S(1)} %fusion.4.refs_0_, bf16[64,2048]{1,0:T(8,128)(2,1)S(1)} %collective-permute-done.16.refs_1_, ...), custom_call_target="tpu_custom_call" | custom-call | flops 2415919104 | tf_op jit(solution)/shard_map/backward/pallas_call | solution.py:160
  137.9 3.0 %collective-permute-done.24.refs_1_ = bf16[64,2048]{1,0:T(8,128)(2,1)S(1)} collective-permute-done((bf16[64,2048]{1,0:T(8,128)(2,1)S(1)}, bf16[64,2048]{1,0:T(8,128)(2,1)S(1)}, u32[]{:S(2)}, u32[]{:S(2)}) %collective-permute-start.24) | collective-permute-done | bytes 262176 | tf_op jit(solution)/shard_map/ppermute | solution.py:35
  141.3 7.6 %collective-permute-done.26.refs_3_ = bf16[64,2048]{1,0:T(8,128)(2,1)S(1)} collective-permute-done((bf16[64,2048]{1,0:T(8,128)(2,1)S(1)}, bf16[64,2048]{1,0:T(8,128)(2,1)S(1)}, u32[]{:S(2)}, u32[]{:S(2)}) %collective-permute-start.26) | collective-permute-done | bytes 262176 | tf_op jit(solution)/shard_map/ppermute | solution.py:35
  149.0 1.8 collective-permute-start.28
  150.8 5.2 %collective-permute-done.28.refs_5_ = bf16[64,2048]{1,0:T(8,128)(2,1)S(1)} collective-permute-done((bf16[64,2048]{1,0:T(8,128)(2,1)S(1)}, bf16[64,2048]{1,0:T(8,128)(2,1)S(1)}, u32[]{:S(2)}, u32[]{:S(2)}) %collective-permute-start.28) | collective-permute-done | bytes 262176 | tf_op jit(solution)/shard_map/ppermute | solution.py:35
  156.3 2.1 %collective-permute-start.30 = (bf16[64,2048]{1,0:T(8,128)(2,1)S(1)}, bf16[64,2048]{1,0:T(8,128)(2,1)S(1)}, u32[]{:S(2)}, u32[]{:S(2)}) collective-permute-start(bf16[64,2048]{1,0:T(8,128)(2,1)S(1)} %fusion.2), channel_id=1, source_target_pairs={{0,2},{1,3},{2,0},{3,1},{4,6},{5,7},{6,4},{7,5},{8,10},{9,11},{10,... | collective-permute-start | bytes 786440 | tf_op jit(solution)/shard_map/ppermute | solution.py:35
  158.4 7.0 %backward.5 = (f32[64,2048]{1,0:T(8,128)S(1)}, bf16[64,2048]{1,0:T(8,128)(2,1)S(1)}, bf16[64,2048]{1,0:T(8,128)(2,1)S(1)}, bf16[64,2048]{1,0:T(8,128)(2,1)S(1)}, f32[8,128]{1,0:T(8,128)S(1)}) custom-call(s32[3]{0:T(128)S(1)} %pad_add_fusion.where_ref, bf16[64,2048]{1,0:T(8,128)(2,1)S(1)} %get-tuple-element.239.refs_0_, ...), custom_call_target="tpu_custom_call" | custom-call | flops 4831838208 | tf_op jit(solution)/shard_map/backward/pallas_call | solution.py:160
  165.6 1.2 collective-permute-done.33
  166.7 1.5 collective-permute-start.34
  168.2 1.9 %collective-permute-start.36 = (bf16[64,2048]{1,0:T(8,128)(2,1)S(1)}, bf16[64,2048]{1,0:T(8,128)(2,1)S(1)}, u32[]{:S(2)}, u32[]{:S(2)}) collective-permute-start(bf16[64,2048]{1,0:T(8,128)(2,1)S(1)} %get-tuple-element.235), channel_id=1, source_target_pairs={{0,2},{1,3},{2,0},{3,1},{4,6},{5,7},{6,4},{7,5},{8,10},{9,11},{10,... | collective-permute-start | bytes 786440 | tf_op jit(solution)/shard_map/ppermute | solution.py:35
  170.3 4.4 %collective-permute-done.32 = bf16[64,2048]{1,0:T(8,128)(2,1)S(1)} collective-permute-done((bf16[64,2048]{1,0:T(8,128)(2,1)S(1)}, bf16[64,2048]{1,0:T(8,128)(2,1)S(1)}, u32[]{:S(2)}, u32[]{:S(2)}) %collective-permute-start.32) | collective-permute-done | bytes 262176 | tf_op jit(solution)/shard_map/ppermute | solution.py:35
  174.8 1.6 collective-permute-start.35
  176.4 2.2 %collective-permute-done.36 = bf16[64,2048]{1,0:T(8,128)(2,1)S(1)} collective-permute-done((bf16[64,2048]{1,0:T(8,128)(2,1)S(1)}, bf16[64,2048]{1,0:T(8,128)(2,1)S(1)}, u32[]{:S(2)}, u32[]{:S(2)}) %collective-permute-start.36) | collective-permute-done | bytes 262176 | tf_op jit(solution)/shard_map/ppermute | solution.py:35
  178.8 3.4 %collective-permute-start.38 = (bf16[64,2048]{1,0:T(8,128)(2,1)S(1)}, bf16[64,2048]{1,0:T(8,128)(2,1)S(1)}, u32[]{:S(2)}, u32[]{:S(2)}) collective-permute-start(bf16[64,2048]{1,0:T(8,128)(2,1)S(1)} %fusion.3), channel_id=1, source_target_pairs={{0,2},{1,3},{2,0},{3,1},{4,6},{5,7},{6,4},{7,5},{8,10},{9,11},{10,... | collective-permute-start | bytes 786440 | tf_op jit(solution)/shard_map/ppermute | solution.py:35
  182.5 5.1 %collective-permute-done.38.side = bf16[64,2048]{1,0:T(8,128)(2,1)S(1)} collective-permute-done((bf16[64,2048]{1,0:T(8,128)(2,1)S(1)}, bf16[64,2048]{1,0:T(8,128)(2,1)S(1)}, u32[]{:S(2)}, u32[]{:S(2)}) %collective-permute-start.38) | collective-permute-done | bytes 262176 | tf_op jit(solution)/shard_map/ppermute | solution.py:35
  187.6 1.7 output.1
  (114 shorter events, 15.0 us)
Async XLA Ops:
  0.0 34.9 %collective-permute-start.4 = (bf16[1,2048,768]{2,1,0:T(8,128)(2,1)}, bf16[1,2048,768]{2,1,0:T(8,128)(2,1)}, u32[]{:S(2)}, u32[]{:S(2)}) collective-permute-start(bf16[1,2048,768]{2,1,0:T(8,128)(2,1)} %refs_0_.1), channel_id=1, source_target_pairs={{0,1},{1,0},{2,3},{3,2},{4,5},{5,4},{6,7},{7,6},{8,9},{9,8},{10,11... | collective-permute-start | bytes 9437192 | tf_op jit(solution)/shard_map/ppermute | solution.py:312
  0.5 34.5 %collective-permute-start.5 = (bf16[1,2048,768]{2,1,0:T(8,128)(2,1)}, bf16[1,2048,768]{2,1,0:T(8,128)(2,1)}, u32[]{:S(2)}, u32[]{:S(2)}) collective-permute-start(bf16[1,2048,768]{2,1,0:T(8,128)(2,1)} %refs_1_.1), channel_id=1, source_target_pairs={{0,1},{1,0},{2,3},{3,2},{4,5},{5,4},{6,7},{7,6},{8,9},{9,8},{10,11... | collective-permute-start | bytes 9437192 | tf_op jit(solution)/shard_map/ppermute | solution.py:312
  0.5 34.4 %collective-permute-start.6 = (bf16[1,768,2048]{2,1,0:T(8,128)(2,1)}, bf16[1,768,2048]{2,1,0:T(8,128)(2,1)}, u32[]{:S(2)}, u32[]{:S(2)}) collective-permute-start(bf16[1,768,2048]{2,1,0:T(8,128)(2,1)} %refs_2_.1), channel_id=1, source_target_pairs={{0,1},{1,0},{2,3},{3,2},{4,5},{5,4},{6,7},{7,6},{8,9},{9,8},{10,11... | collective-permute-start | bytes 9437192 | tf_op jit(solution)/shard_map/ppermute | solution.py:312
  1.8 5.7 %copy-start.4 = (bf16[1,2048,768]{2,1,0:T(8,128)(2,1)S(1)}, bf16[1,2048,768]{2,1,0:T(8,128)(2,1)}, u32[]{:S(2)}) copy-start(bf16[1,2048,768]{2,1,0:T(8,128)(2,1)} %refs_0_.1) | copy-start | bytes 9437188
  3.3 8.7 %copy-start.7 = (bf16[64,4224]{1,0:T(8,128)(2,1)}, bf16[64,4224]{1,0:T(8,128)(2,1)S(1)}, u32[]{:S(2)}) copy-start(bf16[64,4224]{1,0:T(8,128)(2,1)S(1)} %pad_maximum_fusion.refs_0_) | copy-start | bytes 1622020
  3.3 12.8 %collective-permute-start.1 = (bf16[64,4224]{1,0:T(8,128)(2,1)S(1)}, bf16[64,4224]{1,0:T(8,128)(2,1)S(1)}, u32[]{:S(2)}, u32[]{:S(2)}) collective-permute-start(bf16[64,4224]{1,0:T(8,128)(2,1)S(1)} %pad_maximum_fusion.refs_0_), channel_id=1, source_target_pairs={{2,4},{3,5},{4,2},{5,3},{0,1},{1,0},{6,7},{7,6},{10,12},{11,13},{1... | collective-permute-start | bytes 1622024 | tf_op jit(solution)/shard_map/ppermute | solution.py:40
  3.4 16.8 %collective-permute-start = (bf16[64,4224]{1,0:T(8,128)(2,1)S(1)}, bf16[64,4224]{1,0:T(8,128)(2,1)S(1)}, u32[]{:S(2)}, u32[]{:S(2)}) collective-permute-start(bf16[64,4224]{1,0:T(8,128)(2,1)S(1)} %pad_maximum_fusion.refs_0_), channel_id=1, source_target_pairs={{0,2},{1,3},{2,0},{3,1},{4,6},{5,7},{6,4},{7,5},{8,10},{9,11},{10,... | collective-permute-start | bytes 1622024 | tf_op jit(solution)/shard_map/ppermute | solution.py:35
  7.5 1.9 copy-start.5
  9.4 1.9 copy-start.6
  20.2 13.9 %collective-permute-start.2 = (bf16[64,4224]{1,0:T(8,128)(2,1)S(1)}, bf16[64,4224]{1,0:T(8,128)(2,1)S(1)}, u32[]{:S(2)}, u32[]{:S(2)}) collective-permute-start(bf16[64,4224]{1,0:T(8,128)(2,1)S(1)} %collective-permute-done.1.refs_2_), channel_id=1, source_target_pairs={{0,2},{1,3},{2,0},{3,1},{4,6},{5,7},{6,4},{7,5},{8,10},{9,11},{10,... | collective-permute-start | bytes 1622024 | tf_op jit(solution)/shard_map/ppermute | solution.py:35
  22.7 12.2 %collective-permute-start.3 = (bf16[64,4224]{1,0:T(8,128)(2,1)S(1)}, bf16[64,4224]{1,0:T(8,128)(2,1)}, u32[]{:S(2)}, u32[]{:S(2)}) collective-permute-start(bf16[64,4224]{1,0:T(8,128)(2,1)S(1)} %collective-permute-done.refs_1_), channel_id=1, source_target_pairs={{2,4},{3,5},{4,2},{5,3},{0,1},{1,0},{6,7},{7,6},{10,12},{11,13},{1... | collective-permute-start | bytes 1622024 | tf_op jit(solution)/shard_map/ppermute | solution.py:40
  34.9 13.4 %collective-permute-start.7 = (bf16[64,4224]{1,0:T(8,128)(2,1)}, bf16[64,4224]{1,0:T(8,128)(2,1)}, u32[]{:S(2)}, u32[]{:S(2)}) collective-permute-start(bf16[64,4224]{1,0:T(8,128)(2,1)} %collective-permute-done.3.refs_4_), channel_id=1, source_target_pairs={{0,2},{1,3},{2,0},{3,1},{4,6},{5,7},{6,4},{7,5},{8,10},{9,11},{10,... | collective-permute-start | bytes 1622024 | tf_op jit(solution)/shard_map/ppermute | solution.py:35
  42.4 5.9 %copy-start.9 = (bf16[64,4224]{1,0:T(8,128)(2,1)S(1)}, bf16[64,4224]{1,0:T(8,128)(2,1)}, u32[]{:S(2)}) copy-start(bf16[64,4224]{1,0:T(8,128)(2,1)} %pad_maximum_fusion.1.refs_0_) | copy-start | bytes 1622020
  42.4 8.1 %copy-start.1 = (bf16[1,2048,768]{2,1,0:T(8,128)(2,1)S(1)}, bf16[1,2048,768]{2,1,0:T(8,128)(2,1)}, u32[]{:S(2)}) copy-start(bf16[1,2048,768]{2,1,0:T(8,128)(2,1)} %copy-done) | copy-start | bytes 9437188
  42.4 8.1 %copy-start.3 = (bf16[1,768,2048]{2,1,0:T(8,128)(2,1)S(1)}, bf16[1,768,2048]{2,1,0:T(8,128)(2,1)}, u32[]{:S(2)}) copy-start(bf16[1,768,2048]{2,1,0:T(8,128)(2,1)} %copy-done.2) | copy-start | bytes 9437188
  48.3 12.7 %collective-permute-start.9 = (bf16[64,4224]{1,0:T(8,128)(2,1)S(1)}, bf16[64,4224]{1,0:T(8,128)(2,1)S(1)}, u32[]{:S(2)}, u32[]{:S(2)}) collective-permute-start(bf16[64,4224]{1,0:T(8,128)(2,1)S(1)} %copy-done.9), channel_id=1, source_target_pairs={{2,4},{3,5},{4,2},{5,3},{0,1},{1,0},{6,7},{7,6},{10,12},{11,13},{1... | collective-permute-start | bytes 1622024 | tf_op jit(solution)/shard_map/ppermute | solution.py:40
  48.3 14.7 %collective-permute-start.8 = (bf16[64,4224]{1,0:T(8,128)(2,1)S(1)}, bf16[64,4224]{1,0:T(8,128)(2,1)S(1)}, u32[]{:S(2)}, u32[]{:S(2)}) collective-permute-start(bf16[64,4224]{1,0:T(8,128)(2,1)S(1)} %copy-done.9), channel_id=1, source_target_pairs={{0,2},{1,3},{2,0},{3,1},{4,6},{5,7},{6,4},{7,5},{8,10},{9,11},{10,... | collective-permute-start | bytes 1622024 | tf_op jit(solution)/shard_map/ppermute | solution.py:35
  63.1 13.8 %collective-permute-start.10 = (bf16[64,4224]{1,0:T(8,128)(2,1)S(1)}, bf16[64,4224]{1,0:T(8,128)(2,1)S(1)}, u32[]{:S(2)}, u32[]{:S(2)}) collective-permute-start(bf16[64,4224]{1,0:T(8,128)(2,1)S(1)} %pad_maximum_fusion.2), channel_id=1, source_target_pairs={{0,2},{1,3},{2,0},{3,1},{4,6},{5,7},{6,4},{7,5},{8,10},{9,11},{10,... | collective-permute-start | bytes 1622024 | tf_op jit(solution)/shard_map/ppermute | solution.py:35
  63.5 13.4 %collective-permute-start.11 = (bf16[64,4224]{1,0:T(8,128)(2,1)S(1)}, bf16[64,4224]{1,0:T(8,128)(2,1)S(1)}, u32[]{:S(2)}, u32[]{:S(2)}) collective-permute-start(bf16[64,4224]{1,0:T(8,128)(2,1)S(1)} %collective-permute-done.8.refs_1_), channel_id=1, source_target_pairs={{2,4},{3,5},{4,2},{5,3},{0,1},{1,0},{6,7},{7,6},{10,12},{11,13},{1... | collective-permute-start | bytes 1622024 | tf_op jit(solution)/shard_map/ppermute | solution.py:40
  77.0 12.9 %collective-permute-start.12 = (bf16[64,4224]{1,0:T(8,128)(2,1)S(1)}, bf16[64,4224]{1,0:T(8,128)(2,1)S(1)}, u32[]{:S(2)}, u32[]{:S(2)}) collective-permute-start(bf16[64,4224]{1,0:T(8,128)(2,1)S(1)} %pad_maximum_fusion.3), channel_id=1, source_target_pairs={{0,2},{1,3},{2,0},{3,1},{4,6},{5,7},{6,4},{7,5},{8,10},{9,11},{10,... | collective-permute-start | bytes 1622024 | tf_op jit(solution)/shard_map/ppermute | solution.py:35
  78.9 1.6 collective-permute-start.13
  89.9 7.2 %collective-permute-start.15 = (bf16[64,2048]{1,0:T(8,128)(2,1)S(1)}, bf16[64,2048]{1,0:T(8,128)(2,1)S(1)}, u32[]{:S(2)}, u32[]{:S(2)}) collective-permute-start(bf16[64,2048]{1,0:T(8,128)(2,1)S(1)} %add_convert_fusion.9), channel_id=1, source_target_pairs={{2,4},{3,5},{4,2},{5,3},{0,1},{1,0},{6,7},{7,6},{10,12},{11,13},{1... | collective-permute-start | bytes 786440 | tf_op jit(solution)/shard_map/ppermute | solution.py:40
  90.1 8.8 %copy-start.16 = (bf16[128,2048]{1,0:T(8,128)(2,1)S(1)}, bf16[128,2048]{1,0:T(8,128)(2,1)}, u32[]{:S(2)}) copy-start(bf16[128,2048]{1,0:T(8,128)(2,1)} %param.8) | copy-start | bytes 1572868
  90.1 8.8 %collective-permute-start.14 = (bf16[64,2048]{1,0:T(8,128)(2,1)S(1)}, bf16[64,2048]{1,0:T(8,128)(2,1)S(1)}, u32[]{:S(2)}, u32[]{:S(2)}) collective-permute-start(bf16[64,2048]{1,0:T(8,128)(2,1)S(1)} %fusion), channel_id=1, source_target_pairs={{0,2},{1,3},{2,0},{3,1},{4,6},{5,7},{6,4},{7,5},{8,10},{9,11},{10,... | collective-permute-start | bytes 786440 | tf_op jit(solution)/shard_map/ppermute | solution.py:35
  99.0 6.5 %collective-permute-start.17 = (bf16[64,2048]{1,0:T(8,128)(2,1)S(1)}, bf16[64,2048]{1,0:T(8,128)(2,1)S(1)}, u32[]{:S(2)}, u32[]{:S(2)}) collective-permute-start(bf16[64,2048]{1,0:T(8,128)(2,1)S(1)} %fusion.4.refs_0_), channel_id=1, source_target_pairs={{2,4},{3,5},{4,2},{5,3},{0,1},{1,0},{6,7},{7,6},{10,12},{11,13},{1... | collective-permute-start | bytes 786440 | tf_op jit(solution)/shard_map/ppermute | solution.py:40
  99.1 8.7 %collective-permute-start.16 = (bf16[64,2048]{1,0:T(8,128)(2,1)S(1)}, bf16[64,2048]{1,0:T(8,128)(2,1)S(1)}, u32[]{:S(2)}, u32[]{:S(2)}) collective-permute-start(bf16[64,2048]{1,0:T(8,128)(2,1)S(1)} %fusion.4.refs_0_), channel_id=1, source_target_pairs={{0,2},{1,3},{2,0},{3,1},{4,6},{5,7},{6,4},{7,5},{8,10},{9,11},{10,... | collective-permute-start | bytes 786440 | tf_op jit(solution)/shard_map/ppermute | solution.py:35
  107.9 7.9 %collective-permute-start.18 = (bf16[64,2048]{1,0:T(8,128)(2,1)S(1)}, bf16[64,2048]{1,0:T(8,128)(2,1)S(1)}, u32[]{:S(2)}, u32[]{:S(2)}) collective-permute-start(bf16[64,2048]{1,0:T(8,128)(2,1)S(1)} %broadcast_select_fusion.3), channel_id=1, source_target_pairs={{0,2},{1,3},{2,0},{3,1},{4,6},{5,7},{6,4},{7,5},{8,10},{9,11},{10,... | collective-permute-start | bytes 786440 | tf_op jit(solution)/shard_map/ppermute | solution.py:35
  108.2 7.6 %collective-permute-start.19 = (bf16[64,2048]{1,0:T(8,128)(2,1)S(1)}, bf16[64,2048]{1,0:T(8,128)(2,1)S(1)}, u32[]{:S(2)}, u32[]{:S(2)}) collective-permute-start(bf16[64,2048]{1,0:T(8,128)(2,1)S(1)} %collective-permute-done.16.refs_1_), channel_id=1, source_target_pairs={{2,4},{3,5},{4,2},{5,3},{0,1},{1,0},{6,7},{7,6},{10,12},{11,13},{1... | collective-permute-start | bytes 786440 | tf_op jit(solution)/shard_map/ppermute | solution.py:40
  115.9 7.0 %collective-permute-start.20 = (bf16[64,2048]{1,0:T(8,128)(2,1)S(1)}, bf16[64,2048]{1,0:T(8,128)(2,1)S(1)}, u32[]{:S(2)}, u32[]{:S(2)}) collective-permute-start(bf16[64,2048]{1,0:T(8,128)(2,1)S(1)} %broadcast_select_fusion.2), channel_id=1, source_target_pairs={{0,2},{1,3},{2,0},{3,1},{4,6},{5,7},{6,4},{7,5},{8,10},{9,11},{10,... | collective-permute-start | bytes 786440 | tf_op jit(solution)/shard_map/ppermute | solution.py:35
  117.7 5.2 %collective-permute-start.21 = (bf16[64,2048]{1,0:T(8,128)(2,1)S(1)}, bf16[64,2048]{1,0:T(8,128)(2,1)S(1)}, u32[]{:S(2)}, u32[]{:S(2)}) collective-permute-start(bf16[64,2048]{1,0:T(8,128)(2,1)S(1)} %add_convert_fusion.8), channel_id=1, source_target_pairs={{2,4},{3,5},{4,2},{5,3},{0,1},{1,0},{6,7},{7,6},{10,12},{11,13},{1... | collective-permute-start | bytes 786440 | tf_op jit(solution)/shard_map/ppermute | solution.py:40
  123.0 6.5 %collective-permute-start.23 = (bf16[64,2048]{1,0:T(8,128)(2,1)S(1)}, bf16[64,2048]{1,0:T(8,128)(2,1)S(1)}, u32[]{:S(2)}, u32[]{:S(2)}) collective-permute-start(bf16[64,2048]{1,0:T(8,128)(2,1)S(1)} %add_convert_fusion.6), channel_id=1, source_target_pairs={{2,4},{3,5},{4,2},{5,3},{0,1},{1,0},{6,7},{7,6},{10,12},{11,13},{1... | collective-permute-start | bytes 786440 | tf_op jit(solution)/shard_map/ppermute | solution.py:40
  123.2 8.8 %collective-permute-start.22 = (bf16[64,2048]{1,0:T(8,128)(2,1)S(1)}, bf16[64,2048]{1,0:T(8,128)(2,1)S(1)}, u32[]{:S(2)}, u32[]{:S(2)}) collective-permute-start(bf16[64,2048]{1,0:T(8,128)(2,1)S(1)} %fusion.1), channel_id=1, source_target_pairs={{0,2},{1,3},{2,0},{3,1},{4,6},{5,7},{6,4},{7,5},{8,10},{9,11},{10,... | collective-permute-start | bytes 786440 | tf_op jit(solution)/shard_map/ppermute | solution.py:35
  132.1 5.8 %collective-permute-start.25 = (bf16[64,2048]{1,0:T(8,128)(2,1)S(1)}, bf16[64,2048]{1,0:T(8,128)(2,1)S(1)}, u32[]{:S(2)}, u32[]{:S(2)}) collective-permute-start(bf16[64,2048]{1,0:T(8,128)(2,1)S(1)} %get-tuple-element.239.refs_0_), channel_id=1, source_target_pairs={{2,4},{3,5},{4,2},{5,3},{0,1},{1,0},{6,7},{7,6},{10,12},{11,13},{1... | collective-permute-start | bytes 786440 | tf_op jit(solution)/shard_map/ppermute | solution.py:40
  132.2 8.7 %collective-permute-start.24 = (bf16[64,2048]{1,0:T(8,128)(2,1)S(1)}, bf16[64,2048]{1,0:T(8,128)(2,1)S(1)}, u32[]{:S(2)}, u32[]{:S(2)}) collective-permute-start(bf16[64,2048]{1,0:T(8,128)(2,1)S(1)} %get-tuple-element.239.refs_0_), channel_id=1, source_target_pairs={{0,2},{1,3},{2,0},{3,1},{4,6},{5,7},{6,4},{7,5},{8,10},{9,11},{10,... | collective-permute-start | bytes 786440 | tf_op jit(solution)/shard_map/ppermute | solution.py:35
  141.0 7.9 %collective-permute-start.26 = (bf16[64,2048]{1,0:T(8,128)(2,1)S(1)}, bf16[64,2048]{1,0:T(8,128)(2,1)S(1)}, u32[]{:S(2)}, u32[]{:S(2)}) collective-permute-start(bf16[64,2048]{1,0:T(8,128)(2,1)S(1)} %broadcast_select_fusion.1), channel_id=1, source_target_pairs={{0,2},{1,3},{2,0},{3,1},{4,6},{5,7},{6,4},{7,5},{8,10},{9,11},{10,... | collective-permute-start | bytes 786440 | tf_op jit(solution)/shard_map/ppermute | solution.py:35
  141.3 7.6 %collective-permute-start.27 = (bf16[64,2048]{1,0:T(8,128)(2,1)S(1)}, bf16[64,2048]{1,0:T(8,128)(2,1)S(1)}, u32[]{:S(2)}, u32[]{:S(2)}) collective-permute-start(bf16[64,2048]{1,0:T(8,128)(2,1)S(1)} %collective-permute-done.24.refs_1_), channel_id=1, source_target_pairs={{2,4},{3,5},{4,2},{5,3},{0,1},{1,0},{6,7},{7,6},{10,12},{11,13},{1... | collective-permute-start | bytes 786440 | tf_op jit(solution)/shard_map/ppermute | solution.py:40
  149.0 7.0 %collective-permute-start.28 = (bf16[64,2048]{1,0:T(8,128)(2,1)S(1)}, bf16[64,2048]{1,0:T(8,128)(2,1)S(1)}, u32[]{:S(2)}, u32[]{:S(2)}) collective-permute-start(bf16[64,2048]{1,0:T(8,128)(2,1)S(1)} %broadcast_select_fusion), channel_id=1, source_target_pairs={{0,2},{1,3},{2,0},{3,1},{4,6},{5,7},{6,4},{7,5},{8,10},{9,11},{10,... | collective-permute-start | bytes 786440 | tf_op jit(solution)/shard_map/ppermute | solution.py:35
  150.8 5.2 %collective-permute-start.29 = (bf16[64,2048]{1,0:T(8,128)(2,1)S(1)}, bf16[64,2048]{1,0:T(8,128)(2,1)S(1)}, u32[]{:S(2)}, u32[]{:S(2)}) collective-permute-start(bf16[64,2048]{1,0:T(8,128)(2,1)S(1)} %add_convert_fusion.5), channel_id=1, source_target_pairs={{2,4},{3,5},{4,2},{5,3},{0,1},{1,0},{6,7},{7,6},{10,12},{11,13},{1... | collective-permute-start | bytes 786440 | tf_op jit(solution)/shard_map/ppermute | solution.py:40
  156.1 9.3 %collective-permute-start.31 = (bf16[64,2048]{1,0:T(8,128)(2,1)S(1)}, bf16[64,2048]{1,0:T(8,128)(2,1)S(1)}, u32[]{:S(2)}, u32[]{:S(2)}) collective-permute-start(bf16[64,2048]{1,0:T(8,128)(2,1)S(1)} %add_convert_fusion.3), channel_id=1, source_target_pairs={{2,4},{3,5},{4,2},{5,3},{0,1},{1,0},{6,7},{7,6},{10,12},{11,13},{1... | collective-permute-start | bytes 786440 | tf_op jit(solution)/shard_map/ppermute | solution.py:40
  156.3 9.1 %collective-permute-start.30 = (bf16[64,2048]{1,0:T(8,128)(2,1)S(1)}, bf16[64,2048]{1,0:T(8,128)(2,1)S(1)}, u32[]{:S(2)}, u32[]{:S(2)}) collective-permute-start(bf16[64,2048]{1,0:T(8,128)(2,1)S(1)} %fusion.2), channel_id=1, source_target_pairs={{0,2},{1,3},{2,0},{3,1},{4,6},{5,7},{6,4},{7,5},{8,10},{9,11},{10,... | collective-permute-start | bytes 786440 | tf_op jit(solution)/shard_map/ppermute | solution.py:35
  165.4 9.3 %collective-permute-start.32 = (bf16[64,2048]{1,0:T(8,128)(2,1)S(1)}, bf16[64,2048]{1,0:T(8,128)(2,1)S(1)}, u32[]{:S(2)}, u32[]{:S(2)}) collective-permute-start(bf16[64,2048]{1,0:T(8,128)(2,1)S(1)} %get-tuple-element.226), channel_id=1, source_target_pairs={{0,2},{1,3},{2,0},{3,1},{4,6},{5,7},{6,4},{7,5},{8,10},{9,11},{10,... | collective-permute-start | bytes 786440 | tf_op jit(solution)/shard_map/ppermute | solution.py:35
  165.5 1.2 collective-permute-start.33
  166.7 3.6 %collective-permute-start.34 = (f32[8,128]{1,0:T(8,128)S(1)}, f32[8,128]{1,0:T(8,128)S(1)}, u32[]{:S(2)}, u32[]{:S(2)}) collective-permute-start(f32[8,128]{1,0:T(8,128)S(1)} %add.94), channel_id=1, source_target_pairs={{0,8},{8,0},{16,24},{24,16},{1,9},{9,1},{17,25},{25,17},{2,10},{10... | collective-permute-start | bytes 12296 | tf_op jit(solution)/shard_map/ppermute | solution.py:219
  168.2 10.4 %collective-permute-start.36 = (bf16[64,2048]{1,0:T(8,128)(2,1)S(1)}, bf16[64,2048]{1,0:T(8,128)(2,1)S(1)}, u32[]{:S(2)}, u32[]{:S(2)}) collective-permute-start(bf16[64,2048]{1,0:T(8,128)(2,1)S(1)} %get-tuple-element.235), channel_id=1, source_target_pairs={{0,2},{1,3},{2,0},{3,1},{4,6},{5,7},{6,4},{7,5},{8,10},{9,11},{10,... | collective-permute-start | bytes 786440 | tf_op jit(solution)/shard_map/ppermute | solution.py:35
  174.8 3.8 %collective-permute-start.37 = (bf16[64,2048]{1,0:T(8,128)(2,1)S(1)}, bf16[64,2048]{1,0:T(8,128)(2,1)S(1)}, u32[]{:S(2)}, u32[]{:S(2)}) collective-permute-start(bf16[64,2048]{1,0:T(8,128)(2,1)S(1)} %add_convert_fusion.2), channel_id=1, source_target_pairs={{2,4},{3,5},{4,2},{5,3},{0,1},{1,0},{6,7},{7,6},{10,12},{11,13},{1... | collective-permute-start | bytes 786440 | tf_op jit(solution)/shard_map/ppermute | solution.py:40
  174.8 7.6 %collective-permute-start.35 = (f32[8,128]{1,0:T(8,128)S(1)}, f32[8,128]{1,0:T(8,128)S(1)}, u32[]{:S(2)}, u32[]{:S(2)}) collective-permute-start(f32[8,128]{1,0:T(8,128)S(1)} %add.95), channel_id=1, source_target_pairs={{0,16},{8,24},{16,0},{24,8},{1,17},{9,25},{17,1},{25,9},{2,18},{10... | collective-permute-start | bytes 12296 | tf_op jit(solution)/shard_map/ppermute | solution.py:219
  178.7 3.8 %collective-permute-start.39 = (bf16[64,2048]{1,0:T(8,128)(2,1)S(1)}, bf16[64,2048]{1,0:T(8,128)(2,1)S(1)}, u32[]{:S(2)}, u32[]{:S(2)}) collective-permute-start(bf16[64,2048]{1,0:T(8,128)(2,1)S(1)} %add_convert_fusion), channel_id=1, source_target_pairs={{2,4},{3,5},{4,2},{5,3},{0,1},{1,0},{6,7},{7,6},{10,12},{11,13},{1... | collective-permute-start | bytes 786440 | tf_op jit(solution)/shard_map/ppermute | solution.py:40
  178.8 8.8 %collective-permute-start.38 = (bf16[64,2048]{1,0:T(8,128)(2,1)S(1)}, bf16[64,2048]{1,0:T(8,128)(2,1)S(1)}, u32[]{:S(2)}, u32[]{:S(2)}) collective-permute-start(bf16[64,2048]{1,0:T(8,128)(2,1)S(1)} %fusion.3), channel_id=1, source_target_pairs={{0,2},{1,3},{2,0},{3,1},{4,6},{5,7},{6,4},{7,5},{8,10},{9,11},{10,... | collective-permute-start | bytes 786440 | tf_op jit(solution)/shard_map/ppermute | solution.py:35
  (9 other events, 9.9 us)

commit v8 on v7

--- a/solution.py
+++ b/solution.py
@@ -310,60 +310,60 @@
         return side_hop(first)
 
     sib = [lax.ppermute(w, "expert", swap) for w in (w_gate, w_up, w_down)]
-    a_side, a_near, own_weights, load_b = slot(
-        side_hop(load_a), inner_hop(load_a), load((w_gate, w_up, w_down)), load_b
-    )
-    a_near_end, a_far, sib, load_b = slot(side_hop(a_near), inner_hop(a_side), sib, load_b)
+    a_near, a_side, own_weights, load_b = slot(
+        inner_hop(load_a), side_hop(load_a), load((w_gate, w_up, w_down)), load_b
+    )
+    a_far, a_near_end, sib, load_b = slot(inner_hop(a_side), side_hop(a_near), sib, load_b)
     a_far_end, sib_weights, a_parts, load_b = slot(
         side_hop(a_far), load(sib), load((load_a, a_side, a_near, a_near_end, a_far)), load_b
     )
     weights = (own_weights, sib_weights)
 
     everyone = tuple(range(CORES))
-    b_side, b_near, (pa, states_a) = slot(
+    b_near, b_side, (pa, states_a) = slot(
+        inner_hop(load_b),
         side_hop(load_b),
-        inner_hop(load_b),
         forward((*a_parts, a_far_end), everyone),
     )
-    b_near_end, b_far = slot(both_ways(pa[3], b_near), inner_hop(b_side))
+    b_far, b_near_end = slot(inner_hop(b_side), both_ways(pa[3], b_near))
     sa_far = add_rows(pa[3], b_near_end[:, :width])
-    b_far_end, sa_side = slot(both_ways(pa[2], b_far), inner_hop(sa_far))
+    sa_side, b_far_end = slot(inner_hop(sa_far), both_ways(pa[2], b_far))
     sa_near = add_rows(pa[2], b_far_end[:, :width])
     b_parts = (load_b, b_side, b_near, b_near_end, b_far, b_far_end)
-    came, last, (sum_b, states_b) = slot(
-        both_ways(pa[1], add_rows(pa[1], sa_side)), inner_hop(sa_near), forward(b_parts, everyone[:1])
+    last, came, (sum_b, states_b) = slot(
+        inner_hop(sa_near), both_ways(pa[1], add_rows(pa[1], sa_side)), forward(b_parts, everyone[:1])
     )
     jv_a = tangent[:half].astype(jnp.float32) + home(pa, came, last)
 
     ja = jv_a.astype(jnp.bfloat16)
-    side, near, (pb, rest_b) = slot(
-        side_hop(ja), inner_hop(ja), forward(b_parts, everyone[1:], sum_b)
+    near, side, (pb, rest_b) = slot(
+        inner_hop(ja), side_hop(ja), forward(b_parts, everyone[1:], sum_b)
     )
     states_b = [*states_b, *rest_b]
-    near_end, far = slot(both_ways(pb[3], near), inner_hop(side))
+    far, near_end = slot(inner_hop(side), both_ways(pb[3], near))
     s_far = add_rows(pb[3], near_end)
-    far_end, s_side = slot(both_ways(pb[2], far), inner_hop(s_far))
+    s_side, far_end = slot(inner_hop(s_far), both_ways(pb[2], far))
     s_near = add_rows(pb[2], far_end)
     ja_parts = (ja, side, near, near_end, far, far_end)
-    came, last, (sum_a, squares_a) = slot(
+    last, came, (sum_a, squares_a) = slot(
+        inner_hop(s_near),
         both_ways(pb[1], add_rows(pb[1], s_side)),
-        inner_hop(s_near),
         backward(ja_parts, states_a, everyone[:1]),
     )
     jv_b = tangent[half:].astype(jnp.float32) + home(pb, came, last)
 
     jb = jv_b.astype(jnp.bfloat16)
-    side, near, (ga, _) = slot(
-        side_hop(jb), inner_hop(jb), backward(ja_parts, states_a, everyone[1:], earlier=sum_a)
-    )
-    near_end, far = slot(both_ways(ga[3], near), inner_hop(side))
+    near, side, (ga, _) = slot(
+        inner_hop(jb), side_hop(jb), backward(ja_parts, states_a, everyone[1:], earlier=sum_a)
+    )
+    far, near_end = slot(inner_hop(side), both_ways(ga[3], near))
     s_far = add_rows(ga[3], near_end)
-    far_end, s_side = slot(both_ways(ga[2], far), inner_hop(s_far))
+    s_side, far_end = slot(inner_hop(s_far), both_ways(ga[2], far))
     s_near = add_rows(ga[2], far_end)
     jb_parts = (jb, side, near, near_end, far, far_end)
-    came, last, (gb, squares_b) = slot(
+    last, came, (gb, squares_b) = slot(
+        inner_hop(s_near),
         both_ways(ga[1], add_rows(ga[1], s_side)),
-        inner_hop(s_near),
         backward(jb_parts, states_b, everyone),
     )
     whole_a = jv_a + home(ga, came, last)
@@ -375,7 +375,7 @@
         squares = exchange_sum(squares, "dp", step)
         step *= 2
     came, squares = slot(side_hop(gb[3]), squares)
-    came, s_side = slot(side_hop(gb[2]), inner_hop(add_rows(gb[3], came)))
+    s_side, came = slot(inner_hop(add_rows(gb[3], came)), side_hop(gb[2]))
     s_near = add_rows(gb[2], came)
     while step < lines:
         squares = exchange_sum(squares, "dp", step)

time: 190 us -> 186 us (0.979)
  waiting for transfers between devices: 91.1 us -> 75.8 us
  starting transfers between devices: 34.8 us -> 46.6 us
    ppermute x18, waiting for transfers between devices: 88.2 us -> 72.9 us  [side_hop(): return lax.ppermute(rows, 'expert', both_cores(SIDE_PAIRS))]
    ppermute x18, starting transfers between devices: 30 us -> 41.9 us  [side_hop(): return lax.ppermute(rows, 'expert', both_cores(SIDE_PAIRS))]
  transfers between devices with their start and end apart: 40 -> 40, of which waited for: 20 -> 19; matrix products, arithmetic and copies ran while one was open for 2% -> 2% of each run, Pallas kernels for 23% -> 23%
where the time goes in v8:
time: 186 us
  waiting for transfers between devices  75.8 us (41%)
  starting transfers between devices  46.6 us (25%)
  Pallas kernels  44.4 us (24%)
  local copies, waits for them, and re-layouts  15.3 us (8%)
  other arithmetic  3.3 us (2%)
    ppermute x18, waiting for transfers between devices, side_hop(): return lax.ppermute(rows, 'expert', both_cores(SIDE_PAIRS))  72.9 us
    ppermute x18, starting transfers between devices, side_hop(): return lax.ppermute(rows, 'expert', both_cores(SIDE_PAIRS))  41.9 us
    pallas_call x6, Pallas kernels, kernel_call(): pl.pallas_call(kernel, in_specs=[pl.BlockSpec(memory_space=pltpu.SMEM)] +...  36.8 us
    unnamed x34, local copies, waits for them, and re-layouts  13.7 us
    pallas_call x3, Pallas kernels, load(): pl.pallas_call(functools.partial(load_kernel, len(arrays)), in_specs=[pl....  5.89 us
  transfers between devices with their start and end apart: 40, of which 19 were waited for; matrix products, arithmetic and copies ran while one was open for 2% of the time, Pallas kernels for 23%

profile of v8, /device:TPU:0, one launch (start us, length us, event | category | flops | bytes accessed | tf_op | source)
XLA Modules:
  0.0 185.8 jit_solution(15115531891110674726)
XLA Ops:
  1.8 1.4 fusion.8
  3.3 2.6 %collective-permute-start.1 = (bf16[64,4224]{1,0:T(8,128)(2,1)S(1)}, bf16[64,4224]{1,0:T(8,128)(2,1)S(1)}, u32[]{:S(2)}, u32[]{:S(2)}) collective-permute-start(bf16[64,4224]{1,0:T(8,128)(2,1)S(1)} %pad_maximum_fusion.refs_0_), channel_id=1, source_target_pairs={{0,2},{1,3},{2,0},{3,1},{4,6},{5,7},{6,4},{7,5},{8,10},{9,11},{10,... | collective-permute-start | bytes 1622024 | tf_op jit(solution)/shard_map/ppermute | solution.py:35
  6.2 1.9 %copy-done.5 = bf16[1,2048,768]{2,1,0:T(8,128)(2,1)S(1)} copy-done((bf16[1,2048,768]{2,1,0:T(8,128)(2,1)S(1)}, bf16[1,2048,768]{2,1,0:T(8,128)(2,1)}, u32[]{:S(2)}) %copy-start.5) | copy-done | bytes 3145752
  8.1 1.9 %copy-done.6 = bf16[1,768,2048]{2,1,0:T(8,128)(2,1)S(1)} copy-done((bf16[1,768,2048]{2,1,0:T(8,128)(2,1)S(1)}, bf16[1,768,2048]{2,1,0:T(8,128)(2,1)}, u32[]{:S(2)}) %copy-start.6) | copy-done | bytes 3145752
  10.7 1.6 copy-done
  12.3 1.7 copy-done.2
  14.8 4.1 %collective-permute-done.1.refs_1_ = bf16[64,4224]{1,0:T(8,128)(2,1)S(1)} collective-permute-done((bf16[64,4224]{1,0:T(8,128)(2,1)S(1)}, bf16[64,4224]{1,0:T(8,128)(2,1)S(1)}, u32[]{:S(2)}, u32[]{:S(2)}) %collective-permute-start.1) | collective-permute-done | bytes 540704 | tf_op jit(solution)/shard_map/ppermute | solution.py:35
  19.7 4.6 %collective-permute-start.3 = (bf16[64,4224]{1,0:T(8,128)(2,1)S(1)}, bf16[64,4224]{1,0:T(8,128)(2,1)S(1)}, u32[]{:S(2)}, u32[]{:S(2)}) collective-permute-start(bf16[64,4224]{1,0:T(8,128)(2,1)S(1)} %collective-permute-done.refs_2_), channel_id=1, source_target_pairs={{0,2},{1,3},{2,0},{3,1},{4,6},{5,7},{6,4},{7,5},{8,10},{9,11},{10,... | collective-permute-start | bytes 1622024 | tf_op jit(solution)/shard_map/ppermute | solution.py:35
  25.1 10.8 %collective-permute-done.3.refs_3_ = bf16[64,4224]{1,0:T(8,128)(2,1)S(1)} collective-permute-done((bf16[64,4224]{1,0:T(8,128)(2,1)S(1)}, bf16[64,4224]{1,0:T(8,128)(2,1)S(1)}, u32[]{:S(2)}, u32[]{:S(2)}) %collective-permute-start.3) | collective-permute-done | bytes 540704 | tf_op jit(solution)/shard_map/ppermute | solution.py:35
  36.7 1.8 collective-permute-start.7
  42.8 1.3 load.5
  44.1 3.9 %load.4 = (bf16[1,2048,768]{2,1,0:T(8,128)(2,1)S(1)}, bf16[1,2048,768]{2,1,0:T(8,128)(2,1)S(1)}, bf16[1,768,2048]{2,1,0:T(8,128)(2,1)S(1)}) custom-call(bf16[1,2048,768]{2,1,0:T(8,128)(2,1)} %collective-permute-done.4.refs_0_, bf16[1,2048,768]{2,1,0:T(8,128)(2,1)} %collective-permute-done.5.refs_1_, bf16[1,768,2048]{2,1,0:T(8,128)(2,1)} %collective-permute-done.6.refs_2_), custom_call_target="tpu_custom_call" | custom-call | tf_op jit(solution)/shard_map/load/pallas_call | solution.py:206
  48.1 1.7 collective-permute-done.7.refs_5_
  49.8 1.5 collective-permute-start.9
  51.3 10.5 %forward.3 = (f32[64,2048]{1,0:T(8,128)S(1)}, bf16[64,2048]{1,0:T(8,128)(2,1)S(1)}, bf16[64,2048]{1,0:T(8,128)(2,1)S(1)}, bf16[64,2048]{1,0:T(8,128)(2,1)S(1)}, ...) custom-call(s32[3]{0:T(128)S(1)} %pad_add_fusion.where_ref, ...), custom_call_target="tpu_custom_call" | custom-call | flops 8053063680 | tf_op jit(solution)/shard_map/forward/pallas_call | solution.py:160
  61.9 3.7 %collective-permute-start.11 = (bf16[64,4224]{1,0:T(8,128)(2,1)S(1)}, bf16[64,4224]{1,0:T(8,128)(2,1)S(1)}, u32[]{:S(2)}, u32[]{:S(2)}) collective-permute-start(bf16[64,4224]{1,0:T(8,128)(2,1)S(1)} %pad_maximum_fusion.2), channel_id=1, source_target_pairs={{0,2},{1,3},{2,0},{3,1},{4,6},{5,7},{6,4},{7,5},{8,10},{9,11},{10,... | collective-permute-start | bytes 1622024 | tf_op jit(solution)/shard_map/ppermute | solution.py:35
  65.6 11.1 %collective-permute-done.11.refs_3_ = bf16[64,4224]{1,0:T(8,128)(2,1)S(1)} collective-permute-done((bf16[64,4224]{1,0:T(8,128)(2,1)S(1)}, bf16[64,4224]{1,0:T(8,128)(2,1)S(1)}, u32[]{:S(2)}, u32[]{:S(2)}) %collective-permute-start.11) | collective-permute-done | bytes 540704 | tf_op jit(solution)/shard_map/ppermute | solution.py:35
  76.8 1.8 collective-permute-start.13
  78.7 1.5 collective-permute-done.12
  80.2 8.8 %collective-permute-done.13.refs_5_ = bf16[64,4224]{1,0:T(8,128)(2,1)S(1)} collective-permute-done((bf16[64,4224]{1,0:T(8,128)(2,1)S(1)}, bf16[64,4224]{1,0:T(8,128)(2,1)S(1)}, u32[]{:S(2)}, u32[]{:S(2)}) %collective-permute-start.13) | collective-permute-done | bytes 540704 | tf_op jit(solution)/shard_map/ppermute | solution.py:35
  89.2 2.2 %collective-permute-start.15 = (bf16[64,2048]{1,0:T(8,128)(2,1)S(1)}, bf16[64,2048]{1,0:T(8,128)(2,1)S(1)}, u32[]{:S(2)}, u32[]{:S(2)}) collective-permute-start(bf16[64,2048]{1,0:T(8,128)(2,1)S(1)} %fusion), channel_id=1, source_target_pairs={{0,2},{1,3},{2,0},{3,1},{4,6},{5,7},{6,4},{7,5},{8,10},{9,11},{10,... | collective-permute-start | bytes 786440 | tf_op jit(solution)/shard_map/ppermute | solution.py:35
  91.5 5.5 %forward.4 = (f32[256,2048]{1,0:T(8,128)S(1)}, f32[256,768]{1,0:T(8,128)S(1)}, f32[256,768]{1,0:T(8,128)S(1)}) custom-call(s32[3]{0:T(128)S(1)} %pad_add_fusion.where_ref, bf16[64,4224]{1,0:T(8,128)(2,1)S(1)} %copy-done.9, bf16[64,4224]{1,0:T(8,128)(2,1)S(1)} %collective-permute-done.9.refs_1_, bf16[64,4224]{1,0:T(8,128)(2,1)S(1)} %collective-permute-done.8.refs_2_, ...), custom_call_target="tpu_custom_call" | custom-call | flops 4026531840 | tf_op jit(solution)/shard_map/forward/pallas_call | solution.py:160
  98.5 5.3 %forward.5 = (f32[64,2048]{1,0:T(8,128)S(1)}, bf16[64,2048]{1,0:T(8,128)(2,1)S(1)}, bf16[64,2048]{1,0:T(8,128)(2,1)S(1)}, bf16[64,2048]{1,0:T(8,128)(2,1)S(1)}, ...) custom-call(s32[3]{0:T(128)S(1)} %pad_add_fusion.where_ref, bf16[64,4224]{1,0:T(8,128)(2,1)S(1)} %copy-done.9, ...), custom_call_target="tpu_custom_call" | custom-call | flops 4026531840 | tf_op jit(solution)/shard_map/forward/pallas_call | solution.py:160
  103.8 2.2 %collective-permute-done.17.refs_1_ = bf16[64,2048]{1,0:T(8,128)(2,1)S(1)} collective-permute-done((bf16[64,2048]{1,0:T(8,128)(2,1)S(1)}, bf16[64,2048]{1,0:T(8,128)(2,1)S(1)}, u32[]{:S(2)}, u32[]{:S(2)}) %collective-permute-start.17) | collective-permute-done | bytes 262176 | tf_op jit(solution)/shard_map/ppermute | solution.py:35
  106.0 1.8 collective-permute-start.19
  107.8 5.1 %collective-permute-done.19.refs_3_ = bf16[64,2048]{1,0:T(8,128)(2,1)S(1)} collective-permute-done((bf16[64,2048]{1,0:T(8,128)(2,1)S(1)}, bf16[64,2048]{1,0:T(8,128)(2,1)S(1)}, u32[]{:S(2)}, u32[]{:S(2)}) %collective-permute-start.19) | collective-permute-done | bytes 262176 | tf_op jit(solution)/shard_map/ppermute | solution.py:35
  113.0 1.8 collective-permute-start.21
  114.8 4.6 %collective-permute-done.21.refs_5_ = bf16[64,2048]{1,0:T(8,128)(2,1)S(1)} collective-permute-done((bf16[64,2048]{1,0:T(8,128)(2,1)S(1)}, bf16[64,2048]{1,0:T(8,128)(2,1)S(1)}, u32[]{:S(2)}, u32[]{:S(2)}) %collective-permute-start.21) | collective-permute-done | bytes 262176 | tf_op jit(solution)/shard_map/ppermute | solution.py:35
  119.7 3.2 %collective-permute-start.23 = (bf16[64,2048]{1,0:T(8,128)(2,1)S(1)}, bf16[64,2048]{1,0:T(8,128)(2,1)S(1)}, u32[]{:S(2)}, u32[]{:S(2)}) collective-permute-start(bf16[64,2048]{1,0:T(8,128)(2,1)S(1)} %fusion.1), channel_id=1, source_target_pairs={{0,2},{1,3},{2,0},{3,1},{4,6},{5,7},{6,4},{7,5},{8,10},{9,11},{10,... | collective-permute-start | bytes 786440 | tf_op jit(solution)/shard_map/ppermute | solution.py:35
  122.9 4.2 %backward.3 = (f32[256,2048]{1,0:T(8,128)S(1)}, f32[8,128]{1,0:T(8,128)S(1)}) custom-call(s32[3]{0:T(128)S(1)} %pad_add_fusion.where_ref, bf16[64,2048]{1,0:T(8,128)(2,1)S(1)} %fusion.4.refs_0_, bf16[64,2048]{1,0:T(8,128)(2,1)S(1)} %collective-permute-done.17.refs_1_, bf16[64,2048]{1,0:T(8,128)(2,1)S(1)} %collective-permute-done.16.refs_2_, ...), custom_call_target="tpu_custom_call" | custom-call | flops 2415919104 | tf_op jit(solution)/shard_map/backward/pallas_call | solution.py:160
  127.1 1.3 collective-permute-done.23
  129.4 4.3 %backward.4 = (f32[64,2048]{1,0:T(8,128)S(1)}, bf16[64,2048]{1,0:T(8,128)(2,1)S(1)}, bf16[64,2048]{1,0:T(8,128)(2,1)S(1)}, bf16[64,2048]{1,0:T(8,128)(2,1)S(1)}) custom-call(s32[3]{0:T(128)S(1)} %pad_add_fusion.where_ref, bf16[64,2048]{1,0:T(8,128)(2,1)S(1)} %fusion.4.refs_0_, bf16[64,2048]{1,0:T(8,128)(2,1)S(1)} %collective-permute-done.17.refs_1_, ...), custom_call_target="tpu_custom_call" | custom-call | flops 2415919104 | tf_op jit(solution)/shard_map/backward/pallas_call | solution.py:160
  133.7 1.6 collective-permute-done.25.refs_1_
  135.3 1.9 %collective-permute-start.27 = (bf16[64,2048]{1,0:T(8,128)(2,1)S(1)}, bf16[64,2048]{1,0:T(8,128)(2,1)S(1)}, u32[]{:S(2)}, u32[]{:S(2)}) collective-permute-start(bf16[64,2048]{1,0:T(8,128)(2,1)S(1)} %broadcast_select_fusion.1), channel_id=1, source_target_pairs={{0,2},{1,3},{2,0},{3,1},{4,6},{5,7},{6,4},{7,5},{8,10},{9,11},{10,... | collective-permute-start | bytes 786440 | tf_op jit(solution)/shard_map/ppermute | solution.py:35
  137.3 5.3 %collective-permute-done.27.refs_3_ = bf16[64,2048]{1,0:T(8,128)(2,1)S(1)} collective-permute-done((bf16[64,2048]{1,0:T(8,128)(2,1)S(1)}, bf16[64,2048]{1,0:T(8,128)(2,1)S(1)}, u32[]{:S(2)}, u32[]{:S(2)}) %collective-permute-start.27) | collective-permute-done | bytes 262176 | tf_op jit(solution)/shard_map/ppermute | solution.py:35
  142.7 3.4 %collective-permute-start.29 = (bf16[64,2048]{1,0:T(8,128)(2,1)S(1)}, bf16[64,2048]{1,0:T(8,128)(2,1)S(1)}, u32[]{:S(2)}, u32[]{:S(2)}) collective-permute-start(bf16[64,2048]{1,0:T(8,128)(2,1)S(1)} %broadcast_select_fusion), channel_id=1, source_target_pairs={{0,2},{1,3},{2,0},{3,1},{4,6},{5,7},{6,4},{7,5},{8,10},{9,11},{10,... | collective-permute-start | bytes 786440 | tf_op jit(solution)/shard_map/ppermute | solution.py:35
  146.1 5.9 %collective-permute-done.29.refs_5_ = bf16[64,2048]{1,0:T(8,128)(2,1)S(1)} collective-permute-done((bf16[64,2048]{1,0:T(8,128)(2,1)S(1)}, bf16[64,2048]{1,0:T(8,128)(2,1)S(1)}, u32[]{:S(2)}, u32[]{:S(2)}) %collective-permute-start.29) | collective-permute-done | bytes 262176 | tf_op jit(solution)/shard_map/ppermute | solution.py:35
  152.2 3.7 %collective-permute-start.31 = (bf16[64,2048]{1,0:T(8,128)(2,1)S(1)}, bf16[64,2048]{1,0:T(8,128)(2,1)S(1)}, u32[]{:S(2)}, u32[]{:S(2)}) collective-permute-start(bf16[64,2048]{1,0:T(8,128)(2,1)S(1)} %fusion.2), channel_id=1, source_target_pairs={{0,2},{1,3},{2,0},{3,1},{4,6},{5,7},{6,4},{7,5},{8,10},{9,11},{10,... | collective-permute-start | bytes 786440 | tf_op jit(solution)/shard_map/ppermute | solution.py:35
  155.9 7.0 %backward.5 = (f32[64,2048]{1,0:T(8,128)S(1)}, bf16[64,2048]{1,0:T(8,128)(2,1)S(1)}, bf16[64,2048]{1,0:T(8,128)(2,1)S(1)}, bf16[64,2048]{1,0:T(8,128)(2,1)S(1)}, f32[8,128]{1,0:T(8,128)S(1)}) custom-call(s32[3]{0:T(128)S(1)} %pad_add_fusion.where_ref, bf16[64,2048]{1,0:T(8,128)(2,1)S(1)} %get-tuple-element.239.refs_0_, ...), custom_call_target="tpu_custom_call" | custom-call | flops 4831838208 | tf_op jit(solution)/shard_map/backward/pallas_call | solution.py:160
  163.1 1.2 collective-permute-done.33
  164.3 1.5 collective-permute-start.34
  165.7 1.9 %collective-permute-start.37 = (bf16[64,2048]{1,0:T(8,128)(2,1)S(1)}, bf16[64,2048]{1,0:T(8,128)(2,1)S(1)}, u32[]{:S(2)}, u32[]{:S(2)}) collective-permute-start(bf16[64,2048]{1,0:T(8,128)(2,1)S(1)} %get-tuple-element.236), channel_id=1, source_target_pairs={{0,2},{1,3},{2,0},{3,1},{4,6},{5,7},{6,4},{7,5},{8,10},{9,11},{10,... | collective-permute-start | bytes 786440 | tf_op jit(solution)/shard_map/ppermute | solution.py:35
  167.9 2.4 %collective-permute-done.32 = bf16[64,2048]{1,0:T(8,128)(2,1)S(1)} collective-permute-done((bf16[64,2048]{1,0:T(8,128)(2,1)S(1)}, bf16[64,2048]{1,0:T(8,128)(2,1)S(1)}, u32[]{:S(2)}, u32[]{:S(2)}) %collective-permute-start.32) | collective-permute-done | bytes 262176 | tf_op jit(solution)/shard_map/ppermute | solution.py:35
  170.4 1.5 collective-permute-start.35
  172.0 3.0 %collective-permute-done.37 = bf16[64,2048]{1,0:T(8,128)(2,1)S(1)} collective-permute-done((bf16[64,2048]{1,0:T(8,128)(2,1)S(1)}, bf16[64,2048]{1,0:T(8,128)(2,1)S(1)}, u32[]{:S(2)}, u32[]{:S(2)}) %collective-permute-start.37) | collective-permute-done | bytes 262176 | tf_op jit(solution)/shard_map/ppermute | solution.py:35
  175.2 4.5 %collective-permute-start.38 = (bf16[64,2048]{1,0:T(8,128)(2,1)S(1)}, bf16[64,2048]{1,0:T(8,128)(2,1)S(1)}, u32[]{:S(2)}, u32[]{:S(2)}) collective-permute-start(bf16[64,2048]{1,0:T(8,128)(2,1)S(1)} %fusion.3), channel_id=1, source_target_pairs={{0,2},{1,3},{2,0},{3,1},{4,6},{5,7},{6,4},{7,5},{8,10},{9,11},{10,... | collective-permute-start | bytes 786440 | tf_op jit(solution)/shard_map/ppermute | solution.py:35
  180.0 4.1 %collective-permute-done.38.side = bf16[64,2048]{1,0:T(8,128)(2,1)S(1)} collective-permute-done((bf16[64,2048]{1,0:T(8,128)(2,1)S(1)}, bf16[64,2048]{1,0:T(8,128)(2,1)S(1)}, u32[]{:S(2)}, u32[]{:S(2)}) %collective-permute-start.38) | collective-permute-done | bytes 262176 | tf_op jit(solution)/shard_map/ppermute | solution.py:35
  184.1 1.7 output.1
  (114 shorter events, 15.1 us)
Async XLA Ops:
  0.0 36.7 %collective-permute-start.4 = (bf16[1,2048,768]{2,1,0:T(8,128)(2,1)}, bf16[1,2048,768]{2,1,0:T(8,128)(2,1)}, u32[]{:S(2)}, u32[]{:S(2)}) collective-permute-start(bf16[1,2048,768]{2,1,0:T(8,128)(2,1)} %refs_0_.1), channel_id=1, source_target_pairs={{0,1},{1,0},{2,3},{3,2},{4,5},{5,4},{6,7},{7,6},{8,9},{9,8},{10,11... | collective-permute-start | bytes 9437192 | tf_op jit(solution)/shard_map/ppermute | solution.py:312
  0.5 36.2 %collective-permute-start.5 = (bf16[1,2048,768]{2,1,0:T(8,128)(2,1)}, bf16[1,2048,768]{2,1,0:T(8,128)(2,1)}, u32[]{:S(2)}, u32[]{:S(2)}) collective-permute-start(bf16[1,2048,768]{2,1,0:T(8,128)(2,1)} %refs_1_.1), channel_id=1, source_target_pairs={{0,1},{1,0},{2,3},{3,2},{4,5},{5,4},{6,7},{7,6},{8,9},{9,8},{10,11... | collective-permute-start | bytes 9437192 | tf_op jit(solution)/shard_map/ppermute | solution.py:312
  0.5 36.2 %collective-permute-start.6 = (bf16[1,768,2048]{2,1,0:T(8,128)(2,1)}, bf16[1,768,2048]{2,1,0:T(8,128)(2,1)}, u32[]{:S(2)}, u32[]{:S(2)}) collective-permute-start(bf16[1,768,2048]{2,1,0:T(8,128)(2,1)} %refs_2_.1), channel_id=1, source_target_pairs={{0,1},{1,0},{2,3},{3,2},{4,5},{5,4},{6,7},{7,6},{8,9},{9,8},{10,11... | collective-permute-start | bytes 9437192 | tf_op jit(solution)/shard_map/ppermute | solution.py:312
  1.8 4.4 %copy-start.4 = (bf16[1,2048,768]{2,1,0:T(8,128)(2,1)S(1)}, bf16[1,2048,768]{2,1,0:T(8,128)(2,1)}, u32[]{:S(2)}) copy-start(bf16[1,2048,768]{2,1,0:T(8,128)(2,1)} %refs_0_.1) | copy-start | bytes 9437188
  3.3 7.3 %copy-start.7 = (bf16[64,4224]{1,0:T(8,128)(2,1)}, bf16[64,4224]{1,0:T(8,128)(2,1)S(1)}, u32[]{:S(2)}) copy-start(bf16[64,4224]{1,0:T(8,128)(2,1)S(1)} %pad_maximum_fusion.refs_0_) | copy-start | bytes 1622020
  3.3 15.6 %collective-permute-start.1 = (bf16[64,4224]{1,0:T(8,128)(2,1)S(1)}, bf16[64,4224]{1,0:T(8,128)(2,1)S(1)}, u32[]{:S(2)}, u32[]{:S(2)}) collective-permute-start(bf16[64,4224]{1,0:T(8,128)(2,1)S(1)} %pad_maximum_fusion.refs_0_), channel_id=1, source_target_pairs={{0,2},{1,3},{2,0},{3,1},{4,6},{5,7},{6,4},{7,5},{8,10},{9,11},{10,... | collective-permute-start | bytes 1622024 | tf_op jit(solution)/shard_map/ppermute | solution.py:35
  6.0 12.9 %collective-permute-start = (bf16[64,4224]{1,0:T(8,128)(2,1)S(1)}, bf16[64,4224]{1,0:T(8,128)(2,1)S(1)}, u32[]{:S(2)}, u32[]{:S(2)}) collective-permute-start(bf16[64,4224]{1,0:T(8,128)(2,1)S(1)} %pad_maximum_fusion.refs_0_), channel_id=1, source_target_pairs={{2,4},{3,5},{4,2},{5,3},{0,1},{1,0},{6,7},{7,6},{10,12},{11,13},{1... | collective-permute-start | bytes 1622024 | tf_op jit(solution)/shard_map/ppermute | solution.py:40
  6.2 1.9 %copy-start.5 = (bf16[1,2048,768]{2,1,0:T(8,128)(2,1)S(1)}, bf16[1,2048,768]{2,1,0:T(8,128)(2,1)}, u32[]{:S(2)}) copy-start(bf16[1,2048,768]{2,1,0:T(8,128)(2,1)} %refs_1_.1) | copy-start | bytes 9437188
  8.1 1.9 %copy-start.6 = (bf16[1,768,2048]{2,1,0:T(8,128)(2,1)S(1)}, bf16[1,768,2048]{2,1,0:T(8,128)(2,1)}, u32[]{:S(2)}) copy-start(bf16[1,768,2048]{2,1,0:T(8,128)(2,1)} %refs_2_.1) | copy-start | bytes 9437188
  18.9 6.2 %collective-permute-start.2 = (bf16[64,4224]{1,0:T(8,128)(2,1)S(1)}, bf16[64,4224]{1,0:T(8,128)(2,1)}, u32[]{:S(2)}, u32[]{:S(2)}) collective-permute-start(bf16[64,4224]{1,0:T(8,128)(2,1)S(1)} %collective-permute-done.1.refs_1_), channel_id=1, source_target_pairs={{2,4},{3,5},{4,2},{5,3},{0,1},{1,0},{6,7},{7,6},{10,12},{11,13},{1... | collective-permute-start | bytes 1622024 | tf_op jit(solution)/shard_map/ppermute | solution.py:40
  19.7 16.2 %collective-permute-start.3 = (bf16[64,4224]{1,0:T(8,128)(2,1)S(1)}, bf16[64,4224]{1,0:T(8,128)(2,1)S(1)}, u32[]{:S(2)}, u32[]{:S(2)}) collective-permute-start(bf16[64,4224]{1,0:T(8,128)(2,1)S(1)} %collective-permute-done.refs_2_), channel_id=1, source_target_pairs={{0,2},{1,3},{2,0},{3,1},{4,6},{5,7},{6,4},{7,5},{8,10},{9,11},{10,... | collective-permute-start | bytes 1622024 | tf_op jit(solution)/shard_map/ppermute | solution.py:35
  36.7 13.0 %collective-permute-start.7 = (bf16[64,4224]{1,0:T(8,128)(2,1)}, bf16[64,4224]{1,0:T(8,128)(2,1)}, u32[]{:S(2)}, u32[]{:S(2)}) collective-permute-start(bf16[64,4224]{1,0:T(8,128)(2,1)} %collective-permute-done.2.refs_4_), channel_id=1, source_target_pairs={{0,2},{1,3},{2,0},{3,1},{4,6},{5,7},{6,4},{7,5},{8,10},{9,11},{10,... | collective-permute-start | bytes 1622024 | tf_op jit(solution)/shard_map/ppermute | solution.py:35
  44.1 5.7 %copy-start.9 = (bf16[64,4224]{1,0:T(8,128)(2,1)S(1)}, bf16[64,4224]{1,0:T(8,128)(2,1)}, u32[]{:S(2)}) copy-start(bf16[64,4224]{1,0:T(8,128)(2,1)} %pad_maximum_fusion.1.refs_0_) | copy-start | bytes 1622020
  44.1 7.2 %copy-start.1 = (bf16[1,2048,768]{2,1,0:T(8,128)(2,1)S(1)}, bf16[1,2048,768]{2,1,0:T(8,128)(2,1)}, u32[]{:S(2)}) copy-start(bf16[1,2048,768]{2,1,0:T(8,128)(2,1)} %copy-done) | copy-start | bytes 9437188
  44.1 7.2 %copy-start.3 = (bf16[1,768,2048]{2,1,0:T(8,128)(2,1)S(1)}, bf16[1,768,2048]{2,1,0:T(8,128)(2,1)}, u32[]{:S(2)}) copy-start(bf16[1,768,2048]{2,1,0:T(8,128)(2,1)} %copy-done.2) | copy-start | bytes 9437188
  49.8 12.0 %collective-permute-start.9 = (bf16[64,4224]{1,0:T(8,128)(2,1)S(1)}, bf16[64,4224]{1,0:T(8,128)(2,1)S(1)}, u32[]{:S(2)}, u32[]{:S(2)}) collective-permute-start(bf16[64,4224]{1,0:T(8,128)(2,1)S(1)} %copy-done.9), channel_id=1, source_target_pairs={{0,2},{1,3},{2,0},{3,1},{4,6},{5,7},{6,4},{7,5},{8,10},{9,11},{10,... | collective-permute-start | bytes 1622024 | tf_op jit(solution)/shard_map/ppermute | solution.py:35
  51.3 10.5 %collective-permute-start.8 = (bf16[64,4224]{1,0:T(8,128)(2,1)S(1)}, bf16[64,4224]{1,0:T(8,128)(2,1)S(1)}, u32[]{:S(2)}, u32[]{:S(2)}) collective-permute-start(bf16[64,4224]{1,0:T(8,128)(2,1)S(1)} %copy-done.9), channel_id=1, source_target_pairs={{2,4},{3,5},{4,2},{5,3},{0,1},{1,0},{6,7},{7,6},{10,12},{11,13},{1... | collective-permute-start | bytes 1622024 | tf_op jit(solution)/shard_map/ppermute | solution.py:40
  61.9 14.7 %collective-permute-start.11 = (bf16[64,4224]{1,0:T(8,128)(2,1)S(1)}, bf16[64,4224]{1,0:T(8,128)(2,1)S(1)}, u32[]{:S(2)}, u32[]{:S(2)}) collective-permute-start(bf16[64,4224]{1,0:T(8,128)(2,1)S(1)} %pad_maximum_fusion.2), channel_id=1, source_target_pairs={{0,2},{1,3},{2,0},{3,1},{4,6},{5,7},{6,4},{7,5},{8,10},{9,11},{10,... | collective-permute-start | bytes 1622024 | tf_op jit(solution)/shard_map/ppermute | solution.py:35
  65.6 11.1 %collective-permute-start.10 = (bf16[64,4224]{1,0:T(8,128)(2,1)S(1)}, bf16[64,4224]{1,0:T(8,128)(2,1)S(1)}, u32[]{:S(2)}, u32[]{:S(2)}) collective-permute-start(bf16[64,4224]{1,0:T(8,128)(2,1)S(1)} %collective-permute-done.9.refs_1_), channel_id=1, source_target_pairs={{2,4},{3,5},{4,2},{5,3},{0,1},{1,0},{6,7},{7,6},{10,12},{11,13},{1... | collective-permute-start | bytes 1622024 | tf_op jit(solution)/shard_map/ppermute | solution.py:40
  76.8 12.2 %collective-permute-start.13 = (bf16[64,4224]{1,0:T(8,128)(2,1)S(1)}, bf16[64,4224]{1,0:T(8,128)(2,1)S(1)}, u32[]{:S(2)}, u32[]{:S(2)}) collective-permute-start(bf16[64,4224]{1,0:T(8,128)(2,1)S(1)} %pad_maximum_fusion.3), channel_id=1, source_target_pairs={{0,2},{1,3},{2,0},{3,1},{4,6},{5,7},{6,4},{7,5},{8,10},{9,11},{10,... | collective-permute-start | bytes 1622024 | tf_op jit(solution)/shard_map/ppermute | solution.py:35
  78.6 1.6 collective-permute-start.12
  89.0 7.9 %collective-permute-start.14 = (bf16[64,2048]{1,0:T(8,128)(2,1)S(1)}, bf16[64,2048]{1,0:T(8,128)(2,1)S(1)}, u32[]{:S(2)}, u32[]{:S(2)}) collective-permute-start(bf16[64,2048]{1,0:T(8,128)(2,1)S(1)} %add_convert_fusion.10), channel_id=1, source_target_pairs={{2,4},{3,5},{4,2},{5,3},{0,1},{1,0},{6,7},{7,6},{10,12},{11,13},{1... | collective-permute-start | bytes 786440 | tf_op jit(solution)/shard_map/ppermute | solution.py:40
  89.2 8.8 %copy-start.16 = (bf16[128,2048]{1,0:T(8,128)(2,1)S(1)}, bf16[128,2048]{1,0:T(8,128)(2,1)}, u32[]{:S(2)}) copy-start(bf16[128,2048]{1,0:T(8,128)(2,1)} %param.8) | copy-start | bytes 1572868
  89.2 8.8 %collective-permute-start.15 = (bf16[64,2048]{1,0:T(8,128)(2,1)S(1)}, bf16[64,2048]{1,0:T(8,128)(2,1)S(1)}, u32[]{:S(2)}, u32[]{:S(2)}) collective-permute-start(bf16[64,2048]{1,0:T(8,128)(2,1)S(1)} %fusion), channel_id=1, source_target_pairs={{0,2},{1,3},{2,0},{3,1},{4,6},{5,7},{6,4},{7,5},{8,10},{9,11},{10,... | collective-permute-start | bytes 786440 | tf_op jit(solution)/shard_map/ppermute | solution.py:35
  98.1 7.8 %collective-permute-start.17 = (bf16[64,2048]{1,0:T(8,128)(2,1)S(1)}, bf16[64,2048]{1,0:T(8,128)(2,1)S(1)}, u32[]{:S(2)}, u32[]{:S(2)}) collective-permute-start(bf16[64,2048]{1,0:T(8,128)(2,1)S(1)} %fusion.4.refs_0_), channel_id=1, source_target_pairs={{0,2},{1,3},{2,0},{3,1},{4,6},{5,7},{6,4},{7,5},{8,10},{9,11},{10,... | collective-permute-start | bytes 786440 | tf_op jit(solution)/shard_map/ppermute | solution.py:35
  98.5 7.5 %collective-permute-start.16 = (bf16[64,2048]{1,0:T(8,128)(2,1)S(1)}, bf16[64,2048]{1,0:T(8,128)(2,1)S(1)}, u32[]{:S(2)}, u32[]{:S(2)}) collective-permute-start(bf16[64,2048]{1,0:T(8,128)(2,1)S(1)} %fusion.4.refs_0_), channel_id=1, source_target_pairs={{2,4},{3,5},{4,2},{5,3},{0,1},{1,0},{6,7},{7,6},{10,12},{11,13},{1... | collective-permute-start | bytes 786440 | tf_op jit(solution)/shard_map/ppermute | solution.py:40
  106.0 6.9 %collective-permute-start.19 = (bf16[64,2048]{1,0:T(8,128)(2,1)S(1)}, bf16[64,2048]{1,0:T(8,128)(2,1)S(1)}, u32[]{:S(2)}, u32[]{:S(2)}) collective-permute-start(bf16[64,2048]{1,0:T(8,128)(2,1)S(1)} %broadcast_select_fusion.3), channel_id=1, source_target_pairs={{0,2},{1,3},{2,0},{3,1},{4,6},{5,7},{6,4},{7,5},{8,10},{9,11},{10,... | collective-permute-start | bytes 786440 | tf_op jit(solution)/shard_map/ppermute | solution.py:35
  107.8 5.1 %collective-permute-start.18 = (bf16[64,2048]{1,0:T(8,128)(2,1)S(1)}, bf16[64,2048]{1,0:T(8,128)(2,1)S(1)}, u32[]{:S(2)}, u32[]{:S(2)}) collective-permute-start(bf16[64,2048]{1,0:T(8,128)(2,1)S(1)} %collective-permute-done.17.refs_1_), channel_id=1, source_target_pairs={{2,4},{3,5},{4,2},{5,3},{0,1},{1,0},{6,7},{7,6},{10,12},{11,13},{1... | collective-permute-start | bytes 786440 | tf_op jit(solution)/shard_map/ppermute | solution.py:40
  113.0 6.4 %collective-permute-start.21 = (bf16[64,2048]{1,0:T(8,128)(2,1)S(1)}, bf16[64,2048]{1,0:T(8,128)(2,1)S(1)}, u32[]{:S(2)}, u32[]{:S(2)}) collective-permute-start(bf16[64,2048]{1,0:T(8,128)(2,1)S(1)} %broadcast_select_fusion.2), channel_id=1, source_target_pairs={{0,2},{1,3},{2,0},{3,1},{4,6},{5,7},{6,4},{7,5},{8,10},{9,11},{10,... | collective-permute-start | bytes 786440 | tf_op jit(solution)/shard_map/ppermute | solution.py:35
  114.8 4.6 %collective-permute-start.20 = (bf16[64,2048]{1,0:T(8,128)(2,1)S(1)}, bf16[64,2048]{1,0:T(8,128)(2,1)S(1)}, u32[]{:S(2)}, u32[]{:S(2)}) collective-permute-start(bf16[64,2048]{1,0:T(8,128)(2,1)S(1)} %add_convert_fusion.8), channel_id=1, source_target_pairs={{2,4},{3,5},{4,2},{5,3},{0,1},{1,0},{6,7},{7,6},{10,12},{11,13},{1... | collective-permute-start | bytes 786440 | tf_op jit(solution)/shard_map/ppermute | solution.py:40
  119.5 7.6 %collective-permute-start.22 = (bf16[64,2048]{1,0:T(8,128)(2,1)S(1)}, bf16[64,2048]{1,0:T(8,128)(2,1)S(1)}, u32[]{:S(2)}, u32[]{:S(2)}) collective-permute-start(bf16[64,2048]{1,0:T(8,128)(2,1)S(1)} %add_convert_fusion.7), channel_id=1, source_target_pairs={{2,4},{3,5},{4,2},{5,3},{0,1},{1,0},{6,7},{7,6},{10,12},{11,13},{1... | collective-permute-start | bytes 786440 | tf_op jit(solution)/shard_map/ppermute | solution.py:40
  119.7 8.8 %collective-permute-start.23 = (bf16[64,2048]{1,0:T(8,128)(2,1)S(1)}, bf16[64,2048]{1,0:T(8,128)(2,1)S(1)}, u32[]{:S(2)}, u32[]{:S(2)}) collective-permute-start(bf16[64,2048]{1,0:T(8,128)(2,1)S(1)} %fusion.1), channel_id=1, source_target_pairs={{0,2},{1,3},{2,0},{3,1},{4,6},{5,7},{6,4},{7,5},{8,10},{9,11},{10,... | collective-permute-start | bytes 786440 | tf_op jit(solution)/shard_map/ppermute | solution.py:35
  128.6 6.7 %collective-permute-start.25 = (bf16[64,2048]{1,0:T(8,128)(2,1)S(1)}, bf16[64,2048]{1,0:T(8,128)(2,1)S(1)}, u32[]{:S(2)}, u32[]{:S(2)}) collective-permute-start(bf16[64,2048]{1,0:T(8,128)(2,1)S(1)} %get-tuple-element.239.refs_0_), channel_id=1, source_target_pairs={{0,2},{1,3},{2,0},{3,1},{4,6},{5,7},{6,4},{7,5},{8,10},{9,11},{10,... | collective-permute-start | bytes 786440 | tf_op jit(solution)/shard_map/ppermute | solution.py:35
  129.4 5.9 %collective-permute-start.24 = (bf16[64,2048]{1,0:T(8,128)(2,1)S(1)}, bf16[64,2048]{1,0:T(8,128)(2,1)S(1)}, u32[]{:S(2)}, u32[]{:S(2)}) collective-permute-start(bf16[64,2048]{1,0:T(8,128)(2,1)S(1)} %get-tuple-element.239.refs_0_), channel_id=1, source_target_pairs={{2,4},{3,5},{4,2},{5,3},{0,1},{1,0},{6,7},{7,6},{10,12},{11,13},{1... | collective-permute-start | bytes 786440 | tf_op jit(solution)/shard_map/ppermute | solution.py:40
  135.3 7.2 %collective-permute-start.27 = (bf16[64,2048]{1,0:T(8,128)(2,1)S(1)}, bf16[64,2048]{1,0:T(8,128)(2,1)S(1)}, u32[]{:S(2)}, u32[]{:S(2)}) collective-permute-start(bf16[64,2048]{1,0:T(8,128)(2,1)S(1)} %broadcast_select_fusion.1), channel_id=1, source_target_pairs={{0,2},{1,3},{2,0},{3,1},{4,6},{5,7},{6,4},{7,5},{8,10},{9,11},{10,... | collective-permute-start | bytes 786440 | tf_op jit(solution)/shard_map/ppermute | solution.py:35
  137.3 5.3 %collective-permute-start.26 = (bf16[64,2048]{1,0:T(8,128)(2,1)S(1)}, bf16[64,2048]{1,0:T(8,128)(2,1)S(1)}, u32[]{:S(2)}, u32[]{:S(2)}) collective-permute-start(bf16[64,2048]{1,0:T(8,128)(2,1)S(1)} %collective-permute-done.25.refs_1_), channel_id=1, source_target_pairs={{2,4},{3,5},{4,2},{5,3},{0,1},{1,0},{6,7},{7,6},{10,12},{11,13},{1... | collective-permute-start | bytes 786440 | tf_op jit(solution)/shard_map/ppermute | solution.py:40
  142.7 9.3 %collective-permute-start.29 = (bf16[64,2048]{1,0:T(8,128)(2,1)S(1)}, bf16[64,2048]{1,0:T(8,128)(2,1)S(1)}, u32[]{:S(2)}, u32[]{:S(2)}) collective-permute-start(bf16[64,2048]{1,0:T(8,128)(2,1)S(1)} %broadcast_select_fusion), channel_id=1, source_target_pairs={{0,2},{1,3},{2,0},{3,1},{4,6},{5,7},{6,4},{7,5},{8,10},{9,11},{10,... | collective-permute-start | bytes 786440 | tf_op jit(solution)/shard_map/ppermute | solution.py:35
  146.1 5.9 %collective-permute-start.28 = (bf16[64,2048]{1,0:T(8,128)(2,1)S(1)}, bf16[64,2048]{1,0:T(8,128)(2,1)S(1)}, u32[]{:S(2)}, u32[]{:S(2)}) collective-permute-start(bf16[64,2048]{1,0:T(8,128)(2,1)S(1)} %add_convert_fusion.5), channel_id=1, source_target_pairs={{2,4},{3,5},{4,2},{5,3},{0,1},{1,0},{6,7},{7,6},{10,12},{11,13},{1... | collective-permute-start | bytes 786440 | tf_op jit(solution)/shard_map/ppermute | solution.py:40
  152.0 10.9 %collective-permute-start.30 = (bf16[64,2048]{1,0:T(8,128)(2,1)S(1)}, bf16[64,2048]{1,0:T(8,128)(2,1)S(1)}, u32[]{:S(2)}, u32[]{:S(2)}) collective-permute-start(bf16[64,2048]{1,0:T(8,128)(2,1)S(1)} %add_convert_fusion.4), channel_id=1, source_target_pairs={{2,4},{3,5},{4,2},{5,3},{0,1},{1,0},{6,7},{7,6},{10,12},{11,13},{1... | collective-permute-start | bytes 786440 | tf_op jit(solution)/shard_map/ppermute | solution.py:40
  152.2 10.7 %collective-permute-start.31 = (bf16[64,2048]{1,0:T(8,128)(2,1)S(1)}, bf16[64,2048]{1,0:T(8,128)(2,1)S(1)}, u32[]{:S(2)}, u32[]{:S(2)}) collective-permute-start(bf16[64,2048]{1,0:T(8,128)(2,1)S(1)} %fusion.2), channel_id=1, source_target_pairs={{0,2},{1,3},{2,0},{3,1},{4,6},{5,7},{6,4},{7,5},{8,10},{9,11},{10,... | collective-permute-start | bytes 786440 | tf_op jit(solution)/shard_map/ppermute | solution.py:35
  162.9 7.3 %collective-permute-start.32 = (bf16[64,2048]{1,0:T(8,128)(2,1)S(1)}, bf16[64,2048]{1,0:T(8,128)(2,1)S(1)}, u32[]{:S(2)}, u32[]{:S(2)}) collective-permute-start(bf16[64,2048]{1,0:T(8,128)(2,1)S(1)} %get-tuple-element.226), channel_id=1, source_target_pairs={{0,2},{1,3},{2,0},{3,1},{4,6},{5,7},{6,4},{7,5},{8,10},{9,11},{10,... | collective-permute-start | bytes 786440 | tf_op jit(solution)/shard_map/ppermute | solution.py:35
  163.0 1.2 collective-permute-start.33
  164.3 3.6 %collective-permute-start.34 = (f32[8,128]{1,0:T(8,128)S(1)}, f32[8,128]{1,0:T(8,128)S(1)}, u32[]{:S(2)}, u32[]{:S(2)}) collective-permute-start(f32[8,128]{1,0:T(8,128)S(1)} %add.94), channel_id=1, source_target_pairs={{0,8},{8,0},{16,24},{24,16},{1,9},{9,1},{17,25},{25,17},{2,10},{10... | collective-permute-start | bytes 12296 | tf_op jit(solution)/shard_map/ppermute | solution.py:219
  165.7 9.3 %collective-permute-start.37 = (bf16[64,2048]{1,0:T(8,128)(2,1)S(1)}, bf16[64,2048]{1,0:T(8,128)(2,1)S(1)}, u32[]{:S(2)}, u32[]{:S(2)}) collective-permute-start(bf16[64,2048]{1,0:T(8,128)(2,1)S(1)} %get-tuple-element.236), channel_id=1, source_target_pairs={{0,2},{1,3},{2,0},{3,1},{4,6},{5,7},{6,4},{7,5},{8,10},{9,11},{10,... | collective-permute-start | bytes 786440 | tf_op jit(solution)/shard_map/ppermute | solution.py:35
  170.4 4.6 %collective-permute-start.36 = (bf16[64,2048]{1,0:T(8,128)(2,1)S(1)}, bf16[64,2048]{1,0:T(8,128)(2,1)S(1)}, u32[]{:S(2)}, u32[]{:S(2)}) collective-permute-start(bf16[64,2048]{1,0:T(8,128)(2,1)S(1)} %add_convert_fusion.2), channel_id=1, source_target_pairs={{2,4},{3,5},{4,2},{5,3},{0,1},{1,0},{6,7},{7,6},{10,12},{11,13},{1... | collective-permute-start | bytes 786440 | tf_op jit(solution)/shard_map/ppermute | solution.py:40
  170.4 9.5 %collective-permute-start.35 = (f32[8,128]{1,0:T(8,128)S(1)}, f32[8,128]{1,0:T(8,128)S(1)}, u32[]{:S(2)}, u32[]{:S(2)}) collective-permute-start(f32[8,128]{1,0:T(8,128)S(1)} %add.95), channel_id=1, source_target_pairs={{0,16},{8,24},{16,0},{24,8},{1,17},{9,25},{17,1},{25,9},{2,18},{10... | collective-permute-start | bytes 12296 | tf_op jit(solution)/shard_map/ppermute | solution.py:219
  175.1 4.9 %collective-permute-start.39 = (bf16[64,2048]{1,0:T(8,128)(2,1)S(1)}, bf16[64,2048]{1,0:T(8,128)(2,1)S(1)}, u32[]{:S(2)}, u32[]{:S(2)}) collective-permute-start(bf16[64,2048]{1,0:T(8,128)(2,1)S(1)} %add_convert_fusion), channel_id=1, source_target_pairs={{2,4},{3,5},{4,2},{5,3},{0,1},{1,0},{6,7},{7,6},{10,12},{11,13},{1... | collective-permute-start | bytes 786440 | tf_op jit(solution)/shard_map/ppermute | solution.py:40
  175.2 8.9 %collective-permute-start.38 = (bf16[64,2048]{1,0:T(8,128)(2,1)S(1)}, bf16[64,2048]{1,0:T(8,128)(2,1)S(1)}, u32[]{:S(2)}, u32[]{:S(2)}) collective-permute-start(bf16[64,2048]{1,0:T(8,128)(2,1)S(1)} %fusion.3), channel_id=1, source_target_pairs={{0,2},{1,3},{2,0},{3,1},{4,6},{5,7},{6,4},{7,5},{8,10},{9,11},{10,... | collective-permute-start | bytes 786440 | tf_op jit(solution)/shard_map/ppermute | solution.py:35
  (9 other events, 9.9 us)

commit v9 on v8

--- a/solution.py
+++ b/solution.py
@@ -313,10 +313,13 @@
     a_near, a_side, own_weights, load_b = slot(
         inner_hop(load_a), side_hop(load_a), load((w_gate, w_up, w_down)), load_b
     )
-    a_far, a_near_end, sib, load_b = slot(inner_hop(a_side), side_hop(a_near), sib, load_b)
-    a_far_end, sib_weights, a_parts, load_b = slot(
-        side_hop(a_far), load(sib), load((load_a, a_side, a_near, a_near_end, a_far)), load_b
-    )
+    a_near_end, a_far, sib, first_parts, load_b = slot(
+        side_hop(a_near), inner_hop(a_side), sib, load((load_a, a_side, a_near)), load_b
+    )
+    a_far_end, sib_weights, more_parts, load_b = slot(
+        side_hop(a_far), load(sib), load((a_near_end, a_far)), load_b
+    )
+    a_parts = (*first_parts, *more_parts)
     weights = (own_weights, sib_weights)
 
     everyone = tuple(range(CORES))
@@ -380,7 +383,7 @@
     while step < lines:
         squares = exchange_sum(squares, "dp", step)
         step *= 2
-    came, last = side_hop(pick(gb[1], add_rows(gb[1], s_side))), inner_hop(s_near)
+    last, came = slot(inner_hop(s_near), side_hop(pick(gb[1], add_rows(gb[1], s_side))))
     vmem = pl.BlockSpec(memory_space=pltpu.VMEM)
     return pl.pallas_call(
         functools.partial(output_kernel, token_count * width * lines * owners),

time: 186 us -> 185 us (level)
  waiting for transfers between devices: 75.8 us -> 81.3 us
  starting transfers between devices: 46.6 us -> 42.5 us
  local copies, waits for them, and re-layouts: 15.3 us -> 12.9 us
    ppermute x18, waiting for transfers between devices: 72.9 us -> 78.4 us  [side_hop(): return lax.ppermute(rows, 'expert', both_cores(SIDE_PAIRS))]
    ppermute x18, starting transfers between devices: 41.9 us -> 37.7 us  [side_hop(): return lax.ppermute(rows, 'expert', both_cores(SIDE_PAIRS))]
    unnamed x34, local copies, waits for them, and re-layouts: 13.7 us -> 11.4 us
    pallas_call x3 -> x4, Pallas kernels: 5.89 us -> 5.89 us  [load(): pl.pallas_call(functools.partial(load_kernel, len(arrays)), in_specs=[pl....]
  transfers between devices with their start and end apart: 40 -> 40, of which waited for: 19 -> 20; matrix products, arithmetic and copies ran while one was open for 2% -> 2% of each run, Pallas kernels for 23% -> 23%
where the time goes in v9:
time: 185 us
  waiting for transfers between devices  81.3 us (44%)
  Pallas kernels  44.3 us (24%)
  starting transfers between devices  42.5 us (23%)
  local copies, waits for them, and re-layouts  12.9 us (7%)
  other arithmetic  3.29 us (2%)
    ppermute x18, waiting for transfers between devices, side_hop(): return lax.ppermute(rows, 'expert', both_cores(SIDE_PAIRS))  78.4 us
    ppermute x18, starting transfers between devices, side_hop(): return lax.ppermute(rows, 'expert', both_cores(SIDE_PAIRS))  37.7 us
    pallas_call x6, Pallas kernels, kernel_call(): pl.pallas_call(kernel, in_specs=[pl.BlockSpec(memory_space=pltpu.SMEM)] +...  36.7 us
    unnamed x34, local copies, waits for them, and re-layouts  11.4 us
    pallas_call x4, Pallas kernels, load(): pl.pallas_call(functools.partial(load_kernel, len(arrays)), in_specs=[pl....  5.89 us
  transfers between devices with their start and end apart: 40, of which 20 were waited for; matrix products, arithmetic and copies ran while one was open for 2% of the time, Pallas kernels for 23%

profile of v9, /device:TPU:0, one launch (start us, length us, event | category | flops | bytes accessed | tf_op | source)
XLA Modules:
  0.0 184.9 jit_solution(7946995317192556596)
XLA Ops:
  1.8 1.4 fusion.8
  3.3 2.6 %collective-permute-start.1 = (bf16[64,4224]{1,0:T(8,128)(2,1)S(1)}, bf16[64,4224]{1,0:T(8,128)(2,1)S(1)}, u32[]{:S(2)}, u32[]{:S(2)}) collective-permute-start(bf16[64,4224]{1,0:T(8,128)(2,1)S(1)} %pad_maximum_fusion.refs_0_), channel_id=1, source_target_pairs={{0,2},{1,3},{2,0},{3,1},{4,6},{5,7},{6,4},{7,5},{8,10},{9,11},{10,... | collective-permute-start | bytes 1622024 | tf_op jit(solution)/shard_map/ppermute | solution.py:35
  6.2 1.9 %copy-done.5 = bf16[1,2048,768]{2,1,0:T(8,128)(2,1)S(1)} copy-done((bf16[1,2048,768]{2,1,0:T(8,128)(2,1)S(1)}, bf16[1,2048,768]{2,1,0:T(8,128)(2,1)}, u32[]{:S(2)}) %copy-start.5) | copy-done | bytes 3145752
  8.1 1.9 %copy-done.6 = bf16[1,768,2048]{2,1,0:T(8,128)(2,1)S(1)} copy-done((bf16[1,768,2048]{2,1,0:T(8,128)(2,1)S(1)}, bf16[1,768,2048]{2,1,0:T(8,128)(2,1)}, u32[]{:S(2)}) %copy-start.6) | copy-done | bytes 3145752
  10.6 1.6 copy-done
  12.2 1.7 copy-done.2
  14.8 4.1 %collective-permute-done.1.refs_1_ = bf16[64,4224]{1,0:T(8,128)(2,1)S(1)} collective-permute-done((bf16[64,4224]{1,0:T(8,128)(2,1)S(1)}, bf16[64,4224]{1,0:T(8,128)(2,1)S(1)}, u32[]{:S(2)}, u32[]{:S(2)}) %collective-permute-start.1) | collective-permute-done | bytes 540704 | tf_op jit(solution)/shard_map/ppermute | solution.py:35
  18.9 2.9 %collective-permute-start.2 = (bf16[64,4224]{1,0:T(8,128)(2,1)S(1)}, bf16[64,4224]{1,0:T(8,128)(2,1)S(1)}, u32[]{:S(2)}, u32[]{:S(2)}) collective-permute-start(bf16[64,4224]{1,0:T(8,128)(2,1)S(1)} %collective-permute-done.refs_2_), channel_id=1, source_target_pairs={{0,2},{1,3},{2,0},{3,1},{4,6},{5,7},{6,4},{7,5},{8,10},{9,11},{10,... | collective-permute-start | bytes 1622024 | tf_op jit(solution)/shard_map/ppermute | solution.py:35
  24.4 9.6 %collective-permute-done.2.refs_0_ = bf16[64,4224]{1,0:T(8,128)(2,1)S(1)} collective-permute-done((bf16[64,4224]{1,0:T(8,128)(2,1)S(1)}, bf16[64,4224]{1,0:T(8,128)(2,1)S(1)}, u32[]{:S(2)}, u32[]{:S(2)}) %collective-permute-start.2) | collective-permute-done | bytes 540704 | tf_op jit(solution)/shard_map/ppermute | solution.py:35
  34.8 1.8 collective-permute-start.7
  36.6 1.0 copy-done.9
  37.7 1.1 load.7
  38.9 3.9 %load.6 = (bf16[1,2048,768]{2,1,0:T(8,128)(2,1)S(1)}, bf16[1,2048,768]{2,1,0:T(8,128)(2,1)S(1)}, bf16[1,768,2048]{2,1,0:T(8,128)(2,1)S(1)}) custom-call(bf16[1,2048,768]{2,1,0:T(8,128)(2,1)} %collective-permute-done.4.refs_0_, bf16[1,2048,768]{2,1,0:T(8,128)(2,1)} %collective-permute-done.5.refs_1_, bf16[1,768,2048]{2,1,0:T(8,128)(2,1)} %collective-permute-done.6.refs_2_), custom_call_target="tpu_custom_call" | custom-call | tf_op jit(solution)/shard_map/load/pallas_call | solution.py:206
  42.8 5.7 %collective-permute-done.7.refs_5_ = bf16[64,4224]{1,0:T(8,128)(2,1)} collective-permute-done((bf16[64,4224]{1,0:T(8,128)(2,1)}, bf16[64,4224]{1,0:T(8,128)(2,1)}, u32[]{:S(2)}, u32[]{:S(2)}) %collective-permute-start.7) | collective-permute-done | bytes 540704 | tf_op jit(solution)/shard_map/ppermute | solution.py:35
  48.5 1.5 collective-permute-start.9
  50.0 10.5 %forward.3 = (f32[64,2048]{1,0:T(8,128)S(1)}, bf16[64,2048]{1,0:T(8,128)(2,1)S(1)}, bf16[64,2048]{1,0:T(8,128)(2,1)S(1)}, bf16[64,2048]{1,0:T(8,128)(2,1)S(1)}, ...) custom-call(s32[3]{0:T(128)S(1)} %pad_add_fusion.where_ref, ...), custom_call_target="tpu_custom_call" | custom-call | flops 8053063680 | tf_op jit(solution)/shard_map/forward/pallas_call | solution.py:160
  61.0 1.8 collective-permute-start.11
  62.8 12.6 %collective-permute-done.11.refs_3_ = bf16[64,4224]{1,0:T(8,128)(2,1)S(1)} collective-permute-done((bf16[64,4224]{1,0:T(8,128)(2,1)S(1)}, bf16[64,4224]{1,0:T(8,128)(2,1)S(1)}, u32[]{:S(2)}, u32[]{:S(2)}) %collective-permute-start.11) | collective-permute-done | bytes 540704 | tf_op jit(solution)/shard_map/ppermute | solution.py:35
  75.5 1.8 collective-permute-start.13
  77.5 1.5 collective-permute-done.12
  79.0 10.1 %collective-permute-done.13.refs_5_ = bf16[64,4224]{1,0:T(8,128)(2,1)S(1)} collective-permute-done((bf16[64,4224]{1,0:T(8,128)(2,1)S(1)}, bf16[64,4224]{1,0:T(8,128)(2,1)S(1)}, u32[]{:S(2)}, u32[]{:S(2)}) %collective-permute-start.13) | collective-permute-done | bytes 540704 | tf_op jit(solution)/shard_map/ppermute | solution.py:35
  89.3 2.5 %collective-permute-start.15 = (bf16[64,2048]{1,0:T(8,128)(2,1)S(1)}, bf16[64,2048]{1,0:T(8,128)(2,1)S(1)}, u32[]{:S(2)}, u32[]{:S(2)}) collective-permute-start(bf16[64,2048]{1,0:T(8,128)(2,1)S(1)} %fusion), channel_id=1, source_target_pairs={{0,2},{1,3},{2,0},{3,1},{4,6},{5,7},{6,4},{7,5},{8,10},{9,11},{10,... | collective-permute-start | bytes 786440 | tf_op jit(solution)/shard_map/ppermute | solution.py:35
  91.8 5.5 %forward.4 = (f32[256,2048]{1,0:T(8,128)S(1)}, f32[256,768]{1,0:T(8,128)S(1)}, f32[256,768]{1,0:T(8,128)S(1)}) custom-call(s32[3]{0:T(128)S(1)} %pad_add_fusion.where_ref, bf16[64,4224]{1,0:T(8,128)(2,1)S(1)} %copy-done.7, bf16[64,4224]{1,0:T(8,128)(2,1)S(1)} %collective-permute-done.9.refs_1_, bf16[64,4224]{1,0:T(8,128)(2,1)S(1)} %collective-permute-done.8.refs_2_, ...), custom_call_target="tpu_custom_call" | custom-call | flops 4026531840 | tf_op jit(solution)/shard_map/forward/pallas_call | solution.py:160
  98.6 5.3 %forward.5 = (f32[64,2048]{1,0:T(8,128)S(1)}, bf16[64,2048]{1,0:T(8,128)(2,1)S(1)}, bf16[64,2048]{1,0:T(8,128)(2,1)S(1)}, bf16[64,2048]{1,0:T(8,128)(2,1)S(1)}, ...) custom-call(s32[3]{0:T(128)S(1)} %pad_add_fusion.where_ref, bf16[64,4224]{1,0:T(8,128)(2,1)S(1)} %copy-done.7, ...), custom_call_target="tpu_custom_call" | custom-call | flops 4026531840 | tf_op jit(solution)/shard_map/forward/pallas_call | solution.py:160
  103.9 1.9 %collective-permute-done.17.refs_1_ = bf16[64,2048]{1,0:T(8,128)(2,1)S(1)} collective-permute-done((bf16[64,2048]{1,0:T(8,128)(2,1)S(1)}, bf16[64,2048]{1,0:T(8,128)(2,1)S(1)}, u32[]{:S(2)}, u32[]{:S(2)}) %collective-permute-start.17) | collective-permute-done | bytes 262176 | tf_op jit(solution)/shard_map/ppermute | solution.py:35
  105.8 1.8 collective-permute-start.19
  107.6 5.1 %collective-permute-done.19.refs_3_ = bf16[64,2048]{1,0:T(8,128)(2,1)S(1)} collective-permute-done((bf16[64,2048]{1,0:T(8,128)(2,1)S(1)}, bf16[64,2048]{1,0:T(8,128)(2,1)S(1)}, u32[]{:S(2)}, u32[]{:S(2)}) %collective-permute-start.19) | collective-permute-done | bytes 262176 | tf_op jit(solution)/shard_map/ppermute | solution.py:35
  112.8 1.8 collective-permute-start.21
  114.6 4.6 %collective-permute-done.21.refs_5_ = bf16[64,2048]{1,0:T(8,128)(2,1)S(1)} collective-permute-done((bf16[64,2048]{1,0:T(8,128)(2,1)S(1)}, bf16[64,2048]{1,0:T(8,128)(2,1)S(1)}, u32[]{:S(2)}, u32[]{:S(2)}) %collective-permute-start.21) | collective-permute-done | bytes 262176 | tf_op jit(solution)/shard_map/ppermute | solution.py:35
  119.5 4.0 %collective-permute-start.23 = (bf16[64,2048]{1,0:T(8,128)(2,1)S(1)}, bf16[64,2048]{1,0:T(8,128)(2,1)S(1)}, u32[]{:S(2)}, u32[]{:S(2)}) collective-permute-start(bf16[64,2048]{1,0:T(8,128)(2,1)S(1)} %fusion.1), channel_id=1, source_target_pairs={{0,2},{1,3},{2,0},{3,1},{4,6},{5,7},{6,4},{7,5},{8,10},{9,11},{10,... | collective-permute-start | bytes 786440 | tf_op jit(solution)/shard_map/ppermute | solution.py:35
  123.6 4.2 %backward.3 = (f32[256,2048]{1,0:T(8,128)S(1)}, f32[8,128]{1,0:T(8,128)S(1)}) custom-call(s32[3]{0:T(128)S(1)} %pad_add_fusion.where_ref, bf16[64,2048]{1,0:T(8,128)(2,1)S(1)} %fusion.4.refs_0_, bf16[64,2048]{1,0:T(8,128)(2,1)S(1)} %collective-permute-done.17.refs_1_, bf16[64,2048]{1,0:T(8,128)(2,1)S(1)} %collective-permute-done.16.refs_2_, ...), custom_call_target="tpu_custom_call" | custom-call | flops 2415919104 | tf_op jit(solution)/shard_map/backward/pallas_call | solution.py:160
  128.5 2.5 %collective-permute-start.25 = (bf16[64,2048]{1,0:T(8,128)(2,1)S(1)}, bf16[64,2048]{1,0:T(8,128)(2,1)S(1)}, u32[]{:S(2)}, u32[]{:S(2)}) collective-permute-start(bf16[64,2048]{1,0:T(8,128)(2,1)S(1)} %get-tuple-element.243.refs_0_), channel_id=1, source_target_pairs={{0,2},{1,3},{2,0},{3,1},{4,6},{5,7},{6,4},{7,5},{8,10},{9,11},{10,... | collective-permute-start | bytes 786440 | tf_op jit(solution)/shard_map/ppermute | solution.py:35
  131.0 4.3 %backward.4 = (f32[64,2048]{1,0:T(8,128)S(1)}, bf16[64,2048]{1,0:T(8,128)(2,1)S(1)}, bf16[64,2048]{1,0:T(8,128)(2,1)S(1)}, bf16[64,2048]{1,0:T(8,128)(2,1)S(1)}) custom-call(s32[3]{0:T(128)S(1)} %pad_add_fusion.where_ref, bf16[64,2048]{1,0:T(8,128)(2,1)S(1)} %fusion.4.refs_0_, bf16[64,2048]{1,0:T(8,128)(2,1)S(1)} %collective-permute-done.17.refs_1_, ...), custom_call_target="tpu_custom_call" | custom-call | flops 2415919104 | tf_op jit(solution)/shard_map/backward/pallas_call | solution.py:160
  135.4 2.2 %collective-permute-start.27 = (bf16[64,2048]{1,0:T(8,128)(2,1)S(1)}, bf16[64,2048]{1,0:T(8,128)(2,1)S(1)}, u32[]{:S(2)}, u32[]{:S(2)}) collective-permute-start(bf16[64,2048]{1,0:T(8,128)(2,1)S(1)} %broadcast_select_fusion.1), channel_id=1, source_target_pairs={{0,2},{1,3},{2,0},{3,1},{4,6},{5,7},{6,4},{7,5},{8,10},{9,11},{10,... | collective-permute-start | bytes 786440 | tf_op jit(solution)/shard_map/ppermute | solution.py:35
  137.6 6.6 %collective-permute-done.27.refs_3_ = bf16[64,2048]{1,0:T(8,128)(2,1)S(1)} collective-permute-done((bf16[64,2048]{1,0:T(8,128)(2,1)S(1)}, bf16[64,2048]{1,0:T(8,128)(2,1)S(1)}, u32[]{:S(2)}, u32[]{:S(2)}) %collective-permute-start.27) | collective-permute-done | bytes 262176 | tf_op jit(solution)/shard_map/ppermute | solution.py:35
  144.3 1.8 collective-permute-start.29
  146.1 6.1 %collective-permute-done.29.refs_5_ = bf16[64,2048]{1,0:T(8,128)(2,1)S(1)} collective-permute-done((bf16[64,2048]{1,0:T(8,128)(2,1)S(1)}, bf16[64,2048]{1,0:T(8,128)(2,1)S(1)}, u32[]{:S(2)}, u32[]{:S(2)}) %collective-permute-start.29) | collective-permute-done | bytes 262176 | tf_op jit(solution)/shard_map/ppermute | solution.py:35
  152.4 2.5 %collective-permute-start.31 = (bf16[64,2048]{1,0:T(8,128)(2,1)S(1)}, bf16[64,2048]{1,0:T(8,128)(2,1)S(1)}, u32[]{:S(2)}, u32[]{:S(2)}) collective-permute-start(bf16[64,2048]{1,0:T(8,128)(2,1)S(1)} %fusion.2), channel_id=1, source_target_pairs={{0,2},{1,3},{2,0},{3,1},{4,6},{5,7},{6,4},{7,5},{8,10},{9,11},{10,... | collective-permute-start | bytes 786440 | tf_op jit(solution)/shard_map/ppermute | solution.py:35
  154.9 7.0 %backward.5 = (f32[64,2048]{1,0:T(8,128)S(1)}, bf16[64,2048]{1,0:T(8,128)(2,1)S(1)}, bf16[64,2048]{1,0:T(8,128)(2,1)S(1)}, bf16[64,2048]{1,0:T(8,128)(2,1)S(1)}, f32[8,128]{1,0:T(8,128)S(1)}) custom-call(s32[3]{0:T(128)S(1)} %pad_add_fusion.where_ref, bf16[64,2048]{1,0:T(8,128)(2,1)S(1)} %get-tuple-element.243.refs_0_, ...), custom_call_target="tpu_custom_call" | custom-call | flops 4831838208 | tf_op jit(solution)/shard_map/backward/pallas_call | solution.py:160
  162.1 1.2 collective-permute-done.33
  163.3 1.5 collective-permute-start.34
  164.8 1.9 %collective-permute-start.37 = (bf16[64,2048]{1,0:T(8,128)(2,1)S(1)}, bf16[64,2048]{1,0:T(8,128)(2,1)S(1)}, u32[]{:S(2)}, u32[]{:S(2)}) collective-permute-start(bf16[64,2048]{1,0:T(8,128)(2,1)S(1)} %get-tuple-element.236), channel_id=1, source_target_pairs={{0,2},{1,3},{2,0},{3,1},{4,6},{5,7},{6,4},{7,5},{8,10},{9,11},{10,... | collective-permute-start | bytes 786440 | tf_op jit(solution)/shard_map/ppermute | solution.py:35
  166.9 2.7 %collective-permute-done.32 = bf16[64,2048]{1,0:T(8,128)(2,1)S(1)} collective-permute-done((bf16[64,2048]{1,0:T(8,128)(2,1)S(1)}, bf16[64,2048]{1,0:T(8,128)(2,1)S(1)}, u32[]{:S(2)}, u32[]{:S(2)}) %collective-permute-start.32) | collective-permute-done | bytes 262176 | tf_op jit(solution)/shard_map/ppermute | solution.py:35
  169.7 1.6 collective-permute-start.35
  171.3 2.9 %collective-permute-done.37 = bf16[64,2048]{1,0:T(8,128)(2,1)S(1)} collective-permute-done((bf16[64,2048]{1,0:T(8,128)(2,1)S(1)}, bf16[64,2048]{1,0:T(8,128)(2,1)S(1)}, u32[]{:S(2)}, u32[]{:S(2)}) %collective-permute-start.37) | collective-permute-done | bytes 262176 | tf_op jit(solution)/shard_map/ppermute | solution.py:35
  174.4 3.7 %collective-permute-start.39 = (bf16[64,2048]{1,0:T(8,128)(2,1)S(1)}, bf16[64,2048]{1,0:T(8,128)(2,1)S(1)}, u32[]{:S(2)}, u32[]{:S(2)}) collective-permute-start(bf16[64,2048]{1,0:T(8,128)(2,1)S(1)} %fusion.3), channel_id=1, source_target_pairs={{0,2},{1,3},{2,0},{3,1},{4,6},{5,7},{6,4},{7,5},{8,10},{9,11},{10,... | collective-permute-start | bytes 786440 | tf_op jit(solution)/shard_map/ppermute | solution.py:35
  178.3 4.8 %collective-permute-done.39.side = bf16[64,2048]{1,0:T(8,128)(2,1)S(1)} collective-permute-done((bf16[64,2048]{1,0:T(8,128)(2,1)S(1)}, bf16[64,2048]{1,0:T(8,128)(2,1)S(1)}, u32[]{:S(2)}, u32[]{:S(2)}) %collective-permute-start.39) | collective-permute-done | bytes 262176 | tf_op jit(solution)/shard_map/ppermute | solution.py:35
  183.2 1.7 output.1
  (115 shorter events, 11.7 us)
Async XLA Ops:
  0.0 34.7 %collective-permute-start.4 = (bf16[1,2048,768]{2,1,0:T(8,128)(2,1)}, bf16[1,2048,768]{2,1,0:T(8,128)(2,1)}, u32[]{:S(2)}, u32[]{:S(2)}) collective-permute-start(bf16[1,2048,768]{2,1,0:T(8,128)(2,1)} %refs_0_.1), channel_id=1, source_target_pairs={{0,1},{1,0},{2,3},{3,2},{4,5},{5,4},{6,7},{7,6},{8,9},{9,8},{10,11... | collective-permute-start | bytes 9437192 | tf_op jit(solution)/shard_map/ppermute | solution.py:312
  0.5 34.3 %collective-permute-start.5 = (bf16[1,2048,768]{2,1,0:T(8,128)(2,1)}, bf16[1,2048,768]{2,1,0:T(8,128)(2,1)}, u32[]{:S(2)}, u32[]{:S(2)}) collective-permute-start(bf16[1,2048,768]{2,1,0:T(8,128)(2,1)} %refs_1_.1), channel_id=1, source_target_pairs={{0,1},{1,0},{2,3},{3,2},{4,5},{5,4},{6,7},{7,6},{8,9},{9,8},{10,11... | collective-permute-start | bytes 9437192 | tf_op jit(solution)/shard_map/ppermute | solution.py:312
  0.5 34.2 %collective-permute-start.6 = (bf16[1,768,2048]{2,1,0:T(8,128)(2,1)}, bf16[1,768,2048]{2,1,0:T(8,128)(2,1)}, u32[]{:S(2)}, u32[]{:S(2)}) collective-permute-start(bf16[1,768,2048]{2,1,0:T(8,128)(2,1)} %refs_2_.1), channel_id=1, source_target_pairs={{0,1},{1,0},{2,3},{3,2},{4,5},{5,4},{6,7},{7,6},{8,9},{9,8},{10,11... | collective-permute-start | bytes 9437192 | tf_op jit(solution)/shard_map/ppermute | solution.py:312
  1.8 4.3 %copy-start.4 = (bf16[1,2048,768]{2,1,0:T(8,128)(2,1)S(1)}, bf16[1,2048,768]{2,1,0:T(8,128)(2,1)}, u32[]{:S(2)}) copy-start(bf16[1,2048,768]{2,1,0:T(8,128)(2,1)} %refs_0_.1) | copy-start | bytes 9437188
  3.3 15.6 %collective-permute-start.1 = (bf16[64,4224]{1,0:T(8,128)(2,1)S(1)}, bf16[64,4224]{1,0:T(8,128)(2,1)S(1)}, u32[]{:S(2)}, u32[]{:S(2)}) collective-permute-start(bf16[64,4224]{1,0:T(8,128)(2,1)S(1)} %pad_maximum_fusion.refs_0_), channel_id=1, source_target_pairs={{0,2},{1,3},{2,0},{3,1},{4,6},{5,7},{6,4},{7,5},{8,10},{9,11},{10,... | collective-permute-start | bytes 1622024 | tf_op jit(solution)/shard_map/ppermute | solution.py:35
  5.9 12.9 %collective-permute-start = (bf16[64,4224]{1,0:T(8,128)(2,1)S(1)}, bf16[64,4224]{1,0:T(8,128)(2,1)S(1)}, u32[]{:S(2)}, u32[]{:S(2)}) collective-permute-start(bf16[64,4224]{1,0:T(8,128)(2,1)S(1)} %pad_maximum_fusion.refs_0_), channel_id=1, source_target_pairs={{2,4},{3,5},{4,2},{5,3},{0,1},{1,0},{6,7},{7,6},{10,12},{11,13},{1... | collective-permute-start | bytes 1622024 | tf_op jit(solution)/shard_map/ppermute | solution.py:40
  18.9 15.0 %collective-permute-start.2 = (bf16[64,4224]{1,0:T(8,128)(2,1)S(1)}, bf16[64,4224]{1,0:T(8,128)(2,1)S(1)}, u32[]{:S(2)}, u32[]{:S(2)}) collective-permute-start(bf16[64,4224]{1,0:T(8,128)(2,1)S(1)} %collective-permute-done.refs_2_), channel_id=1, source_target_pairs={{0,2},{1,3},{2,0},{3,1},{4,6},{5,7},{6,4},{7,5},{8,10},{9,11},{10,... | collective-permute-start | bytes 1622024 | tf_op jit(solution)/shard_map/ppermute | solution.py:35
  21.8 13.0 %collective-permute-start.3 = (bf16[64,4224]{1,0:T(8,128)(2,1)S(1)}, bf16[64,4224]{1,0:T(8,128)(2,1)}, u32[]{:S(2)}, u32[]{:S(2)}) collective-permute-start(bf16[64,4224]{1,0:T(8,128)(2,1)S(1)} %collective-permute-done.1.refs_1_), channel_id=1, source_target_pairs={{2,4},{3,5},{4,2},{5,3},{0,1},{1,0},{6,7},{7,6},{10,12},{11,13},{1... | collective-permute-start | bytes 1622024 | tf_op jit(solution)/shard_map/ppermute | solution.py:40
  34.8 13.7 %collective-permute-start.7 = (bf16[64,4224]{1,0:T(8,128)(2,1)}, bf16[64,4224]{1,0:T(8,128)(2,1)}, u32[]{:S(2)}, u32[]{:S(2)}) collective-permute-start(bf16[64,4224]{1,0:T(8,128)(2,1)} %collective-permute-done.3.refs_1_), channel_id=1, source_target_pairs={{0,2},{1,3},{2,0},{3,1},{4,6},{5,7},{6,4},{7,5},{8,10},{9,11},{10,... | collective-permute-start | bytes 1622024 | tf_op jit(solution)/shard_map/ppermute | solution.py:35
  38.8 9.7 %copy-start.7 = (bf16[64,4224]{1,0:T(8,128)(2,1)S(1)}, bf16[64,4224]{1,0:T(8,128)(2,1)}, u32[]{:S(2)}) copy-start(bf16[64,4224]{1,0:T(8,128)(2,1)} %pad_maximum_fusion.1.refs_0_) | copy-start | bytes 1622020
  38.8 11.2 %copy-start.1 = (bf16[1,2048,768]{2,1,0:T(8,128)(2,1)S(1)}, bf16[1,2048,768]{2,1,0:T(8,128)(2,1)}, u32[]{:S(2)}) copy-start(bf16[1,2048,768]{2,1,0:T(8,128)(2,1)} %copy-done) | copy-start | bytes 9437188
  38.8 11.2 %copy-start.3 = (bf16[1,768,2048]{2,1,0:T(8,128)(2,1)S(1)}, bf16[1,768,2048]{2,1,0:T(8,128)(2,1)}, u32[]{:S(2)}) copy-start(bf16[1,768,2048]{2,1,0:T(8,128)(2,1)} %copy-done.2) | copy-start | bytes 9437188
  38.8 11.2 %copy-start.11 = (bf16[64,4224]{1,0:T(8,128)(2,1)S(1)}, bf16[64,4224]{1,0:T(8,128)(2,1)}, u32[]{:S(2)}) copy-start(bf16[64,4224]{1,0:T(8,128)(2,1)} %copy-done.10) | copy-start | bytes 1622020
  38.9 11.2 %copy-start.13 = (bf16[64,4224]{1,0:T(8,128)(2,1)S(1)}, bf16[64,4224]{1,0:T(8,128)(2,1)}, u32[]{:S(2)}) copy-start(bf16[64,4224]{1,0:T(8,128)(2,1)} %copy-done.12) | copy-start | bytes 1622020
  38.9 11.2 %copy-start.15 = (bf16[64,4224]{1,0:T(8,128)(2,1)S(1)}, bf16[64,4224]{1,0:T(8,128)(2,1)}, u32[]{:S(2)}) copy-start(bf16[64,4224]{1,0:T(8,128)(2,1)} %copy-done.14) | copy-start | bytes 1622020
  48.5 12.4 %collective-permute-start.9 = (bf16[64,4224]{1,0:T(8,128)(2,1)S(1)}, bf16[64,4224]{1,0:T(8,128)(2,1)S(1)}, u32[]{:S(2)}, u32[]{:S(2)}) collective-permute-start(bf16[64,4224]{1,0:T(8,128)(2,1)S(1)} %copy-done.7), channel_id=1, source_target_pairs={{0,2},{1,3},{2,0},{3,1},{4,6},{5,7},{6,4},{7,5},{8,10},{9,11},{10,... | collective-permute-start | bytes 1622024 | tf_op jit(solution)/shard_map/ppermute | solution.py:35
  50.0 10.9 %collective-permute-start.8 = (bf16[64,4224]{1,0:T(8,128)(2,1)S(1)}, bf16[64,4224]{1,0:T(8,128)(2,1)S(1)}, u32[]{:S(2)}, u32[]{:S(2)}) collective-permute-start(bf16[64,4224]{1,0:T(8,128)(2,1)S(1)} %copy-done.7), channel_id=1, source_target_pairs={{2,4},{3,5},{4,2},{5,3},{0,1},{1,0},{6,7},{7,6},{10,12},{11,13},{1... | collective-permute-start | bytes 1622024 | tf_op jit(solution)/shard_map/ppermute | solution.py:40
  61.0 14.4 %collective-permute-start.11 = (bf16[64,4224]{1,0:T(8,128)(2,1)S(1)}, bf16[64,4224]{1,0:T(8,128)(2,1)S(1)}, u32[]{:S(2)}, u32[]{:S(2)}) collective-permute-start(bf16[64,4224]{1,0:T(8,128)(2,1)S(1)} %pad_maximum_fusion.2), channel_id=1, source_target_pairs={{0,2},{1,3},{2,0},{3,1},{4,6},{5,7},{6,4},{7,5},{8,10},{9,11},{10,... | collective-permute-start | bytes 1622024 | tf_op jit(solution)/shard_map/ppermute | solution.py:35
  62.8 12.6 %collective-permute-start.10 = (bf16[64,4224]{1,0:T(8,128)(2,1)S(1)}, bf16[64,4224]{1,0:T(8,128)(2,1)S(1)}, u32[]{:S(2)}, u32[]{:S(2)}) collective-permute-start(bf16[64,4224]{1,0:T(8,128)(2,1)S(1)} %collective-permute-done.9.refs_1_), channel_id=1, source_target_pairs={{2,4},{3,5},{4,2},{5,3},{0,1},{1,0},{6,7},{7,6},{10,12},{11,13},{1... | collective-permute-start | bytes 1622024 | tf_op jit(solution)/shard_map/ppermute | solution.py:40
  75.5 13.6 %collective-permute-start.13 = (bf16[64,4224]{1,0:T(8,128)(2,1)S(1)}, bf16[64,4224]{1,0:T(8,128)(2,1)S(1)}, u32[]{:S(2)}, u32[]{:S(2)}) collective-permute-start(bf16[64,4224]{1,0:T(8,128)(2,1)S(1)} %pad_maximum_fusion.3), channel_id=1, source_target_pairs={{0,2},{1,3},{2,0},{3,1},{4,6},{5,7},{6,4},{7,5},{8,10},{9,11},{10,... | collective-permute-start | bytes 1622024 | tf_op jit(solution)/shard_map/ppermute | solution.py:35
  77.4 1.6 collective-permute-start.12
  89.1 8.2 %collective-permute-start.14 = (bf16[64,2048]{1,0:T(8,128)(2,1)S(1)}, bf16[64,2048]{1,0:T(8,128)(2,1)S(1)}, u32[]{:S(2)}, u32[]{:S(2)}) collective-permute-start(bf16[64,2048]{1,0:T(8,128)(2,1)S(1)} %add_convert_fusion.10), channel_id=1, source_target_pairs={{2,4},{3,5},{4,2},{5,3},{0,1},{1,0},{6,7},{7,6},{10,12},{11,13},{1... | collective-permute-start | bytes 786440 | tf_op jit(solution)/shard_map/ppermute | solution.py:40
  89.3 8.8 %copy-start.16 = (bf16[128,2048]{1,0:T(8,128)(2,1)S(1)}, bf16[128,2048]{1,0:T(8,128)(2,1)}, u32[]{:S(2)}) copy-start(bf16[128,2048]{1,0:T(8,128)(2,1)} %param.8) | copy-start | bytes 1572868
  89.3 8.8 %collective-permute-start.15 = (bf16[64,2048]{1,0:T(8,128)(2,1)S(1)}, bf16[64,2048]{1,0:T(8,128)(2,1)S(1)}, u32[]{:S(2)}, u32[]{:S(2)}) collective-permute-start(bf16[64,2048]{1,0:T(8,128)(2,1)S(1)} %fusion), channel_id=1, source_target_pairs={{0,2},{1,3},{2,0},{3,1},{4,6},{5,7},{6,4},{7,5},{8,10},{9,11},{10,... | collective-permute-start | bytes 786440 | tf_op jit(solution)/shard_map/ppermute | solution.py:35
  98.2 7.5 %collective-permute-start.17 = (bf16[64,2048]{1,0:T(8,128)(2,1)S(1)}, bf16[64,2048]{1,0:T(8,128)(2,1)S(1)}, u32[]{:S(2)}, u32[]{:S(2)}) collective-permute-start(bf16[64,2048]{1,0:T(8,128)(2,1)S(1)} %fusion.4.refs_0_), channel_id=1, source_target_pairs={{0,2},{1,3},{2,0},{3,1},{4,6},{5,7},{6,4},{7,5},{8,10},{9,11},{10,... | collective-permute-start | bytes 786440 | tf_op jit(solution)/shard_map/ppermute | solution.py:35
  98.6 7.2 %collective-permute-start.16 = (bf16[64,2048]{1,0:T(8,128)(2,1)S(1)}, bf16[64,2048]{1,0:T(8,128)(2,1)S(1)}, u32[]{:S(2)}, u32[]{:S(2)}) collective-permute-start(bf16[64,2048]{1,0:T(8,128)(2,1)S(1)} %fusion.4.refs_0_), channel_id=1, source_target_pairs={{2,4},{3,5},{4,2},{5,3},{0,1},{1,0},{6,7},{7,6},{10,12},{11,13},{1... | collective-permute-start | bytes 786440 | tf_op jit(solution)/shard_map/ppermute | solution.py:40
  105.8 6.9 %collective-permute-start.19 = (bf16[64,2048]{1,0:T(8,128)(2,1)S(1)}, bf16[64,2048]{1,0:T(8,128)(2,1)S(1)}, u32[]{:S(2)}, u32[]{:S(2)}) collective-permute-start(bf16[64,2048]{1,0:T(8,128)(2,1)S(1)} %broadcast_select_fusion.3), channel_id=1, source_target_pairs={{0,2},{1,3},{2,0},{3,1},{4,6},{5,7},{6,4},{7,5},{8,10},{9,11},{10,... | collective-permute-start | bytes 786440 | tf_op jit(solution)/shard_map/ppermute | solution.py:35
  107.6 5.1 %collective-permute-start.18 = (bf16[64,2048]{1,0:T(8,128)(2,1)S(1)}, bf16[64,2048]{1,0:T(8,128)(2,1)S(1)}, u32[]{:S(2)}, u32[]{:S(2)}) collective-permute-start(bf16[64,2048]{1,0:T(8,128)(2,1)S(1)} %collective-permute-done.17.refs_1_), channel_id=1, source_target_pairs={{2,4},{3,5},{4,2},{5,3},{0,1},{1,0},{6,7},{7,6},{10,12},{11,13},{1... | collective-permute-start | bytes 786440 | tf_op jit(solution)/shard_map/ppermute | solution.py:40
  112.8 6.4 %collective-permute-start.21 = (bf16[64,2048]{1,0:T(8,128)(2,1)S(1)}, bf16[64,2048]{1,0:T(8,128)(2,1)S(1)}, u32[]{:S(2)}, u32[]{:S(2)}) collective-permute-start(bf16[64,2048]{1,0:T(8,128)(2,1)S(1)} %broadcast_select_fusion.2), channel_id=1, source_target_pairs={{0,2},{1,3},{2,0},{3,1},{4,6},{5,7},{6,4},{7,5},{8,10},{9,11},{10,... | collective-permute-start | bytes 786440 | tf_op jit(solution)/shard_map/ppermute | solution.py:35
  114.6 4.6 %collective-permute-start.20 = (bf16[64,2048]{1,0:T(8,128)(2,1)S(1)}, bf16[64,2048]{1,0:T(8,128)(2,1)S(1)}, u32[]{:S(2)}, u32[]{:S(2)}) collective-permute-start(bf16[64,2048]{1,0:T(8,128)(2,1)S(1)} %add_convert_fusion.8), channel_id=1, source_target_pairs={{2,4},{3,5},{4,2},{5,3},{0,1},{1,0},{6,7},{7,6},{10,12},{11,13},{1... | collective-permute-start | bytes 786440 | tf_op jit(solution)/shard_map/ppermute | solution.py:40
  119.3 8.4 %collective-permute-start.22 = (bf16[64,2048]{1,0:T(8,128)(2,1)S(1)}, bf16[64,2048]{1,0:T(8,128)(2,1)S(1)}, u32[]{:S(2)}, u32[]{:S(2)}) collective-permute-start(bf16[64,2048]{1,0:T(8,128)(2,1)S(1)} %add_convert_fusion.7), channel_id=1, source_target_pairs={{2,4},{3,5},{4,2},{5,3},{0,1},{1,0},{6,7},{7,6},{10,12},{11,13},{1... | collective-permute-start | bytes 786440 | tf_op jit(solution)/shard_map/ppermute | solution.py:40
  119.5 8.8 %collective-permute-start.23 = (bf16[64,2048]{1,0:T(8,128)(2,1)S(1)}, bf16[64,2048]{1,0:T(8,128)(2,1)S(1)}, u32[]{:S(2)}, u32[]{:S(2)}) collective-permute-start(bf16[64,2048]{1,0:T(8,128)(2,1)S(1)} %fusion.1), channel_id=1, source_target_pairs={{0,2},{1,3},{2,0},{3,1},{4,6},{5,7},{6,4},{7,5},{8,10},{9,11},{10,... | collective-permute-start | bytes 786440 | tf_op jit(solution)/shard_map/ppermute | solution.py:35
  128.5 6.9 %collective-permute-start.25 = (bf16[64,2048]{1,0:T(8,128)(2,1)S(1)}, bf16[64,2048]{1,0:T(8,128)(2,1)S(1)}, u32[]{:S(2)}, u32[]{:S(2)}) collective-permute-start(bf16[64,2048]{1,0:T(8,128)(2,1)S(1)} %get-tuple-element.243.refs_0_), channel_id=1, source_target_pairs={{0,2},{1,3},{2,0},{3,1},{4,6},{5,7},{6,4},{7,5},{8,10},{9,11},{10,... | collective-permute-start | bytes 786440 | tf_op jit(solution)/shard_map/ppermute | solution.py:35
  131.0 4.4 %collective-permute-start.24 = (bf16[64,2048]{1,0:T(8,128)(2,1)S(1)}, bf16[64,2048]{1,0:T(8,128)(2,1)S(1)}, u32[]{:S(2)}, u32[]{:S(2)}) collective-permute-start(bf16[64,2048]{1,0:T(8,128)(2,1)S(1)} %get-tuple-element.243.refs_0_), channel_id=1, source_target_pairs={{2,4},{3,5},{4,2},{5,3},{0,1},{1,0},{6,7},{7,6},{10,12},{11,13},{1... | collective-permute-start | bytes 786440 | tf_op jit(solution)/shard_map/ppermute | solution.py:40
  135.4 8.7 %collective-permute-start.27 = (bf16[64,2048]{1,0:T(8,128)(2,1)S(1)}, bf16[64,2048]{1,0:T(8,128)(2,1)S(1)}, u32[]{:S(2)}, u32[]{:S(2)}) collective-permute-start(bf16[64,2048]{1,0:T(8,128)(2,1)S(1)} %broadcast_select_fusion.1), channel_id=1, source_target_pairs={{0,2},{1,3},{2,0},{3,1},{4,6},{5,7},{6,4},{7,5},{8,10},{9,11},{10,... | collective-permute-start | bytes 786440 | tf_op jit(solution)/shard_map/ppermute | solution.py:35
  137.6 6.6 %collective-permute-start.26 = (bf16[64,2048]{1,0:T(8,128)(2,1)S(1)}, bf16[64,2048]{1,0:T(8,128)(2,1)S(1)}, u32[]{:S(2)}, u32[]{:S(2)}) collective-permute-start(bf16[64,2048]{1,0:T(8,128)(2,1)S(1)} %collective-permute-done.25.refs_1_), channel_id=1, source_target_pairs={{2,4},{3,5},{4,2},{5,3},{0,1},{1,0},{6,7},{7,6},{10,12},{11,13},{1... | collective-permute-start | bytes 786440 | tf_op jit(solution)/shard_map/ppermute | solution.py:40
  144.3 7.9 %collective-permute-start.29 = (bf16[64,2048]{1,0:T(8,128)(2,1)S(1)}, bf16[64,2048]{1,0:T(8,128)(2,1)S(1)}, u32[]{:S(2)}, u32[]{:S(2)}) collective-permute-start(bf16[64,2048]{1,0:T(8,128)(2,1)S(1)} %broadcast_select_fusion), channel_id=1, source_target_pairs={{0,2},{1,3},{2,0},{3,1},{4,6},{5,7},{6,4},{7,5},{8,10},{9,11},{10,... | collective-permute-start | bytes 786440 | tf_op jit(solution)/shard_map/ppermute | solution.py:35
  146.1 6.1 %collective-permute-start.28 = (bf16[64,2048]{1,0:T(8,128)(2,1)S(1)}, bf16[64,2048]{1,0:T(8,128)(2,1)S(1)}, u32[]{:S(2)}, u32[]{:S(2)}) collective-permute-start(bf16[64,2048]{1,0:T(8,128)(2,1)S(1)} %add_convert_fusion.5), channel_id=1, source_target_pairs={{2,4},{3,5},{4,2},{5,3},{0,1},{1,0},{6,7},{7,6},{10,12},{11,13},{1... | collective-permute-start | bytes 786440 | tf_op jit(solution)/shard_map/ppermute | solution.py:40
  152.2 9.7 %collective-permute-start.30 = (bf16[64,2048]{1,0:T(8,128)(2,1)S(1)}, bf16[64,2048]{1,0:T(8,128)(2,1)S(1)}, u32[]{:S(2)}, u32[]{:S(2)}) collective-permute-start(bf16[64,2048]{1,0:T(8,128)(2,1)S(1)} %add_convert_fusion.4), channel_id=1, source_target_pairs={{2,4},{3,5},{4,2},{5,3},{0,1},{1,0},{6,7},{7,6},{10,12},{11,13},{1... | collective-permute-start | bytes 786440 | tf_op jit(solution)/shard_map/ppermute | solution.py:40
  152.4 9.6 %collective-permute-start.31 = (bf16[64,2048]{1,0:T(8,128)(2,1)S(1)}, bf16[64,2048]{1,0:T(8,128)(2,1)S(1)}, u32[]{:S(2)}, u32[]{:S(2)}) collective-permute-start(bf16[64,2048]{1,0:T(8,128)(2,1)S(1)} %fusion.2), channel_id=1, source_target_pairs={{0,2},{1,3},{2,0},{3,1},{4,6},{5,7},{6,4},{7,5},{8,10},{9,11},{10,... | collective-permute-start | bytes 786440 | tf_op jit(solution)/shard_map/ppermute | solution.py:35
  162.0 7.6 %collective-permute-start.32 = (bf16[64,2048]{1,0:T(8,128)(2,1)S(1)}, bf16[64,2048]{1,0:T(8,128)(2,1)S(1)}, u32[]{:S(2)}, u32[]{:S(2)}) collective-permute-start(bf16[64,2048]{1,0:T(8,128)(2,1)S(1)} %get-tuple-element.228), channel_id=1, source_target_pairs={{0,2},{1,3},{2,0},{3,1},{4,6},{5,7},{6,4},{7,5},{8,10},{9,11},{10,... | collective-permute-start | bytes 786440 | tf_op jit(solution)/shard_map/ppermute | solution.py:35
  162.1 1.2 collective-permute-start.33
  163.3 3.6 %collective-permute-start.34 = (f32[8,128]{1,0:T(8,128)S(1)}, f32[8,128]{1,0:T(8,128)S(1)}, u32[]{:S(2)}, u32[]{:S(2)}) collective-permute-start(f32[8,128]{1,0:T(8,128)S(1)} %add.94), channel_id=1, source_target_pairs={{0,8},{8,0},{16,24},{24,16},{1,9},{9,1},{17,25},{25,17},{2,10},{10... | collective-permute-start | bytes 12296 | tf_op jit(solution)/shard_map/ppermute | solution.py:219
  164.8 9.4 %collective-permute-start.37 = (bf16[64,2048]{1,0:T(8,128)(2,1)S(1)}, bf16[64,2048]{1,0:T(8,128)(2,1)S(1)}, u32[]{:S(2)}, u32[]{:S(2)}) collective-permute-start(bf16[64,2048]{1,0:T(8,128)(2,1)S(1)} %get-tuple-element.236), channel_id=1, source_target_pairs={{0,2},{1,3},{2,0},{3,1},{4,6},{5,7},{6,4},{7,5},{8,10},{9,11},{10,... | collective-permute-start | bytes 786440 | tf_op jit(solution)/shard_map/ppermute | solution.py:35
  169.6 4.5 %collective-permute-start.36 = (bf16[64,2048]{1,0:T(8,128)(2,1)S(1)}, bf16[64,2048]{1,0:T(8,128)(2,1)S(1)}, u32[]{:S(2)}, u32[]{:S(2)}) collective-permute-start(bf16[64,2048]{1,0:T(8,128)(2,1)S(1)} %add_convert_fusion.2), channel_id=1, source_target_pairs={{2,4},{3,5},{4,2},{5,3},{0,1},{1,0},{6,7},{7,6},{10,12},{11,13},{1... | collective-permute-start | bytes 786440 | tf_op jit(solution)/shard_map/ppermute | solution.py:40
  169.7 8.6 %collective-permute-start.35 = (f32[8,128]{1,0:T(8,128)S(1)}, f32[8,128]{1,0:T(8,128)S(1)}, u32[]{:S(2)}, u32[]{:S(2)}) collective-permute-start(f32[8,128]{1,0:T(8,128)S(1)} %add.95), channel_id=1, source_target_pairs={{0,16},{8,24},{16,0},{24,8},{1,17},{9,25},{17,1},{25,9},{2,18},{10... | collective-permute-start | bytes 12296 | tf_op jit(solution)/shard_map/ppermute | solution.py:219
  174.2 4.1 %collective-permute-start.38 = (bf16[64,2048]{1,0:T(8,128)(2,1)S(1)}, bf16[64,2048]{1,0:T(8,128)(2,1)S(1)}, u32[]{:S(2)}, u32[]{:S(2)}) collective-permute-start(bf16[64,2048]{1,0:T(8,128)(2,1)S(1)} %add_convert_fusion.1), channel_id=1, source_target_pairs={{2,4},{3,5},{4,2},{5,3},{0,1},{1,0},{6,7},{7,6},{10,12},{11,13},{1... | collective-permute-start | bytes 786440 | tf_op jit(solution)/shard_map/ppermute | solution.py:40
  174.4 8.8 %collective-permute-start.39 = (bf16[64,2048]{1,0:T(8,128)(2,1)S(1)}, bf16[64,2048]{1,0:T(8,128)(2,1)S(1)}, u32[]{:S(2)}, u32[]{:S(2)}) collective-permute-start(bf16[64,2048]{1,0:T(8,128)(2,1)S(1)} %fusion.3), channel_id=1, source_target_pairs={{0,2},{1,3},{2,0},{3,1},{4,6},{5,7},{6,4},{7,5},{8,10},{9,11},{10,... | collective-permute-start | bytes 786440 | tf_op jit(solution)/shard_map/ppermute | solution.py:35
  (9 other events, 11.3 us)

commit v10 on v9

--- a/solution.py
+++ b/solution.py
@@ -328,7 +328,7 @@
         side_hop(load_b),
         forward((*a_parts, a_far_end), everyone),
     )
-    b_far, b_near_end = slot(inner_hop(b_side), both_ways(pa[3], b_near))
+    b_far, b_near_end = (inner_hop(b_side), both_ways(pa[3], b_near))
     sa_far = add_rows(pa[3], b_near_end[:, :width])
     sa_side, b_far_end = slot(inner_hop(sa_far), both_ways(pa[2], b_far))
     sa_near = add_rows(pa[2], b_far_end[:, :width])
@@ -345,7 +345,7 @@
     states_b = [*states_b, *rest_b]
     far, near_end = slot(inner_hop(side), both_ways(pb[3], near))
     s_far = add_rows(pb[3], near_end)
-    s_side, far_end = slot(inner_hop(s_far), both_ways(pb[2], far))
+    s_side, far_end = (inner_hop(s_far), both_ways(pb[2], far))
     s_near = add_rows(pb[2], far_end)
     ja_parts = (ja, side, near, near_end, far, far_end)
     last, came, (sum_a, squares_a) = slot(
@@ -361,7 +361,7 @@
     )
     far, near_end = slot(inner_hop(side), both_ways(ga[3], near))
     s_far = add_rows(ga[3], near_end)
-    s_side, far_end = slot(inner_hop(s_far), both_ways(ga[2], far))
+    s_side, far_end = (inner_hop(s_far), both_ways(ga[2], far))
     s_near = add_rows(ga[2], far_end)
     jb_parts = (jb, side, near, near_end, far, far_end)
     last, came, (gb, squares_b) = slot(

time: 185 us -> 181 us (0.978)
  waiting for transfers between devices: 81.3 us -> 70.9 us
  starting transfers between devices: 42.5 us -> 48.9 us
    ppermute x18, waiting for transfers between devices: 78.4 us -> 68 us  [side_hop(): return lax.ppermute(rows, 'expert', both_cores(SIDE_PAIRS))]
    ppermute x18, starting transfers between devices: 37.7 us -> 43.8 us  [side_hop(): return lax.ppermute(rows, 'expert', both_cores(SIDE_PAIRS))]
  transfers between devices with their start and end apart: 40 -> 40, of which waited for: 20 -> 20; matrix products, arithmetic and copies ran while one was open for 2% -> 2% of each run, Pallas kernels for 23% -> 24%
where the time goes in v10:
time: 181 us
  waiting for transfers between devices  70.9 us (39%)
  starting transfers between devices  48.9 us (27%)
  Pallas kernels  44.4 us (25%)
  local copies, waits for them, and re-layouts  12.9 us (7%)
  other arithmetic  3.29 us (2%)
    ppermute x18, waiting for transfers between devices, side_hop(): return lax.ppermute(rows, 'expert', both_cores(SIDE_PAIRS))  68 us
    ppermute x18, starting transfers between devices, side_hop(): return lax.ppermute(rows, 'expert', both_cores(SIDE_PAIRS))  43.8 us
    pallas_call x6, Pallas kernels, kernel_call(): pl.pallas_call(kernel, in_specs=[pl.BlockSpec(memory_space=pltpu.SMEM)] +...  36.8 us
    unnamed x34, local copies, waits for them, and re-layouts  11.4 us
    pallas_call x4, Pallas kernels, load(): pl.pallas_call(functools.partial(load_kernel, len(arrays)), in_specs=[pl....  5.89 us
  transfers between devices with their start and end apart: 40, of which 20 were waited for; matrix products, arithmetic and copies ran while one was open for 2% of the time, Pallas kernels for 24%

profile of v10, /device:TPU:0, one launch (start us, length us, event | category | flops | bytes accessed | tf_op | source)
XLA Modules:
  0.0 180.9 jit_solution(8777282049034720953)
XLA Ops:
  1.8 1.4 fusion.8
  3.3 2.6 %collective-permute-start.1 = (bf16[64,4224]{1,0:T(8,128)(2,1)S(1)}, bf16[64,4224]{1,0:T(8,128)(2,1)S(1)}, u32[]{:S(2)}, u32[]{:S(2)}) collective-permute-start(bf16[64,4224]{1,0:T(8,128)(2,1)S(1)} %pad_maximum_fusion.refs_0_), channel_id=1, source_target_pairs={{0,2},{1,3},{2,0},{3,1},{4,6},{5,7},{6,4},{7,5},{8,10},{9,11},{10,... | collective-permute-start | bytes 1622024 | tf_op jit(solution)/shard_map/ppermute | solution.py:35
  6.2 1.9 %copy-done.5 = bf16[1,2048,768]{2,1,0:T(8,128)(2,1)S(1)} copy-done((bf16[1,2048,768]{2,1,0:T(8,128)(2,1)S(1)}, bf16[1,2048,768]{2,1,0:T(8,128)(2,1)}, u32[]{:S(2)}) %copy-start.5) | copy-done | bytes 3145752
  8.1 1.9 %copy-done.6 = bf16[1,768,2048]{2,1,0:T(8,128)(2,1)S(1)} copy-done((bf16[1,768,2048]{2,1,0:T(8,128)(2,1)S(1)}, bf16[1,768,2048]{2,1,0:T(8,128)(2,1)}, u32[]{:S(2)}) %copy-start.6) | copy-done | bytes 3145752
  10.6 1.6 copy-done
  12.2 1.7 copy-done.2
  14.8 4.1 %collective-permute-done.1.refs_1_ = bf16[64,4224]{1,0:T(8,128)(2,1)S(1)} collective-permute-done((bf16[64,4224]{1,0:T(8,128)(2,1)S(1)}, bf16[64,4224]{1,0:T(8,128)(2,1)S(1)}, u32[]{:S(2)}, u32[]{:S(2)}) %collective-permute-start.1) | collective-permute-done | bytes 540704 | tf_op jit(solution)/shard_map/ppermute | solution.py:35
  18.9 2.9 %collective-permute-start.2 = (bf16[64,4224]{1,0:T(8,128)(2,1)S(1)}, bf16[64,4224]{1,0:T(8,128)(2,1)S(1)}, u32[]{:S(2)}, u32[]{:S(2)}) collective-permute-start(bf16[64,4224]{1,0:T(8,128)(2,1)S(1)} %collective-permute-done.refs_2_), channel_id=1, source_target_pairs={{0,2},{1,3},{2,0},{3,1},{4,6},{5,7},{6,4},{7,5},{8,10},{9,11},{10,... | collective-permute-start | bytes 1622024 | tf_op jit(solution)/shard_map/ppermute | solution.py:35
  24.4 9.6 %collective-permute-done.2.refs_0_ = bf16[64,4224]{1,0:T(8,128)(2,1)S(1)} collective-permute-done((bf16[64,4224]{1,0:T(8,128)(2,1)S(1)}, bf16[64,4224]{1,0:T(8,128)(2,1)S(1)}, u32[]{:S(2)}, u32[]{:S(2)}) %collective-permute-start.2) | collective-permute-done | bytes 540704 | tf_op jit(solution)/shard_map/ppermute | solution.py:35
  34.8 1.8 collective-permute-start.7
  38.9 3.9 %load.6 = (bf16[1,2048,768]{2,1,0:T(8,128)(2,1)S(1)}, bf16[1,2048,768]{2,1,0:T(8,128)(2,1)S(1)}, bf16[1,768,2048]{2,1,0:T(8,128)(2,1)S(1)}) custom-call(bf16[1,2048,768]{2,1,0:T(8,128)(2,1)} %collective-permute-done.4.refs_0_, bf16[1,2048,768]{2,1,0:T(8,128)(2,1)} %collective-permute-done.5.refs_1_, bf16[1,768,2048]{2,1,0:T(8,128)(2,1)} %collective-permute-done.6.refs_2_), custom_call_target="tpu_custom_call" | custom-call | tf_op jit(solution)/shard_map/load/pallas_call | solution.py:206
  42.8 5.7 %collective-permute-done.7.refs_5_ = bf16[64,4224]{1,0:T(8,128)(2,1)} collective-permute-done((bf16[64,4224]{1,0:T(8,128)(2,1)}, bf16[64,4224]{1,0:T(8,128)(2,1)}, u32[]{:S(2)}, u32[]{:S(2)}) %collective-permute-start.7) | collective-permute-done | bytes 540704 | tf_op jit(solution)/shard_map/ppermute | solution.py:35
  48.5 1.5 collective-permute-start.9
  50.0 10.5 %forward.3 = (f32[64,2048]{1,0:T(8,128)S(1)}, bf16[64,2048]{1,0:T(8,128)(2,1)S(1)}, bf16[64,2048]{1,0:T(8,128)(2,1)S(1)}, bf16[64,2048]{1,0:T(8,128)(2,1)S(1)}, ...) custom-call(s32[3]{0:T(128)S(1)} %pad_add_fusion.where_ref, ...), custom_call_target="tpu_custom_call" | custom-call | flops 8053063680 | tf_op jit(solution)/shard_map/forward/pallas_call | solution.py:160
  61.2 3.3 %collective-permute-start.10 = (bf16[64,4224]{1,0:T(8,128)(2,1)S(1)}, bf16[64,4224]{1,0:T(8,128)(2,1)S(1)}, u32[]{:S(2)}, u32[]{:S(2)}) collective-permute-start(bf16[64,4224]{1,0:T(8,128)(2,1)S(1)} %pad_maximum_fusion.2), channel_id=1, source_target_pairs={{0,2},{1,3},{2,0},{3,1},{4,6},{5,7},{6,4},{7,5},{8,10},{9,11},{10,... | collective-permute-start | bytes 1622024 | tf_op jit(solution)/shard_map/ppermute | solution.py:35
  64.6 9.8 %collective-permute-start.13 = (bf16[64,4224]{1,0:T(8,128)(2,1)S(1)}, bf16[64,4224]{1,0:T(8,128)(2,1)S(1)}, u32[]{:S(2)}, u32[]{:S(2)}) collective-permute-start(bf16[64,4224]{1,0:T(8,128)(2,1)S(1)} %pad_maximum_fusion.3), channel_id=1, source_target_pairs={{0,2},{1,3},{2,0},{3,1},{4,6},{5,7},{6,4},{7,5},{8,10},{9,11},{10,... | collective-permute-start | bytes 1622024 | tf_op jit(solution)/shard_map/ppermute | solution.py:35
  74.4 3.3 %collective-permute-done.10.refs_3_ = bf16[64,4224]{1,0:T(8,128)(2,1)S(1)} collective-permute-done((bf16[64,4224]{1,0:T(8,128)(2,1)S(1)}, bf16[64,4224]{1,0:T(8,128)(2,1)S(1)}, u32[]{:S(2)}, u32[]{:S(2)}) %collective-permute-start.10) | collective-permute-done | bytes 540704 | tf_op jit(solution)/shard_map/ppermute | solution.py:35
  77.8 1.5 collective-permute-done.11
  79.3 8.1 %collective-permute-done.13.refs_5_ = bf16[64,4224]{1,0:T(8,128)(2,1)S(1)} collective-permute-done((bf16[64,4224]{1,0:T(8,128)(2,1)S(1)}, bf16[64,4224]{1,0:T(8,128)(2,1)S(1)}, u32[]{:S(2)}, u32[]{:S(2)}) %collective-permute-start.13) | collective-permute-done | bytes 540704 | tf_op jit(solution)/shard_map/ppermute | solution.py:35
  87.7 1.4 collective-permute-start.15
  89.1 5.5 %forward.4 = (f32[256,2048]{1,0:T(8,128)S(1)}, f32[256,768]{1,0:T(8,128)S(1)}, f32[256,768]{1,0:T(8,128)S(1)}) custom-call(s32[3]{0:T(128)S(1)} %pad_add_fusion.where_ref, bf16[64,4224]{1,0:T(8,128)(2,1)S(1)} %copy-done.7, bf16[64,4224]{1,0:T(8,128)(2,1)S(1)} %collective-permute-done.9.refs_1_, bf16[64,4224]{1,0:T(8,128)(2,1)S(1)} %collective-permute-done.8.refs_2_, ...), custom_call_target="tpu_custom_call" | custom-call | flops 4026531840 | tf_op jit(solution)/shard_map/forward/pallas_call | solution.py:160
  94.6 1.8 %collective-permute-done.15 = bf16[64,2048]{1,0:T(8,128)(2,1)S(1)} collective-permute-done((bf16[64,2048]{1,0:T(8,128)(2,1)S(1)}, bf16[64,2048]{1,0:T(8,128)(2,1)S(1)}, u32[]{:S(2)}, u32[]{:S(2)}) %collective-permute-start.15) | collective-permute-done | bytes 262176 | tf_op jit(solution)/shard_map/ppermute | solution.py:35
  96.9 5.3 %forward.5 = (f32[64,2048]{1,0:T(8,128)S(1)}, bf16[64,2048]{1,0:T(8,128)(2,1)S(1)}, bf16[64,2048]{1,0:T(8,128)(2,1)S(1)}, bf16[64,2048]{1,0:T(8,128)(2,1)S(1)}, ...) custom-call(s32[3]{0:T(128)S(1)} %pad_add_fusion.where_ref, bf16[64,4224]{1,0:T(8,128)(2,1)S(1)} %copy-done.7, ...), custom_call_target="tpu_custom_call" | custom-call | flops 4026531840 | tf_op jit(solution)/shard_map/forward/pallas_call | solution.py:160
  102.2 2.3 %collective-permute-done.17.refs_1_ = bf16[64,2048]{1,0:T(8,128)(2,1)S(1)} collective-permute-done((bf16[64,2048]{1,0:T(8,128)(2,1)S(1)}, bf16[64,2048]{1,0:T(8,128)(2,1)S(1)}, u32[]{:S(2)}, u32[]{:S(2)}) %collective-permute-start.17) | collective-permute-done | bytes 262176 | tf_op jit(solution)/shard_map/ppermute | solution.py:35
  104.6 1.8 collective-permute-start.19
  106.4 5.3 %collective-permute-done.19.refs_3_ = bf16[64,2048]{1,0:T(8,128)(2,1)S(1)} collective-permute-done((bf16[64,2048]{1,0:T(8,128)(2,1)S(1)}, bf16[64,2048]{1,0:T(8,128)(2,1)S(1)}, u32[]{:S(2)}, u32[]{:S(2)}) %collective-permute-start.19) | collective-permute-done | bytes 262176 | tf_op jit(solution)/shard_map/ppermute | solution.py:35
  111.7 1.8 collective-permute-start.20
  113.7 4.5 %collective-permute-done.20.refs_5_ = bf16[64,2048]{1,0:T(8,128)(2,1)S(1)} collective-permute-done((bf16[64,2048]{1,0:T(8,128)(2,1)S(1)}, bf16[64,2048]{1,0:T(8,128)(2,1)S(1)}, u32[]{:S(2)}, u32[]{:S(2)}) %collective-permute-start.20) | collective-permute-done | bytes 262176 | tf_op jit(solution)/shard_map/ppermute | solution.py:35
  118.4 3.2 %collective-permute-start.23 = (bf16[64,2048]{1,0:T(8,128)(2,1)S(1)}, bf16[64,2048]{1,0:T(8,128)(2,1)S(1)}, u32[]{:S(2)}, u32[]{:S(2)}) collective-permute-start(bf16[64,2048]{1,0:T(8,128)(2,1)S(1)} %fusion.1), channel_id=1, source_target_pairs={{0,2},{1,3},{2,0},{3,1},{4,6},{5,7},{6,4},{7,5},{8,10},{9,11},{10,... | collective-permute-start | bytes 786440 | tf_op jit(solution)/shard_map/ppermute | solution.py:35
  121.6 4.2 %backward.3 = (f32[256,2048]{1,0:T(8,128)S(1)}, f32[8,128]{1,0:T(8,128)S(1)}) custom-call(s32[3]{0:T(128)S(1)} %pad_add_fusion.where_ref, bf16[64,2048]{1,0:T(8,128)(2,1)S(1)} %fusion.4.refs_0_, bf16[64,2048]{1,0:T(8,128)(2,1)S(1)} %collective-permute-done.17.refs_1_, bf16[64,2048]{1,0:T(8,128)(2,1)S(1)} %collective-permute-done.16.refs_2_, ...), custom_call_target="tpu_custom_call" | custom-call | flops 2415919104 | tf_op jit(solution)/shard_map/backward/pallas_call | solution.py:160
  125.9 1.3 collective-permute-done.23
  128.2 4.3 %backward.4 = (f32[64,2048]{1,0:T(8,128)S(1)}, bf16[64,2048]{1,0:T(8,128)(2,1)S(1)}, bf16[64,2048]{1,0:T(8,128)(2,1)S(1)}, bf16[64,2048]{1,0:T(8,128)(2,1)S(1)}) custom-call(s32[3]{0:T(128)S(1)} %pad_add_fusion.where_ref, bf16[64,2048]{1,0:T(8,128)(2,1)S(1)} %fusion.4.refs_0_, bf16[64,2048]{1,0:T(8,128)(2,1)S(1)} %collective-permute-done.17.refs_1_, ...), custom_call_target="tpu_custom_call" | custom-call | flops 2415919104 | tf_op jit(solution)/shard_map/backward/pallas_call | solution.py:160
  132.5 1.5 collective-permute-done.25.refs_1_
  134.1 1.8 %collective-permute-start.27 = (bf16[64,2048]{1,0:T(8,128)(2,1)S(1)}, bf16[64,2048]{1,0:T(8,128)(2,1)S(1)}, u32[]{:S(2)}, u32[]{:S(2)}) collective-permute-start(bf16[64,2048]{1,0:T(8,128)(2,1)S(1)} %broadcast_select_fusion.1), channel_id=1, source_target_pairs={{0,2},{1,3},{2,0},{3,1},{4,6},{5,7},{6,4},{7,5},{8,10},{9,11},{10,... | collective-permute-start | bytes 786440 | tf_op jit(solution)/shard_map/ppermute | solution.py:35
  135.9 5.5 %collective-permute-done.27.refs_3_ = bf16[64,2048]{1,0:T(8,128)(2,1)S(1)} collective-permute-done((bf16[64,2048]{1,0:T(8,128)(2,1)S(1)}, bf16[64,2048]{1,0:T(8,128)(2,1)S(1)}, u32[]{:S(2)}, u32[]{:S(2)}) %collective-permute-start.27) | collective-permute-done | bytes 262176 | tf_op jit(solution)/shard_map/ppermute | solution.py:35
  141.4 1.8 collective-permute-start.28
  143.3 4.5 %collective-permute-done.28.refs_5_ = bf16[64,2048]{1,0:T(8,128)(2,1)S(1)} collective-permute-done((bf16[64,2048]{1,0:T(8,128)(2,1)S(1)}, bf16[64,2048]{1,0:T(8,128)(2,1)S(1)}, u32[]{:S(2)}, u32[]{:S(2)}) %collective-permute-start.28) | collective-permute-done | bytes 262176 | tf_op jit(solution)/shard_map/ppermute | solution.py:35
  148.1 3.0 %collective-permute-start.31 = (bf16[64,2048]{1,0:T(8,128)(2,1)S(1)}, bf16[64,2048]{1,0:T(8,128)(2,1)S(1)}, u32[]{:S(2)}, u32[]{:S(2)}) collective-permute-start(bf16[64,2048]{1,0:T(8,128)(2,1)S(1)} %fusion.2), channel_id=1, source_target_pairs={{0,2},{1,3},{2,0},{3,1},{4,6},{5,7},{6,4},{7,5},{8,10},{9,11},{10,... | collective-permute-start | bytes 786440 | tf_op jit(solution)/shard_map/ppermute | solution.py:35
  151.1 7.0 %backward.5 = (f32[64,2048]{1,0:T(8,128)S(1)}, bf16[64,2048]{1,0:T(8,128)(2,1)S(1)}, bf16[64,2048]{1,0:T(8,128)(2,1)S(1)}, bf16[64,2048]{1,0:T(8,128)(2,1)S(1)}, f32[8,128]{1,0:T(8,128)S(1)}) custom-call(s32[3]{0:T(128)S(1)} %pad_add_fusion.where_ref, bf16[64,2048]{1,0:T(8,128)(2,1)S(1)} %get-tuple-element.231.refs_0_, ...), custom_call_target="tpu_custom_call" | custom-call | flops 4831838208 | tf_op jit(solution)/shard_map/backward/pallas_call | solution.py:160
  158.3 1.2 collective-permute-done.33
  159.5 1.5 collective-permute-start.34
  160.9 1.9 %collective-permute-start.37 = (bf16[64,2048]{1,0:T(8,128)(2,1)S(1)}, bf16[64,2048]{1,0:T(8,128)(2,1)S(1)}, u32[]{:S(2)}, u32[]{:S(2)}) collective-permute-start(bf16[64,2048]{1,0:T(8,128)(2,1)S(1)} %get-tuple-element.224), channel_id=1, source_target_pairs={{0,2},{1,3},{2,0},{3,1},{4,6},{5,7},{6,4},{7,5},{8,10},{9,11},{10,... | collective-permute-start | bytes 786440 | tf_op jit(solution)/shard_map/ppermute | solution.py:35
  163.1 2.4 %collective-permute-done.32 = bf16[64,2048]{1,0:T(8,128)(2,1)S(1)} collective-permute-done((bf16[64,2048]{1,0:T(8,128)(2,1)S(1)}, bf16[64,2048]{1,0:T(8,128)(2,1)S(1)}, u32[]{:S(2)}, u32[]{:S(2)}) %collective-permute-start.32) | collective-permute-done | bytes 262176 | tf_op jit(solution)/shard_map/ppermute | solution.py:35
  165.6 1.6 collective-permute-start.35
  167.2 3.0 %collective-permute-done.37 = bf16[64,2048]{1,0:T(8,128)(2,1)S(1)} collective-permute-done((bf16[64,2048]{1,0:T(8,128)(2,1)S(1)}, bf16[64,2048]{1,0:T(8,128)(2,1)S(1)}, u32[]{:S(2)}, u32[]{:S(2)}) %collective-permute-start.37) | collective-permute-done | bytes 262176 | tf_op jit(solution)/shard_map/ppermute | solution.py:35
  170.4 3.7 %collective-permute-start.39 = (bf16[64,2048]{1,0:T(8,128)(2,1)S(1)}, bf16[64,2048]{1,0:T(8,128)(2,1)S(1)}, u32[]{:S(2)}, u32[]{:S(2)}) collective-permute-start(bf16[64,2048]{1,0:T(8,128)(2,1)S(1)} %fusion.3), channel_id=1, source_target_pairs={{0,2},{1,3},{2,0},{3,1},{4,6},{5,7},{6,4},{7,5},{8,10},{9,11},{10,... | collective-permute-start | bytes 786440 | tf_op jit(solution)/shard_map/ppermute | solution.py:35
  174.4 4.8 %collective-permute-done.39.side = bf16[64,2048]{1,0:T(8,128)(2,1)S(1)} collective-permute-done((bf16[64,2048]{1,0:T(8,128)(2,1)S(1)}, bf16[64,2048]{1,0:T(8,128)(2,1)S(1)}, u32[]{:S(2)}, u32[]{:S(2)}) %collective-permute-start.39) | collective-permute-done | bytes 262176 | tf_op jit(solution)/shard_map/ppermute | solution.py:35
  179.2 1.7 output.1
  (115 shorter events, 13.7 us)
Async XLA Ops:
  0.0 34.7 %collective-permute-start.4 = (bf16[1,2048,768]{2,1,0:T(8,128)(2,1)}, bf16[1,2048,768]{2,1,0:T(8,128)(2,1)}, u32[]{:S(2)}, u32[]{:S(2)}) collective-permute-start(bf16[1,2048,768]{2,1,0:T(8,128)(2,1)} %refs_0_.1), channel_id=1, source_target_pairs={{0,1},{1,0},{2,3},{3,2},{4,5},{5,4},{6,7},{7,6},{8,9},{9,8},{10,11... | collective-permute-start | bytes 9437192 | tf_op jit(solution)/shard_map/ppermute | solution.py:312
  0.5 34.3 %collective-permute-start.5 = (bf16[1,2048,768]{2,1,0:T(8,128)(2,1)}, bf16[1,2048,768]{2,1,0:T(8,128)(2,1)}, u32[]{:S(2)}, u32[]{:S(2)}) collective-permute-start(bf16[1,2048,768]{2,1,0:T(8,128)(2,1)} %refs_1_.1), channel_id=1, source_target_pairs={{0,1},{1,0},{2,3},{3,2},{4,5},{5,4},{6,7},{7,6},{8,9},{9,8},{10,11... | collective-permute-start | bytes 9437192 | tf_op jit(solution)/shard_map/ppermute | solution.py:312
  0.5 34.2 %collective-permute-start.6 = (bf16[1,768,2048]{2,1,0:T(8,128)(2,1)}, bf16[1,768,2048]{2,1,0:T(8,128)(2,1)}, u32[]{:S(2)}, u32[]{:S(2)}) collective-permute-start(bf16[1,768,2048]{2,1,0:T(8,128)(2,1)} %refs_2_.1), channel_id=1, source_target_pairs={{0,1},{1,0},{2,3},{3,2},{4,5},{5,4},{6,7},{7,6},{8,9},{9,8},{10,11... | collective-permute-start | bytes 9437192 | tf_op jit(solution)/shard_map/ppermute | solution.py:312
  1.8 4.3 %copy-start.4 = (bf16[1,2048,768]{2,1,0:T(8,128)(2,1)S(1)}, bf16[1,2048,768]{2,1,0:T(8,128)(2,1)}, u32[]{:S(2)}) copy-start(bf16[1,2048,768]{2,1,0:T(8,128)(2,1)} %refs_0_.1) | copy-start | bytes 9437188
  3.3 15.6 %collective-permute-start.1 = (bf16[64,4224]{1,0:T(8,128)(2,1)S(1)}, bf16[64,4224]{1,0:T(8,128)(2,1)S(1)}, u32[]{:S(2)}, u32[]{:S(2)}) collective-permute-start(bf16[64,4224]{1,0:T(8,128)(2,1)S(1)} %pad_maximum_fusion.refs_0_), channel_id=1, source_target_pairs={{0,2},{1,3},{2,0},{3,1},{4,6},{5,7},{6,4},{7,5},{8,10},{9,11},{10,... | collective-permute-start | bytes 1622024 | tf_op jit(solution)/shard_map/ppermute | solution.py:35
  5.9 12.9 %collective-permute-start = (bf16[64,4224]{1,0:T(8,128)(2,1)S(1)}, bf16[64,4224]{1,0:T(8,128)(2,1)S(1)}, u32[]{:S(2)}, u32[]{:S(2)}) collective-permute-start(bf16[64,4224]{1,0:T(8,128)(2,1)S(1)} %pad_maximum_fusion.refs_0_), channel_id=1, source_target_pairs={{2,4},{3,5},{4,2},{5,3},{0,1},{1,0},{6,7},{7,6},{10,12},{11,13},{1... | collective-permute-start | bytes 1622024 | tf_op jit(solution)/shard_map/ppermute | solution.py:40
  18.9 15.0 %collective-permute-start.2 = (bf16[64,4224]{1,0:T(8,128)(2,1)S(1)}, bf16[64,4224]{1,0:T(8,128)(2,1)S(1)}, u32[]{:S(2)}, u32[]{:S(2)}) collective-permute-start(bf16[64,4224]{1,0:T(8,128)(2,1)S(1)} %collective-permute-done.refs_2_), channel_id=1, source_target_pairs={{0,2},{1,3},{2,0},{3,1},{4,6},{5,7},{6,4},{7,5},{8,10},{9,11},{10,... | collective-permute-start | bytes 1622024 | tf_op jit(solution)/shard_map/ppermute | solution.py:35
  21.8 13.0 %collective-permute-start.3 = (bf16[64,4224]{1,0:T(8,128)(2,1)S(1)}, bf16[64,4224]{1,0:T(8,128)(2,1)}, u32[]{:S(2)}, u32[]{:S(2)}) collective-permute-start(bf16[64,4224]{1,0:T(8,128)(2,1)S(1)} %collective-permute-done.1.refs_1_), channel_id=1, source_target_pairs={{2,4},{3,5},{4,2},{5,3},{0,1},{1,0},{6,7},{7,6},{10,12},{11,13},{1... | collective-permute-start | bytes 1622024 | tf_op jit(solution)/shard_map/ppermute | solution.py:40
  34.8 13.7 %collective-permute-start.7 = (bf16[64,4224]{1,0:T(8,128)(2,1)}, bf16[64,4224]{1,0:T(8,128)(2,1)}, u32[]{:S(2)}, u32[]{:S(2)}) collective-permute-start(bf16[64,4224]{1,0:T(8,128)(2,1)} %collective-permute-done.3.refs_1_), channel_id=1, source_target_pairs={{0,2},{1,3},{2,0},{3,1},{4,6},{5,7},{6,4},{7,5},{8,10},{9,11},{10,... | collective-permute-start | bytes 1622024 | tf_op jit(solution)/shard_map/ppermute | solution.py:35
  38.8 9.7 %copy-start.7 = (bf16[64,4224]{1,0:T(8,128)(2,1)S(1)}, bf16[64,4224]{1,0:T(8,128)(2,1)}, u32[]{:S(2)}) copy-start(bf16[64,4224]{1,0:T(8,128)(2,1)} %pad_maximum_fusion.1.refs_0_) | copy-start | bytes 1622020
  38.8 11.2 %copy-start.1 = (bf16[1,2048,768]{2,1,0:T(8,128)(2,1)S(1)}, bf16[1,2048,768]{2,1,0:T(8,128)(2,1)}, u32[]{:S(2)}) copy-start(bf16[1,2048,768]{2,1,0:T(8,128)(2,1)} %copy-done) | copy-start | bytes 9437188
  38.8 11.2 %copy-start.3 = (bf16[1,768,2048]{2,1,0:T(8,128)(2,1)S(1)}, bf16[1,768,2048]{2,1,0:T(8,128)(2,1)}, u32[]{:S(2)}) copy-start(bf16[1,768,2048]{2,1,0:T(8,128)(2,1)} %copy-done.2) | copy-start | bytes 9437188
  38.8 11.2 %copy-start.11 = (bf16[64,4224]{1,0:T(8,128)(2,1)S(1)}, bf16[64,4224]{1,0:T(8,128)(2,1)}, u32[]{:S(2)}) copy-start(bf16[64,4224]{1,0:T(8,128)(2,1)} %copy-done.10) | copy-start | bytes 1622020
  38.9 11.2 %copy-start.13 = (bf16[64,4224]{1,0:T(8,128)(2,1)S(1)}, bf16[64,4224]{1,0:T(8,128)(2,1)}, u32[]{:S(2)}) copy-start(bf16[64,4224]{1,0:T(8,128)(2,1)} %copy-done.12) | copy-start | bytes 1622020
  38.9 11.2 %copy-start.15 = (bf16[64,4224]{1,0:T(8,128)(2,1)S(1)}, bf16[64,4224]{1,0:T(8,128)(2,1)}, u32[]{:S(2)}) copy-start(bf16[64,4224]{1,0:T(8,128)(2,1)} %copy-done.14) | copy-start | bytes 1622020
  48.5 12.4 %collective-permute-start.9 = (bf16[64,4224]{1,0:T(8,128)(2,1)S(1)}, bf16[64,4224]{1,0:T(8,128)(2,1)S(1)}, u32[]{:S(2)}, u32[]{:S(2)}) collective-permute-start(bf16[64,4224]{1,0:T(8,128)(2,1)S(1)} %copy-done.7), channel_id=1, source_target_pairs={{0,2},{1,3},{2,0},{3,1},{4,6},{5,7},{6,4},{7,5},{8,10},{9,11},{10,... | collective-permute-start | bytes 1622024 | tf_op jit(solution)/shard_map/ppermute | solution.py:35
  50.0 10.9 %collective-permute-start.8 = (bf16[64,4224]{1,0:T(8,128)(2,1)S(1)}, bf16[64,4224]{1,0:T(8,128)(2,1)S(1)}, u32[]{:S(2)}, u32[]{:S(2)}) collective-permute-start(bf16[64,4224]{1,0:T(8,128)(2,1)S(1)} %copy-done.7), channel_id=1, source_target_pairs={{2,4},{3,5},{4,2},{5,3},{0,1},{1,0},{6,7},{7,6},{10,12},{11,13},{1... | collective-permute-start | bytes 1622024 | tf_op jit(solution)/shard_map/ppermute | solution.py:40
  61.0 3.5 %collective-permute-start.12 = (bf16[64,4224]{1,0:T(8,128)(2,1)S(1)}, bf16[64,4224]{1,0:T(8,128)(2,1)S(1)}, u32[]{:S(2)}, u32[]{:S(2)}) collective-permute-start(bf16[64,4224]{1,0:T(8,128)(2,1)S(1)} %collective-permute-done.9.refs_1_), channel_id=1, source_target_pairs={{2,4},{3,5},{4,2},{5,3},{0,1},{1,0},{6,7},{7,6},{10,12},{11,13},{1... | collective-permute-start | bytes 1622024 | tf_op jit(solution)/shard_map/ppermute | solution.py:40
  61.2 16.5 %collective-permute-start.10 = (bf16[64,4224]{1,0:T(8,128)(2,1)S(1)}, bf16[64,4224]{1,0:T(8,128)(2,1)S(1)}, u32[]{:S(2)}, u32[]{:S(2)}) collective-permute-start(bf16[64,4224]{1,0:T(8,128)(2,1)S(1)} %pad_maximum_fusion.2), channel_id=1, source_target_pairs={{0,2},{1,3},{2,0},{3,1},{4,6},{5,7},{6,4},{7,5},{8,10},{9,11},{10,... | collective-permute-start | bytes 1622024 | tf_op jit(solution)/shard_map/ppermute | solution.py:35
  64.6 22.8 %collective-permute-start.13 = (bf16[64,4224]{1,0:T(8,128)(2,1)S(1)}, bf16[64,4224]{1,0:T(8,128)(2,1)S(1)}, u32[]{:S(2)}, u32[]{:S(2)}) collective-permute-start(bf16[64,4224]{1,0:T(8,128)(2,1)S(1)} %pad_maximum_fusion.3), channel_id=1, source_target_pairs={{0,2},{1,3},{2,0},{3,1},{4,6},{5,7},{6,4},{7,5},{8,10},{9,11},{10,... | collective-permute-start | bytes 1622024 | tf_op jit(solution)/shard_map/ppermute | solution.py:35
  77.7 1.6 collective-permute-start.11
  87.5 7.1 %collective-permute-start.14 = (bf16[64,2048]{1,0:T(8,128)(2,1)S(1)}, bf16[64,2048]{1,0:T(8,128)(2,1)S(1)}, u32[]{:S(2)}, u32[]{:S(2)}) collective-permute-start(bf16[64,2048]{1,0:T(8,128)(2,1)S(1)} %add_convert_fusion.10), channel_id=1, source_target_pairs={{2,4},{3,5},{4,2},{5,3},{0,1},{1,0},{6,7},{7,6},{10,12},{11,13},{1... | collective-permute-start | bytes 786440 | tf_op jit(solution)/shard_map/ppermute | solution.py:40
  87.6 8.8 %copy-start.16 = (bf16[128,2048]{1,0:T(8,128)(2,1)S(1)}, bf16[128,2048]{1,0:T(8,128)(2,1)}, u32[]{:S(2)}) copy-start(bf16[128,2048]{1,0:T(8,128)(2,1)} %param.8) | copy-start | bytes 1572868
  87.7 8.8 %collective-permute-start.15 = (bf16[64,2048]{1,0:T(8,128)(2,1)S(1)}, bf16[64,2048]{1,0:T(8,128)(2,1)S(1)}, u32[]{:S(2)}, u32[]{:S(2)}) collective-permute-start(bf16[64,2048]{1,0:T(8,128)(2,1)S(1)} %fusion), channel_id=1, source_target_pairs={{0,2},{1,3},{2,0},{3,1},{4,6},{5,7},{6,4},{7,5},{8,10},{9,11},{10,... | collective-permute-start | bytes 786440 | tf_op jit(solution)/shard_map/ppermute | solution.py:35
  96.6 8.0 %collective-permute-start.17 = (bf16[64,2048]{1,0:T(8,128)(2,1)S(1)}, bf16[64,2048]{1,0:T(8,128)(2,1)S(1)}, u32[]{:S(2)}, u32[]{:S(2)}) collective-permute-start(bf16[64,2048]{1,0:T(8,128)(2,1)S(1)} %fusion.4.refs_0_), channel_id=1, source_target_pairs={{0,2},{1,3},{2,0},{3,1},{4,6},{5,7},{6,4},{7,5},{8,10},{9,11},{10,... | collective-permute-start | bytes 786440 | tf_op jit(solution)/shard_map/ppermute | solution.py:35
  96.9 7.6 %collective-permute-start.16 = (bf16[64,2048]{1,0:T(8,128)(2,1)S(1)}, bf16[64,2048]{1,0:T(8,128)(2,1)S(1)}, u32[]{:S(2)}, u32[]{:S(2)}) collective-permute-start(bf16[64,2048]{1,0:T(8,128)(2,1)S(1)} %fusion.4.refs_0_), channel_id=1, source_target_pairs={{2,4},{3,5},{4,2},{5,3},{0,1},{1,0},{6,7},{7,6},{10,12},{11,13},{1... | collective-permute-start | bytes 786440 | tf_op jit(solution)/shard_map/ppermute | solution.py:40
  104.6 7.1 %collective-permute-start.19 = (bf16[64,2048]{1,0:T(8,128)(2,1)S(1)}, bf16[64,2048]{1,0:T(8,128)(2,1)S(1)}, u32[]{:S(2)}, u32[]{:S(2)}) collective-permute-start(bf16[64,2048]{1,0:T(8,128)(2,1)S(1)} %broadcast_select_fusion.3), channel_id=1, source_target_pairs={{0,2},{1,3},{2,0},{3,1},{4,6},{5,7},{6,4},{7,5},{8,10},{9,11},{10,... | collective-permute-start | bytes 786440 | tf_op jit(solution)/shard_map/ppermute | solution.py:35
  106.4 5.3 %collective-permute-start.18 = (bf16[64,2048]{1,0:T(8,128)(2,1)S(1)}, bf16[64,2048]{1,0:T(8,128)(2,1)S(1)}, u32[]{:S(2)}, u32[]{:S(2)}) collective-permute-start(bf16[64,2048]{1,0:T(8,128)(2,1)S(1)} %collective-permute-done.17.refs_1_), channel_id=1, source_target_pairs={{2,4},{3,5},{4,2},{5,3},{0,1},{1,0},{6,7},{7,6},{10,12},{11,13},{1... | collective-permute-start | bytes 786440 | tf_op jit(solution)/shard_map/ppermute | solution.py:40
  111.7 6.4 %collective-permute-start.20 = (bf16[64,2048]{1,0:T(8,128)(2,1)S(1)}, bf16[64,2048]{1,0:T(8,128)(2,1)S(1)}, u32[]{:S(2)}, u32[]{:S(2)}) collective-permute-start(bf16[64,2048]{1,0:T(8,128)(2,1)S(1)} %broadcast_select_fusion.2), channel_id=1, source_target_pairs={{0,2},{1,3},{2,0},{3,1},{4,6},{5,7},{6,4},{7,5},{8,10},{9,11},{10,... | collective-permute-start | bytes 786440 | tf_op jit(solution)/shard_map/ppermute | solution.py:35
  113.6 4.7 %collective-permute-start.22 = (bf16[64,2048]{1,0:T(8,128)(2,1)S(1)}, bf16[64,2048]{1,0:T(8,128)(2,1)S(1)}, u32[]{:S(2)}, u32[]{:S(2)}) collective-permute-start(bf16[64,2048]{1,0:T(8,128)(2,1)S(1)} %add_convert_fusion.7), channel_id=1, source_target_pairs={{2,4},{3,5},{4,2},{5,3},{0,1},{1,0},{6,7},{7,6},{10,12},{11,13},{1... | collective-permute-start | bytes 786440 | tf_op jit(solution)/shard_map/ppermute | solution.py:40
  118.2 7.6 %collective-permute-start.21 = (bf16[64,2048]{1,0:T(8,128)(2,1)S(1)}, bf16[64,2048]{1,0:T(8,128)(2,1)S(1)}, u32[]{:S(2)}, u32[]{:S(2)}) collective-permute-start(bf16[64,2048]{1,0:T(8,128)(2,1)S(1)} %add_convert_fusion.8), channel_id=1, source_target_pairs={{2,4},{3,5},{4,2},{5,3},{0,1},{1,0},{6,7},{7,6},{10,12},{11,13},{1... | collective-permute-start | bytes 786440 | tf_op jit(solution)/shard_map/ppermute | solution.py:40
  118.4 8.8 %collective-permute-start.23 = (bf16[64,2048]{1,0:T(8,128)(2,1)S(1)}, bf16[64,2048]{1,0:T(8,128)(2,1)S(1)}, u32[]{:S(2)}, u32[]{:S(2)}) collective-permute-start(bf16[64,2048]{1,0:T(8,128)(2,1)S(1)} %fusion.1), channel_id=1, source_target_pairs={{0,2},{1,3},{2,0},{3,1},{4,6},{5,7},{6,4},{7,5},{8,10},{9,11},{10,... | collective-permute-start | bytes 786440 | tf_op jit(solution)/shard_map/ppermute | solution.py:35
  127.3 6.7 %collective-permute-start.25 = (bf16[64,2048]{1,0:T(8,128)(2,1)S(1)}, bf16[64,2048]{1,0:T(8,128)(2,1)S(1)}, u32[]{:S(2)}, u32[]{:S(2)}) collective-permute-start(bf16[64,2048]{1,0:T(8,128)(2,1)S(1)} %get-tuple-element.231.refs_0_), channel_id=1, source_target_pairs={{0,2},{1,3},{2,0},{3,1},{4,6},{5,7},{6,4},{7,5},{8,10},{9,11},{10,... | collective-permute-start | bytes 786440 | tf_op jit(solution)/shard_map/ppermute | solution.py:35
  128.2 5.8 %collective-permute-start.24 = (bf16[64,2048]{1,0:T(8,128)(2,1)S(1)}, bf16[64,2048]{1,0:T(8,128)(2,1)S(1)}, u32[]{:S(2)}, u32[]{:S(2)}) collective-permute-start(bf16[64,2048]{1,0:T(8,128)(2,1)S(1)} %get-tuple-element.231.refs_0_), channel_id=1, source_target_pairs={{2,4},{3,5},{4,2},{5,3},{0,1},{1,0},{6,7},{7,6},{10,12},{11,13},{1... | collective-permute-start | bytes 786440 | tf_op jit(solution)/shard_map/ppermute | solution.py:40
  134.1 7.3 %collective-permute-start.27 = (bf16[64,2048]{1,0:T(8,128)(2,1)S(1)}, bf16[64,2048]{1,0:T(8,128)(2,1)S(1)}, u32[]{:S(2)}, u32[]{:S(2)}) collective-permute-start(bf16[64,2048]{1,0:T(8,128)(2,1)S(1)} %broadcast_select_fusion.1), channel_id=1, source_target_pairs={{0,2},{1,3},{2,0},{3,1},{4,6},{5,7},{6,4},{7,5},{8,10},{9,11},{10,... | collective-permute-start | bytes 786440 | tf_op jit(solution)/shard_map/ppermute | solution.py:35
  135.9 5.5 %collective-permute-start.26 = (bf16[64,2048]{1,0:T(8,128)(2,1)S(1)}, bf16[64,2048]{1,0:T(8,128)(2,1)S(1)}, u32[]{:S(2)}, u32[]{:S(2)}) collective-permute-start(bf16[64,2048]{1,0:T(8,128)(2,1)S(1)} %collective-permute-done.25.refs_1_), channel_id=1, source_target_pairs={{2,4},{3,5},{4,2},{5,3},{0,1},{1,0},{6,7},{7,6},{10,12},{11,13},{1... | collective-permute-start | bytes 786440 | tf_op jit(solution)/shard_map/ppermute | solution.py:40
  141.4 6.4 %collective-permute-start.28 = (bf16[64,2048]{1,0:T(8,128)(2,1)S(1)}, bf16[64,2048]{1,0:T(8,128)(2,1)S(1)}, u32[]{:S(2)}, u32[]{:S(2)}) collective-permute-start(bf16[64,2048]{1,0:T(8,128)(2,1)S(1)} %broadcast_select_fusion), channel_id=1, source_target_pairs={{0,2},{1,3},{2,0},{3,1},{4,6},{5,7},{6,4},{7,5},{8,10},{9,11},{10,... | collective-permute-start | bytes 786440 | tf_op jit(solution)/shard_map/ppermute | solution.py:35
  143.3 4.7 %collective-permute-start.30 = (bf16[64,2048]{1,0:T(8,128)(2,1)S(1)}, bf16[64,2048]{1,0:T(8,128)(2,1)S(1)}, u32[]{:S(2)}, u32[]{:S(2)}) collective-permute-start(bf16[64,2048]{1,0:T(8,128)(2,1)S(1)} %add_convert_fusion.4), channel_id=1, source_target_pairs={{2,4},{3,5},{4,2},{5,3},{0,1},{1,0},{6,7},{7,6},{10,12},{11,13},{1... | collective-permute-start | bytes 786440 | tf_op jit(solution)/shard_map/ppermute | solution.py:40
  147.9 10.2 %collective-permute-start.29 = (bf16[64,2048]{1,0:T(8,128)(2,1)S(1)}, bf16[64,2048]{1,0:T(8,128)(2,1)S(1)}, u32[]{:S(2)}, u32[]{:S(2)}) collective-permute-start(bf16[64,2048]{1,0:T(8,128)(2,1)S(1)} %add_convert_fusion.5), channel_id=1, source_target_pairs={{2,4},{3,5},{4,2},{5,3},{0,1},{1,0},{6,7},{7,6},{10,12},{11,13},{1... | collective-permute-start | bytes 786440 | tf_op jit(solution)/shard_map/ppermute | solution.py:40
  148.1 10.0 %collective-permute-start.31 = (bf16[64,2048]{1,0:T(8,128)(2,1)S(1)}, bf16[64,2048]{1,0:T(8,128)(2,1)S(1)}, u32[]{:S(2)}, u32[]{:S(2)}) collective-permute-start(bf16[64,2048]{1,0:T(8,128)(2,1)S(1)} %fusion.2), channel_id=1, source_target_pairs={{0,2},{1,3},{2,0},{3,1},{4,6},{5,7},{6,4},{7,5},{8,10},{9,11},{10,... | collective-permute-start | bytes 786440 | tf_op jit(solution)/shard_map/ppermute | solution.py:35
  158.1 7.3 %collective-permute-start.32 = (bf16[64,2048]{1,0:T(8,128)(2,1)S(1)}, bf16[64,2048]{1,0:T(8,128)(2,1)S(1)}, u32[]{:S(2)}, u32[]{:S(2)}) collective-permute-start(bf16[64,2048]{1,0:T(8,128)(2,1)S(1)} %get-tuple-element.216), channel_id=1, source_target_pairs={{0,2},{1,3},{2,0},{3,1},{4,6},{5,7},{6,4},{7,5},{8,10},{9,11},{10,... | collective-permute-start | bytes 786440 | tf_op jit(solution)/shard_map/ppermute | solution.py:35
  158.2 1.2 collective-permute-start.33
  159.5 3.6 %collective-permute-start.34 = (f32[8,128]{1,0:T(8,128)S(1)}, f32[8,128]{1,0:T(8,128)S(1)}, u32[]{:S(2)}, u32[]{:S(2)}) collective-permute-start(f32[8,128]{1,0:T(8,128)S(1)} %add.94), channel_id=1, source_target_pairs={{0,8},{8,0},{16,24},{24,16},{1,9},{9,1},{17,25},{25,17},{2,10},{10... | collective-permute-start | bytes 12296 | tf_op jit(solution)/shard_map/ppermute | solution.py:219
  160.9 9.2 %collective-permute-start.37 = (bf16[64,2048]{1,0:T(8,128)(2,1)S(1)}, bf16[64,2048]{1,0:T(8,128)(2,1)S(1)}, u32[]{:S(2)}, u32[]{:S(2)}) collective-permute-start(bf16[64,2048]{1,0:T(8,128)(2,1)S(1)} %get-tuple-element.224), channel_id=1, source_target_pairs={{0,2},{1,3},{2,0},{3,1},{4,6},{5,7},{6,4},{7,5},{8,10},{9,11},{10,... | collective-permute-start | bytes 786440 | tf_op jit(solution)/shard_map/ppermute | solution.py:35
  165.5 4.7 %collective-permute-start.36 = (bf16[64,2048]{1,0:T(8,128)(2,1)S(1)}, bf16[64,2048]{1,0:T(8,128)(2,1)S(1)}, u32[]{:S(2)}, u32[]{:S(2)}) collective-permute-start(bf16[64,2048]{1,0:T(8,128)(2,1)S(1)} %add_convert_fusion.2), channel_id=1, source_target_pairs={{2,4},{3,5},{4,2},{5,3},{0,1},{1,0},{6,7},{7,6},{10,12},{11,13},{1... | collective-permute-start | bytes 786440 | tf_op jit(solution)/shard_map/ppermute | solution.py:40
  165.6 8.7 %collective-permute-start.35 = (f32[8,128]{1,0:T(8,128)S(1)}, f32[8,128]{1,0:T(8,128)S(1)}, u32[]{:S(2)}, u32[]{:S(2)}) collective-permute-start(f32[8,128]{1,0:T(8,128)S(1)} %add.95), channel_id=1, source_target_pairs={{0,16},{8,24},{16,0},{24,8},{1,17},{9,25},{17,1},{25,9},{2,18},{10... | collective-permute-start | bytes 12296 | tf_op jit(solution)/shard_map/ppermute | solution.py:219
  170.3 4.1 %collective-permute-start.38 = (bf16[64,2048]{1,0:T(8,128)(2,1)S(1)}, bf16[64,2048]{1,0:T(8,128)(2,1)S(1)}, u32[]{:S(2)}, u32[]{:S(2)}) collective-permute-start(bf16[64,2048]{1,0:T(8,128)(2,1)S(1)} %add_convert_fusion.1), channel_id=1, source_target_pairs={{2,4},{3,5},{4,2},{5,3},{0,1},{1,0},{6,7},{7,6},{10,12},{11,13},{1... | collective-permute-start | bytes 786440 | tf_op jit(solution)/shard_map/ppermute | solution.py:40
  170.4 8.8 %collective-permute-start.39 = (bf16[64,2048]{1,0:T(8,128)(2,1)S(1)}, bf16[64,2048]{1,0:T(8,128)(2,1)S(1)}, u32[]{:S(2)}, u32[]{:S(2)}) collective-permute-start(bf16[64,2048]{1,0:T(8,128)(2,1)S(1)} %fusion.3), channel_id=1, source_target_pairs={{0,2},{1,3},{2,0},{3,1},{4,6},{5,7},{6,4},{7,5},{8,10},{9,11},{10,... | collective-permute-start | bytes 786440 | tf_op jit(solution)/shard_map/ppermute | solution.py:35
  (9 other events, 11.3 us)
